TPU v7x, 32 devices: a whole 2x2x4 slice. The times are simulated.
32 devices in a mesh: head: 4 (over y, x), blk: 8 (over z, core).
Axes of the slice: x: 2, y: 2, z: 4, core: 2. Of those that a mesh axis runs over, the one named last changes fastest.
Arguments:
- tokens: bfloat16 [4096, 2048], P(('blk', 'head')), may hold values from -8 to 8
- segments: int32 [4096], P(('blk', 'head')), may hold values from 0 to 32, as said below
- cotangent: bfloat16 [4096, 2048], P(('blk', 'head')), may hold values from -8 to 8
- first_gain: bfloat16 [2048], P(('head', 'blk')), may hold values from 0.5 to 1.5
- first_shift: bfloat16 [2048], P(('head', 'blk')), may hold values from -1.25 to 1.25
- query_proj: bfloat16 [2048, 2048], P(('head', 'blk')), may hold values from -0.1875 to 0.1875
- key_proj: bfloat16 [2048, 2048], P(('head', 'blk')), may hold values from -0.1875 to 0.1875
- value_proj: bfloat16 [2048, 2048], P(('head', 'blk')), may hold values from -0.125 to 0.125
- query_bias: bfloat16 [2048], P(('head', 'blk')), may hold values from -1.75 to 1.75
- value_bias: bfloat16 [2048], P(('head', 'blk')), may hold values from -0.625 to 0.625
- out_proj: bfloat16 [2048, 2048], P(('head', 'blk')), may hold values from -0.5 to 0.5
- out_bias: bfloat16 [2048], P(('head', 'blk')), may hold values from -1.75 to 1.75
- second_gain: bfloat16 [2048], P(('head', 'blk')), may hold values from 0.5 to 1.5
- second_shift: bfloat16 [2048], P(('head', 'blk')), may hold values from -1.25 to 1.25
- up_proj: bfloat16 [2048, 8192], P(('head', 'blk')), may hold values from -0.125 to 0.125
- up_bias: bfloat16 [8192], P(('head', 'blk')), may hold values from -1.75 to 1.75
- down_proj: bfloat16 [8192, 2048], P(('head', 'blk')), may hold values from -0.0625 to 0.0625
- down_bias: bfloat16 [2048], P(('head', 'blk')), may hold values from -1.75 to 1.75
Outputs:
- output: bfloat16 [4096, 2048], P(('blk', 'head'))
- tokens_grad: bfloat16 [4096, 2048], P(('blk', 'head'))
- first_gain_grad: float32 [2048], P(('head', 'blk'))
- first_shift_grad: float32 [2048], P(('head', 'blk'))
- query_proj_grad: float32 [2048, 2048], P(('head', 'blk'))
- key_proj_grad: float32 [2048, 2048], P(('head', 'blk'))
- value_proj_grad: float32 [2048, 2048], P(('head', 'blk'))
- query_bias_grad: float32 [2048], P(('head', 'blk'))
- value_bias_grad: float32 [2048], P(('head', 'blk'))
- out_proj_grad: float32 [2048, 2048], P(('head', 'blk'))
- out_bias_grad: float32 [2048], P(('head', 'blk'))
- second_gain_grad: float32 [2048], P(('head', 'blk'))
- second_shift_grad: float32 [2048], P(('head', 'blk'))
- up_proj_grad: float32 [2048, 8192], P(('head', 'blk'))
- up_bias_grad: float32 [8192], P(('head', 'blk'))
- down_proj_grad: float32 [8192, 2048], P(('head', 'blk'))
- down_bias_grad: float32 [2048], P(('head', 'blk'))
Inputs may be any that keep to these rules, and one draw needn't show every extreme that they name: `segments`: segment numbers never fall along the sequence, and every number from 0 to 32 names at least one token. Document 16 begins within the first 512 tokens and ends within the last 512 tokens; the documents numbered below it lie before it and those numbered above it after it.
All inputs are finite; a program needn't handle non-finite values.
Results may differ from a plain program's by a relative error of at most 0.017.
Values may be sent and summed in bfloat16 or wider, within the bound.
No kernel may reach another device: no remote copies, remote signals or barrier semaphores. Data moves between devices by JAX's collectives and lax.ppermute only.
A program may use at most 384 MiB of HBM per device.

v0:
```python
import jax
import jax.numpy as jnp
from jax import lax
from jax.sharding import PartitionSpec as P

D = 2048
H = 16
DH = 128


norm_epsilon = 1e-05
masked_fill = -1e30


def from_behind(x, axis, by):
    length = lax.axis_size(axis)
    return lax.ppermute(x, axis, [(i, (i + by) % length) for i in range(length)])


def matmul(left, right):
    return jnp.dot(left, right, preferred_element_type=jnp.float32)


def cross_rows(left, right):
    return lax.dot_general(
        left, right, (((0,), (0,)), ((), ())), preferred_element_type=jnp.float32
    )


def times_transposed(left, right):
    return lax.dot_general(
        left, right, (((1,), (1,)), ((), ())), preferred_element_type=jnp.float32
    )


def norm_parts(values):
    row_mean = jnp.mean(values, axis=-1, keepdims=True)
    centered = values - row_mean
    row_var = jnp.mean(centered * centered, axis=-1, keepdims=True)
    inverse = lax.rsqrt(row_var + norm_epsilon)
    return (centered * inverse, inverse)


def norm_back(grad_out, normal_hat, inverse, gain):
    scaled_grad = grad_out * gain
    return inverse * (
        scaled_grad
        - jnp.mean(scaled_grad, axis=-1, keepdims=True)
        - normal_hat * jnp.mean(scaled_grad * normal_hat, axis=-1, keepdims=True)
    )


def block_scores(query_heads, key_block, key_start, query_pos, query_seg, seq_ids, scaling):
    length = key_block.shape[0]
    key_pos = key_start + jnp.arange(length, dtype=jnp.int32)
    key_seg = lax.dynamic_slice_in_dim(seq_ids, key_start, length)
    allowed = (key_pos[None, :] <= query_pos[:, None]) & (key_seg[None, :] == query_seg[:, None])
    raw_scores = jnp.einsum(
        "qhd,khd->hqk", query_heads, key_block, preferred_element_type=jnp.float32
    )
    return jnp.where(allowed[None], scaling * raw_scores, masked_fill)


def over_keys(step_fn, running, portion):
    length = portion.shape[0]
    sub_rows = length
    while sub_rows > 2048 and sub_rows % 2 == 0:
        sub_rows = sub_rows // 2

    def inner_step(sub_index, current):
        window = lax.dynamic_slice_in_dim(portion, sub_index * sub_rows, sub_rows, 0)
        return step_fn(current, window, sub_index * sub_rows)

    return lax.fori_loop(0, length // sub_rows, inner_step, running)


def local(
    tokens,
    segments,
    cotangent,
    first_gain,
    first_shift,
    query_proj,
    key_proj,
    value_proj,
    query_bias,
    value_bias,
    out_proj,
    out_bias,
    second_gain,
    second_shift,
    up_proj,
    up_bias,
    down_proj,
    down_bias,
):
    head_ways = lax.axis_size("head")
    blocks = lax.axis_size("blk")
    my_block = lax.axis_index("blk")
    tok_rows = tokens.shape[0]
    local_heads = H // head_ways
    block_rows = tok_rows * head_ways
    scaling = DH ** (-0.5)
    (
        seg_pieces,
        gain_first,
        shift_first,
        query_full,
        key_full,
        value_full,
        qbias_full,
        vbias_full,
        out_full,
        obias_full,
        gain_second,
        shift_second,
        up_full,
        upbias_full,
        down_full,
        downbias_full,
    ) = (
        lax.all_gather(segments.astype(jnp.bfloat16), ("head", "blk"), axis=0, tiled=True),
        lax.all_gather(first_gain, ("head", "blk"), axis=0, tiled=True),
        lax.all_gather(first_shift, ("head", "blk"), axis=0, tiled=True),
        lax.all_gather(query_proj, ("head", "blk"), axis=0, tiled=True),
        lax.all_gather(key_proj, ("head", "blk"), axis=0, tiled=True),
        lax.all_gather(value_proj, ("head", "blk"), axis=0, tiled=True),
        lax.all_gather(query_bias, ("head", "blk"), axis=0, tiled=True),
        lax.all_gather(value_bias, ("head", "blk"), axis=0, tiled=True),
        lax.all_gather(out_proj, ("head", "blk"), axis=0, tiled=True),
        lax.all_gather(out_bias, ("head", "blk"), axis=0, tiled=True),
        lax.all_gather(second_gain, ("head", "blk"), axis=0, tiled=True),
        lax.all_gather(second_shift, ("head", "blk"), axis=0, tiled=True),
        lax.all_gather(up_proj, ("head", "blk"), axis=0, tiled=True),
        lax.all_gather(up_bias, ("head", "blk"), axis=0, tiled=True),
        lax.all_gather(down_proj, ("head", "blk"), axis=0, tiled=True),
        lax.all_gather(down_bias, ("head", "blk"), axis=0, tiled=True),
    )
    seq_ids = (
        seg_pieces.reshape(head_ways, blocks, tok_rows)
        .transpose(1, 0, 2)
        .reshape(-1)
        .astype(jnp.float32)
    )
    query_pos = my_block * block_rows + jnp.arange(block_rows, dtype=jnp.int32)
    query_seg = lax.dynamic_slice_in_dim(seq_ids, my_block * block_rows, block_rows)
    tokens_f = tokens.astype(jnp.float32)
    hat_first, inv_first = norm_parts(tokens_f)
    normed = (hat_first * gain_first.astype(jnp.float32) + shift_first.astype(jnp.float32)).astype(
        jnp.bfloat16
    )
    query_tok = (matmul(normed, query_full) + qbias_full.astype(jnp.float32)).astype(jnp.bfloat16)
    key_tok = matmul(normed, key_full).astype(jnp.bfloat16)
    value_tok = (matmul(normed, value_full) + vbias_full.astype(jnp.float32)).astype(jnp.bfloat16)
    head_shape = (tok_rows, H, DH)
    query_heads, key_heads, value_heads = (
        lax.all_to_all(
            query_tok.reshape(head_shape), "head", split_axis=1, concat_axis=0, tiled=True
        ),
        lax.all_to_all(
            key_tok.reshape(head_shape), "head", split_axis=1, concat_axis=0, tiled=True
        ),
        lax.all_to_all(
            value_tok.reshape(head_shape), "head", split_axis=1, concat_axis=0, tiled=True
        ),
    )

    def stat_step(running, key_block, key_start):
        row_high, row_total = running
        scores = block_scores(
            query_heads, key_block, key_start, query_pos, query_seg, seq_ids, scaling
        )
        new_high = jnp.maximum(row_high, jnp.max(scores, axis=-1))
        weights = jnp.exp(scores - new_high[..., None])
        row_total = row_total * jnp.exp(row_high - new_high) + jnp.sum(weights, axis=-1)
        return (new_high, row_total)

    stats_start = (
        jnp.full((local_heads, block_rows), masked_fill, jnp.float32),
        jnp.zeros((local_heads, block_rows), jnp.float32),
    )
    row_high, row_total = over_keys(
        stat_step, stats_start, lax.all_gather(key_heads, "blk", axis=0, tiled=True)
    )
    log_total = row_high + jnp.log(row_total)
    key_value = jnp.stack([key_heads, value_heads], axis=1)

    def out_step(running, pair_block, key_start):
        scores = block_scores(
            query_heads, pair_block[:, 0], key_start, query_pos, query_seg, seq_ids, scaling
        )
        attn_prob = jnp.exp(scores - log_total[..., None]).astype(jnp.bfloat16)
        return running + jnp.einsum(
            "hqk,khd->qhd", attn_prob, pair_block[:, 1], preferred_element_type=jnp.float32
        )

    attn_heads = over_keys(
        out_step,
        jnp.zeros((block_rows, local_heads, DH), jnp.float32),
        lax.all_gather(key_value, "blk", axis=0, tiled=True),
    )
    mixed_back = lax.all_to_all(
        attn_heads.astype(jnp.bfloat16), "head", split_axis=0, concat_axis=1, tiled=True
    )
    mixed_tok = mixed_back.reshape(tok_rows, D)
    hidden = tokens_f + (matmul(mixed_tok, out_full) + obias_full.astype(jnp.float32))
    hat_second, inv_second = norm_parts(hidden)
    second = (
        hat_second * gain_second.astype(jnp.float32) + shift_second.astype(jnp.float32)
    ).astype(jnp.bfloat16)
    up_value = matmul(second, up_full) + upbias_full.astype(jnp.float32)
    active = jax.nn.gelu(up_value, approximate=False).astype(jnp.bfloat16)
    result = hidden + (matmul(active, down_full) + downbias_full.astype(jnp.float32))
    output = result.astype(jnp.bfloat16)
    upstream = cotangent.astype(jnp.float32)
    down_grad, downbias_grad = (
        lax.psum_scatter(
            cross_rows(active, cotangent), ("head", "blk"), scatter_dimension=0, tiled=True
        ),
        lax.psum_scatter(
            jnp.sum(upstream, axis=0), ("head", "blk"), scatter_dimension=0, tiled=True
        ),
    )
    d_active = times_transposed(cotangent, down_full)
    gelu_slope = (
        0.5 * (1.0 + lax.erf(up_value * 0.7071067811865476))
        + up_value * jnp.exp(-0.5 * up_value * up_value) * 0.3989422804014327
    )
    d_upper = (d_active * gelu_slope).astype(jnp.bfloat16)
    up_grad = cross_rows(second, d_upper)
    upbias_grad = jnp.sum(d_upper.astype(jnp.float32), axis=0)
    d_second = times_transposed(d_upper, up_full)
    gain2_grad = jnp.sum(d_second * hat_second, axis=0)
    shift2_grad = jnp.sum(d_second, axis=0)
    d_hidden = upstream + norm_back(
        d_second, hat_second, inv_second, gain_second.astype(jnp.float32)
    )
    mlp_sums = (
        lax.psum_scatter(gain2_grad, ("head", "blk"), scatter_dimension=0, tiled=True),
        lax.psum_scatter(shift2_grad, ("head", "blk"), scatter_dimension=0, tiled=True),
        lax.psum_scatter(up_grad, ("head", "blk"), scatter_dimension=0, tiled=True),
        lax.psum_scatter(upbias_grad, ("head", "blk"), scatter_dimension=0, tiled=True),
    )
    d_branch = d_hidden.astype(jnp.bfloat16)
    out_grad = cross_rows(mixed_tok, d_branch)
    outbias_grad = jnp.sum(d_branch.astype(jnp.float32), axis=0)
    d_mixed = times_transposed(d_branch, out_full).astype(jnp.bfloat16)
    d_heads = lax.all_to_all(
        d_mixed.reshape(head_shape), "head", split_axis=1, concat_axis=0, tiled=True
    )
    row_delta = jnp.einsum("qhd,qhd->hq", d_heads.astype(jnp.float32), attn_heads)
    all_pairs = lax.all_gather(key_value, "blk", axis=0, tiled=True)

    def cycle_step(step_index, running):
        travel_grads, query_grad = running
        source = (my_block - step_index) % blocks
        key_start = source * block_rows
        visiting = lax.dynamic_slice_in_dim(all_pairs, key_start, block_rows, 0)
        scores = block_scores(
            query_heads, visiting[:, 0], key_start, query_pos, query_seg, seq_ids, scaling
        )
        attn_prob = jnp.exp(scores - log_total[..., None])
        prob_low = attn_prob.astype(jnp.bfloat16)
        d_probs = jnp.einsum(
            "qhd,khd->hqk", d_heads, visiting[:, 1], preferred_element_type=jnp.float32
        )
        d_scores = (attn_prob * (d_probs - row_delta[..., None])).astype(jnp.bfloat16)
        query_grad = query_grad + scaling * jnp.einsum(
            "hqk,khd->qhd", d_scores, visiting[:, 0], preferred_element_type=jnp.float32
        )
        key_grad = scaling * jnp.einsum(
            "hqk,qhd->khd", d_scores, query_heads, preferred_element_type=jnp.float32
        )
        value_grad = jnp.einsum(
            "hqk,qhd->khd", prob_low, d_heads, preferred_element_type=jnp.float32
        )
        travel_grads = travel_grads + jnp.stack([key_grad, value_grad], axis=1)
        travel_grads = from_behind(travel_grads.astype(jnp.bfloat16), "blk", 1).astype(
            travel_grads.dtype
        )
        return (travel_grads, query_grad)

    cycle_start = (
        jnp.zeros((block_rows, 2, local_heads, DH), jnp.float32),
        jnp.zeros((block_rows, local_heads, DH), jnp.float32),
    )
    travel_grads, query_grad = lax.fori_loop(0, blocks, cycle_step, cycle_start)
    dq_tok, dk_tok, dv_tok = (
        lax.all_to_all(
            query_grad.astype(jnp.bfloat16), "head", split_axis=0, concat_axis=1, tiled=True
        ),
        lax.all_to_all(
            travel_grads[:, 0].astype(jnp.bfloat16), "head", split_axis=0, concat_axis=1, tiled=True
        ),
        lax.all_to_all(
            travel_grads[:, 1].astype(jnp.bfloat16), "head", split_axis=0, concat_axis=1, tiled=True
        ),
    )
    dq_tok = dq_tok.reshape(tok_rows, D)
    dk_tok = dk_tok.reshape(tok_rows, D)
    dv_tok = dv_tok.reshape(tok_rows, D)
    query_grad_w = cross_rows(normed, dq_tok)
    key_grad_w = cross_rows(normed, dk_tok)
    value_grad_w = cross_rows(normed, dv_tok)
    qbias_grad = jnp.sum(dq_tok.astype(jnp.float32), axis=0)
    vbias_grad = jnp.sum(dv_tok.astype(jnp.float32), axis=0)
    d_normed = (
        times_transposed(dq_tok, query_full)
        + times_transposed(dk_tok, key_full)
        + times_transposed(dv_tok, value_full)
    )
    gain1_grad = jnp.sum(d_normed * hat_first, axis=0)
    shift1_grad = jnp.sum(d_normed, axis=0)
    tokens_grad = (
        d_hidden + norm_back(d_normed, hat_first, inv_first, gain_first.astype(jnp.float32))
    ).astype(jnp.bfloat16)
    attn_sums = (
        lax.psum_scatter(gain1_grad, ("head", "blk"), scatter_dimension=0, tiled=True),
        lax.psum_scatter(shift1_grad, ("head", "blk"), scatter_dimension=0, tiled=True),
        lax.psum_scatter(query_grad_w, ("head", "blk"), scatter_dimension=0, tiled=True),
        lax.psum_scatter(key_grad_w, ("head", "blk"), scatter_dimension=0, tiled=True),
        lax.psum_scatter(value_grad_w, ("head", "blk"), scatter_dimension=0, tiled=True),
        lax.psum_scatter(qbias_grad, ("head", "blk"), scatter_dimension=0, tiled=True),
        lax.psum_scatter(vbias_grad, ("head", "blk"), scatter_dimension=0, tiled=True),
        lax.psum_scatter(out_grad, ("head", "blk"), scatter_dimension=0, tiled=True),
        lax.psum_scatter(outbias_grad, ("head", "blk"), scatter_dimension=0, tiled=True),
    )
    return (
        output,
        tokens_grad,
        attn_sums[0],
        attn_sums[1],
        attn_sums[2],
        attn_sums[3],
        attn_sums[4],
        attn_sums[5],
        attn_sums[6],
        attn_sums[7],
        attn_sums[8],
        mlp_sums[0],
        mlp_sums[1],
        mlp_sums[2],
        mlp_sums[3],
        down_grad,
        downbias_grad,
    )


def solution(mesh):
    return jax.shard_map(
        local,
        mesh=mesh,
        in_specs=(
            P(("blk", "head"), None),
            P(("blk", "head")),
            P(("blk", "head"), None),
            P(("head", "blk")),
            P(("head", "blk")),
            P(("head", "blk"), None),
            P(("head", "blk"), None),
            P(("head", "blk"), None),
            P(("head", "blk")),
            P(("head", "blk")),
            P(("head", "blk"), None),
            P(("head", "blk")),
            P(("head", "blk")),
            P(("head", "blk")),
            P(("head", "blk"), None),
            P(("head", "blk")),
            P(("head", "blk"), None),
            P(("head", "blk")),
        ),
        out_specs=(
            P(("blk", "head"), None),
            P(("blk", "head"), None),
            P(("head", "blk")),
            P(("head", "blk")),
            P(("head", "blk"), None),
            P(("head", "blk"), None),
            P(("head", "blk"), None),
            P(("head", "blk")),
            P(("head", "blk")),
            P(("head", "blk"), None),
            P(("head", "blk")),
            P(("head", "blk")),
            P(("head", "blk")),
            P(("head", "blk"), None),
            P(("head", "blk")),
            P(("head", "blk"), None),
            P(("head", "blk")),
        ),
        check_vma=False,
    )
```

profile of v0, /device:TPU:8, one launch (start us, length us, event | category | flops | bytes accessed | tf_op | source)
XLA Modules:
  0.0 3483.7 jit_solution(9530366411711013884)
XLA Ops:
  16.2 41.6 %all-reduce.18 = (bf16[2048]{0:T(1024)(128)(2,1)S(1)}, bf16[2048]{0:T(1024)(128)(2,1)S(1)}, bf16[2048]{0:T(1024)(128)(2,1)S(1)}, bf16[2048]{0:T(1024)(128)(2,1)S...) all-reduce(bf16[2048]{0:T(1024)(128)(2,1)S(1)} %dynamic-update-slic, ...), channel_id=1, replica_groups=mesh['head'=4,'blk'=8] {'head','blk'}, use_global_device_ids=true, to_apply=%add.2 | all-reduce | flops 16384 | bytes 65536
  60.4 29.5 all-gather.11.cloned.1.call-done
  89.9 4.9 fusion.80
  94.9 13.5 all_to_all.129
  109.4 60.9 %all-gather.13.cloned.1.call-done = bf16[2048,2048]{1,0:T(8,128)(2,1)} async-done(((bf16[64,2048]{1,0:T(8,128)(2,1)}), bf16[2048,2048]{1,0:T(8,128)(2,1)}) %all-gather.13.cloned.1.call-update) | async-done | bytes 8388624 | tf_op jit(solution)/shard_map/all_gather | solution.py:127
  170.2 4.7 fusion.79
  175.1 13.5 all_to_all.130
  191.8 58.6 %all-gather.17.cloned.1.call-done = bf16[2048,2048]{1,0:T(8,128)(2,1)} async-done(((bf16[64,2048]{1,0:T(8,128)(2,1)}), bf16[2048,2048]{1,0:T(8,128)(2,1)}) %all-gather.17.cloned.1.call-update) | async-done | bytes 8388624 | tf_op jit(solution)/shard_map/all_gather | solution.py:125
  250.4 4.7 fusion.78
  256.1 3.5 all-to-all-start.2
  259.6 37.3 %all-gather = bf16[32,1,128]{2,1,0:T(2,128)(2,1)S(1)} all-gather(bf16[1,1,128]{2,1,0:T(2,128)(2,1)S(1)} %convert_bitcast_fusion), channel_id=1, replica_groups=mesh['head'=4,'blk'=8] {'head','blk'}, dimensions={0}, use_global_device_ids=true | all-gather | bytes 8448 | tf_op jit(solution)/shard_map/all_gather | solution.py:122
  297.1 36.7 %while.48 = (s32[]{:T(128)}, f32[4,512]{1,0:T(4,128)S(1)}, f32[4,512]{1,0:T(4,128)S(1)}, f32[4096]{0:T(1024)S(1)}, f32[512]{0:T(512)S(1)}, /*index=5*/bf16[4096,...) while((s32[]{:T(128)}, f32[4,512]{1,0:T(4,128)S(1)}, ...), condition=%wide.region_5.6_spmd.clone, body=%wide.region_2.5_spmd.clone.sunk | while | flops 1106260480 | bytes 39475396 | solution.py:74
  298.2 9.1 fusion.161
  307.3 8.5 exponential_reduce_fusion.2
  316.9 8.9 fusion.161
  325.9 7.9 exponential_reduce_fusion.2
  333.8 44.6 %all-gather.15.cloned.1.call-done = bf16[4096,2,4,128]{3,0,2,1:T(8,128)(2,1)} async-done(((bf16[512,2,4,128]{3,0,2,1:T(8,128)(2,1)}), bf16[4096,2,4,128]{3,0,2,1:T(8,128)(2,1)}) %all-gather.15.cloned.1.call-update) | async-done | bytes 8388624 | tf_op jit(solution)/shard_map/all_gather | solution.py:200
  378.5 17.9 while.49
  379.5 7.9 fusion.165
  388.5 7.9 fusion.165
  397.5 3.9 all-to-all-start.3
  401.5 39.7 %all-gather.1 = bf16[32,1,256]{2,1,0:T(2,128)(2,1)S(1)} all-gather(bf16[1,1,256]{2,1,0:T(2,128)(2,1)S(1)} %reshape.336), channel_id=1, replica_groups=mesh['head'=4,'blk'=8] {'head','blk'}, dimensions={0}, use_global_device_ids=true | all-gather | bytes 16896 | tf_op jit(solution)/shard_map/all_gather | solution.py:135
  441.6 18.8 all-gather.21.cloned.1.call-done
  460.4 4.7 fusion.107
  465.4 189.5 %all-gather.23.cloned.1.call-done = bf16[2048,8192]{1,0:T(8,128)(2,1)} async-done(((bf16[64,8192]{1,0:T(8,128)(2,1)}), bf16[2048,8192]{1,0:T(8,128)(2,1)}) %all-gather.23.cloned.1.call-update) | async-done | bytes 33554448 | tf_op jit(solution)/shard_map/all_gather | solution.py:134
  655.0 17.2 convolution_add_fusion
  672.2 178.7 %all-gather.25.cloned.1.call-done = bf16[8192,2048]{1,0:T(8,128)(2,1)} async-done(((bf16[256,2048]{1,0:T(8,128)(2,1)}), bf16[8192,2048]{1,0:T(8,128)(2,1)}) %all-gather.25.cloned.1.call-update) | async-done | bytes 33554448 | tf_op jit(solution)/shard_map/all_gather | solution.py:136
  850.9 19.1 convert_reduce_fusion
  870.0 19.7 multiply_reduce_fusion.1
  892.3 6.6 fusion.81
  899.9 3.9 all-to-all-start.4
  903.9 8.7 all-to-all-done.4
  916.3 201.6 %while.50 = (s32[]{:T(128)}, f32[512,2,4,128]{3,0,2,1:T(8,128)}, f32[512,4,128]{0,2,1:T(8,128)}, s32[]{:T(128)}, f32[4096]{0:T(1024)S(1)}, /*index=5*/f32[512]{0...) while((s32[]{:T(128)}, f32[512,2,4,128]{3,0,2,1:T(8,128)}, ...), condition=%wide.region_13.14_spmd.clone, body=%wide.region_12.13_spmd.clone.sunk | while | flops 1357120512 | bytes 52732416 | solution.py:287
  926.9 12.0 collective-permute-done
  952.5 11.6 collective-permute-done
  977.7 11.6 collective-permute-done
  1002.9 11.6 collective-permute-done
  1028.0 11.6 collective-permute-done
  1053.2 11.6 collective-permute-done
  1078.4 11.6 collective-permute-done
  1103.6 11.6 collective-permute-done
  1120.3 3.5 all-to-all-start.5
  1123.7 2.9 copy.140
  1127.8 4.4 all-to-all-done.5
  1132.3 10.6 all_to_all.131
  1142.8 3.5 all-to-all-start.7
  1147.3 5.6 all-to-all-done.7
  1156.4 6.5 fusion.108
  1162.9 6.5 convolution_add_fusion.3
  1169.4 4.6 fusion.89
  1174.2 8.2 fusion.91
  1183.0 8.2 fusion.99
  1192.3 8.2 fusion.97
  1200.6 8.3 fusion.95
  1210.1 24.9 fusion.94
  1236.0 28.7 fusion.104
  1265.4 20.8 fusion.71
  1287.5 24.4 all-reduce.21.cloned.1.call-done
  1323.3 171.1 %reduce-scatter.13.cloned.1.call-done = f32[64,2048]{1,0:T(8,128)} async-done(((f32[2048,2048]{1,0:T(8,128)}), f32[64,2048]{1,0:T(8,128)}) %reduce-scatter.13.cloned.1.call-update) | async-done | bytes 524304 | tf_op jit(solution)/shard_map/reduce_scatter | solution.py:325
  1494.4 187.4 %reduce-scatter.7.cloned.1.call-done = f32[64,2048]{1,0:T(8,128)} async-done(((f32[2048,2048]{1,0:T(8,128)}), f32[64,2048]{1,0:T(8,128)}) %reduce-scatter.7.cloned.1.call-update) | async-done | bytes 524304 | tf_op jit(solution)/shard_map/reduce_scatter | solution.py:320
  1681.7 187.2 %reduce-scatter.9.cloned.1.call-done = f32[64,2048]{1,0:T(8,128)} async-done(((f32[2048,2048]{1,0:T(8,128)}), f32[64,2048]{1,0:T(8,128)}) %reduce-scatter.9.cloned.1.call-update) | async-done | bytes 524304 | tf_op jit(solution)/shard_map/reduce_scatter | solution.py:321
  1868.9 187.3 %reduce-scatter.11.cloned.1.call-done = f32[64,2048]{1,0:T(8,128)} async-done(((f32[2048,2048]{1,0:T(8,128)}), f32[64,2048]{1,0:T(8,128)}) %reduce-scatter.11.cloned.1.call-update) | async-done | bytes 524304 | tf_op jit(solution)/shard_map/reduce_scatter | solution.py:322
  2056.3 711.6 %reduce-scatter.15.cloned.1.call-done = f32[64,8192]{1,0:T(8,128)} async-done(((f32[2048,8192]{1,0:T(8,128)}), f32[64,8192]{1,0:T(8,128)}) %reduce-scatter.15.cloned.1.call-update) | async-done | bytes 2097168 | tf_op jit(solution)/shard_map/reduce_scatter | solution.py:241
  2767.8 708.8 %reduce-scatter.17.cloned.1.call-done = f32[256,2048]{1,0:T(8,128)} async-done(((f32[8192,2048]{1,0:T(8,128)}), f32[256,2048]{1,0:T(8,128)}) %reduce-scatter.17.cloned.1.call-update) | async-done | bytes 2097168 | tf_op jit(solution)/shard_map/reduce_scatter | solution.py:217
  (340 shorter events, 163.5 us)
Async XLA Ops:
  7.2 82.7 %all-gather.11.cloned.1.call-start = ((), (), s32[]{:S(2)}) async-start(), calls=%async_computation.14 | async-start | bytes 8650752 | tf_op jit(solution)/shard_map/all_gather | solution.py:126
  7.9 162.3 %all-gather.13.cloned.1.call-start = ((), (), s32[]{:S(2)}) async-start(), calls=%async_computation.15 | async-start | bytes 8650752 | tf_op jit(solution)/shard_map/all_gather | solution.py:127
  8.7 241.7 %all-gather.17.cloned.1.call-start = ((), (), s32[]{:S(2)}) async-start(), calls=%async_computation.17 | async-start | bytes 8650752 | tf_op jit(solution)/shard_map/all_gather | solution.py:125
  9.4 287.7 %all-gather.19.cloned.1.call-start = ((), (), s32[]{:S(2)}) async-start(), calls=%async_computation.18 | async-start | bytes 4718592 | tf_op jit(solution)/shard_map/all_gather | solution.py:183
  57.8 192.6 %copy-start.22 = (f32[2048]{0:T(1024)}, f32[2048]{0:T(1024)S(1)}, u32[]{:S(2)}) copy-start(f32[2048]{0:T(1024)S(1)} %convert_element_type.161) | copy-start | bytes 24580
  57.8 192.6 %copy-start.18 = (f32[2048]{0:T(1024)}, f32[2048]{0:T(1024)S(1)}, u32[]{:S(2)}) copy-start(f32[2048]{0:T(1024)S(1)} %convert_element_type.160) | copy-start | bytes 24580
  59.0 191.4 %copy-start.24 = (f32[128]{0:T(128)}, f32[128]{0:T(128)S(1)}, u32[]{:S(2)}) copy-start(f32[128]{0:T(128)S(1)} %broadcast_multiply_fusion.5) | copy-start | bytes 1540
  60.4 190.0 %copy-start.26 = (f32[128]{0:T(128)}, f32[128]{0:T(128)S(1)}, u32[]{:S(2)}) copy-start(f32[128]{0:T(128)S(1)} %add_rsqrt_fusion.1) | copy-start | bytes 1540
  60.4 109.8 %copy-start.3 = (bf16[128,2048]{1,0:T(8,128)(2,1)S(1)}, bf16[128,2048]{1,0:T(8,128)(2,1)}, u32[]{:S(2)}) copy-start(bf16[128,2048]{1,0:T(8,128)(2,1)} %param.24) | copy-start | bytes 1572868
  109.3 269.2 %all-gather.15.cloned.1.call-start = ((), (), s32[]{:S(2)}) async-start(), calls=%async_computation.16 | async-start | bytes 9437184 | tf_op jit(solution)/shard_map/all_gather | solution.py:200
  109.3 79.3 %copy-start.9 = (bf16[4,128,4,128]{3,1,0,2:T(8,128)(2,1)S(1)}, bf16[4,128,4,128]{3,1,0,2:T(8,128)(2,1)}, u32[]{:S(2)}) copy-start(bf16[4,128,4,128]{3,1,0,2:T(8,128)(2,1)} %copy.97) | copy-start | bytes 1572868
  189.7 270.7 %all-gather.21.cloned.1.call-start = ((), (), s32[]{:S(2)}) async-start(), calls=%async_computation.19 | async-start | bytes 8650752 | tf_op jit(solution)/shard_map/all_gather | solution.py:130
  190.3 464.6 %all-gather.23.cloned.1.call-start = ((), (), s32[]{:S(2)}) async-start(), calls=%async_computation.20 | async-start | bytes 34603008 | tf_op jit(solution)/shard_map/all_gather | solution.py:134
  191.1 659.9 %all-gather.25.cloned.1.call-start = ((), (), s32[]{:S(2)}) async-start(), calls=%async_computation.21 | async-start | bytes 34603008 | tf_op jit(solution)/shard_map/all_gather | solution.py:136
  191.8 67.8 %copy-start.31 = (s32[128]{0:T(128)S(1)}, s32[128]{0:T(128)}, u32[]{:S(2)}) copy-start(s32[128]{0:T(128)} %param.25) | copy-start | bytes 1540
  256.1 40.9 %all-to-all-start.2 = ((bf16[128,16,128]{2,0,1:T(8,128)(2,1)}), bf16[128,16,128]{2,0,1:T(8,128)(2,1)S(1)}, u32[]{:S(2)}, u32[]{:S(2)}) async-start(bf16[128,16,128]{2,0,1:T(8,128)(2,1)} %bitcast.176), calls=%async_computation.2 | async-start | bytes 1048576 | tf_op jit(solution)/shard_map/all_to_all | solution.py:157
  378.5 23.0 copy-start.32
  396.4 44.9 %copy-start.12 = (f32[512,4,128]{0,2,1:T(8,128)}, f32[512,4,128]{0,2,1:T(8,128)S(1)}, u32[]{:S(2)}) copy-start(f32[512,4,128]{0,2,1:T(8,128)S(1)} %get-tuple-element.586) | copy-start | bytes 3145732
  397.5 43.6 %all-to-all-start.3 = ((bf16[512,4,128]{2,1,0:T(4,128)(2,1)}), bf16[512,4,128]{2,1,0:T(4,128)(2,1)S(1)}, u32[]{:S(2)}, u32[]{:S(2)}) async-start(bf16[512,4,128]{2,1,0:T(4,128)(2,1)} %copy.104), calls=%async_computation.3 | async-start | bytes 1048576 | tf_op jit(solution)/shard_map/all_to_all | solution.py:202
  441.6 23.6 copy-start.7
  465.2 424.6 %copy-start.1 = (f32[128,2048]{1,0:T(8,128)}, f32[128,2048]{1,0:T(8,128)S(1)}, u32[]{:S(2)}) copy-start(f32[128,2048]{1,0:T(8,128)S(1)} %get-tuple-element.798) | copy-start | bytes 3145732
  655.0 196.0 %copy-start.20 = (bf16[128,2048]{1,0:T(8,128)(2,1)S(1)}, bf16[128,2048]{1,0:T(8,128)(2,1)}, u32[]{:S(2)}) copy-start(bf16[128,2048]{1,0:T(8,128)(2,1)} %param.26) | copy-start | bytes 1572868
  892.3 6.7 copy-start.4
  899.0 17.1 copy-start.13
  899.9 12.6 all-to-all-start.4
  916.3 2.2 copy-start.16
  919.7 3.4 copy-start
  924.3 14.5 collective-permute-start
  944.8 3.4 copy-start
  949.5 14.5 collective-permute-start
  966.7 2.2 copy-start.16
  970.0 3.4 copy-start
  974.7 14.5 collective-permute-start
  995.2 3.4 copy-start
  999.9 14.5 collective-permute-start
  1020.4 3.4 copy-start
  1025.1 14.5 collective-permute-start
  1045.6 3.4 copy-start
  1050.3 14.5 collective-permute-start
  1070.8 3.4 copy-start
  1075.5 14.5 collective-permute-start
  1096.0 3.4 copy-start
  1100.7 14.5 collective-permute-start
  1120.3 12.0 all-to-all-start.5
  1142.8 10.0 all-to-all-start.7
  1146.3 165.6 %all-reduce.21.cloned.1.call-start = ((), (), s32[]{:S(2)}) async-start(), calls=%async_computation.28 | async-start | bytes 196608
  1147.3 15.6 copy-start.10
  1156.4 13.0 slice-start
  1162.8 6.5 slice-start.1
  1162.9 6.5 copy-start.19
  1162.9 6.5 copy-start.25
  1162.9 6.5 copy-start.27
  1169.4 4.7 copy-start.5
  1169.4 4.7 copy-start.8
  1174.1 320.3 %reduce-scatter.13.cloned.1.call-start = ((), (), s32[]{:S(2)}) async-start(), calls=%async_computation.25 | async-start | bytes 17301504 | tf_op jit(solution)/shard_map/reduce_scatter | solution.py:325
  1182.4 499.4 %reduce-scatter.7.cloned.1.call-start = ((), (), s32[]{:S(2)}) async-start(), calls=%async_computation.22 | async-start | bytes 17301504 | tf_op jit(solution)/shard_map/reduce_scatter | solution.py:320
  1191.3 677.7 %reduce-scatter.9.cloned.1.call-start = ((), (), s32[]{:S(2)}) async-start(), calls=%async_computation.23 | async-start | bytes 17301504 | tf_op jit(solution)/shard_map/reduce_scatter | solution.py:321
  1200.5 855.8 %reduce-scatter.11.cloned.1.call-start = ((), (), s32[]{:S(2)}) async-start(), calls=%async_computation.24 | async-start | bytes 17301504 | tf_op jit(solution)/shard_map/reduce_scatter | solution.py:322
  1208.9 1559.0 %reduce-scatter.15.cloned.1.call-start = ((), (), s32[]{:S(2)}) async-start(), calls=%async_computation.26 | async-start | bytes 69206016 | tf_op jit(solution)/shard_map/reduce_scatter | solution.py:241
  1235.0 2241.7 %reduce-scatter.17.cloned.1.call-start = ((), (), s32[]{:S(2)}) async-start(), calls=%async_computation.27 | async-start | bytes 69206016 | tf_op jit(solution)/shard_map/reduce_scatter | solution.py:217
  1265.3 20.9 copy-start.30
  1265.3 20.9 copy-start.29
  1265.3 20.9 copy-start.6
  1265.3 20.9 copy-start.14
  (20 other events, 29.7 us)
Sparse Core Ops, SparseCore 0:
  11.0 78.8 all-gather.10
  92.9 77.3 all-gather.12
  173.2 77.1 all-gather.16
  252.4 44.3 all-gather.18
  298.9 79.5 all-gather.14
  381.3 79.0 all-gather.20
  463.4 191.5 all-gather.22
  657.9 192.9 all-gather.24
  1174.2 137.6 all-reduce.20
  1314.7 179.6 reduce-scatter.12
  1497.3 184.3 reduce-scatter.6
  1684.6 184.3 reduce-scatter.8
  1871.9 184.3 reduce-scatter.10
  2059.2 708.6 reduce-scatter.14
  2770.7 705.8 reduce-scatter.16
where the time goes:
time: 3500 us; the launch traced here: 3480 us
  waiting for transfers between devices  2870 us (82%)
  matrix products  313 us (9%)
  blocking collectives  156 us (4%)
  other arithmetic  63.7 us (2%)
  local copies, waits for them, and re-layouts  40.6 us (1%)
    reduce_scatter x1, waiting for transfers between devices, local(): lax.psum_scatter(up_grad, ('head', 'blk'), scatter_dimension=0, tiled=True)  712 us
    reduce_scatter x1, waiting for transfers between devices, local(): lax.psum_scatter(cross_rows(active, cotangent), ('head', 'blk'), scatter_...  709 us
    all_gather x1, waiting for transfers between devices, local(): lax.all_gather(up_proj, ('head', 'blk'), axis=0, tiled=True)  190 us
    reduce_scatter x1, waiting for transfers between devices, local(): lax.psum_scatter(query_grad_w, ('head', 'blk'), scatter_dimension=0, tile...  187 us
    reduce_scatter x1, waiting for transfers between devices, local(): lax.psum_scatter(value_grad_w, ('head', 'blk'), scatter_dimension=0, tile...  187 us
    reduce_scatter x1, waiting for transfers between devices, local(): lax.psum_scatter(key_grad_w, ('head', 'blk'), scatter_dimension=0, tiled=...  187 us
    all_gather x1, waiting for transfers between devices, local(): lax.all_gather(down_proj, ('head', 'blk'), axis=0, tiled=True)  179 us
    reduce_scatter x1, waiting for transfers between devices, local(): lax.psum_scatter(out_grad, ('head', 'blk'), scatter_dimension=0, tiled=True)  171 us
  transfers between devices with their start and end apart: 28, of which 25 were waited for; matrix products, arithmetic and copies ran while one was open for 7% of the time, Pallas kernels for 0%

commit v1 on v0

v1 whole, which is shorter than its diff:
```python
import functools

import jax
import jax.numpy as jnp
from jax import lax
from jax.experimental import pallas as pl
from jax.experimental.pallas import tpu as pltpu
from jax.sharding import PartitionSpec as P

D = 2048
H = 16
DH = 128

norm_epsilon = 1e-05
masked_fill = -1e30
tile = 256
bf16 = jnp.bfloat16
f32 = jnp.float32
log2_e = 1.4426950408889634
vmem_bytes = 48 * 1024 * 1024


def matmul(left, right):
    return jnp.dot(left, right, preferred_element_type=f32)


def cross_rows(left, right):
    return lax.dot_general(left, right, (((0,), (0,)), ((), ())), preferred_element_type=f32)


def times_transposed(left, right):
    return lax.dot_general(left, right, (((1,), (1,)), ((), ())), preferred_element_type=f32)


def norm_parts(values):
    row_mean = jnp.mean(values, axis=-1, keepdims=True)
    centered = values - row_mean
    row_var = jnp.mean(centered * centered, axis=-1, keepdims=True)
    inverse = lax.rsqrt(row_var + norm_epsilon)
    return (centered * inverse, inverse)


def norm_back(grad_out, normal_hat, inverse, gain):
    scaled_grad = grad_out * gain
    return inverse * (
        scaled_grad
        - jnp.mean(scaled_grad, axis=-1, keepdims=True)
        - normal_hat * jnp.mean(scaled_grad * normal_hat, axis=-1, keepdims=True)
    )


def swap(v, axis, mask):
    size = lax.axis_size(axis)
    return lax.ppermute(v, axis, [(i, i ^ mask) for i in range(size)])


def next_chip(v):
    size = lax.axis_size("blk")
    return lax.ppermute(v, "blk", [(i, (i + 2) % size) for i in range(size)])


def pick(v, index):
    return lax.dynamic_index_in_dim(v, index, 0, keepdims=False)


def put(v, part, index):
    return lax.dynamic_update_index_in_dim(v, part, index, 0)


def bits_of(size):
    return [1 << k for k in range(size.bit_length() - 1)]


def gather_ring(v):
    chips = lax.axis_size("blk") // 2
    pairs = []
    held = v
    for step in range(chips):
        later = next_chip(held) if step < chips - 1 else None
        pairs.append((held, swap(held, "blk", 1)))
        held = later
    return pairs


def scatter_ring(chunk, parts):
    chips = lax.axis_size("blk") // 2
    moving = [None] * parts
    for step in list(range(1, chips)) + [0]:
        term = chunk(step)
        rows = term.shape[0] // 2
        sub = rows // parts
        sums = []
        for part in range(parts):
            low, high = part * sub, (part + 1) * sub
            crossing = swap(term[rows + low : rows + high].astype(bf16), "blk", 1)
            total = term[low:high] + crossing.astype(f32)
            if moving[part] is not None:
                total = total + moving[part].astype(f32)
            if step != 0:
                moving[part] = next_chip(total.astype(bf16))
            else:
                sums.append(total)
    return jnp.concatenate(sums, axis=0) if parts > 1 else sums[0]


def gather_head(v):
    size = lax.axis_size("head")
    if size == 4:
        half = v.shape[0] // 2
        one, two = swap(v, "head", 1), swap(v, "head", 2)
        low = swap(two[:half], "head", 1)
        high = swap(one[half:], "head", 2)
        return [v, one, two, jnp.concatenate([low, high], axis=0)]
    held = [v]
    for bit in bits_of(size):
        held = held + [swap(part, "head", bit) for part in held]
    return held


def scatter_head(chunk):
    size = lax.axis_size("head")
    if size == 4:
        far = chunk(3).astype(bf16)
        half = far.shape[0] // 2
        low = swap(far[:half], "head", 1)
        high = swap(far[half:], "head", 2)
        one, two = chunk(1), chunk(2)
        one = jnp.concatenate([one[:half], one[half:] + high.astype(f32)], axis=0)
        two = jnp.concatenate([two[:half] + low.astype(f32), two[half:]], axis=0)
        one = swap(one.astype(bf16), "head", 1)
        two = swap(two.astype(bf16), "head", 2)
        return chunk(0) + one.astype(f32) + two.astype(f32)
    terms = [chunk(m) for m in range(size)]
    for bit in reversed(bits_of(size)):
        terms = [
            terms[m] + swap(terms[m | bit].astype(bf16), "head", bit).astype(f32) for m in range(bit)
        ]
    return terms[0]


def place_head(blocks, mine):
    out = jnp.zeros((len(blocks),) + blocks[0].shape, blocks[0].dtype)
    for mask, block in enumerate(blocks):
        out = put(out, block, mine ^ mask)
    return out


def exchange(pieces, axis, mine, group):
    out = pieces
    for mask in range(1, group):
        out = put(out, swap(pick(pieces, mine ^ mask), axis, mask), mine ^ mask)
    return out


def spread_rows(row, head, blk):
    n_head, n_blk = lax.axis_size("head"), lax.axis_size("blk")
    table = jnp.zeros((n_head * n_blk, row.shape[0]), row.dtype)
    table = put(table, row, head * n_blk + blk)
    for axis, size in (("head", n_head), ("blk", n_blk)):
        for bit in bits_of(size):
            table = table + swap(table, axis, bit)
    return table.reshape(n_head, n_blk, row.shape[0])


def sum_rows(table, head, blk):
    for axis, mine in (("head", head), ("blk", blk)):
        size = table.shape[0]
        for bit in reversed(bits_of(size)):
            halves = table.reshape((2, bit) + table.shape[1:])
            side = (mine // bit) % 2
            table = pick(halves, side) + swap(pick(halves, 1 - side), axis, bit)
        table = table[0]
    return table


def attend_tile(t, groups, factor, refs):
    q_pos, first, query = refs[:3]
    key_pos = refs[3 : 3 + groups]
    keys = refs[3 + groups : 3 + 2 * groups]
    values = refs[3 + 2 * groups : 3 + 3 * groups]
    out, log_total = refs[3 + 3 * groups :]
    high = jnp.full((tile, 1), masked_fill, f32)
    total = jnp.zeros((tile, 1), f32)
    acc = jnp.zeros((tile, DH), f32)
    seen = pl.ds(0, (t + 1) * tile)
    for m in range(groups):
        scores = times_transposed(query[...], keys[m][seen, :]) * factor
        pos = key_pos[m][:, seen]
        keep = (pos >= first[...]) & (pos <= q_pos[...])
        scores = jnp.where(keep, scores, masked_fill)
        new_high = jnp.maximum(high, jnp.max(scores, axis=-1, keepdims=True))
        weights = jnp.exp2(scores - new_high)
        shrink = jnp.exp2(high - new_high)
        total = total * shrink + jnp.sum(weights, axis=-1, keepdims=True)
        acc = acc * shrink + matmul(weights.astype(bf16), values[m][seen, :])
        high = new_high
    out[...] = (acc / total).astype(bf16)
    log_row = jnp.transpose(jnp.broadcast_to(high + jnp.log2(total), (tile, DH)))
    log_total[0] = log_row[0:1, :]


def attend_kernel(tiles, groups, factor, *refs):
    for t in range(tiles):
        pl.when(pl.program_id(1) == t)(functools.partial(attend_tile, t, groups, factor, refs))


def attend(q_pos, first, key_pos, query, keys, values):
    rows, width = query.shape
    groups = len(keys)
    heads = width // DH
    tiles = rows // tile
    column = pl.BlockSpec((tile, 1), lambda i, t: (t, 0))
    line = pl.BlockSpec((1, rows), lambda i, t: (0, 0))
    some = pl.BlockSpec((tile, DH), lambda i, t: (t, i))
    block = pl.BlockSpec((rows, DH), lambda i, t: (0, i))
    pairs = rows * rows * groups * heads // 2
    return pl.pallas_call(
        functools.partial(attend_kernel, tiles, groups, log2_e * DH**-0.5),
        grid=(heads, tiles),
        in_specs=[column, column, some] + [line] * groups + [block] * (2 * groups),
        out_specs=[some, pl.BlockSpec((1, 1, tile), lambda i, t: (i, 0, t))],
        out_shape=[
            jax.ShapeDtypeStruct((rows, width), bf16),
            jax.ShapeDtypeStruct((heads, 1, rows), f32),
        ],
        compiler_params=pltpu.CompilerParams(vmem_limit_bytes=vmem_bytes),
        cost_estimate=pl.CostEstimate(
            flops=4 * pairs * DH, bytes_accessed=4 * rows * width * groups, transcendentals=pairs
        ),
        name="attend",
    )(q_pos, first, query, *key_pos, *keys, *values)


def attend_back_tile(t, factor, scaling, carried, refs):
    q_pos, first, k_pos, log_total, delta, query, d_out, keys, values = refs[:9]
    dq, dk, dv = refs[-3:]
    rows = query.shape[0]
    ahead = pl.ds(t * tile, rows - t * tile)
    k_tile, v_tile = keys[...], values[...]
    q_part, d_part = query[ahead, :], d_out[ahead, :]
    scores = times_transposed(k_tile, q_part) * factor
    pos = k_pos[...]
    keep = (pos >= first[:, ahead]) & (pos <= q_pos[:, ahead])
    probs = jnp.where(keep, jnp.exp2(scores - log_total[0, :, ahead]), 0.0)
    dv[...] = matmul(probs.astype(bf16), d_part).astype(bf16)
    d_probs = times_transposed(v_tile, d_part)
    d_scores = (probs * (d_probs - delta[0, :, ahead])).astype(bf16)
    dk[...] = (scaling * matmul(d_scores, q_part)).astype(bf16)
    term = scaling * cross_rows(d_scores, k_tile)
    if t > 0:
        dq[ahead, :] += term
    elif carried:
        dq[...] = refs[9][...] + term
    else:
        dq[...] = term


def attend_back_kernel(tiles, factor, scaling, carried, *refs):
    for t in range(tiles):
        pl.when(pl.program_id(1) == t)(
            functools.partial(attend_back_tile, t, factor, scaling, carried, refs)
        )


def attend_back(q_pos, first, k_pos, log_total, delta, query, d_out, keys, values, dq_in):
    rows, width = query.shape
    heads = width // DH
    tiles = rows // tile
    column = pl.BlockSpec((tile, 1), lambda i, t: (t, 0))
    line = pl.BlockSpec((1, rows), lambda i, t: (0, 0))
    stat = pl.BlockSpec((1, 1, rows), lambda i, t: (i, 0, 0))
    some = pl.BlockSpec((tile, DH), lambda i, t: (t, i))
    block = pl.BlockSpec((rows, DH), lambda i, t: (0, i))
    pairs = rows * rows * heads // 2
    carried = dq_in is not None
    return pl.pallas_call(
        functools.partial(
            attend_back_kernel, tiles, log2_e * DH**-0.5, DH**-0.5, carried
        ),
        grid=(heads, tiles),
        in_specs=[line, line, column, stat, stat, block, block, some, some]
        + [block] * (1 if carried else 0),
        out_specs=[block, some, some],
        out_shape=[
            jax.ShapeDtypeStruct((rows, width), f32),
            jax.ShapeDtypeStruct((rows, width), bf16),
            jax.ShapeDtypeStruct((rows, width), bf16),
        ],
        compiler_params=pltpu.CompilerParams(vmem_limit_bytes=vmem_bytes),
        cost_estimate=pl.CostEstimate(
            flops=10 * pairs * DH, bytes_accessed=20 * rows * width, transcendentals=pairs
        ),
        name="attend_back",
    )(q_pos, first, k_pos, log_total, delta, query, d_out, keys, values, *([dq_in] if carried else []))


def local(
    tokens,
    segments,
    cotangent,
    first_gain,
    first_shift,
    query_proj,
    key_proj,
    value_proj,
    query_bias,
    value_bias,
    out_proj,
    out_bias,
    second_gain,
    second_shift,
    up_proj,
    up_bias,
    down_proj,
    down_bias,
):
    n_head, n_blk = lax.axis_size("head"), lax.axis_size("blk")
    head, blk = lax.axis_index("head"), lax.axis_index("blk")
    chips = n_blk // 2
    chip, core = blk // 2, blk % 2
    tok = tokens.shape[0]
    rows = tok * n_blk
    w_rows = query_proj.shape[0]
    ff_rows = down_proj.shape[0]
    team = DH // w_rows
    sets = n_blk // team
    each = n_head // team
    place = blk % team
    own_heads = each * DH

    def block_at(step, other):
        return 2 * ((chip - step + chips) % chips) + (core ^ other)

    with jax.named_scope("vectors"):
        small = [
            first_gain,
            first_shift,
            query_bias,
            value_bias,
            out_bias,
            second_gain,
            second_shift,
            down_bias,
            up_bias,
            segments.astype(bf16),
        ]
        table = spread_rows(jnp.concatenate(small), head, blk)

        def vector(index):
            return table[:, :, index * w_rows : (index + 1) * w_rows].reshape(D).astype(f32)

        def own_head_part(full):
            part = full.reshape(n_head, sets, DH)
            part = lax.dynamic_index_in_dim(part, blk // team, 1, keepdims=False)
            return lax.dynamic_slice_in_dim(part, place * each, each, 0).reshape(own_heads)

        gain_first, shift_first = vector(0), vector(1)
        q_bias, v_bias = own_head_part(vector(2)), own_head_part(vector(3))
        o_bias, gain_second, shift_second, d_bias = vector(4), vector(5), vector(6), vector(7)
        base = 8 * w_rows
        u_bias = table[:, :, base : base + ff_rows]
        u_bias = lax.dynamic_index_in_dim(u_bias, blk, 1, keepdims=False).reshape(-1).astype(f32)
        seq = table[:, :, base + ff_rows :].astype(f32)
        seg_rows = pick(seq, head).reshape(rows)
        seg_all = seq.transpose(1, 0, 2).reshape(-1)
        first_pos = jnp.sum((seg_all[None, :] < seg_rows[:, None]).astype(f32), axis=1)
        order = jnp.arange(rows, dtype=jnp.int32)

        def positions(of_head):
            return ((order // tok * n_head + of_head) * tok + order % tok).astype(f32)

        q_pos = positions(head)
        k_pos = [positions(head ^ m) for m in range(n_head)]

    with jax.named_scope("qkv_weights"):
        fused = jnp.stack([query_proj, key_proj, value_proj], axis=1)
        fused = fused.reshape(w_rows, 3, team, each, sets, DH).transpose(4, 2, 0, 1, 3, 5)
        fused = exchange(fused.reshape(n_blk, w_rows, 3 * own_heads), "blk", blk, n_blk)
        fused = gather_head(fused.reshape(n_blk * w_rows, 3 * own_heads))
        qkv_w = place_head(fused, head).reshape(D, 3 * own_heads)

    with jax.named_scope("tokens_gather"):
        tokens_all = jnp.zeros((n_blk, tok, D), bf16)
        for step, (mine, other) in enumerate(gather_ring(tokens)):
            tokens_all = put(tokens_all, mine, block_at(step, 0))
            tokens_all = put(tokens_all, other, block_at(step, 1))
        tokens_all = tokens_all.reshape(rows, D)

    with jax.named_scope("qkv"):
        hat_all, _ = norm_parts(tokens_all.astype(f32))
        normed = (hat_all * gain_first + shift_first).astype(bf16)
        qkv_bias = jnp.concatenate([q_bias, jnp.zeros_like(q_bias), v_bias])
        qkv = (matmul(normed, qkv_w) + qkv_bias).astype(bf16)
        query = qkv[:, :own_heads]

    with jax.named_scope("kv_gather"):
        pairs = gather_head(qkv[:, own_heads:])
        keys = [pair[:, :own_heads] for pair in pairs]
        values = [pair[:, own_heads:] for pair in pairs]

    with jax.named_scope("out_weights"):
        blocks = place_head(gather_head(out_proj), head)
        blocks = blocks.reshape(team, each, w_rows, D)
        out_w = exchange(blocks, "blk", place, team)
        out_w = out_w.transpose(1, 0, 2, 3).reshape(own_heads, D)

    with jax.named_scope("up_weights"):
        up_part = up_proj.reshape(w_rows, n_head, n_blk, ff_rows).transpose(2, 0, 1, 3)
        up_part = up_part.reshape(n_blk, w_rows, n_head * ff_rows)
        up_part = exchange(up_part, "blk", blk, n_blk)
        up_part = gather_head(up_part.reshape(n_blk * w_rows, n_head * ff_rows))
        up_w = place_head(up_part, head).reshape(D, n_head * ff_rows)

    with jax.named_scope("down_weights"):
        down_w = place_head(gather_head(down_proj), head).reshape(n_head * ff_rows, D)

    with jax.named_scope("dy_gather"):
        dy = [jnp.concatenate(pair, axis=0) for pair in gather_ring(cotangent)]

    with jax.named_scope("attention"):
        mixed, log_total = attend(
            q_pos[:, None],
            first_pos[:, None],
            [pos[None, :] for pos in k_pos],
            query,
            keys,
            values,
        )

    def two_blocks(array, step):
        part = array.reshape((n_blk, tok) + array.shape[1:])
        return jnp.concatenate([pick(part, block_at(step, 0)), pick(part, block_at(step, 1))], axis=0)

    with jax.named_scope("branch"):
        branch = scatter_ring(lambda step: matmul(two_blocks(mixed, step), out_w), 2)
        own = tokens.astype(f32)
        hidden = own + (branch + o_bias)
        hat_second, inv_second = norm_parts(hidden)
        second_own = (hat_second * gain_second + shift_second).astype(bf16)

    with jax.named_scope("mlp"):
        second = [jnp.concatenate(pair, axis=0) for pair in gather_ring(second_own)]
        active, d_upper = [None] * chips, [None] * chips

        def mlp_chunk(step):
            upper = matmul(second[step], up_w) + u_bias
            phi = 0.5 * (1.0 + lax.erf(upper * 0.7071067811865476))
            active[step] = (upper * phi).astype(bf16)
            slope = phi + upper * jnp.exp(-0.5 * upper * upper) * 0.3989422804014327
            d_active = times_transposed(dy[step], down_w)
            d_upper[step] = (d_active * slope).astype(bf16)
            return times_transposed(d_upper[step], up_w)

        d_second = scatter_ring(mlp_chunk, 2)
        upstream = cotangent.astype(f32)
        d_hidden = upstream + norm_back(d_second, hat_second, inv_second, gain_second)
        d_branch_own = d_hidden.astype(bf16)

    with jax.named_scope("d_branch_gather"):
        d_branch = jnp.zeros((n_blk, tok, D), bf16)
        for step, (mine, other) in enumerate(gather_ring(d_branch_own)):
            d_branch = put(d_branch, mine, block_at(step, 0))
            d_branch = put(d_branch, other, block_at(step, 1))
        d_branch = d_branch.reshape(rows, D)
        d_mixed = times_transposed(d_branch, out_w).astype(bf16)
        delta = jnp.sum(
            (d_mixed.astype(f32) * mixed.astype(f32)).reshape(rows, each, DH), axis=-1
        ).T.reshape(each, 1, rows)

    with jax.named_scope("attention_back"):
        done = {}
        dq = None

        def kv_grad(m):
            nonlocal dq
            dq, dk, dv = attend_back(
                q_pos[None, :],
                first_pos[None, :],
                k_pos[m][:, None],
                log_total,
                delta,
                query,
                d_mixed,
                keys[m],
                values[m],
                dq,
            )
            return jnp.concatenate([dk, dv], axis=1).astype(f32)

        d_kv = scatter_head(kv_grad).astype(bf16)
        d_qkv = jnp.concatenate([dq.astype(bf16), d_kv], axis=1)

    with jax.named_scope("d_normed"):
        first_sums = []

        def normed_chunk(step):
            term = times_transposed(two_blocks(d_qkv, step), qkv_w)
            hat = two_blocks(hat_all, step)
            first_sums.append((jnp.sum(term * hat, axis=0), jnp.sum(term, axis=0)))
            return term

        d_normed = scatter_ring(normed_chunk, 2)
        hat_first, inv_first = norm_parts(own)
        tokens_grad = (d_hidden + norm_back(d_normed, hat_first, inv_first, gain_first)).astype(bf16)

    with jax.named_scope("output"):
        out_sum = scatter_ring(lambda step: matmul(active[step], down_w), 2)
        output = (hidden + (out_sum + d_bias)).astype(bf16)

    def columns(array, m, width):
        return lax.dynamic_slice_in_dim(array, (head ^ m) * width, width, 1)

    with jax.named_scope("down_grad"):
        active_all, dy_all = jnp.concatenate(active, axis=0), jnp.concatenate(dy, axis=0)
        down_grad = scatter_head(lambda m: cross_rows(columns(active_all, m, ff_rows), dy_all))

    with jax.named_scope("up_grad"):
        second_all, d_upper_all = jnp.concatenate(second, axis=0), jnp.concatenate(d_upper, axis=0)
        slab = n_blk * w_rows
        up_grad = scatter_head(lambda m: cross_rows(columns(second_all, m, slab), d_upper_all))
        up_grad = up_grad.astype(bf16).reshape(n_blk, w_rows, n_head, ff_rows)
        up_grad = exchange(up_grad, "blk", blk, n_blk)
        up_grad = up_grad.transpose(1, 2, 0, 3).reshape(w_rows, -1).astype(f32)

    with jax.named_scope("out_grad"):
        out_term = cross_rows(mixed, d_branch).astype(bf16)
        out_term = out_term.reshape(each, team, w_rows, D).transpose(1, 0, 2, 3)
        out_term = exchange(out_term, "blk", place, team).reshape(n_head, w_rows, D).astype(f32)
        out_grad = scatter_head(lambda m: pick(out_term, head ^ m))

    with jax.named_scope("qkv_grad"):
        qkv_grad = scatter_head(lambda m: cross_rows(columns(normed, m, slab), d_qkv))
        qkv_grad = qkv_grad.astype(bf16).reshape(n_blk, w_rows, 3 * own_heads)
        qkv_grad = exchange(qkv_grad, "blk", blk, n_blk)
        qkv_grad = qkv_grad.reshape(sets, team, w_rows, 3, each, DH).transpose(3, 2, 1, 4, 0, 5)
        qkv_grad = qkv_grad.reshape(3, w_rows, D).astype(f32)

    with jax.named_scope("vector_grads"):
        full = [
            sum(pair[0] for pair in first_sums),
            sum(pair[1] for pair in first_sums),
            jnp.sum(d_branch_own.astype(f32), axis=0),
            jnp.sum(d_second * hat_second, axis=0),
            jnp.sum(d_second, axis=0),
            jnp.sum(upstream, axis=0),
        ]
        parts = [v.reshape(n_head, n_blk, w_rows) for v in full]
        up_sum = sum(jnp.sum(part.astype(f32), axis=0) for part in d_upper)
        up_table = jnp.zeros((n_blk, n_head, ff_rows), f32)
        up_table = put(up_table, up_sum.reshape(n_head, ff_rows), blk)
        parts.append(up_table.transpose(1, 0, 2))
        for v in (dq.astype(bf16), d_kv[:, own_heads:]):
            head_sum = jnp.sum(v.astype(f32), axis=0).reshape(each, 1, DH)
            head_table = jnp.zeros((n_head, sets, DH), f32)
            head_table = lax.dynamic_update_slice(
                head_table, head_sum, (place * each, blk // team, 0)
            )
            parts.append(head_table.reshape(n_head, n_blk, w_rows))
        sums = sum_rows(jnp.concatenate(parts, axis=2), head, blk)
        cuts = [sums[i * w_rows : (i + 1) * w_rows] for i in range(6)]
        up_bias_grad = sums[6 * w_rows : 6 * w_rows + ff_rows]
        rest = sums[6 * w_rows + ff_rows :]

    return (
        output,
        tokens_grad,
        cuts[0],
        cuts[1],
        qkv_grad[0],
        qkv_grad[1],
        qkv_grad[2],
        rest[:w_rows],
        rest[w_rows:],
        out_grad,
        cuts[2],
        cuts[3],
        cuts[4],
        up_grad,
        up_bias_grad,
        down_grad,
        cuts[5],
    )


def solution(mesh):
    by_token = P(("blk", "head"), None)
    matrix = P(("head", "blk"), None)
    vector = P(("head", "blk"))
    return jax.shard_map(
        local,
        mesh=mesh,
        in_specs=(
            by_token,
            P(("blk", "head")),
            by_token,
            vector,
            vector,
            matrix,
            matrix,
            matrix,
            vector,
            vector,
            matrix,
            vector,
            vector,
            vector,
            matrix,
            vector,
            matrix,
            vector,
        ),
        out_specs=(
            by_token,
            by_token,
            vector,
            vector,
            matrix,
            matrix,
            matrix,
            vector,
            vector,
            matrix,
            vector,
            vector,
            vector,
            matrix,
            vector,
            matrix,
            vector,
        ),
        check_vma=False,
    )
```

time: 3500 us -> 898 us (0.26)
  waiting for transfers between devices: 2870 us -> 374 us
  matrix products: 313 us -> 131 us
  blocking collectives: 156 us -> 0 us
  starting transfers between devices: 20.1 us -> 144 us
  local copies, waits for them, and re-layouts: 40.6 us -> 130 us
  Pallas kernels: 0 us -> 47.3 us
    reduce_scatter x6 -> x0, waiting for transfers between devices: 2150 us -> none  [the longest x1 712 us: local(): lax.psum_scatter(up_grad, ('head', 'blk'), scatter_dimension=0, tiled=True)]
    all_gather x8 -> x0, waiting for transfers between devices: 581 us -> none  [the longest x1 190 us: local(): lax.all_gather(up_proj, ('head', 'blk'), axis=0, tiled=True)]
    ppermute x8 -> x164, waiting for transfers between devices: 93.1 us -> 374 us  [the longest x128 247 us: swap(): return lax.ppermute(v, axis, [(i, i ^ mask) for i in range(size)])]
    ppermute x8 -> x164, starting transfers between devices: 0.57 us -> 144 us  [the longest x128 92.6 us: swap(): return lax.ppermute(v, axis, [(i, i ^ mask) for i in range(size)])]
    dot_general x50 -> x13, matrix products: 164 us -> 39.7 us  [matmul(): return jnp.dot(left, right, preferred_element_type=f32)]
    all_gather x2 -> x0, blocking collectives: 76.9 us -> none  [the longest x1 39.7 us: local(): lax.all_gather(up_bias, ('head', 'blk'), axis=0, tiled=True)]
    dot_general x6 -> x13, matrix products: 86.4 us -> 33.2 us  [cross_rows(): lax.dot_general(left, right, (((0,), (0,)), ((), ())), preferred_element_...]
    pallas_call x0 -> x5, Pallas kernels: none -> 47.3 us  [the longest x4 31 us: attend_back(): pl.pallas_call(functools.partial(attend_back_kernel, tiles, log2_e * DH *...]
  transfers between devices with their start and end apart: 28 -> 164, of which waited for: 25 -> 67; matrix products, arithmetic and copies ran while one was open for 7% -> 30% of each run, Pallas kernels for 0% -> 5%
where the time goes in v1:
time: 898 us; the launch traced here: 889 us
  waiting for transfers between devices  374 us (42%)
  starting transfers between devices  144 us (16%)
  matrix products  131 us (15%)
  local copies, waits for them, and re-layouts  130 us (14%)
  other arithmetic  59.2 us (7%)
  Pallas kernels  47.3 us (5%)
    ppermute x128, waiting for transfers between devices, swap(): return lax.ppermute(v, axis, [(i, i ^ mask) for i in range(size)])  247 us
    ppermute x36, waiting for transfers between devices, next_chip(): return lax.ppermute(v, 'blk', [(i, (i + 2) % size) for i in range(size)])  126 us
    ppermute x128, starting transfers between devices, swap(): return lax.ppermute(v, axis, [(i, i ^ mask) for i in range(size)])  92.6 us
    dot_general x13, matrix products, times_transposed(): lax.dot_general(left, right, (((1,), (1,)), ((), ())), preferred_element_...  57.7 us
    ppermute x36, starting transfers between devices, next_chip(): return lax.ppermute(v, 'blk', [(i, (i + 2) % size) for i in range(size)])  51.3 us
    dot_general x13, matrix products, matmul(): return jnp.dot(left, right, preferred_element_type=f32)  39.7 us
    dynamic_update_slice x56, local copies, waits for them, and re-layouts, put(): return lax.dynamic_update_index_in_dim(v, part, index, 0)  37.1 us
    dot_general x13, matrix products, cross_rows(): lax.dot_general(left, right, (((0,), (0,)), ((), ())), preferred_element_...  33.2 us
  transfers between devices with their start and end apart: 164, of which 67 were waited for; matrix products, arithmetic and copies ran while one was open for 30% of the time, Pallas kernels for 5%

profile of v1, /device:TPU:8, one launch (start us, length us, event | category | flops | bytes accessed | tf_op | source)
XLA Modules:
  0.0 888.7 jit_solution(2908064741074130449)
XLA Ops:
  52.0 4.5 collective-permute-done.15
  68.1 5.5 collective-permute-done.18
  73.6 5.7 collective-permute-start.3
  87.6 12.1 %collective-permute-done.48 = bf16[64,1024]{1,0:T(8,128)(2,1)S(1)} collective-permute-done((bf16[64,1024]{1,0:T(8,128)(2,1)S(1)}, bf16[64,1024]{1,0:T(8,128)(2,1)S(1)}, u32[]{:S(2)}, u32[]{:S(2)}) %collective-permute-start.48) | collective-permute-done | bytes 131104 | tf_op jit(solution)/shard_map/up_weights/ppermute | solution.py:54
  102.5 4.2 collective-permute-done.50
  106.6 4.4 collective-permute-start.52
  112.0 9.9 %collective-permute-done.52 = bf16[64,1024]{1,0:T(8,128)(2,1)S(1)} collective-permute-done((bf16[64,1024]{1,0:T(8,128)(2,1)S(1)}, bf16[64,1024]{1,0:T(8,128)(2,1)S(1)}, u32[]{:S(2)}, u32[]{:S(2)}) %collective-permute-start.52) | collective-permute-done | bytes 131104 | tf_op jit(solution)/shard_map/up_weights/ppermute | solution.py:54
  152.6 27.1 %collective-permute-done.19 = bf16[512,768]{1,0:T(8,128)(2,1)S(1)} collective-permute-done((bf16[512,768]{1,0:T(8,128)(2,1)}, bf16[512,768]{1,0:T(8,128)(2,1)S(1)}, u32[]{:S(2)}, u32[]{:S(2)}) %collective-permute-start.19) | collective-permute-done | bytes 786464 | tf_op jit(solution)/shard_map/qkv_weights/ppermute | solution.py:54
  187.3 11.1 %collective-permute-done.8 = bf16[128,2048]{1,0:T(8,128)(2,1)S(1)} collective-permute-done((bf16[128,2048]{1,0:T(8,128)(2,1)}, bf16[128,2048]{1,0:T(8,128)(2,1)S(1)}, u32[]{:S(2)}, u32[]{:S(2)}) %collective-permute-start.8) | collective-permute-done | bytes 524320 | tf_op jit(solution)/shard_map/tokens_gather/ppermute | solution.py:59
  202.8 9.3 %collective-permute-done.85 = bf16[128,2048]{1,0:T(8,128)(2,1)S(1)} collective-permute-done((bf16[128,2048]{1,0:T(8,128)(2,1)}, bf16[128,2048]{1,0:T(8,128)(2,1)S(1)}, u32[]{:S(2)}, u32[]{:S(2)}) %collective-permute-start.85) | collective-permute-done | bytes 524320 | tf_op jit(solution)/shard_map/dy_gather/ppermute | solution.py:59
  220.4 7.9 collective-permute-done.10
  239.0 6.1 subtract_multiply_fusion
  245.1 5.3 add_convert_fusion.1
  255.4 10.0 %collective-permute-done.57 = bf16[256,1024]{1,0:T(8,128)(2,1)S(1)} collective-permute-done((bf16[256,1024]{1,0:T(8,128)(2,1)S(1)}, bf16[256,1024]{1,0:T(8,128)(2,1)S(1)}, u32[]{:S(2)}, u32[]{:S(2)}) %collective-permute-start.57) | collective-permute-done | bytes 524320 | tf_op jit(solution)/shard_map/up_weights/ppermute | solution.py:54
  266.6 20.3 %collective-permute-done.24 = bf16[1024,512]{1,0:T(8,128)(2,1)S(1)} collective-permute-done((bf16[1024,512]{1,0:T(8,128)(2,1)S(1)}, bf16[1024,512]{1,0:T(8,128)(2,1)S(1)}, u32[]{:S(2)}, u32[]{:S(2)}) %collective-permute-start.24) | collective-permute-done | bytes 1048608 | tf_op jit(solution)/shard_map/kv_gather/ppermute | solution.py:54
  288.5 11.5 %collective-permute-done.25 = bf16[512,512]{1,0:T(8,128)(2,1)S(1)} collective-permute-done((bf16[512,512]{1,0:T(8,128)(2,1)S(1)}, bf16[512,512]{1,0:T(8,128)(2,1)S(1)}, u32[]{:S(2)}, u32[]{:S(2)}) %collective-permute-start.25) | collective-permute-done | bytes 524320 | tf_op jit(solution)/shard_map/kv_gather/ppermute | solution.py:54
  301.2 16.3 %attend.1 = (bf16[1024,256]{1,0:T(8,128)(2,1)S(1)}, f32[2,1,1024]{2,1,0:T(1,128)S(1)}) custom-call(f32[1024,1]{1,0:T(8,128)S(1)} %fusion.101.refs_0_.refs_2_, f32[1024,1]{1,0:T(8,128)S(1)} %copy.88.refs_1_, bf16[1024,256]{1,0:T(8,128)(2,1)S(1)} %get-tuple-element.134.refs_2_.refs_5_, f32[1,1024]{1,0:T(1,128)S(1)} %get-tuple-element.291.refs_3_.refs_0_, ...), custom_call_target="tpu_custom_call" | custom-call | flops 2147483648 | bytes 4194304 | tf_op jit(solution)/shard_map/attention/attend/pallas_call | solution.py:217
  323.7 7.5 collective-permute-done.36
  331.2 5.1 collective-permute-done.43
  339.3 7.9 collective-permute-done.37
  347.3 4.1 collective-permute-done.44
  353.8 4.8 fusion.3
  358.6 3.8 collective-permute-done.38
  373.5 4.3 multiply_convert_fusion.3
  377.9 4.9 fusion.296
  382.7 3.8 convert_reduce_fusion.9
  386.5 5.0 fusion.292
  402.7 3.9 convert_reduce_fusion.8
  411.9 4.3 collective-permute-start.65
  425.3 3.8 convert_reduce_fusion.7
  441.3 4.0 collective-permute-done.72
  445.3 4.9 collective-permute-done.79
  458.7 5.6 fusion.295
  470.3 4.7 convert_reduce_fusion.6
  475.0 5.0 fusion.291
  495.7 4.5 collective-permute-done.73
  500.3 4.7 collective-permute-done.80
  508.9 6.2 collective-permute-done.102
  516.5 4.2 collective-permute-done.95
  539.5 9.5 %collective-permute-done.151 = bf16[256,1024]{1,0:T(8,128)(2,1)S(1)} collective-permute-done((bf16[256,1024]{1,0:T(8,128)(2,1)S(1)}, bf16[256,1024]{1,0:T(8,128)(2,1)S(1)}, u32[]{:S(2)}, u32[]{:S(2)}) %collective-permute-start.151) | collective-permute-done | bytes 524320 | tf_op jit(solution)/shard_map/up_grad/ppermute | solution.py:54
  563.5 28.4 %collective-permute-done.150 = bf16[512,1024]{1,0:T(8,128)(2,1)} collective-permute-done((bf16[512,1024]{1,0:T(8,128)(2,1)}, bf16[512,1024]{1,0:T(8,128)(2,1)}, u32[]{:S(2)}, u32[]{:S(2)}) %collective-permute-start.150) | collective-permute-done | bytes 1048608 | tf_op jit(solution)/shard_map/up_grad/ppermute | solution.py:54
  592.9 4.8 add_convert_fusion.2
  601.4 5.6 fusion.4
  607.5 4.5 collective-permute-start.108
  616.9 11.6 %collective-permute-done.154 = bf16[64,4,256]{2,1,0:T(4,128)(2,1)S(1)} collective-permute-done((bf16[64,4,256]{2,1,0:T(4,128)(2,1)S(1)}, bf16[64,4,256]{2,1,0:T(4,128)(2,1)S(1)}, u32[]{:S(2)}, u32[]{:S(2)}) %collective-permute-start.154) | collective-permute-done | bytes 131104 | tf_op jit(solution)/shard_map/up_grad/ppermute | solution.py:54
  633.9 7.7 collective-permute-done.157
  641.6 4.9 collective-permute-done.158
  659.6 5.0 convert_multiply_fusion
  676.2 7.7 attend_back.4
  683.9 7.6 attend_back.5
  694.2 7.6 attend_back.6
  702.0 8.1 attend_back.7
  720.6 25.5 %collective-permute-done.146 = bf16[64,2048]{1,0:T(8,128)(2,1)S(1)} collective-permute-done((bf16[64,2048]{1,0:T(8,128)(2,1)S(1)}, bf16[64,2048]{1,0:T(8,128)(2,1)S(1)}, u32[]{:S(2)}, u32[]{:S(2)}) %collective-permute-start.146) | collective-permute-done | bytes 262176 | tf_op jit(solution)/shard_map/out_grad/ppermute | solution.py:54
  756.7 4.8 fusion.252
  761.6 4.8 fusion.251
  766.4 4.8 fusion.253
  771.2 4.7 fusion.254
  806.1 4.5 collective-permute-done.118
  810.6 5.0 collective-permute-done.125
  821.5 6.1 collective-permute-done.119
  834.9 7.7 collective-permute-done.120
  846.4 5.1 collective-permute-done.136
  858.7 3.8 collective-permute-start.140
  865.4 8.6 collective-permute-done.140
  (835 shorter events, 408.3 us)
Async XLA Ops:
  0.7 139.1 %collective-permute-start.5 = (bf16[128,2048]{1,0:T(8,128)(2,1)}, bf16[128,2048]{1,0:T(8,128)(2,1)}, u32[]{:S(2)}, u32[]{:S(2)}) collective-permute-start(bf16[128,2048]{1,0:T(8,128)(2,1)} %param.18), channel_id=1, source_target_pairs={{0,1},{1,0},{2,3},{3,2},{4,5},{5,4},{6,7},{7,6},{8,9},{9,8},{10,11... | collective-permute-start | bytes 1572872 | tf_op jit(solution)/shard_map/tokens_gather/ppermute | solution.py:54
  0.7 141.7 %collective-permute-start.6 = (bf16[128,2048]{1,0:T(8,128)(2,1)}, bf16[128,2048]{1,0:T(8,128)(2,1)}, u32[]{:S(2)}, u32[]{:S(2)}) collective-permute-start(bf16[128,2048]{1,0:T(8,128)(2,1)} %param.18), channel_id=1, source_target_pairs={{0,2},{1,3},{2,4},{3,5},{4,6},{5,7},{6,0},{7,1},{8,10},{9,11},{10,... | collective-permute-start | bytes 1572872 | tf_op jit(solution)/shard_map/tokens_gather/ppermute | solution.py:59
  8.8 26.3 %collective-permute-start.12 = (bf16[64,768]{1,0:T(8,128)(2,1)}, bf16[64,768]{1,0:T(8,128)(2,1)S(1)}, u32[]{:S(2)}, u32[]{:S(2)}) collective-permute-start(bf16[64,768]{1,0:T(8,128)(2,1)} %dynamic-slice_bitcast_fusion.47), channel_id=1, source_target_pairs={{0,1},{1,0},{2,3},{3,2},{4,5},{5,4},{6,7},{7,6},{8,9},{9,8},{10,11... | collective-permute-start | bytes 294920 | tf_op jit(solution)/shard_map/qkv_weights/ppermute | solution.py:54
  11.2 21.8 %collective-permute-start = (bf16[32,896]{1,0:T(8,128)(2,1)}, bf16[32,896]{1,0:T(8,128)(2,1)}, u32[]{:S(2)}, u32[]{:S(2)}) collective-permute-start(bf16[32,896]{1,0:T(8,128)(2,1)} %dynamic_update_slice.211), channel_id=1, source_target_pairs={{0,8},{8,0},{16,24},{24,16},{1,9},{9,1},{17,25},{25,17},{2,10},{10... | collective-permute-start | bytes 172040 | tf_op jit(solution)/shard_map/vectors/ppermute | solution.py:54
  12.7 70.4 %collective-permute-start.27 = (bf16[64,2048]{1,0:T(8,128)(2,1)}, bf16[64,2048]{1,0:T(8,128)(2,1)}, u32[]{:S(2)}, u32[]{:S(2)}) collective-permute-start(bf16[64,2048]{1,0:T(8,128)(2,1)} %param.28), channel_id=1, source_target_pairs={{0,8},{8,0},{16,24},{24,16},{1,9},{9,1},{17,25},{25,17},{2,10},{10... | collective-permute-start | bytes 786440 | tf_op jit(solution)/shard_map/out_weights/ppermute | solution.py:54
  43.0 43.2 %collective-permute-start.28 = (bf16[64,2048]{1,0:T(8,128)(2,1)}, bf16[64,2048]{1,0:T(8,128)(2,1)S(1)}, u32[]{:S(2)}, u32[]{:S(2)}) collective-permute-start(bf16[64,2048]{1,0:T(8,128)(2,1)} %param.28), channel_id=1, source_target_pairs={{0,16},{8,24},{16,0},{24,8},{1,17},{9,25},{17,1},{25,9},{2,18},{10... | collective-permute-start | bytes 786440 | tf_op jit(solution)/shard_map/out_weights/ppermute | solution.py:54
  82.2 64.2 %collective-permute-start.84 = (bf16[128,2048]{1,0:T(8,128)(2,1)S(1)}, bf16[128,2048]{1,0:T(8,128)(2,1)}, u32[]{:S(2)}, u32[]{:S(2)}) collective-permute-start(bf16[128,2048]{1,0:T(8,128)(2,1)S(1)} %copy-done.59), channel_id=1, source_target_pairs={{0,2},{1,3},{2,4},{3,5},{4,6},{5,7},{6,0},{7,1},{8,10},{9,11},{10,... | collective-permute-start | bytes 1572872 | tf_op jit(solution)/shard_map/dy_gather/ppermute | solution.py:59
  83.0 16.7 %collective-permute-start.48 = (bf16[64,1024]{1,0:T(8,128)(2,1)S(1)}, bf16[64,1024]{1,0:T(8,128)(2,1)S(1)}, u32[]{:S(2)}, u32[]{:S(2)}) collective-permute-start(bf16[64,1024]{1,0:T(8,128)(2,1)S(1)} %get-tuple-element.178), channel_id=1, source_target_pairs={{0,2},{1,3},{2,0},{3,1},{4,6},{5,7},{6,4},{7,5},{8,10},{9,11},{10,... | collective-permute-start | bytes 393224 | tf_op jit(solution)/shard_map/up_weights/ppermute | solution.py:54
  136.6 47.2 %collective-permute-start.58 = (bf16[256,2048]{1,0:T(8,128)(2,1)}, bf16[256,2048]{1,0:T(8,128)(2,1)S(1)}, u32[]{:S(2)}, u32[]{:S(2)}) collective-permute-start(bf16[256,2048]{1,0:T(8,128)(2,1)} %param.34), channel_id=1, source_target_pairs={{0,8},{8,0},{16,24},{24,16},{1,9},{9,1},{17,25},{25,17},{2,10},{10... | collective-permute-start | bytes 3145736 | tf_op jit(solution)/shard_map/down_weights/ppermute | solution.py:54
  139.8 62.5 %collective-permute-start.59 = (bf16[256,2048]{1,0:T(8,128)(2,1)}, bf16[256,2048]{1,0:T(8,128)(2,1)S(1)}, u32[]{:S(2)}, u32[]{:S(2)}) collective-permute-start(bf16[256,2048]{1,0:T(8,128)(2,1)} %param.34), channel_id=1, source_target_pairs={{0,16},{8,24},{16,0},{24,8},{1,17},{9,25},{17,1},{25,9},{2,18},{10... | collective-permute-start | bytes 3145736 | tf_op jit(solution)/shard_map/down_weights/ppermute | solution.py:54
  144.3 35.4 %collective-permute-start.19 = (bf16[512,768]{1,0:T(8,128)(2,1)}, bf16[512,768]{1,0:T(8,128)(2,1)S(1)}, u32[]{:S(2)}, u32[]{:S(2)}) collective-permute-start(bf16[512,768]{1,0:T(8,128)(2,1)} %bitcast.425), channel_id=1, source_target_pairs={{0,8},{8,0},{16,24},{24,16},{1,9},{9,1},{17,25},{25,17},{2,10},{10... | collective-permute-start | bytes 2359304 | tf_op jit(solution)/shard_map/qkv_weights/ppermute | solution.py:54
  146.4 36.3 %collective-permute-start.20 = (bf16[512,768]{1,0:T(8,128)(2,1)}, bf16[512,768]{1,0:T(8,128)(2,1)S(1)}, u32[]{:S(2)}, u32[]{:S(2)}) collective-permute-start(bf16[512,768]{1,0:T(8,128)(2,1)} %bitcast.426), channel_id=1, source_target_pairs={{0,16},{8,24},{16,0},{24,8},{1,17},{9,25},{17,1},{25,9},{2,18},{10... | collective-permute-start | bytes 2359304 | tf_op jit(solution)/shard_map/qkv_weights/ppermute | solution.py:54
  149.9 63.4 %collective-permute-start.54 = (bf16[512,1024]{1,0:T(8,128)(2,1)S(1)}, bf16[512,1024]{1,0:T(8,128)(2,1)S(1)}, u32[]{:S(2)}, u32[]{:S(2)}) collective-permute-start(bf16[512,1024]{1,0:T(8,128)(2,1)S(1)} %bitcast.421), channel_id=1, source_target_pairs={{0,8},{8,0},{16,24},{24,16},{1,9},{9,1},{17,25},{25,17},{2,10},{10... | collective-permute-start | bytes 3145736 | tf_op jit(solution)/shard_map/up_weights/ppermute | solution.py:54
  179.7 36.0 %collective-permute-start.55 = (bf16[512,1024]{1,0:T(8,128)(2,1)S(1)}, bf16[512,1024]{1,0:T(8,128)(2,1)S(1)}, u32[]{:S(2)}, u32[]{:S(2)}) collective-permute-start(bf16[512,1024]{1,0:T(8,128)(2,1)S(1)} %bitcast.422), channel_id=1, source_target_pairs={{0,16},{8,24},{16,0},{24,8},{1,17},{9,25},{17,1},{25,9},{2,18},{10... | collective-permute-start | bytes 3145736 | tf_op jit(solution)/shard_map/up_weights/ppermute | solution.py:54
  200.5 18.0 %collective-permute-start.21 = (bf16[256,768]{1,0:T(8,128)(2,1)S(1)}, bf16[256,768]{1,0:T(8,128)(2,1)S(1)}, u32[]{:S(2)}, u32[]{:S(2)}) collective-permute-start(bf16[256,768]{1,0:T(8,128)(2,1)S(1)} %slice.670), channel_id=1, source_target_pairs={{0,8},{8,0},{16,24},{24,16},{1,9},{9,1},{17,25},{25,17},{2,10},{10... | collective-permute-start | bytes 1179656 | tf_op jit(solution)/shard_map/qkv_weights/ppermute | solution.py:54
  202.2 16.8 %collective-permute-start.22 = (bf16[256,768]{1,0:T(8,128)(2,1)S(1)}, bf16[256,768]{1,0:T(8,128)(2,1)S(1)}, u32[]{:S(2)}, u32[]{:S(2)}) collective-permute-start(bf16[256,768]{1,0:T(8,128)(2,1)S(1)} %slice.671), channel_id=1, source_target_pairs={{0,16},{8,24},{16,0},{24,8},{1,17},{9,25},{17,1},{25,9},{2,18},{10... | collective-permute-start | bytes 1179656 | tf_op jit(solution)/shard_map/qkv_weights/ppermute | solution.py:54
  215.7 36.9 %collective-permute-start.60 = (bf16[128,2048]{1,0:T(8,128)(2,1)S(1)}, bf16[128,2048]{1,0:T(8,128)(2,1)S(1)}, u32[]{:S(2)}, u32[]{:S(2)}) collective-permute-start(bf16[128,2048]{1,0:T(8,128)(2,1)S(1)} %slice.710), channel_id=1, source_target_pairs={{0,8},{8,0},{16,24},{24,16},{1,9},{9,1},{17,25},{25,17},{2,10},{10... | collective-permute-start | bytes 1572872 | tf_op jit(solution)/shard_map/down_weights/ppermute | solution.py:54
  218.6 35.6 %collective-permute-start.61 = (bf16[128,2048]{1,0:T(8,128)(2,1)S(1)}, bf16[128,2048]{1,0:T(8,128)(2,1)S(1)}, u32[]{:S(2)}, u32[]{:S(2)}) collective-permute-start(bf16[128,2048]{1,0:T(8,128)(2,1)S(1)} %slice.711), channel_id=1, source_target_pairs={{0,16},{8,24},{16,0},{24,8},{1,17},{9,25},{17,1},{25,9},{2,18},{10... | collective-permute-start | bytes 1572872 | tf_op jit(solution)/shard_map/down_weights/ppermute | solution.py:54
  219.0 31.5 %collective-permute-start.89 = (bf16[128,2048]{1,0:T(8,128)(2,1)S(1)}, bf16[128,2048]{1,0:T(8,128)(2,1)S(1)}, u32[]{:S(2)}, u32[]{:S(2)}) collective-permute-start(bf16[128,2048]{1,0:T(8,128)(2,1)S(1)} %collective-permute-done.85), channel_id=1, source_target_pairs={{0,1},{1,0},{2,3},{3,2},{4,5},{5,4},{6,7},{7,6},{8,9},{9,8},{10,11... | collective-permute-start | bytes 1572872 | tf_op jit(solution)/shard_map/dy_gather/ppermute | solution.py:54
  219.9 31.2 %collective-permute-start.86 = (bf16[128,2048]{1,0:T(8,128)(2,1)S(1)}, bf16[128,2048]{1,0:T(8,128)(2,1)}, u32[]{:S(2)}, u32[]{:S(2)}) collective-permute-start(bf16[128,2048]{1,0:T(8,128)(2,1)S(1)} %collective-permute-done.85), channel_id=1, source_target_pairs={{0,2},{1,3},{2,4},{3,5},{4,6},{5,7},{6,0},{7,1},{8,10},{9,11},{10,... | collective-permute-start | bytes 1572872 | tf_op jit(solution)/shard_map/dy_gather/ppermute | solution.py:59
  230.2 25.1 %collective-permute-start.56 = (bf16[256,1024]{1,0:T(8,128)(2,1)S(1)}, bf16[256,1024]{1,0:T(8,128)(2,1)S(1)}, u32[]{:S(2)}, u32[]{:S(2)}) collective-permute-start(bf16[256,1024]{1,0:T(8,128)(2,1)S(1)} %slice.707), channel_id=1, source_target_pairs={{0,8},{8,0},{16,24},{24,16},{1,9},{9,1},{17,25},{25,17},{2,10},{10... | collective-permute-start | bytes 1572872 | tf_op jit(solution)/shard_map/up_weights/ppermute | solution.py:54
  251.1 35.8 %collective-permute-start.24 = (bf16[1024,512]{1,0:T(8,128)(2,1)S(1)}, bf16[1024,512]{1,0:T(8,128)(2,1)S(1)}, u32[]{:S(2)}, u32[]{:S(2)}) collective-permute-start(bf16[1024,512]{1,0:T(8,128)(2,1)S(1)} %slice.676), channel_id=1, source_target_pairs={{0,16},{8,24},{16,0},{24,8},{1,17},{9,25},{17,1},{25,9},{2,18},{10... | collective-permute-start | bytes 3145736 | tf_op jit(solution)/shard_map/kv_gather/ppermute | solution.py:54
  252.6 34.8 %collective-permute-start.23 = (bf16[1024,512]{1,0:T(8,128)(2,1)S(1)}, bf16[1024,512]{1,0:T(8,128)(2,1)S(1)}, u32[]{:S(2)}, u32[]{:S(2)}) collective-permute-start(bf16[1024,512]{1,0:T(8,128)(2,1)S(1)} %slice.676), channel_id=1, source_target_pairs={{0,8},{8,0},{16,24},{24,16},{1,9},{9,1},{17,25},{25,17},{2,10},{10... | collective-permute-start | bytes 3145736 | tf_op jit(solution)/shard_map/kv_gather/ppermute | solution.py:54
  254.1 117.6 %collective-permute-start.87 = (bf16[128,2048]{1,0:T(8,128)(2,1)}, bf16[128,2048]{1,0:T(8,128)(2,1)}, u32[]{:S(2)}, u32[]{:S(2)}) collective-permute-start(bf16[128,2048]{1,0:T(8,128)(2,1)} %collective-permute-done.86), channel_id=1, source_target_pairs={{0,1},{1,0},{2,3},{3,2},{4,5},{5,4},{6,7},{7,6},{8,9},{9,8},{10,11... | collective-permute-start | bytes 1572872 | tf_op jit(solution)/shard_map/dy_gather/ppermute | solution.py:54
  338.8 19.8 %collective-permute-start.32 = (bf16[64,2048]{1,0:T(8,128)(2,1)S(1)}, bf16[64,2048]{1,0:T(8,128)(2,1)S(1)}, u32[]{:S(2)}, u32[]{:S(2)}) collective-permute-start(bf16[64,2048]{1,0:T(8,128)(2,1)S(1)} %get-tuple-element.180), channel_id=1, source_target_pairs={{0,1},{1,0},{2,3},{3,2},{4,5},{5,4},{6,7},{7,6},{8,9},{9,8},{10,11... | collective-permute-start | bytes 786440 | tf_op jit(solution)/shard_map/branch/ppermute | solution.py:54
  338.9 19.7 %collective-permute-start.39 = (bf16[64,2048]{1,0:T(8,128)(2,1)S(1)}, bf16[64,2048]{1,0:T(8,128)(2,1)S(1)}, u32[]{:S(2)}, u32[]{:S(2)}) collective-permute-start(bf16[64,2048]{1,0:T(8,128)(2,1)S(1)} %get-tuple-element.181), channel_id=1, source_target_pairs={{0,1},{1,0},{2,3},{3,2},{4,5},{5,4},{6,7},{7,6},{8,9},{9,8},{10,11... | collective-permute-start | bytes 786440 | tf_op jit(solution)/shard_map/branch/ppermute | solution.py:54
  372.8 19.6 %collective-permute-start.63 = (bf16[128,2048]{1,0:T(8,128)(2,1)S(1)}, bf16[128,2048]{1,0:T(8,128)(2,1)S(1)}, u32[]{:S(2)}, u32[]{:S(2)}) collective-permute-start(bf16[128,2048]{1,0:T(8,128)(2,1)S(1)} %get-tuple-element.59), channel_id=1, source_target_pairs={{0,2},{1,3},{2,4},{3,5},{4,6},{5,7},{6,0},{7,1},{8,10},{9,11},{10,... | collective-permute-start | bytes 1572872 | tf_op jit(solution)/shard_map/mlp/ppermute | solution.py:59
  392.4 18.5 %collective-permute-start.64 = (bf16[128,2048]{1,0:T(8,128)(2,1)S(1)}, bf16[128,2048]{1,0:T(8,128)(2,1)S(1)}, u32[]{:S(2)}, u32[]{:S(2)}) collective-permute-start(bf16[128,2048]{1,0:T(8,128)(2,1)S(1)} %collective-permute-done.63), channel_id=1, source_target_pairs={{0,2},{1,3},{2,4},{3,5},{4,6},{5,7},{6,0},{7,1},{8,10},{9,11},{10,... | collective-permute-start | bytes 1572872 | tf_op jit(solution)/shard_map/mlp/ppermute | solution.py:59
  411.9 21.6 %collective-permute-start.65 = (bf16[128,2048]{1,0:T(8,128)(2,1)S(1)}, bf16[128,2048]{1,0:T(8,128)(2,1)S(1)}, u32[]{:S(2)}, u32[]{:S(2)}) collective-permute-start(bf16[128,2048]{1,0:T(8,128)(2,1)S(1)} %collective-permute-done.64), channel_id=1, source_target_pairs={{0,2},{1,3},{2,4},{3,5},{4,6},{5,7},{6,0},{7,1},{8,10},{9,11},{10,... | collective-permute-start | bytes 1572872 | tf_op jit(solution)/shard_map/mlp/ppermute | solution.py:59
  416.3 17.8 %collective-permute-start.100 = (bf16[64,2048]{1,0:T(8,128)(2,1)S(1)}, bf16[64,2048]{1,0:T(8,128)(2,1)S(1)}, u32[]{:S(2)}, u32[]{:S(2)}) collective-permute-start(bf16[64,2048]{1,0:T(8,128)(2,1)S(1)} %get-tuple-element.104), channel_id=1, source_target_pairs={{0,2},{1,3},{2,4},{3,5},{4,6},{5,7},{6,0},{7,1},{8,10},{9,11},{10,... | collective-permute-start | bytes 786440 | tf_op jit(solution)/shard_map/mlp/ppermute | solution.py:59
  417.2 22.5 %collective-permute-start.93 = (bf16[64,2048]{1,0:T(8,128)(2,1)S(1)}, bf16[64,2048]{1,0:T(8,128)(2,1)S(1)}, u32[]{:S(2)}, u32[]{:S(2)}) collective-permute-start(bf16[64,2048]{1,0:T(8,128)(2,1)S(1)} %get-tuple-element.103), channel_id=1, source_target_pairs={{0,2},{1,3},{2,4},{3,5},{4,6},{5,7},{6,0},{7,1},{8,10},{9,11},{10,... | collective-permute-start | bytes 786440 | tf_op jit(solution)/shard_map/mlp/ppermute | solution.py:59
  434.1 16.1 %collective-permute-start.79 = (bf16[64,2048]{1,0:T(8,128)(2,1)S(1)}, bf16[64,2048]{1,0:T(8,128)(2,1)S(1)}, u32[]{:S(2)}, u32[]{:S(2)}) collective-permute-start(bf16[64,2048]{1,0:T(8,128)(2,1)S(1)} %get-tuple-element.112), channel_id=1, source_target_pairs={{0,2},{1,3},{2,4},{3,5},{4,6},{5,7},{6,0},{7,1},{8,10},{9,11},{10,... | collective-permute-start | bytes 786440 | tf_op jit(solution)/shard_map/output/ppermute | solution.py:59
  445.3 77.5 %collective-permute-start.62 = (bf16[64,2048]{1,0:T(8,128)(2,1)}, bf16[64,2048]{1,0:T(8,128)(2,1)S(1)}, u32[]{:S(2)}, u32[]{:S(2)}) collective-permute-start(bf16[64,2048]{1,0:T(8,128)(2,1)} %get-tuple-element.165), channel_id=1, source_target_pairs={{0,1},{1,0},{2,3},{3,2},{4,5},{5,4},{6,7},{7,6},{8,9},{9,8},{10,11... | collective-permute-start | bytes 786440 | tf_op jit(solution)/shard_map/output/ppermute | solution.py:54
  450.2 40.5 %collective-permute-start.101 = (bf16[64,2048]{1,0:T(8,128)(2,1)}, bf16[64,2048]{1,0:T(8,128)(2,1)}, u32[]{:S(2)}, u32[]{:S(2)}) collective-permute-start(bf16[64,2048]{1,0:T(8,128)(2,1)} %get-tuple-element.102), channel_id=1, source_target_pairs={{0,2},{1,3},{2,4},{3,5},{4,6},{5,7},{6,0},{7,1},{8,10},{9,11},{10,... | collective-permute-start | bytes 786440 | tf_op jit(solution)/shard_map/mlp/ppermute | solution.py:59
  452.7 40.5 %collective-permute-start.94 = (bf16[64,2048]{1,0:T(8,128)(2,1)}, bf16[64,2048]{1,0:T(8,128)(2,1)}, u32[]{:S(2)}, u32[]{:S(2)}) collective-permute-start(bf16[64,2048]{1,0:T(8,128)(2,1)} %get-tuple-element.101), channel_id=1, source_target_pairs={{0,2},{1,3},{2,4},{3,5},{4,6},{5,7},{6,0},{7,1},{8,10},{9,11},{10,... | collective-permute-start | bytes 786440 | tf_op jit(solution)/shard_map/mlp/ppermute | solution.py:59
  507.9 16.6 %collective-permute-start.75 = (bf16[64,2048]{1,0:T(8,128)(2,1)S(1)}, bf16[64,2048]{1,0:T(8,128)(2,1)S(1)}, u32[]{:S(2)}, u32[]{:S(2)}) collective-permute-start(bf16[64,2048]{1,0:T(8,128)(2,1)S(1)} %copy-done.87), channel_id=1, source_target_pairs={{0,1},{1,0},{2,3},{3,2},{4,5},{5,4},{6,7},{7,6},{8,9},{9,8},{10,11... | collective-permute-start | bytes 786440 | tf_op jit(solution)/shard_map/output/ppermute | solution.py:54
  508.0 26.1 %collective-permute-start.160 = (bf16[128,2048]{1,0:T(8,128)(2,1)S(1)}, bf16[128,2048]{1,0:T(8,128)(2,1)S(1)}, u32[]{:S(2)}, u32[]{:S(2)}) collective-permute-start(bf16[128,2048]{1,0:T(8,128)(2,1)S(1)} %copy-done.81), channel_id=1, source_target_pairs={{0,16},{8,24},{16,0},{24,8},{1,17},{9,25},{17,1},{25,9},{2,18},{10... | collective-permute-start | bytes 1572872 | tf_op jit(solution)/shard_map/down_grad/ppermute | solution.py:54
  522.8 29.0 %collective-permute-start.162 = (bf16[128,2048]{1,0:T(8,128)(2,1)S(1)}, bf16[128,2048]{1,0:T(8,128)(2,1)S(1)}, u32[]{:S(2)}, u32[]{:S(2)}) collective-permute-start(bf16[128,2048]{1,0:T(8,128)(2,1)S(1)} %copy-done.80), channel_id=1, source_target_pairs={{0,8},{8,0},{16,24},{24,16},{1,9},{9,1},{17,25},{25,17},{2,10},{10... | collective-permute-start | bytes 1572872 | tf_op jit(solution)/shard_map/down_grad/ppermute | solution.py:54
  526.3 22.7 %collective-permute-start.151 = (bf16[256,1024]{1,0:T(8,128)(2,1)S(1)}, bf16[256,1024]{1,0:T(8,128)(2,1)S(1)}, u32[]{:S(2)}, u32[]{:S(2)}) collective-permute-start(bf16[256,1024]{1,0:T(8,128)(2,1)S(1)} %get-tuple-element.145), channel_id=1, source_target_pairs={{0,8},{8,0},{16,24},{24,16},{1,9},{9,1},{17,25},{25,17},{2,10},{10... | collective-permute-start | bytes 1572872 | tf_op jit(solution)/shard_map/up_grad/ppermute | solution.py:54
  534.1 24.1 %collective-permute-start.103 = (bf16[128,2048]{1,0:T(8,128)(2,1)}, bf16[128,2048]{1,0:T(8,128)(2,1)}, u32[]{:S(2)}, u32[]{:S(2)}) collective-permute-start(bf16[128,2048]{1,0:T(8,128)(2,1)} %get-tuple-element.67), channel_id=1, source_target_pairs={{0,1},{1,0},{2,3},{3,2},{4,5},{5,4},{6,7},{7,6},{8,9},{9,8},{10,11... | collective-permute-start | bytes 1572872 | tf_op jit(solution)/shard_map/d_branch_gather/ppermute | solution.py:54
  534.1 25.6 %collective-permute-start.104 = (bf16[128,2048]{1,0:T(8,128)(2,1)}, bf16[128,2048]{1,0:T(8,128)(2,1)}, u32[]{:S(2)}, u32[]{:S(2)}) collective-permute-start(bf16[128,2048]{1,0:T(8,128)(2,1)} %get-tuple-element.67), channel_id=1, source_target_pairs={{0,2},{1,3},{2,4},{3,5},{4,6},{5,7},{6,0},{7,1},{8,10},{9,11},{10,... | collective-permute-start | bytes 1572872 | tf_op jit(solution)/shard_map/d_branch_gather/ppermute | solution.py:59
  537.0 64.3 %collective-permute-start.161 = (bf16[256,2048]{1,0:T(8,128)(2,1)}, bf16[256,2048]{1,0:T(8,128)(2,1)}, u32[]{:S(2)}, u32[]{:S(2)}) collective-permute-start(bf16[256,2048]{1,0:T(8,128)(2,1)} %pad_maximum_fusion.8), channel_id=1, source_target_pairs={{0,8},{8,0},{16,24},{24,16},{1,9},{9,1},{17,25},{25,17},{2,10},{10... | collective-permute-start | bytes 3145736 | tf_op jit(solution)/shard_map/down_grad/ppermute | solution.py:54
  549.0 43.0 %collective-permute-start.150 = (bf16[512,1024]{1,0:T(8,128)(2,1)}, bf16[512,1024]{1,0:T(8,128)(2,1)}, u32[]{:S(2)}, u32[]{:S(2)}) collective-permute-start(bf16[512,1024]{1,0:T(8,128)(2,1)} %pad_maximum_fusion.6), channel_id=1, source_target_pairs={{0,8},{8,0},{16,24},{24,16},{1,9},{9,1},{17,25},{25,17},{2,10},{10... | collective-permute-start | bytes 3145736 | tf_op jit(solution)/shard_map/up_grad/ppermute | solution.py:54
  551.9 41.0 %collective-permute-start.152 = (bf16[512,1024]{1,0:T(8,128)(2,1)}, bf16[512,1024]{1,0:T(8,128)(2,1)}, u32[]{:S(2)}, u32[]{:S(2)}) collective-permute-start(bf16[512,1024]{1,0:T(8,128)(2,1)} %pad_maximum_fusion.7), channel_id=1, source_target_pairs={{0,16},{8,24},{16,0},{24,8},{1,17},{9,25},{17,1},{25,9},{2,18},{10... | collective-permute-start | bytes 3145736 | tf_op jit(solution)/shard_map/up_grad/ppermute | solution.py:54
  558.2 43.2 %collective-permute-start.163 = (bf16[256,2048]{1,0:T(8,128)(2,1)}, bf16[256,2048]{1,0:T(8,128)(2,1)}, u32[]{:S(2)}, u32[]{:S(2)}) collective-permute-start(bf16[256,2048]{1,0:T(8,128)(2,1)} %pad_maximum_fusion.9), channel_id=1, source_target_pairs={{0,16},{8,24},{16,0},{24,8},{1,17},{9,25},{17,1},{25,9},{2,18},{10... | collective-permute-start | bytes 3145736 | tf_op jit(solution)/shard_map/down_grad/ppermute | solution.py:54
  559.7 52.2 %collective-permute-start.105 = (bf16[128,2048]{1,0:T(8,128)(2,1)}, bf16[128,2048]{1,0:T(8,128)(2,1)}, u32[]{:S(2)}, u32[]{:S(2)}) collective-permute-start(bf16[128,2048]{1,0:T(8,128)(2,1)} %collective-permute-done.104), channel_id=1, source_target_pairs={{0,1},{1,0},{2,3},{3,2},{4,5},{5,4},{6,7},{7,6},{8,9},{9,8},{10,11... | collective-permute-start | bytes 1572872 | tf_op jit(solution)/shard_map/d_branch_gather/ppermute | solution.py:54
  607.1 46.4 %collective-permute-start.107 = (bf16[128,2048]{1,0:T(8,128)(2,1)S(1)}, bf16[128,2048]{1,0:T(8,128)(2,1)S(1)}, u32[]{:S(2)}, u32[]{:S(2)}) collective-permute-start(bf16[128,2048]{1,0:T(8,128)(2,1)S(1)} %collective-permute-done.106), channel_id=1, source_target_pairs={{0,1},{1,0},{2,3},{3,2},{4,5},{5,4},{6,7},{7,6},{8,9},{9,8},{10,11... | collective-permute-start | bytes 1572872 | tf_op jit(solution)/shard_map/d_branch_gather/ppermute | solution.py:54
  607.5 45.9 %collective-permute-start.108 = (bf16[128,2048]{1,0:T(8,128)(2,1)S(1)}, bf16[128,2048]{1,0:T(8,128)(2,1)S(1)}, u32[]{:S(2)}, u32[]{:S(2)}) collective-permute-start(bf16[128,2048]{1,0:T(8,128)(2,1)S(1)} %collective-permute-done.106), channel_id=1, source_target_pairs={{0,2},{1,3},{2,4},{3,5},{4,6},{5,7},{6,0},{7,1},{8,10},{9,11},{10,... | collective-permute-start | bytes 1572872 | tf_op jit(solution)/shard_map/d_branch_gather/ppermute | solution.py:59
  615.2 16.1 %collective-permute-start.155 = (bf16[64,4,256]{2,1,0:T(4,128)(2,1)S(1)}, bf16[64,4,256]{2,1,0:T(4,128)(2,1)S(1)}, u32[]{:S(2)}, u32[]{:S(2)}) collective-permute-start(bf16[64,4,256]{2,1,0:T(4,128)(2,1)S(1)} %get-tuple-element.141), channel_id=1, source_target_pairs={{0,3},{1,2},{2,1},{3,0},{4,7},{5,6},{6,5},{7,4},{8,11},{9,10},{10,... | collective-permute-start | bytes 393224 | tf_op jit(solution)/shard_map/up_grad/ppermute | solution.py:54
  616.4 16.0 %collective-permute-start.156 = (bf16[64,4,256]{2,1,0:T(4,128)(2,1)S(1)}, bf16[64,4,256]{2,1,0:T(4,128)(2,1)S(1)}, u32[]{:S(2)}, u32[]{:S(2)}) collective-permute-start(bf16[64,4,256]{2,1,0:T(4,128)(2,1)S(1)} %get-tuple-element.140), channel_id=1, source_target_pairs={{0,4},{1,5},{2,6},{3,7},{4,0},{5,1},{6,2},{7,3},{8,12},{9,13},{10,... | collective-permute-start | bytes 393224 | tf_op jit(solution)/shard_map/up_grad/ppermute | solution.py:54
  632.4 16.9 %collective-permute-start.159 = (bf16[64,4,256]{2,1,0:T(4,128)(2,1)S(1)}, bf16[64,4,256]{2,1,0:T(4,128)(2,1)S(1)}, u32[]{:S(2)}, u32[]{:S(2)}) collective-permute-start(bf16[64,4,256]{2,1,0:T(4,128)(2,1)S(1)} %get-tuple-element.137), channel_id=1, source_target_pairs={{0,7},{1,6},{2,5},{3,4},{4,3},{5,2},{6,1},{7,0},{8,15},{9,14},{10,... | collective-permute-start | bytes 393224 | tf_op jit(solution)/shard_map/up_grad/ppermute | solution.py:54
  665.5 44.6 %collective-permute-start.144 = (bf16[2,64,2048]{2,1,0:T(8,128)(2,1)}, bf16[2,64,2048]{2,1,0:T(8,128)(2,1)}, u32[]{:S(2)}, u32[]{:S(2)}) collective-permute-start(bf16[2,64,2048]{2,1,0:T(8,128)(2,1)} %dynamic-slice_bitcast_fusion.8), channel_id=1, source_target_pairs={{0,1},{1,0},{2,3},{3,2},{4,5},{5,4},{6,7},{7,6},{8,9},{9,8},{10,11... | collective-permute-start | bytes 1572872 | tf_op jit(solution)/shard_map/out_grad/ppermute | solution.py:54
  691.8 21.6 %collective-permute-start.110 = (bf16[512,512]{1,0:T(8,128)(2,1)S(1)}, bf16[512,512]{1,0:T(8,128)(2,1)S(1)}, u32[]{:S(2)}, u32[]{:S(2)}) collective-permute-start(bf16[512,512]{1,0:T(8,128)(2,1)S(1)} %get-tuple-element.154), channel_id=1, source_target_pairs={{0,16},{8,24},{16,0},{24,8},{1,17},{9,25},{17,1},{25,9},{2,18},{10... | collective-permute-start | bytes 1572872 | tf_op jit(solution)/shard_map/attention_back/ppermute | solution.py:54
  692.7 23.6 %collective-permute-start.112 = (bf16[512,512]{1,0:T(8,128)(2,1)S(1)}, bf16[512,512]{1,0:T(8,128)(2,1)S(1)}, u32[]{:S(2)}, u32[]{:S(2)}) collective-permute-start(bf16[512,512]{1,0:T(8,128)(2,1)S(1)} %get-tuple-element.155), channel_id=1, source_target_pairs={{0,8},{8,0},{16,24},{24,16},{1,9},{9,1},{17,25},{25,17},{2,10},{10... | collective-permute-start | bytes 1572872 | tf_op jit(solution)/shard_map/attention_back/ppermute | solution.py:54
  714.6 34.8 %collective-permute-start.111 = (bf16[1024,512]{1,0:T(8,128)(2,1)}, bf16[1024,512]{1,0:T(8,128)(2,1)}, u32[]{:S(2)}, u32[]{:S(2)}) collective-permute-start(bf16[1024,512]{1,0:T(8,128)(2,1)} %pad_maximum_fusion.4), channel_id=1, source_target_pairs={{0,8},{8,0},{16,24},{24,16},{1,9},{9,1},{17,25},{25,17},{2,10},{10... | collective-permute-start | bytes 3145736 | tf_op jit(solution)/shard_map/attention_back/ppermute | solution.py:54
  717.6 31.8 %collective-permute-start.113 = (bf16[1024,512]{1,0:T(8,128)(2,1)}, bf16[1024,512]{1,0:T(8,128)(2,1)S(1)}, u32[]{:S(2)}, u32[]{:S(2)}) collective-permute-start(bf16[1024,512]{1,0:T(8,128)(2,1)} %pad_maximum_fusion.5), channel_id=1, source_target_pairs={{0,16},{8,24},{16,0},{24,8},{1,17},{9,25},{17,1},{25,9},{2,18},{10... | collective-permute-start | bytes 3145736 | tf_op jit(solution)/shard_map/attention_back/ppermute | solution.py:54
  719.5 26.5 %collective-permute-start.146 = (bf16[64,2048]{1,0:T(8,128)(2,1)S(1)}, bf16[64,2048]{1,0:T(8,128)(2,1)S(1)}, u32[]{:S(2)}, u32[]{:S(2)}) collective-permute-start(bf16[64,2048]{1,0:T(8,128)(2,1)S(1)} %pad_maximum_fusion.12), channel_id=1, source_target_pairs={{0,8},{8,0},{16,24},{24,16},{1,9},{9,1},{17,25},{25,17},{2,10},{10... | collective-permute-start | bytes 786440 | tf_op jit(solution)/shard_map/out_grad/ppermute | solution.py:54
  719.6 27.8 %collective-permute-start.148 = (bf16[64,2048]{1,0:T(8,128)(2,1)S(1)}, bf16[64,2048]{1,0:T(8,128)(2,1)}, u32[]{:S(2)}, u32[]{:S(2)}) collective-permute-start(bf16[64,2048]{1,0:T(8,128)(2,1)S(1)} %pad_maximum_fusion.13), channel_id=1, source_target_pairs={{0,16},{8,24},{16,0},{24,8},{1,17},{9,25},{17,1},{25,9},{2,18},{10... | collective-permute-start | bytes 786440 | tf_op jit(solution)/shard_map/out_grad/ppermute | solution.py:54
  779.0 26.6 %collective-permute-start.116 = (bf16[64,2048]{1,0:T(8,128)(2,1)}, bf16[64,2048]{1,0:T(8,128)(2,1)}, u32[]{:S(2)}, u32[]{:S(2)}) collective-permute-start(bf16[64,2048]{1,0:T(8,128)(2,1)} %get-tuple-element.150), channel_id=1, source_target_pairs={{0,1},{1,0},{2,3},{3,2},{4,5},{5,4},{6,7},{7,6},{8,9},{9,8},{10,11... | collective-permute-start | bytes 786440 | tf_op jit(solution)/shard_map/d_normed/ppermute | solution.py:54
  784.4 33.1 %collective-permute-start.133 = (bf16[256,768]{1,0:T(8,128)(2,1)}, bf16[256,768]{1,0:T(8,128)(2,1)}, u32[]{:S(2)}, u32[]{:S(2)}) collective-permute-start(bf16[256,768]{1,0:T(8,128)(2,1)} %get-tuple-element.201), channel_id=1, source_target_pairs={{0,16},{8,24},{16,0},{24,8},{1,17},{9,25},{17,1},{25,9},{2,18},{10... | collective-permute-start | bytes 1179656 | tf_op jit(solution)/shard_map/qkv_grad/ppermute | solution.py:54
  805.7 26.3 %collective-permute-start.135 = (bf16[256,768]{1,0:T(8,128)(2,1)S(1)}, bf16[256,768]{1,0:T(8,128)(2,1)S(1)}, u32[]{:S(2)}, u32[]{:S(2)}) collective-permute-start(bf16[256,768]{1,0:T(8,128)(2,1)S(1)} %copy-done.86), channel_id=1, source_target_pairs={{0,8},{8,0},{16,24},{24,16},{1,9},{9,1},{17,25},{25,17},{2,10},{10... | collective-permute-start | bytes 1179656 | tf_op jit(solution)/shard_map/qkv_grad/ppermute | solution.py:54
  827.6 18.8 %collective-permute-start.134 = (bf16[512,768]{1,0:T(8,128)(2,1)S(1)}, bf16[512,768]{1,0:T(8,128)(2,1)S(1)}, u32[]{:S(2)}, u32[]{:S(2)}) collective-permute-start(bf16[512,768]{1,0:T(8,128)(2,1)S(1)} %pad_maximum_fusion.10), channel_id=1, source_target_pairs={{0,8},{8,0},{16,24},{24,16},{1,9},{9,1},{17,25},{25,17},{2,10},{10... | collective-permute-start | bytes 2359304 | tf_op jit(solution)/shard_map/qkv_grad/ppermute | solution.py:54
  834.3 17.2 %collective-permute-start.136 = (bf16[512,768]{1,0:T(8,128)(2,1)S(1)}, bf16[512,768]{1,0:T(8,128)(2,1)S(1)}, u32[]{:S(2)}, u32[]{:S(2)}) collective-permute-start(bf16[512,768]{1,0:T(8,128)(2,1)S(1)} %pad_maximum_fusion.11), channel_id=1, source_target_pairs={{0,16},{8,24},{16,0},{24,8},{1,17},{9,25},{17,1},{25,9},{2,18},{10... | collective-permute-start | bytes 2359304 | tf_op jit(solution)/shard_map/qkv_grad/ppermute | solution.py:54
  862.5 16.3 %collective-permute-start.142 = (bf16[64,768]{1,0:T(8,128)(2,1)S(1)}, bf16[64,768]{1,0:T(8,128)(2,1)S(1)}, u32[]{:S(2)}, u32[]{:S(2)}) collective-permute-start(bf16[64,768]{1,0:T(8,128)(2,1)S(1)} %get-tuple-element.195), channel_id=1, source_target_pairs={{0,6},{1,7},{2,4},{3,5},{4,2},{5,3},{6,0},{7,1},{8,14},{9,15},{10,... | collective-permute-start | bytes 294920 | tf_op jit(solution)/shard_map/qkv_grad/ppermute | solution.py:54
  (210 other events, 2917.3 us)

commit v2 on v1

v2 whole, which is shorter than its diff:
```python
import functools

import jax
import jax.numpy as jnp
from jax import lax
from jax.experimental import pallas as pl
from jax.experimental.pallas import tpu as pltpu
from jax.sharding import PartitionSpec as P

D = 2048
H = 16
DH = 128

norm_epsilon = 1e-05
masked_fill = -1e30
tile = 256
bf16 = jnp.bfloat16
f32 = jnp.float32
log2_e = 1.4426950408889634
vmem_bytes = 48 * 1024 * 1024


def matmul(left, right):
    return jnp.dot(left, right, preferred_element_type=f32)


def cross_rows(left, right):
    return lax.dot_general(left, right, (((0,), (0,)), ((), ())), preferred_element_type=f32)


def times_transposed(left, right):
    return lax.dot_general(left, right, (((1,), (1,)), ((), ())), preferred_element_type=f32)


def norm_parts(values):
    row_mean = jnp.mean(values, axis=-1, keepdims=True)
    centered = values - row_mean
    row_var = jnp.mean(centered * centered, axis=-1, keepdims=True)
    inverse = lax.rsqrt(row_var + norm_epsilon)
    return (centered * inverse, inverse)


def norm_back(grad_out, normal_hat, inverse, gain):
    scaled_grad = grad_out * gain
    return inverse * (
        scaled_grad
        - jnp.mean(scaled_grad, axis=-1, keepdims=True)
        - normal_hat * jnp.mean(scaled_grad * normal_hat, axis=-1, keepdims=True)
    )


def swap(v, axis, mask):
    size = lax.axis_size(axis)
    return lax.ppermute(v, axis, [(i, i ^ mask) for i in range(size)])


def ring_order(chips):
    return list(range(0, chips, 2)) + [k for k in range(chips - 1, 0, -1) if k % 2]


def next_chip(v):
    chips = lax.axis_size("blk") // 2
    order = ring_order(chips)
    moves = [(order[k], order[(k + 1) % chips]) for k in range(chips)]
    return lax.ppermute(v, "blk", [(2 * a + c, 2 * b + c) for a, b in moves for c in range(2)])


def pick(v, index):
    return lax.dynamic_index_in_dim(v, index, 0, keepdims=False)


def put(v, part, index):
    return lax.dynamic_update_index_in_dim(v, part, index, 0)


def bits_of(size):
    return [1 << k for k in range(size.bit_length() - 1)]


def blank(shape, dtype):
    return pl.pallas_call(
        lambda out: None,
        out_shape=jax.ShapeDtypeStruct(shape, dtype),
        out_specs=pl.BlockSpec(memory_space=pl.ANY),
        name="blank",
    )()


def hold(*values):
    return lax.optimization_barrier(values)


def gather_head(v):
    size = lax.axis_size("head")
    if size == 4:
        half = v.shape[0] // 2
        one, two = swap(v, "head", 1), swap(v, "head", 2)
        low = swap(two[:half], "head", 1)
        high = swap(one[half:], "head", 2)
        return [v, one, two, jnp.concatenate([low, high], axis=0)]
    held = [v]
    for bit in bits_of(size):
        held = held + [swap(part, "head", bit) for part in held]
    return held


def scatter_head(chunk):
    size = lax.axis_size("head")
    if size == 4:
        far = chunk(3).astype(bf16)
        half = far.shape[0] // 2
        low = swap(far[:half], "head", 1)
        high = swap(far[half:], "head", 2)
        one, two = chunk(1), chunk(2)
        one = jnp.concatenate([one[:half], one[half:] + high.astype(f32)], axis=0)
        two = jnp.concatenate([two[:half] + low.astype(f32), two[half:]], axis=0)
        one = swap(one.astype(bf16), "head", 1)
        two = swap(two.astype(bf16), "head", 2)
        return chunk(0) + one.astype(f32) + two.astype(f32)
    terms = [chunk(m) for m in range(size)]
    for bit in reversed(bits_of(size)):
        terms = [
            terms[m] + swap(terms[m | bit].astype(bf16), "head", bit).astype(f32) for m in range(bit)
        ]
    return terms[0]


def exchange(pieces, axis, mine, group):
    out = pieces
    for mask in range(1, group):
        out = put(out, swap(pick(pieces, mine ^ mask), axis, mask), mine ^ mask)
    return out


def scalars(*values):
    return jnp.stack([jnp.asarray(v, jnp.int32) for v in values])


def local_call(kernel, out_shapes, scalar, *arrays, name):
    return pl.pallas_call(
        kernel,
        in_specs=[pl.BlockSpec(memory_space=pltpu.SMEM)]
        + [pl.BlockSpec(memory_space=pltpu.VMEM)] * len(arrays),
        out_specs=[pl.BlockSpec(memory_space=pltpu.VMEM)] * len(out_shapes),
        out_shape=[jax.ShapeDtypeStruct(shape, dtype) for shape, dtype in out_shapes],
        compiler_params=pltpu.CompilerParams(vmem_limit_bytes=vmem_bytes),
        name=name,
    )(scalar, *arrays)


def place(blocks, at):
    count = len(blocks)

    def kernel(at_ref, *refs):
        for k in range(count):
            refs[count][at_ref[k]] = refs[k][...]

    shape = ((count,) + blocks[0].shape, blocks[0].dtype)
    return local_call(kernel, [shape], at, *blocks, name="place")[0]


def lanes(start, size):
    return pl.ds(pl.multiple_of(start, DH), size)


def split_columns(arrays, width, columns_of, core, chips, name):
    rows = arrays[0].shape[0]

    def kernel(core_ref, *refs):
        sources, (mine, other) = refs[:-2], refs[-2:]
        me = core_ref[0]
        for chip in range(chips):
            for out, index in ((mine, me), (other, 1 - me)):
                starts, run = columns_of(2 * chip + index)
                for p, source in enumerate(sources):
                    for i, start in enumerate(starts):
                        low = p * width + i * run
                        out[chip, :, low : low + run] = source[:, lanes(start, run)]

    shape = ((chips, rows, len(arrays) * width), arrays[0].dtype)
    return local_call(kernel, [shape, shape], scalars(core), *arrays, name=name)


def pair_up(mine, other, chip, core):
    chips = mine.shape[0]

    def kernel(at, mine_ref, other_ref, *outs):
        for m in range(chips):
            outs[m][at[1]] = mine_ref[at[0] ^ m]
            outs[m][1 - at[1]] = other_ref[at[0] ^ m]

    shape = ((2,) + mine.shape[1:], mine.dtype)
    return local_call(kernel, [shape] * chips, scalars(chip, core), mine, other, name="pair_up")


def swap_chips(pieces):
    return [pieces[0]] + [swap(pieces[m], "blk", 2 * m) for m in range(1, len(pieces))]


def merge_columns(pieces, count, width, columns_of, chip, name):
    chips = len(pieces)
    rows = pieces[0].shape[1]
    total = 2 * chips * width

    def kernel(at, *refs):
        sources, outs = refs[:chips], refs[chips:]
        for m in range(chips):
            for core in range(2):
                starts, run = columns_of(2 * (at[0] ^ m) + core)
                for p in range(count):
                    for i, start in enumerate(starts):
                        low = p * width + i * run
                        outs[p][:, lanes(start, run)] = sources[m][core, :, low : low + run].astype(
                            f32
                        )

    shapes = [((rows, total), f32)] * count
    return local_call(kernel, shapes, scalars(chip), *pieces, name=name)


def sum_rows(table, head, blk):
    for axis, mine in (("head", head), ("blk", blk)):
        size = table.shape[0]
        for bit in reversed(bits_of(size)):
            halves = table.reshape((2, bit) + table.shape[1:])
            side = (mine // bit) % 2
            table = pick(halves, side) + swap(pick(halves, 1 - side), axis, bit)
        table = table[0]
    return table


def attend_tile(t, groups, factor, refs):
    q_pos, first, query = refs[:3]
    key_pos = refs[3 : 3 + groups]
    keys = refs[3 + groups : 3 + 2 * groups]
    values = refs[3 + 2 * groups : 3 + 3 * groups]
    out, log_total = refs[3 + 3 * groups :]
    high = jnp.full((tile, 1), masked_fill, f32)
    total = jnp.zeros((tile, 1), f32)
    acc = jnp.zeros((tile, DH), f32)
    seen = pl.ds(0, (t + 1) * tile)
    for m in range(groups):
        scores = times_transposed(query[...], keys[m][0, seen, :]) * factor
        pos = key_pos[m][:, seen]
        keep = (pos >= first[...]) & (pos <= q_pos[...])
        scores = jnp.where(keep, scores, masked_fill)
        new_high = jnp.maximum(high, jnp.max(scores, axis=-1, keepdims=True))
        weights = jnp.exp2(scores - new_high)
        shrink = jnp.exp2(high - new_high)
        total = total * shrink + jnp.sum(weights, axis=-1, keepdims=True)
        acc = acc * shrink + matmul(weights.astype(bf16), values[m][0, seen, :])
        high = new_high
    out[...] = (acc / total).astype(bf16)
    log_row = jnp.transpose(jnp.broadcast_to(high + jnp.log2(total), (tile, DH)))
    log_total[0] = log_row[0:1, :]


def attend_kernel(tiles, groups, factor, *refs):
    for t in range(tiles):
        pl.when(pl.program_id(1) == t)(functools.partial(attend_tile, t, groups, factor, refs))


def attend(q_pos, first, key_pos, query, key_values):
    rows, width = query.shape
    groups = len(key_values)
    heads = width // DH
    tiles = rows // tile
    column = pl.BlockSpec((tile, 1), lambda i, t: (t, 0))
    line = pl.BlockSpec((1, rows), lambda i, t: (0, 0))
    some = pl.BlockSpec((tile, DH), lambda i, t: (t, i))
    key = pl.BlockSpec((1, rows, DH), lambda i, t: (0, 0, i))
    value = pl.BlockSpec((1, rows, DH), lambda i, t: (1, 0, i))
    pairs = rows * rows * groups * heads // 2
    return pl.pallas_call(
        functools.partial(attend_kernel, tiles, groups, log2_e * DH**-0.5),
        grid=(heads, tiles),
        in_specs=[column, column, some] + [line] * groups + [key] * groups + [value] * groups,
        out_specs=[some, pl.BlockSpec((1, 1, tile), lambda i, t: (i, 0, t))],
        out_shape=[
            jax.ShapeDtypeStruct((rows, width), bf16),
            jax.ShapeDtypeStruct((heads, 1, rows), f32),
        ],
        compiler_params=pltpu.CompilerParams(vmem_limit_bytes=vmem_bytes),
        cost_estimate=pl.CostEstimate(
            flops=4 * pairs * DH, bytes_accessed=4 * rows * width * groups, transcendentals=pairs
        ),
        name="attend",
    )(q_pos, first, query, *key_pos, *key_values, *key_values)


def row_dots_kernel(left, right, out):
    products = left[...].astype(f32) * right[...].astype(f32)
    out[0] = jnp.sum(jnp.transpose(products), axis=0, keepdims=True)


def row_dots(left, right):
    rows, width = left.shape
    heads = width // DH
    block = pl.BlockSpec((rows, DH), lambda i: (0, i))
    return pl.pallas_call(
        row_dots_kernel,
        grid=(heads,),
        in_specs=[block, block],
        out_specs=pl.BlockSpec((1, 1, rows), lambda i: (i, 0, 0)),
        out_shape=jax.ShapeDtypeStruct((heads, 1, rows), f32),
        compiler_params=pltpu.CompilerParams(vmem_limit_bytes=vmem_bytes),
        name="row_dots",
    )(left, right)


def attend_back_tile(t, factor, scaling, carried, refs):
    q_pos, first, k_pos, log_total, delta, query, d_out, keys, values = refs[:9]
    dq, d_kv = refs[-2:]
    rows = query.shape[0]
    ahead = pl.ds(t * tile, rows - t * tile)
    k_tile, v_tile = keys[0], values[0]
    q_part, d_part = query[ahead, :], d_out[ahead, :]
    scores = times_transposed(k_tile, q_part) * factor
    pos = k_pos[...]
    keep = (pos >= first[:, ahead]) & (pos <= q_pos[:, ahead])
    probs = jnp.where(keep, jnp.exp2(scores - log_total[0, :, ahead]), 0.0)
    d_kv[1] = matmul(probs.astype(bf16), d_part).astype(bf16)
    d_probs = times_transposed(v_tile, d_part)
    d_scores = (probs * (d_probs - delta[0, :, ahead])).astype(bf16)
    d_kv[0] = (scaling * matmul(d_scores, q_part)).astype(bf16)
    term = scaling * cross_rows(d_scores, k_tile)
    if t > 0:
        dq[ahead, :] += term
    elif carried:
        dq[...] = refs[9][...] + term
    else:
        dq[...] = term


def attend_back_kernel(tiles, factor, scaling, carried, *refs):
    for t in range(tiles):
        pl.when(pl.program_id(1) == t)(
            functools.partial(attend_back_tile, t, factor, scaling, carried, refs)
        )


def attend_back(q_pos, first, k_pos, log_total, delta, query, d_out, key_value, dq_in):
    rows, width = query.shape
    heads = width // DH
    tiles = rows // tile
    column = pl.BlockSpec((tile, 1), lambda i, t: (t, 0))
    line = pl.BlockSpec((1, rows), lambda i, t: (0, 0))
    stat = pl.BlockSpec((1, 1, rows), lambda i, t: (i, 0, 0))
    key = pl.BlockSpec((1, tile, DH), lambda i, t: (0, t, i))
    value = pl.BlockSpec((1, tile, DH), lambda i, t: (1, t, i))
    both = pl.BlockSpec((2, tile, DH), lambda i, t: (0, t, i))
    block = pl.BlockSpec((rows, DH), lambda i, t: (0, i))
    pairs = rows * rows * heads // 2
    carried = dq_in is not None
    return pl.pallas_call(
        functools.partial(attend_back_kernel, tiles, log2_e * DH**-0.5, DH**-0.5, carried),
        grid=(heads, tiles),
        in_specs=[line, line, column, stat, stat, block, block, key, value]
        + [block] * (1 if carried else 0),
        out_specs=[block, both],
        out_shape=[
            jax.ShapeDtypeStruct((rows, width), f32),
            jax.ShapeDtypeStruct((2, rows, width), bf16),
        ],
        compiler_params=pltpu.CompilerParams(vmem_limit_bytes=vmem_bytes),
        cost_estimate=pl.CostEstimate(
            flops=10 * pairs * DH, bytes_accessed=20 * rows * width, transcendentals=pairs
        ),
        name="attend_back",
    )(
        q_pos,
        first,
        k_pos,
        log_total,
        delta,
        query,
        d_out,
        key_value,
        key_value,
        *([dq_in] if carried else []),
    )


def local(
    tokens,
    segments,
    cotangent,
    first_gain,
    first_shift,
    query_proj,
    key_proj,
    value_proj,
    query_bias,
    value_bias,
    out_proj,
    out_bias,
    second_gain,
    second_shift,
    up_proj,
    up_bias,
    down_proj,
    down_bias,
):
    n_head, n_blk = lax.axis_size("head"), lax.axis_size("blk")
    head, blk = lax.axis_index("head"), lax.axis_index("blk")
    chips = n_blk // 2
    chip, core = blk // 2, blk % 2
    tok = tokens.shape[0]
    rows = tok * n_blk
    w_rows = query_proj.shape[0]
    ff_rows = down_proj.shape[0]
    team = DH // w_rows
    sets = n_blk // team
    each = n_head // team
    place_in = blk % team
    own_heads = each * DH

    ring = ring_order(chips)
    behind = jnp.array(
        [[ring[(ring.index(z) - k) % chips] for k in range(chips)] for z in range(chips)], jnp.int32
    )
    behind = pick(behind, chip)
    behind = [behind[k] for k in range(chips)]

    def chunk_of(array, step):
        return array[step * 2 * tok : (step + 1) * 2 * tok]

    def place_of(step, other):
        return (2 * behind[step] + (core ^ other)) * tok

    def ordered_chunk(array, step):
        return jnp.concatenate(
            [lax.dynamic_slice_in_dim(array, place_of(step, other), tok, 0) for other in (0, 1)]
        )

    def fill(buffer, chunk, step):
        return lax.dynamic_update_slice_in_dim(buffer, chunk, step * 2 * tok, 0)

    def fill_pair(buffer, mine, other, step):
        buffer = lax.dynamic_update_slice_in_dim(buffer, mine, step * 2 * tok, 0)
        return lax.dynamic_update_slice_in_dim(buffer, other, step * 2 * tok + tok, 0)

    order = jnp.arange(rows, dtype=jnp.int32)

    def positions(of_head):
        return ((order // tok * n_head + of_head) * tok + order % tok).astype(f32)

    square = n_head == 4

    def head_columns(b):
        at = (b % team) * each
        return [((at + i) * sets + b // team) * DH for i in range(each)], DH

    def ff_columns(b):
        return [(h * n_blk + b) * ff_rows for h in range(n_head)], ff_rows

    heads_at = scalars(*[head ^ m for m in range(n_head)])
    chips_at = scalars(*[chip ^ m for m in range(chips)])

    with jax.named_scope("tokens_gather"):
        tok_mine, tok_other = [tokens], []
        tok_mine.append(next_chip(tokens))

    with jax.named_scope("vectors"):
        small = [
            first_gain,
            first_shift,
            query_bias,
            value_bias,
            out_bias,
            second_gain,
            second_shift,
            down_bias,
            up_bias,
            segments.astype(bf16),
        ]
        small = jnp.concatenate(small)[None]
        for bit in bits_of(n_head):
            small = jnp.concatenate([small, swap(small, "head", bit)])
        small = jnp.concatenate([small, swap(small, "blk", 1)])
        small_parts = [small]
        small_parts.append(next_chip(small))

    with jax.named_scope("qkv_weights"):
        mine, other = split_columns(
            [query_proj, key_proj, value_proj], own_heads, head_columns, core, chips, "split_heads"
        )
        pieces = pair_up(mine, swap(other, "blk", 1), chip, core)

    pieces, small_parts, up_proj, tokens = hold(pieces, small_parts, up_proj, tokens)

    with jax.named_scope("qkv_weights"):
        pieces = swap_chips(pieces)
        fused = place(pieces, chips_at).reshape(n_blk * w_rows, 3 * own_heads)
    with jax.named_scope("tokens_gather"):
        tok_other.append(swap(tokens, "blk", 1))
    with jax.named_scope("vectors"):
        if len(small_parts) < chips:
            small_parts.append(next_chip(small_parts[-1]))

    fused, small_parts, tok_mine, tok_other, up_proj = hold(
        fused, small_parts, tok_mine, tok_other, up_proj
    )

    normed = blank((rows, D), bf16)
    stats = {}
    table = None

    def small_table():
        width = small_parts[0].shape[1]
        source = jnp.concatenate(small_parts)
        index = jnp.arange(n_head * n_blk, dtype=jnp.int32)
        from_chip = jnp.repeat(jnp.stack(behind), 2 * n_head)
        from_core = core ^ (index // n_head % 2)
        from_row = (head ^ (index % n_head)) * n_blk + 2 * from_chip + from_core
        select = (from_row[None, :] == index[:, None]).astype(bf16)
        return matmul(select, source).reshape(n_head, n_blk, width)

    def vector(index):
        return table[:, :, index * w_rows : (index + 1) * w_rows].reshape(D)

    def add_normed(buffer, step):
        for other, piece in enumerate((tok_mine[step], tok_other[step])):
            values = piece.astype(f32)
            row_mean = jnp.mean(values, axis=-1, keepdims=True)
            centered = values - row_mean
            inverse = lax.rsqrt(jnp.mean(centered * centered, axis=-1, keepdims=True) + norm_epsilon)
            stats[step, other] = (row_mean, inverse)
            out = (centered * inverse * gain_first + shift_first).astype(bf16)
            buffer = lax.dynamic_update_slice_in_dim(buffer, out, place_of(step, other), 0)
        return buffer

    filled = 0
    for step in range(1, chips):
        with jax.named_scope("tokens_gather"):
            if step < chips - 1:
                tok_mine.append(next_chip(tok_mine[step]))
            if step < chips - 1:
                tok_other.append(swap(tok_mine[step], "blk", 1))
        with jax.named_scope("qkv_weights"):
            if step == 1 and square:
                fused_parts = [fused, swap(fused, "head", 1), swap(fused, "head", 2)]
            if step == 2 and square:
                half = fused.shape[0] // 2
                low = swap(fused_parts[2][:half], "head", 1)
                high = swap(fused_parts[1][half:], "head", 2)
            if step == 1 and not square:
                fused_parts = gather_head(fused)
        with jax.named_scope("vectors"):
            if table is not None and filled == 0:
                gain_first, shift_first = vector(0), vector(1)
            if len(small_parts) < chips:
                small_parts.append(next_chip(small_parts[-1]))
            elif table is None:
                table = small_table()
                gain_first, shift_first = vector(0), vector(1)
        if table is not None and step < chips - 1:
            with jax.named_scope("qkv"):
                while filled < min(step, filled + 2):
                    normed = add_normed(normed, filled)
                    filled += 1
        if step == 1:
            with jax.named_scope("up_weights"):
                up_mine, up_other = split_columns(
                    [up_proj], n_head * ff_rows, ff_columns, core, chips, "split_up"
                )
        if step < chips - 1:
            tok_mine, tok_other, small_parts, normed, stats, table, up_mine, up_other = hold(
                tok_mine, tok_other, small_parts, normed, stats, table, up_mine, up_other
            )
            if step == 2 and square:
                fused_parts, low, high = hold(fused_parts, low, high)
        if step == chips - 2:
            (fused_parts, tok_mine, tok_other, normed, stats, cotangent, up_other, table) = hold(
                fused_parts, tok_mine, tok_other, normed, stats, cotangent, up_other, table
            )
            if square and step == 2:
                low, high, cotangent, out_proj = hold(low, high, cotangent, out_proj)

    with jax.named_scope("tokens_gather"):
        tok_other.append(swap(tok_mine[chips - 1], "blk", 1))
    with jax.named_scope("vectors"):

        def own_head_part(full):
            part = full.reshape(n_head, sets, DH)
            part = lax.dynamic_index_in_dim(part, blk // team, 1, keepdims=False)
            return lax.dynamic_slice_in_dim(part, place_in * each, each, 0).reshape(own_heads)

        q_bias, v_bias = own_head_part(vector(2)), own_head_part(vector(3))
        qkv_bias = jnp.concatenate([q_bias, jnp.zeros_like(q_bias), v_bias])
    with jax.named_scope("dy_gather"):
        dy_mine, dy_other = [cotangent], []
        dy_mine.append(next_chip(cotangent))
    with jax.named_scope("up_weights"):
        up_pieces = pair_up(up_mine, swap(up_other, "blk", 1), chip, core)
    with jax.named_scope("out_weights"):
        if square:
            out_parts = [out_proj, swap(out_proj, "head", 1), swap(out_proj, "head", 2)]
        else:
            out_parts = gather_head(out_proj)
    with jax.named_scope("qkv"):
        if square:
            half = fused.shape[0] // 2
            fused_parts = [part.reshape(2, half, -1) for part in fused_parts]
            blocks = [part[k] for part in fused_parts for k in (0, 1)] + [low, high]
            qkv_w = place(blocks, jnp.stack([2 * heads_at, 2 * heads_at + 1], axis=1).reshape(-1))
        else:
            qkv_w = place(fused_parts, heads_at)
        qkv_w = qkv_w.reshape(D, 3 * own_heads)
        while filled < chips:
            normed = add_normed(normed, filled)
            filled += 1
        qkv = (matmul(normed, qkv_w) + qkv_bias).astype(bf16)
        query = qkv[:, :own_heads]
        kv = jnp.stack([qkv[:, own_heads : 2 * own_heads], qkv[:, 2 * own_heads :]])

    query, kv, up_pieces, normed, stats, out_parts, cotangent, dy_mine, down_proj, qkv_w = hold(
        query, kv, up_pieces, normed, stats, out_parts, cotangent, dy_mine, down_proj, qkv_w
    )

    with jax.named_scope("kv_gather"):
        if square:
            kv_parts = [kv, swap(kv, "head", 1), swap(kv, "head", 2)]
        else:
            kv_parts = gather_head(kv)
    with jax.named_scope("up_weights"):
        up_pieces = swap_chips(up_pieces)
        up_part = place(up_pieces, chips_at).reshape(n_blk * w_rows, n_head * ff_rows)
    with jax.named_scope("vectors"):
        o_bias, gain_second, shift_second, d_bias = vector(4), vector(5), vector(6), vector(7)
        base = 8 * w_rows
        u_bias = table[:, :, base : base + ff_rows]
        u_bias = lax.dynamic_index_in_dim(u_bias, blk, 1, keepdims=False).reshape(-1)
        seq = table[:, :, base + ff_rows :]
        seg_all = seq.transpose(1, 0, 2).reshape(-1)
        seg_rows = pick(seq, head).reshape(rows)
        first_pos = jnp.sum((seg_all[None, :] < seg_rows[:, None]).astype(f32), axis=1)
        q_pos = positions(head)
        k_pos = [positions(head ^ m) for m in range(n_head)]
        vectors = (o_bias, gain_second, shift_second, d_bias, u_bias)
        as_column = lambda v: v[:, None]
        as_line = lambda v: v[None, :]
        spots = (
            as_column(q_pos),
            as_column(first_pos),
            as_line(q_pos),
            as_line(first_pos),
            [as_line(pos) for pos in k_pos],
            [as_column(pos) for pos in k_pos],
        )
    kv_parts, up_part, dy_mine, vectors, spots = hold(kv_parts, up_part, dy_mine, vectors, spots)
    o_bias, gain_second, shift_second, d_bias, u_bias = vectors

    dy_all = blank((rows, D), bf16)
    with jax.named_scope("kv_gather"):
        if square:
            low = swap(kv_parts[2][0], "head", 1)
            high = swap(kv_parts[1][1], "head", 2)
            kv_parts = kv_parts + [jnp.stack([low, high])]
    with jax.named_scope("out_weights"):
        if square:
            half = w_rows // 2
            low = swap(out_parts[2][:half], "head", 1)
            high = swap(out_parts[1][half:], "head", 2)
            out_parts = out_parts + [jnp.concatenate([low, high])]
    with jax.named_scope("dy_gather"):
        if chips > 2:
            dy_mine.append(next_chip(dy_mine[1]))
    kv_parts, dy_mine, up_part, out_parts, down_proj, cotangent = hold(
        kv_parts, dy_mine, up_part, out_parts, down_proj, cotangent
    )

    with jax.named_scope("up_weights"):
        up_w = lax.all_gather(up_part, "head", axis=0, tiled=True)
    with jax.named_scope("down_weights"):
        if square:
            down_parts = [down_proj, swap(down_proj, "head", 1), swap(down_proj, "head", 2)]
        else:
            down_parts = gather_head(down_proj)
    with jax.named_scope("dy_gather"):
        dy_other.append(swap(cotangent, "blk", 1))
        for step in range(2, chips - 1):
            dy_mine.append(next_chip(dy_mine[step]))
    with jax.named_scope("out_weights"):
        out_w = place(out_parts, heads_at).reshape(team, each, w_rows, D)
        out_w = exchange(out_w, "blk", place_in, team)
        out_w = out_w.transpose(1, 0, 2, 3).reshape(own_heads, D)
    with jax.named_scope("attention"):
        mixed, log_total = attend(spots[0], spots[1], spots[4], query, kv_parts)
    mixed, dy_mine, dy_other, out_w = hold(mixed, dy_mine, dy_other, out_w)

    def cross(term):
        return (term[0], swap(term[1], "blk", 1))

    def sum_of(pair):
        return pair[0].astype(f32) + pair[1].astype(f32)

    def onward(ready, moving):
        total = ready if moving is None else ready + moving.astype(f32)
        return next_chip(total.astype(bf16))

    with jax.named_scope("branch"):

        def branch_term(step):
            return [
                matmul(lax.dynamic_slice_in_dim(mixed, place_of(step, other), tok, 0), out_w).astype(bf16)
                for other in (0, 1)
            ]

        ready = sum_of(cross(branch_term(1)))
        term = branch_term(2 % chips)
        ready, term, dy_mine, dy_other = hold(ready, term, dy_mine, dy_other)
        moving = None
        for step in range(1, chips):
            moving = onward(ready, moving)
            ready = sum_of(cross(term))
            if step < chips - 1:
                term = branch_term((step + 2) % chips)
            with jax.named_scope("dy_gather"):
                if step == 1:
                    dy_all = fill_pair(dy_all, dy_mine[0], dy_other[0], 0)
                if step < chips - 1:
                    dy_other.append(swap(dy_mine[step], "blk", 1))
                    if step > 1:
                        dy_all = fill_pair(dy_all, dy_mine[step - 1], dy_other[step - 1], step - 1)
                else:
                    dy_all = fill_pair(dy_all, dy_mine[step - 1], dy_other[step - 1], step - 1)
            with jax.named_scope("down_weights"):
                if square and step == 3:
                    half = ff_rows // 2
                    low = swap(down_parts[2][:half], "head", 1)
                    high = swap(down_parts[1][half:], "head", 2)
                    down_parts = [part.reshape(2, half, D) for part in down_parts]
                    blocks = [part[k] for part in down_parts for k in (0, 1)] + [low, high]
                    at = jnp.stack([2 * heads_at, 2 * heads_at + 1], axis=1).reshape(-1)
                    down_w = place(blocks, at).reshape(n_head * ff_rows, D)
                if not square and step == 1:
                    down_w = place(down_parts, heads_at).reshape(n_head * ff_rows, D)
            if square and step == 2:
                down_parts, moving, ready, term, dy_mine, dy_other, dy_all = hold(
                    down_parts, moving, ready, term, dy_mine, dy_other, dy_all
                )
            else:
                moving, ready, term, dy_mine, dy_other, dy_all = hold(
                    moving, ready, term, dy_mine, dy_other, dy_all
                )
        with jax.named_scope("dy_gather"):
            dy_other.append(swap(dy_mine[chips - 1], "blk", 1))
            dy_all = fill_pair(dy_all, dy_mine[chips - 1], dy_other[chips - 1], chips - 1)
        own = tokens.astype(f32)
        hidden = own + (ready + moving.astype(f32) + o_bias)
        hat_second, inv_second = norm_parts(hidden)
        second_own = (hat_second * gain_second + shift_second).astype(bf16)
    hidden, second_own, inv_second = hold(hidden, second_own, inv_second)

    with jax.named_scope("mlp"):
        second_all = blank((rows, D), bf16)
        active_all = blank((rows, n_head * ff_rows), bf16)
        d_upper_all = blank((rows, n_head * ff_rows), bf16)
        sec_mine, sec_other = [second_own], []
        terms = {}

        def mlp_chunk(step, second_all, active_all, d_upper_all):
            second_all = fill_pair(second_all, sec_mine[step], sec_other[step], step)
            upper = matmul(chunk_of(second_all, step), up_w) + u_bias
            phi = 0.5 * (1.0 + lax.erf(upper * 0.7071067811865476))
            active = (upper * phi).astype(bf16)
            slope = phi + upper * jnp.exp(-0.5 * upper * upper) * 0.3989422804014327
            d_active = times_transposed(chunk_of(dy_all, step), down_w)
            d_upper = (d_active * slope).astype(bf16)
            terms[step] = [
                times_transposed(d_upper[:tok], up_w).astype(bf16),
                times_transposed(d_upper[tok:], up_w).astype(bf16),
            ]
            return second_all, fill(active_all, active, step), fill(d_upper_all, d_upper, step)

        for step in range(chips):
            if step < chips - 1:
                sec_mine.append(next_chip(sec_mine[step]))
            if step > 0:
                second_all, active_all, d_upper_all = mlp_chunk(
                    step - 1, second_all, active_all, d_upper_all
                )
                if step == chips - 1:
                    ready = sum_of(cross(terms[1]))
            sec_other.append(swap(sec_mine[step], "blk", 1))
            ready, sec_mine, sec_other, terms, second_all, active_all, d_upper_all = hold(
                ready, sec_mine, sec_other, terms, second_all, active_all, d_upper_all
            )
        moving = None
        for step in range(1, chips):
            moving = onward(ready, moving)
            if step == 1:
                second_all, active_all, d_upper_all = mlp_chunk(
                    chips - 1, second_all, active_all, d_upper_all
                )
            ready = sum_of(cross(terms[(step + 1) % chips]))
            if step == 2:
                with jax.named_scope("up_grad"):
                    up_term = cross_rows(second_all, d_upper_all).astype(bf16)
                moving, ready, terms, second_all, active_all, d_upper_all, up_term = hold(
                    moving, ready, terms, second_all, active_all, d_upper_all, up_term
                )
            elif step == 3:
                with jax.named_scope("down_grad"):
                    down_term = cross_rows(active_all, dy_all).astype(bf16)
                moving, ready, terms, down_term = hold(moving, ready, terms, down_term)
            else:
                moving, ready, terms, second_all, active_all, d_upper_all = hold(
                    moving, ready, terms, second_all, active_all, d_upper_all
                )
        d_second = ready + moving.astype(f32)
        upstream = cotangent.astype(f32)
        d_hidden = upstream + norm_back(d_second, hat_second, inv_second, gain_second)
        d_branch_own = d_hidden.astype(bf16)

    def sum_heads(terms):
        return lax.psum_scatter(terms, "head", scatter_dimension=0, tiled=True)

    with jax.named_scope("up_grad"):
        up_sum = sum_heads(up_term)
    d_hidden, d_branch_own, active_all, d_second = hold(
        d_hidden, d_branch_own, active_all, d_second
    )

    with jax.named_scope("d_branch_gather"):
        d_branch = blank((rows, D), bf16)
        mine, other = [d_branch_own], []

        def fill_ordered(buffer, step):
            buffer = lax.dynamic_update_slice_in_dim(buffer, mine[step], place_of(step, 0), 0)
            return lax.dynamic_update_slice_in_dim(buffer, other[step], place_of(step, 1), 0)

        for step in range(chips):
            if step < chips - 1:
                mine.append(next_chip(mine[step]))
            if step > 0:
                d_branch = fill_ordered(d_branch, step - 1)
            other.append(swap(mine[step], "blk", 1))
            if step == 1:
                with jax.named_scope("output"):
                    outs = [
                        [
                            matmul(chunk_of(active_all, k)[:tok], down_w).astype(bf16),
                            matmul(chunk_of(active_all, k)[tok:], down_w).astype(bf16),
                        ]
                        for k in range(chips)
                    ]
                mine, other, d_branch, outs = hold(mine, other, d_branch, outs)
            else:
                mine, other, d_branch = hold(mine, other, d_branch)
        d_branch = fill_ordered(d_branch, chips - 1)
        d_mixed = times_transposed(d_branch, out_w).astype(bf16)
        delta = row_dots(d_mixed, mixed)
    d_mixed, delta, d_branch, up_sum, down_term, mixed = hold(
        d_mixed, delta, d_branch, up_sum, down_term, mixed
    )
    with jax.named_scope("down_grad"):
        down_grad = sum_heads(down_term)

    dq = None

    def kv_grad(m):
        return attend_back(
            spots[2],
            spots[3],
            spots[5][m],
            log_total,
            delta,
            query,
            d_mixed,
            kv_parts[m],
            dq,
        )

    d_kv = {}
    moving = None
    with jax.named_scope("output"):
        ready = sum_of(cross(outs[1]))

    def output_step(step, ready, moving):
        return sum_of(cross(outs[(step + 1) % chips])), onward(ready, moving)

    out_step = 1
    for m in reversed(range(n_head)):
        with jax.named_scope("attention_back"):
            if square and m == 2:
                low = swap(d_kv[3][0], "head", 1)
                high = swap(d_kv[3][1], "head", 2)
            if square and m == 0:
                one = jnp.stack(
                    [d_kv[1][0], (d_kv[1][1].astype(f32) + high.astype(f32)).astype(bf16)]
                )
                two = jnp.stack(
                    [(d_kv[2][0].astype(f32) + low.astype(f32)).astype(bf16), d_kv[2][1]]
                )
                one, two = swap(one, "head", 1), swap(two, "head", 2)
            dq, d_kv[m] = kv_grad(m)
        if m % 2 == 0 and out_step < chips:
            with jax.named_scope("output"):
                ready, moving = output_step(out_step, ready, moving)
                out_step += 1
        if m == 1:
            with jax.named_scope("out_grad"):
                out_term = cross_rows(mixed, d_branch).astype(bf16)
                out_term = out_term.reshape(each, team, w_rows, D).transpose(1, 0, 2, 3)
                out_term = exchange(out_term, "blk", place_in, team)
        if square and m == 1:
            low, high, dq, d_kv, d_mixed, ready, moving, out_term = hold(
                low, high, dq, d_kv, d_mixed, ready, moving, out_term
            )
        elif m > 0:
            dq, d_kv, d_mixed = hold(dq, d_kv, d_mixed)
    with jax.named_scope("up_grad"):
        up_sum = up_sum.reshape(chips, 2, w_rows, n_head * ff_rows)
        up_mine = lax.dynamic_index_in_dim(up_sum, core, 1, keepdims=False)
        up_other = lax.dynamic_index_in_dim(up_sum, 1 - core, 1, keepdims=False)
        up_pieces = pair_up(up_mine, swap(up_other, "blk", 1), chip, core)
    with jax.named_scope("output"):
        while out_step < chips:
            ready, moving = output_step(out_step, ready, moving)
            out_step += 1
    with jax.named_scope("attention_back"):
        if square:
            d_kv = (d_kv[0].astype(f32) + one.astype(f32) + two.astype(f32)).astype(bf16)
        else:
            d_kv = scatter_head(lambda m: d_kv[m].astype(f32)).astype(bf16)
        d_qkv = jnp.concatenate([dq.astype(bf16), d_kv[0], d_kv[1]], axis=1)
    d_qkv, ready, moving, up_pieces, out_term, down_grad = hold(
        d_qkv, ready, moving, up_pieces, out_term, down_grad
    )
    with jax.named_scope("out_grad"):
        out_grad = sum_heads(out_term.reshape(n_head * w_rows, D))

    first_sums = []

    def normed_term(step):
        halves = []
        for other, piece in enumerate((tok_mine[step], tok_other[step])):
            part = lax.dynamic_slice_in_dim(d_qkv, place_of(step, other), tok, 0)
            term = times_transposed(part, qkv_w)
            row_mean, inverse = stats[step, other]
            hat = (piece.astype(f32) - row_mean) * inverse
            first_sums.append((jnp.sum(term * hat, axis=0), jnp.sum(term, axis=0)))
            halves.append(term.astype(bf16))
        return halves

    slab = n_blk * w_rows
    with jax.named_scope("d_normed"):
        term = normed_term(1)
    (term,) = hold(term)
    with jax.named_scope("d_normed"):
        ready_normed = sum_of(cross(term))
    with jax.named_scope("qkv_grad"):
        if square:
            qkv_term = cross_rows(normed, d_qkv).astype(bf16).reshape(n_head, slab, 3 * own_heads)
            far = pick(qkv_term, head ^ 3)
        else:
            far = qkv_term = d_qkv
    with jax.named_scope("output"):
        output = (hidden + (ready + moving.astype(f32) + d_bias)).astype(bf16)
    ready, qkv_term, far, output = hold(ready_normed, qkv_term, far, output)
    with jax.named_scope("d_normed"):
        term = normed_term(2 % chips)
    moving = None
    for step in range(1, chips):
        with jax.named_scope("d_normed"):
            moving = onward(ready, moving)
            ready = sum_of(cross(term))
            if step < chips - 1:
                term = normed_term((step + 2) % chips)
        with jax.named_scope("qkv_grad"):
            if square and step == 1:
                low = swap(far[: slab // 2], "head", 1)
                high = swap(far[slab // 2 :], "head", 2)
                one, two = pick(qkv_term, head ^ 1), pick(qkv_term, head ^ 2)
            if square and step == 2:
                one = jnp.concatenate([one[: slab // 2], one[slab // 2 :] + high])
                two = jnp.concatenate([two[: slab // 2] + low, two[slab // 2 :]])
                one, two = swap(one, "head", 1), swap(two, "head", 2)
        if step == 2:
            with jax.named_scope("down_grad"):
                down_grad = down_grad.astype(f32)
        if square and step == 1:
            ready, term, moving, low, high, one, two, first_sums = hold(
                ready, term, moving, low, high, one, two, first_sums
            )
        elif step == 2:
            ready, term, moving, first_sums, down_grad = hold(
                ready, term, moving, first_sums, down_grad
            )
        else:
            ready, term, moving, first_sums = hold(ready, term, moving, first_sums)
    with jax.named_scope("up_grad"):
        up_pieces = swap_chips(up_pieces)
        (up_grad,) = merge_columns(
            up_pieces, 1, n_head * ff_rows, ff_columns, chip, "merge_up"
        )
    with jax.named_scope("d_normed"):
        d_normed = ready + moving.astype(f32)
        hat_first, inv_first = norm_parts(own)
        tokens_grad = (d_hidden + norm_back(d_normed, hat_first, inv_first, gain_first)).astype(bf16)

    with jax.named_scope("qkv_grad"):
        if square:
            qkv_grad = pick(qkv_term, head).astype(f32) + one.astype(f32) + two.astype(f32)
        else:
            qkv_grad = scatter_head(
                lambda m: cross_rows(
                    lax.dynamic_slice_in_dim(normed, (head ^ m) * slab, slab, 1), d_qkv
                )
            )
        qkv_grad = qkv_grad.astype(bf16).reshape(chips, 2, w_rows, 3 * own_heads)
        qkv_mine = lax.dynamic_index_in_dim(qkv_grad, core, 1, keepdims=False)
        qkv_other = lax.dynamic_index_in_dim(qkv_grad, 1 - core, 1, keepdims=False)
        pieces = swap_chips(pair_up(qkv_mine, swap(qkv_other, "blk", 1), chip, core))
        qkv_grad = merge_columns(pieces, 3, own_heads, head_columns, chip, "merge_heads")

    with jax.named_scope("vector_grads"):
        full = [
            sum(pair[0] for pair in first_sums),
            sum(pair[1] for pair in first_sums),
            jnp.sum(d_branch_own.astype(f32), axis=0),
            jnp.sum(d_second * hat_second, axis=0),
            jnp.sum(d_second, axis=0),
            jnp.sum(upstream, axis=0),
        ]
        parts = [v.reshape(n_head, n_blk, w_rows) for v in full]
        up_row = jnp.sum(d_upper_all.astype(f32), axis=0)
        up_table = jnp.zeros((n_blk, n_head, ff_rows), f32)
        up_table = put(up_table, up_row.reshape(n_head, ff_rows), blk)
        parts.append(up_table.transpose(1, 0, 2))
        for v in (dq.astype(bf16), d_kv[1]):
            bias_sum = jnp.sum(v.astype(f32), axis=0).reshape(each, 1, DH)
            head_table = jnp.zeros((n_head, sets, DH), f32)
            head_table = lax.dynamic_update_slice(
                head_table, bias_sum, (place_in * each, blk // team, 0)
            )
            parts.append(head_table.reshape(n_head, n_blk, w_rows))
        sums = sum_rows(jnp.concatenate(parts, axis=2), head, blk)
        cuts = [sums[i * w_rows : (i + 1) * w_rows] for i in range(6)]
        up_bias_grad = sums[6 * w_rows : 6 * w_rows + ff_rows]
        rest = sums[6 * w_rows + ff_rows :]

    return (
        output,
        tokens_grad,
        cuts[0],
        cuts[1],
        qkv_grad[0],
        qkv_grad[1],
        qkv_grad[2],
        rest[:w_rows],
        rest[w_rows:],
        out_grad.astype(f32),
        cuts[2],
        cuts[3],
        cuts[4],
        up_grad,
        up_bias_grad,
        down_grad.astype(f32),
        cuts[5],
    )


def solution(mesh):
    by_token = P(("blk", "head"), None)
    matrix = P(("head", "blk"), None)
    vector = P(("head", "blk"))
    return jax.shard_map(
        local,
        mesh=mesh,
        in_specs=(
            by_token,
            P(("blk", "head")),
            by_token,
            vector,
            vector,
            matrix,
            matrix,
            matrix,
            vector,
            vector,
            matrix,
            vector,
            vector,
            vector,
            matrix,
            vector,
            matrix,
            vector,
        ),
        out_specs=(
            by_token,
            by_token,
            vector,
            vector,
            matrix,
            matrix,
            matrix,
            vector,
            vector,
            matrix,
            vector,
            vector,
            vector,
            matrix,
            vector,
            matrix,
            vector,
        ),
        check_vma=False,
    )
```

time: 898 us -> 679 us (0.76)
  waiting for transfers between devices: 374 us -> 241 us
  starting transfers between devices: 144 us -> 73 us
  local copies, waits for them, and re-layouts: 130 us -> 66.5 us
  other arithmetic: 59.2 us -> 92.7 us
  between operations: 3.86 us -> 19.1 us
  Pallas kernels: 47.3 us -> 61.7 us
  matrix products: 131 us -> 117 us
    ppermute x128 -> x82, waiting for transfers between devices: 247 us -> 124 us  [swap(): return lax.ppermute(v, axis, [(i, i ^ mask) for i in range(size)])]
    ppermute x128 -> x82, starting transfers between devices: 92.6 us -> 49.9 us  [swap(): return lax.ppermute(v, axis, [(i, i ^ mask) for i in range(size)])]
    dynamic_update_slice x56 -> x3, local copies, waits for them, and re-layouts: 37.1 us -> 1.25 us  [put(): return lax.dynamic_update_index_in_dim(v, part, index, 0)]
    ppermute x36 -> x27, starting transfers between devices: 51.3 us -> 22.5 us  [next_chip(): lax.ppermute(v, 'blk', [(2 * a + c, 2 * b + c) for a, b in moves for c in...]
    dynamic_update_slice x2 -> x26, local copies, waits for them, and re-layouts: 0.23 us -> 20.3 us  [the longest x8 11 us: fill_pair(): buffer = lax.dynamic_update_slice_in_dim(buffer, mine, step * 2 * tok, 0)]
    pallas_call x0 -> x20, Pallas kernels: none -> 15.6 us  [the longest x13 14.9 us: local_call(): pl.pallas_call(kernel, in_specs=[pl.BlockSpec(memory_space=pltpu.SMEM)] +...]
    reduce_sum x4 -> x17, other arithmetic: 3.95 us -> 19.3 us  [the longest x8 9.58 us: add_normed(): jnp.mean(centered * centered, axis=-1, keepdims=True) + norm_epsilon]
    squeeze x18 -> x9, local copies, waits for them, and re-layouts: 11.2 us -> 1.1 us  [pick(): return lax.dynamic_index_in_dim(v, index, 0, keepdims=False)]
  transfers between devices with their start and end apart: 164 -> 113, of which waited for: 67 -> 45; matrix products, arithmetic and copies ran while one was open for 30% -> 38% of each run, Pallas kernels for 5% -> 9%
where the time goes in v2:
time: 679 us; the launch traced here: 671 us
  waiting for transfers between devices  241 us (35%)
  matrix products  117 us (17%)
  other arithmetic  92.7 us (14%)
  starting transfers between devices  73 us (11%)
  local copies, waits for them, and re-layouts  66.5 us (10%)
  Pallas kernels  61.7 us (9%)
  between operations  19.1 us (3%)
    ppermute x82, waiting for transfers between devices, swap(): return lax.ppermute(v, axis, [(i, i ^ mask) for i in range(size)])  124 us
    ppermute x27, waiting for transfers between devices, next_chip(): lax.ppermute(v, 'blk', [(2 * a + c, 2 * b + c) for a, b in moves for c in...  117 us
    dot_general x21, matrix products, times_transposed(): lax.dot_general(left, right, (((1,), (1,)), ((), ())), preferred_element_...  55.3 us
    ppermute x82, starting transfers between devices, swap(): return lax.ppermute(v, axis, [(i, i ^ mask) for i in range(size)])  49.9 us
    dot_general x22, matrix products, matmul(): return jnp.dot(left, right, preferred_element_type=f32)  34.4 us
    pallas_call x4, Pallas kernels, attend_back(): pl.pallas_call(functools.partial(attend_back_kernel, tiles, log2_e * DH *...  30.2 us
    dot_general x4, matrix products, cross_rows(): lax.dot_general(left, right, (((0,), (0,)), ((), ())), preferred_element_...  27.3 us
    ppermute x27, starting transfers between devices, next_chip(): lax.ppermute(v, 'blk', [(2 * a + c, 2 * b + c) for a, b in moves for c in...  22.5 us
  transfers between devices with their start and end apart: 113, of which 45 were waited for; matrix products, arithmetic and copies ran while one was open for 38% of the time, Pallas kernels for 9%

profile of v2, /device:TPU:8, one launch (start us, length us, event | category | flops | bytes accessed | tf_op | source)
XLA Modules:
  0.0 670.9 jit_solution(3934768602173520643)
XLA Ops:
  8.0 6.1 concatenate.65
  26.4 11.9 %collective-permute-done.4 = bf16[8,896]{1,0:T(8,128)(2,1)S(1)} collective-permute-done((bf16[8,896]{1,0:T(8,128)(2,1)S(1)}, bf16[8,896]{1,0:T(8,128)(2,1)S(1)}, u32[]{:S(2)}, u32[]{:S(2)}) %collective-permute-start.4) | collective-permute-done | bytes 14368 | tf_op jit(solution)/shard_map/vectors/ppermute | solution.py:65
  39.0 3.0 collective-permute-start.6
  43.1 3.8 collective-permute-done.5.refs_1_
  49.4 6.7 %collective-permute-done.6.refs_2_ = bf16[2,64,768]{2,1,0:T(8,128)(2,1)S(1)} collective-permute-done((bf16[2,64,768]{2,1,0:T(8,128)(2,1)S(1)}, bf16[2,64,768]{2,1,0:T(8,128)(2,1)S(1)}, u32[]{:S(2)}, u32[]{:S(2)}) %collective-permute-start.6) | collective-permute-done | bytes 196640 | tf_op jit(solution)/shard_map/qkv_weights/ppermute | solution.py:54
  56.1 4.4 collective-permute-done.7.refs_3_
  61.3 2.7 add_multiply_fusion.5
  64.2 3.0 collective-permute-start.17
  102.2 6.1 collective-permute-done.13.refs_6_
  124.8 3.2 collective-permute-start.24
  139.0 6.8 %add_convert_fusion = bf16[1024,768]{1,0:T(8,128)(2,1)S(1)} fusion(bf16[1024,2048]{1,0:T(8,128)(2,1)S(1)} %fusion.141, bf16[2048,768]{1,0:T(8,128)(2,1)} %bitcast.280, f32[768]{0:T(1024)S(1)} %pad_maximum_fusion.10), kind=kOutput, calls=%fused_computation.5 | convolution fusion | flops 3222798336 | bytes 8915968 | tf_op jit(solution)/shard_map/qkv/dot_general | solution.py:24
  161.6 4.3 collective-permute-done.27.refs_1_
  165.9 10.0 %collective-permute-done.28.refs_2_ = bf16[2,64,1024]{2,1,0:T(8,128)(2,1)S(1)} collective-permute-done((bf16[2,64,1024]{2,1,0:T(8,128)(2,1)}, bf16[2,64,1024]{2,1,0:T(8,128)(2,1)S(1)}, u32[]{:S(2)}, u32[]{:S(2)}) %collective-permute-start.28) | collective-permute-done | bytes 262176 | tf_op jit(solution)/shard_map/up_weights/ppermute | solution.py:54
  175.9 5.9 collective-permute-done.29.refs_3_
  192.3 8.3 %collective-permute-done.33 = bf16[32,2048]{1,0:T(8,128)(2,1)} collective-permute-done((bf16[32,2048]{1,0:T(8,128)(2,1)}, bf16[32,2048]{1,0:T(8,128)(2,1)}, u32[]{:S(2)}, u32[]{:S(2)}) %collective-permute-start.33) | collective-permute-done | bytes 131104 | tf_op jit(solution)/shard_map/out_weights/ppermute | solution.py:54
  215.9 16.0 %attend.1 = (bf16[1024,256]{1,0:T(8,128)(2,1)S(1)}, f32[2,1,1024]{2,1,0:T(1,128)S(1)}) custom-call(f32[1024,1]{1,0:T(8,128)S(1)} %copy-done.4, f32[1024,1]{1,0:T(8,128)S(1)} %copy-done.8, bf16[1024,256]{1,0:T(8,128)(2,1)S(1)} %copy-done.9, f32[1,1024]{1,0:T(1,128)S(1)} %get-tuple-element.512.refs_3_.refs_0_, f32[1,1024]{1,0:T(1,128)S(1)} %get-tuple-element.513.refs_4_, ...), custom_call_target="tpu_custom_call" | custom-call | flops 2147483648 | bytes 4194304 | tf_op jit(solution)/shard_map/attention/attend/pallas_call | solution.py:274
  242.6 10.3 %collective-permute-done.41 = bf16[128,2048]{1,0:T(8,128)(2,1)S(1)} collective-permute-done((bf16[128,2048]{1,0:T(8,128)(2,1)S(1)}, bf16[128,2048]{1,0:T(8,128)(2,1)S(1)}, u32[]{:S(2)}, u32[]{:S(2)}) %collective-permute-start.41) | collective-permute-done | bytes 524320 | tf_op jit(solution)/shard_map/branch/ppermute | solution.py:65
  256.0 12.4 %collective-permute-done.44 = bf16[128,2048]{1,0:T(8,128)(2,1)S(1)} collective-permute-done((bf16[128,2048]{1,0:T(8,128)(2,1)S(1)}, bf16[128,2048]{1,0:T(8,128)(2,1)S(1)}, u32[]{:S(2)}, u32[]{:S(2)}) %collective-permute-start.44) | collective-permute-done | bytes 524320 | tf_op jit(solution)/shard_map/branch/ppermute | solution.py:65
  276.2 7.6 %collective-permute-done.47 = bf16[128,2048]{1,0:T(8,128)(2,1)S(1)} collective-permute-done((bf16[128,2048]{1,0:T(8,128)(2,1)S(1)}, bf16[128,2048]{1,0:T(8,128)(2,1)S(1)}, u32[]{:S(2)}, u32[]{:S(2)}) %collective-permute-start.47) | collective-permute-done | bytes 524320 | tf_op jit(solution)/shard_map/branch/ppermute | solution.py:65
  287.8 2.9 place.9
  290.7 8.9 %collective-permute-done.49 = bf16[128,2048]{1,0:T(8,128)(2,1)} collective-permute-done((bf16[128,2048]{1,0:T(8,128)(2,1)S(1)}, bf16[128,2048]{1,0:T(8,128)(2,1)}, u32[]{:S(2)}, u32[]{:S(2)}) %collective-permute-start.49) | collective-permute-done | bytes 524320 | tf_op jit(solution)/shard_map/mlp/ppermute | solution.py:65
  302.1 4.8 fusion.128
  306.9 2.9 constant_dynamic-update-slice_fusion.17
  320.4 2.6 fusion.129
  323.1 2.8 constant_dynamic-update-slice_fusion.14
  333.5 2.6 fusion.130
  336.1 2.8 constant_dynamic-update-slice_fusion.11
  345.0 2.6 fusion.131
  347.6 3.5 constant_dynamic-update-slice_fusion.8
  358.5 8.5 %convolution_convert_fusion.1 = bf16[2048,1024]{1,0:T(8,128)(2,1)} fusion(bf16[1024,2048]{1,0:T(8,128)(2,1)} %constant_dynamic-update-slice_fusion.9, bf16[1024,1024]{1,0:T(8,128)(2,1)S(1)} %get-tuple-element.791), kind=kOutput, calls=%fused_computation.3 | convolution fusion | flops 4297064448 | bytes 10485760 | tf_op jit(solution)/shard_map/mlp/up_grad/dot_general | solution.py:28
  369.3 4.8 collective-permute-done.62
  376.9 9.8 %convolution_convert_fusion = bf16[1024,2048]{1,0:T(8,128)(2,1)} fusion(bf16[1024,1024]{1,0:T(8,128)(2,1)} %copy-done.44, bf16[1024,2048]{1,0:T(8,128)(2,1)} %constant_dynamic-update-slice_fusion.20), kind=kOutput, calls=%fused_computation.2 | convolution fusion | flops 4297064448 | bytes 10485760 | tf_op jit(solution)/shard_map/mlp/down_grad/dot_general | solution.py:28
  388.2 4.2 collective-permute-done.64
  406.5 3.7 collective-permute-done.66
  411.9 11.9 %collective-permute-done.68 = bf16[128,2048]{1,0:T(8,128)(2,1)S(1)} collective-permute-done((bf16[128,2048]{1,0:T(8,128)(2,1)S(1)}, bf16[128,2048]{1,0:T(8,128)(2,1)S(1)}, u32[]{:S(2)}, u32[]{:S(2)}) %collective-permute-start.68) | collective-permute-done | bytes 524320 | tf_op jit(solution)/shard_map/d_branch_gather/ppermute | solution.py:65
  424.1 12.4 %collective-permute-done.70 = bf16[128,2048]{1,0:T(8,128)(2,1)S(1)} collective-permute-done((bf16[128,2048]{1,0:T(8,128)(2,1)S(1)}, bf16[128,2048]{1,0:T(8,128)(2,1)S(1)}, u32[]{:S(2)}, u32[]{:S(2)}) %collective-permute-start.70) | collective-permute-done | bytes 524320 | tf_op jit(solution)/shard_map/d_branch_gather/ppermute | solution.py:65
  451.7 4.0 convolution_convert_fusion.3
  456.2 7.5 %attend_back.4 = (f32[1024,256]{1,0:T(8,128)S(1)}, bf16[2,1024,256]{2,1,0:T(8,128)(2,1)S(1)}) custom-call(f32[1,1024]{1,0:T(1,128)S(1)} %get-tuple-element.512.refs_3_.refs_0_, f32[1,1024]{1,0:T(1,128)S(1)} %bitcast.255, f32[1024,1]{1,0:T(8,128)S(1)} %copy-done.14, f32[2,1,1024]{2,1,0:T(1,128)S(1)} %get-tuple-element.531.refs_3_, ...), custom_call_target="tpu_custom_call" | custom-call | flops 1342177280 | bytes 5242880 | tf_op jit(solution)/shard_map/attention_back/attend_back/pallas_call | solution.py:355
  463.7 7.6 %attend_back.5 = (f32[1024,256]{1,0:T(8,128)S(1)}, bf16[2,1024,256]{2,1,0:T(8,128)(2,1)S(1)}) custom-call(f32[1,1024]{1,0:T(1,128)S(1)} %get-tuple-element.512.refs_3_.refs_0_, f32[1,1024]{1,0:T(1,128)S(1)} %bitcast.256, f32[1024,1]{1,0:T(8,128)S(1)} %copy-done.13, f32[2,1,1024]{2,1,0:T(1,128)S(1)} %get-tuple-element.531.refs_3_, ...), custom_call_target="tpu_custom_call" | custom-call | flops 1342177280 | bytes 5242880 | tf_op jit(solution)/shard_map/attention_back/attend_back/pallas_call | solution.py:355
  475.0 7.6 %attend_back.6 = (f32[1024,256]{1,0:T(8,128)S(1)}, bf16[2,1024,256]{2,1,0:T(8,128)(2,1)S(1)}) custom-call(f32[1,1024]{1,0:T(1,128)S(1)} %get-tuple-element.512.refs_3_.refs_0_, f32[1,1024]{1,0:T(1,128)S(1)} %bitcast.257, f32[1024,1]{1,0:T(8,128)S(1)} %copy-done.12, f32[2,1,1024]{2,1,0:T(1,128)S(1)} %get-tuple-element.531.refs_3_, ...), custom_call_target="tpu_custom_call" | custom-call | flops 1342177280 | bytes 5242880 | tf_op jit(solution)/shard_map/attention_back/attend_back/pallas_call | solution.py:355
  483.3 9.8 %collective-permute-done.73 = bf16[1024,256]{1,0:T(8,128)(2,1)S(1)} collective-permute-done((bf16[1024,256]{1,0:T(8,128)(2,1)}, bf16[1024,256]{1,0:T(8,128)(2,1)S(1)}, u32[]{:S(2)}, u32[]{:S(2)}) %collective-permute-start.73) | collective-permute-done | bytes 524320 | tf_op jit(solution)/shard_map/attention_back/ppermute | solution.py:54
  496.3 2.7 collective-permute-start.83
  503.8 7.6 %attend_back.7 = (f32[1024,256]{1,0:T(8,128)S(1)}, bf16[2,1024,256]{2,1,0:T(8,128)(2,1)S(1)}) custom-call(f32[1,1024]{1,0:T(1,128)S(1)} %get-tuple-element.512.refs_3_.refs_0_, f32[1,1024]{1,0:T(1,128)S(1)} %bitcast.258, f32[1024,1]{1,0:T(8,128)S(1)} %copy-done.5, f32[2,1,1024]{2,1,0:T(1,128)S(1)} %get-tuple-element.531.refs_3_, ...), custom_call_target="tpu_custom_call" | custom-call | flops 1342177280 | bytes 5242880 | tf_op jit(solution)/shard_map/attention_back/attend_back/pallas_call | solution.py:355
  516.3 7.0 %collective-permute-done.79 = bf16[2,1024,256]{2,1,0:T(8,128)(2,1)} collective-permute-done((bf16[2,1024,256]{2,1,0:T(8,128)(2,1)}, bf16[2,1024,256]{2,1,0:T(8,128)(2,1)}, u32[]{:S(2)}, u32[]{:S(2)}) %collective-permute-start.79) | collective-permute-done | bytes 1048608 | tf_op jit(solution)/shard_map/attention_back/ppermute | solution.py:54
  532.5 4.4 fusion.244
  536.9 5.0 convolution_convert_fusion.2
  542.0 3.7 fusion.246
  545.7 3.7 fusion.247
  552.5 3.9 fusion.243
  556.4 3.7 fusion.240
  563.7 3.7 fusion.242
  571.1 2.8 collective-permute-start.89
  574.0 2.5 fusion.245
  576.6 9.2 %collective-permute-done.89 = bf16[256,768]{1,0:T(8,128)(2,1)S(1)} collective-permute-done((bf16[256,768]{1,0:T(8,128)(2,1)S(1)}, bf16[256,768]{1,0:T(8,128)(2,1)S(1)}, u32[]{:S(2)}, u32[]{:S(2)}) %collective-permute-start.89) | collective-permute-done | bytes 393248 | tf_op jit(solution)/shard_map/qkv_grad/ppermute | solution.py:54
  590.4 12.8 %collective-permute-done.92 = bf16[128,2048]{1,0:T(8,128)(2,1)S(1)} collective-permute-done((bf16[128,2048]{1,0:T(8,128)(2,1)S(1)}, bf16[128,2048]{1,0:T(8,128)(2,1)S(1)}, u32[]{:S(2)}, u32[]{:S(2)}) %collective-permute-start.92) | collective-permute-done | bytes 524320 | tf_op jit(solution)/shard_map/d_normed/ppermute | solution.py:65
  603.6 2.8 collective-permute-done.100
  608.7 10.1 %collective-permute-done.94 = bf16[128,2048]{1,0:T(8,128)(2,1)S(1)} collective-permute-done((bf16[128,2048]{1,0:T(8,128)(2,1)S(1)}, bf16[128,2048]{1,0:T(8,128)(2,1)S(1)}, u32[]{:S(2)}, u32[]{:S(2)}) %collective-permute-start.94) | collective-permute-done | bytes 524320 | tf_op jit(solution)/shard_map/d_normed/ppermute | solution.py:65
  620.7 2.6 collective-permute-done.95
  627.5 4.5 collective-permute-done.97
  632.1 3.6 collective-permute-done.98
  635.8 2.5 fusion.32
  645.5 4.1 collective-permute-done.103.refs_1_
  649.5 7.6 %collective-permute-done.104.refs_2_ = bf16[2,64,768]{2,1,0:T(8,128)(2,1)S(1)} collective-permute-done((bf16[2,64,768]{2,1,0:T(8,128)(2,1)S(1)}, bf16[2,64,768]{2,1,0:T(8,128)(2,1)S(1)}, u32[]{:S(2)}, u32[]{:S(2)}) %collective-permute-start.104) | collective-permute-done | bytes 196640 | tf_op jit(solution)/shard_map/qkv_grad/ppermute | solution.py:54
  657.1 5.5 collective-permute-done.105.refs_3_
  (660 shorter events, 275.4 us)
Async XLA Ops:
  7.2 294.9 %all-gather.2.cloned.1.call-start = ((), (), s32[]{:S(2)}) async-start(), calls=%async_computation.3 | async-start | bytes 5242880 | tf_op jit(solution)/shard_map/up_weights/all_gather | solution.py:674
  22.6 38.6 %collective-permute-start.9 = (bf16[128,2048]{1,0:T(8,128)(2,1)}, bf16[128,2048]{1,0:T(8,128)(2,1)}, u32[]{:S(2)}, u32[]{:S(2)}) collective-permute-start(bf16[128,2048]{1,0:T(8,128)(2,1)} %param.19), channel_id=1, source_target_pairs={{0,4},{1,5},{4,6},{5,7},{6,2},{7,3},{2,0},{3,1},{8,12},{9,13},{12,... | collective-permute-start | bytes 1572872 | tf_op jit(solution)/shard_map/tokens_gather/ppermute | solution.py:65
  38.3 22.8 %collective-permute-start.10 = (bf16[128,2048]{1,0:T(8,128)(2,1)}, bf16[128,2048]{1,0:T(8,128)(2,1)}, u32[]{:S(2)}, u32[]{:S(2)}) collective-permute-start(bf16[128,2048]{1,0:T(8,128)(2,1)} %param.19), channel_id=1, source_target_pairs={{0,1},{1,0},{2,3},{3,2},{4,5},{5,4},{6,7},{7,6},{8,9},{9,8},{10,11... | collective-permute-start | bytes 1572872 | tf_op jit(solution)/shard_map/tokens_gather/ppermute | solution.py:54
  39.0 17.1 %collective-permute-start.6 = (bf16[2,64,768]{2,1,0:T(8,128)(2,1)S(1)}, bf16[2,64,768]{2,1,0:T(8,128)(2,1)S(1)}, u32[]{:S(2)}, u32[]{:S(2)}) collective-permute-start(bf16[2,64,768]{2,1,0:T(8,128)(2,1)S(1)} %get-tuple-element.421), channel_id=1, source_target_pairs={{0,4},{1,5},{2,6},{3,7},{4,0},{5,1},{6,2},{7,3},{8,12},{9,13},{10,... | collective-permute-start | bytes 589832 | tf_op jit(solution)/shard_map/qkv_weights/ppermute | solution.py:54
  42.1 18.5 %collective-permute-start.7 = (bf16[2,64,768]{2,1,0:T(8,128)(2,1)S(1)}, bf16[2,64,768]{2,1,0:T(8,128)(2,1)S(1)}, u32[]{:S(2)}, u32[]{:S(2)}) collective-permute-start(bf16[2,64,768]{2,1,0:T(8,128)(2,1)S(1)} %get-tuple-element.422), channel_id=1, source_target_pairs={{0,6},{1,7},{2,4},{3,5},{4,2},{5,3},{6,0},{7,1},{8,14},{9,15},{10,... | collective-permute-start | bytes 589832 | tf_op jit(solution)/shard_map/qkv_weights/ppermute | solution.py:54
  70.1 25.6 %collective-permute-start.12 = (bf16[512,768]{1,0:T(8,128)(2,1)S(1)}, bf16[512,768]{1,0:T(8,128)(2,1)}, u32[]{:S(2)}, u32[]{:S(2)}) collective-permute-start(bf16[512,768]{1,0:T(8,128)(2,1)S(1)} %bitcast.251), channel_id=1, source_target_pairs={{0,16},{8,24},{16,0},{24,8},{1,17},{9,25},{17,1},{25,9},{2,18},{10... | collective-permute-start | bytes 2359304 | tf_op jit(solution)/shard_map/qkv_weights/ppermute | solution.py:54
  71.6 25.7 %collective-permute-start.11 = (bf16[512,768]{1,0:T(8,128)(2,1)S(1)}, bf16[512,768]{1,0:T(8,128)(2,1)}, u32[]{:S(2)}, u32[]{:S(2)}) collective-permute-start(bf16[512,768]{1,0:T(8,128)(2,1)S(1)} %bitcast.252), channel_id=1, source_target_pairs={{0,8},{8,0},{16,24},{24,16},{1,9},{9,1},{17,25},{25,17},{2,10},{10... | collective-permute-start | bytes 2359304 | tf_op jit(solution)/shard_map/qkv_weights/ppermute | solution.py:54
  75.9 26.3 %collective-permute-start.18 = (bf16[128,2048]{1,0:T(8,128)(2,1)}, bf16[128,2048]{1,0:T(8,128)(2,1)}, u32[]{:S(2)}, u32[]{:S(2)}) collective-permute-start(bf16[128,2048]{1,0:T(8,128)(2,1)} %collective-permute-done.15), channel_id=1, source_target_pairs={{0,4},{1,5},{4,6},{5,7},{6,2},{7,3},{2,0},{3,1},{8,12},{9,13},{12,... | collective-permute-start | bytes 1572872 | tf_op jit(solution)/shard_map/tokens_gather/ppermute | solution.py:65
  75.9 26.3 %collective-permute-start.19 = (bf16[128,2048]{1,0:T(8,128)(2,1)}, bf16[128,2048]{1,0:T(8,128)(2,1)S(1)}, u32[]{:S(2)}, u32[]{:S(2)}) collective-permute-start(bf16[128,2048]{1,0:T(8,128)(2,1)} %collective-permute-done.15), channel_id=1, source_target_pairs={{0,1},{1,0},{2,3},{3,2},{4,5},{5,4},{6,7},{7,6},{8,9},{9,8},{10,11... | collective-permute-start | bytes 1572872 | tf_op jit(solution)/shard_map/tokens_gather/ppermute | solution.py:54
  109.6 24.3 %collective-permute-start.20 = (bf16[128,2048]{1,0:T(8,128)(2,1)}, bf16[128,2048]{1,0:T(8,128)(2,1)}, u32[]{:S(2)}, u32[]{:S(2)}) collective-permute-start(bf16[128,2048]{1,0:T(8,128)(2,1)} %collective-permute-done.18), channel_id=1, source_target_pairs={{0,1},{1,0},{2,3},{3,2},{4,5},{5,4},{6,7},{7,6},{8,9},{9,8},{10,11... | collective-permute-start | bytes 1572872 | tf_op jit(solution)/shard_map/tokens_gather/ppermute | solution.py:54
  110.9 37.2 %collective-permute-start.22 = (bf16[64,2048]{1,0:T(8,128)(2,1)}, bf16[64,2048]{1,0:T(8,128)(2,1)S(1)}, u32[]{:S(2)}, u32[]{:S(2)}) collective-permute-start(bf16[64,2048]{1,0:T(8,128)(2,1)} %refs_0_.3), channel_id=1, source_target_pairs={{0,8},{8,0},{16,24},{24,16},{1,9},{9,1},{17,25},{25,17},{2,10},{10... | collective-permute-start | bytes 786440 | tf_op jit(solution)/shard_map/out_weights/ppermute | solution.py:54
  112.5 35.7 %collective-permute-start.23 = (bf16[64,2048]{1,0:T(8,128)(2,1)}, bf16[64,2048]{1,0:T(8,128)(2,1)}, u32[]{:S(2)}, u32[]{:S(2)}) collective-permute-start(bf16[64,2048]{1,0:T(8,128)(2,1)} %refs_0_.3), channel_id=1, source_target_pairs={{0,16},{8,24},{16,0},{24,8},{1,17},{9,25},{17,1},{25,9},{2,18},{10... | collective-permute-start | bytes 786440 | tf_op jit(solution)/shard_map/out_weights/ppermute | solution.py:54
  114.0 32.7 %collective-permute-start.21 = (bf16[4,64,1024]{2,1,0:T(8,128)(2,1)}, bf16[4,64,1024]{2,1,0:T(8,128)(2,1)S(1)}, u32[]{:S(2)}, u32[]{:S(2)}) collective-permute-start(bf16[4,64,1024]{2,1,0:T(8,128)(2,1)} %get-tuple-element.484), channel_id=1, source_target_pairs={{0,1},{1,0},{2,3},{3,2},{4,5},{5,4},{6,7},{7,6},{8,9},{9,8},{10,11... | collective-permute-start | bytes 1572872 | tf_op jit(solution)/shard_map/up_weights/ppermute | solution.py:54
  124.8 23.4 %collective-permute-start.24 = (bf16[128,2048]{1,0:T(8,128)(2,1)}, bf16[128,2048]{1,0:T(8,128)(2,1)S(1)}, u32[]{:S(2)}, u32[]{:S(2)}) collective-permute-start(bf16[128,2048]{1,0:T(8,128)(2,1)} %param.21), channel_id=1, source_target_pairs={{0,4},{1,5},{4,6},{5,7},{6,2},{7,3},{2,0},{3,1},{8,12},{9,13},{12,... | collective-permute-start | bytes 1572872 | tf_op jit(solution)/shard_map/dy_gather/ppermute | solution.py:65
  148.9 35.4 %collective-permute-start.25 = (bf16[2,1024,256]{2,1,0:T(8,128)(2,1)S(1)}, bf16[2,1024,256]{2,1,0:T(8,128)(2,1)S(1)}, u32[]{:S(2)}, u32[]{:S(2)}) collective-permute-start(bf16[2,1024,256]{2,1,0:T(8,128)(2,1)S(1)} %pad_maximum_fusion.1.refs_7_.refs_11_.refs_8_), channel_id=1, source_target_pairs={{0,8},{8,0},{16,24},{24,16},{1,9},{9,1},{17,25},{25,17},{2,10},{10... | collective-permute-start | bytes 3145736 | tf_op jit(solution)/shard_map/kv_gather/ppermute | solution.py:54
  149.5 34.9 %collective-permute-start.26 = (bf16[2,1024,256]{2,1,0:T(8,128)(2,1)S(1)}, bf16[2,1024,256]{2,1,0:T(8,128)(2,1)S(1)}, u32[]{:S(2)}, u32[]{:S(2)}) collective-permute-start(bf16[2,1024,256]{2,1,0:T(8,128)(2,1)S(1)} %pad_maximum_fusion.1.refs_7_.refs_11_.refs_8_), channel_id=1, source_target_pairs={{0,16},{8,24},{16,0},{24,8},{1,17},{9,25},{17,1},{25,9},{2,18},{10... | collective-permute-start | bytes 3145736 | tf_op jit(solution)/shard_map/kv_gather/ppermute | solution.py:54
  155.7 20.2 %collective-permute-start.28 = (bf16[2,64,1024]{2,1,0:T(8,128)(2,1)}, bf16[2,64,1024]{2,1,0:T(8,128)(2,1)S(1)}, u32[]{:S(2)}, u32[]{:S(2)}) collective-permute-start(bf16[2,64,1024]{2,1,0:T(8,128)(2,1)} %copy-done.27), channel_id=1, source_target_pairs={{0,4},{1,5},{2,6},{3,7},{4,0},{5,1},{6,2},{7,3},{8,12},{9,13},{10,... | collective-permute-start | bytes 786440 | tf_op jit(solution)/shard_map/up_weights/ppermute | solution.py:54
  157.6 24.2 %collective-permute-start.29 = (bf16[2,64,1024]{2,1,0:T(8,128)(2,1)}, bf16[2,64,1024]{2,1,0:T(8,128)(2,1)S(1)}, u32[]{:S(2)}, u32[]{:S(2)}) collective-permute-start(bf16[2,64,1024]{2,1,0:T(8,128)(2,1)} %copy-done.26), channel_id=1, source_target_pairs={{0,6},{1,7},{2,4},{3,5},{4,2},{5,3},{6,0},{7,1},{8,14},{9,15},{10,... | collective-permute-start | bytes 786440 | tf_op jit(solution)/shard_map/up_weights/ppermute | solution.py:54
  185.2 18.5 %collective-permute-start.30 = (bf16[1024,256]{1,0:T(8,128)(2,1)}, bf16[1024,256]{1,0:T(8,128)(2,1)}, u32[]{:S(2)}, u32[]{:S(2)}) collective-permute-start(bf16[1024,256]{1,0:T(8,128)(2,1)} %slice_bitcast_fusion.7), channel_id=1, source_target_pairs={{0,8},{8,0},{16,24},{24,16},{1,9},{9,1},{17,25},{25,17},{2,10},{10... | collective-permute-start | bytes 1572872 | tf_op jit(solution)/shard_map/kv_gather/ppermute | solution.py:54
  187.5 16.2 %collective-permute-start.31 = (bf16[1024,256]{1,0:T(8,128)(2,1)}, bf16[1024,256]{1,0:T(8,128)(2,1)}, u32[]{:S(2)}, u32[]{:S(2)}) collective-permute-start(bf16[1024,256]{1,0:T(8,128)(2,1)} %slice_bitcast_fusion.6), channel_id=1, source_target_pairs={{0,16},{8,24},{16,0},{24,8},{1,17},{9,25},{17,1},{25,9},{2,18},{10... | collective-permute-start | bytes 1572872 | tf_op jit(solution)/shard_map/kv_gather/ppermute | solution.py:54
  189.0 16.9 %collective-permute-start.32 = (bf16[128,2048]{1,0:T(8,128)(2,1)}, bf16[128,2048]{1,0:T(8,128)(2,1)}, u32[]{:S(2)}, u32[]{:S(2)}) collective-permute-start(bf16[128,2048]{1,0:T(8,128)(2,1)} %copy-done.73), channel_id=1, source_target_pairs={{0,4},{1,5},{4,6},{5,7},{6,2},{7,3},{2,0},{3,1},{8,12},{9,13},{12,... | collective-permute-start | bytes 1572872 | tf_op jit(solution)/shard_map/dy_gather/ppermute | solution.py:65
  209.0 23.1 %collective-permute-start.39 = (bf16[2,64,2048]{2,1,0:T(8,128)(2,1)}, bf16[2,64,2048]{2,1,0:T(8,128)(2,1)}, u32[]{:S(2)}, u32[]{:S(2)}) collective-permute-start(bf16[2,64,2048]{2,1,0:T(8,128)(2,1)} %dynamic-slice_bitcast_fusion.6), channel_id=1, source_target_pairs={{0,1},{1,0},{2,3},{3,2},{4,5},{5,4},{6,7},{7,6},{8,9},{9,8},{10,11... | collective-permute-start | bytes 1572872 | tf_op jit(solution)/shard_map/out_weights/ppermute | solution.py:54
  210.2 45.7 %collective-permute-start.35 = (bf16[256,2048]{1,0:T(8,128)(2,1)}, bf16[256,2048]{1,0:T(8,128)(2,1)}, u32[]{:S(2)}, u32[]{:S(2)}) collective-permute-start(bf16[256,2048]{1,0:T(8,128)(2,1)} %param.35), channel_id=1, source_target_pairs={{0,8},{8,0},{16,24},{24,16},{1,9},{9,1},{17,25},{25,17},{2,10},{10... | collective-permute-start | bytes 3145736 | tf_op jit(solution)/shard_map/down_weights/ppermute | solution.py:54
  210.7 45.2 %collective-permute-start.36 = (bf16[256,2048]{1,0:T(8,128)(2,1)}, bf16[256,2048]{1,0:T(8,128)(2,1)}, u32[]{:S(2)}, u32[]{:S(2)}) collective-permute-start(bf16[256,2048]{1,0:T(8,128)(2,1)} %param.35), channel_id=1, source_target_pairs={{0,16},{8,24},{16,0},{24,8},{1,17},{9,25},{17,1},{25,9},{2,18},{10... | collective-permute-start | bytes 3145736 | tf_op jit(solution)/shard_map/down_weights/ppermute | solution.py:54
  212.3 21.0 %collective-permute-start.37 = (bf16[128,2048]{1,0:T(8,128)(2,1)}, bf16[128,2048]{1,0:T(8,128)(2,1)}, u32[]{:S(2)}, u32[]{:S(2)}) collective-permute-start(bf16[128,2048]{1,0:T(8,128)(2,1)} %collective-permute-done.32), channel_id=1, source_target_pairs={{0,4},{1,5},{4,6},{5,7},{6,2},{7,3},{2,0},{3,1},{8,12},{9,13},{12,... | collective-permute-start | bytes 1572872 | tf_op jit(solution)/shard_map/dy_gather/ppermute | solution.py:65
  212.3 21.0 %collective-permute-start.38 = (bf16[128,2048]{1,0:T(8,128)(2,1)}, bf16[128,2048]{1,0:T(8,128)(2,1)}, u32[]{:S(2)}, u32[]{:S(2)}) collective-permute-start(bf16[128,2048]{1,0:T(8,128)(2,1)} %param.21), channel_id=1, source_target_pairs={{0,1},{1,0},{2,3},{3,2},{4,5},{5,4},{6,7},{7,6},{8,9},{9,8},{10,11... | collective-permute-start | bytes 1572872 | tf_op jit(solution)/shard_map/dy_gather/ppermute | solution.py:54
  212.3 229.8 %reduce-scatter.4.cloned.1.call-start = ((), (), s32[]{:S(2)}) async-start(), calls=%async_computation.4 | async-start | bytes 5242880 | tf_op jit(solution)/shard_map/up_grad/reduce_scatter | solution.py:818
  237.7 15.2 %collective-permute-start.41 = (bf16[128,2048]{1,0:T(8,128)(2,1)S(1)}, bf16[128,2048]{1,0:T(8,128)(2,1)S(1)}, u32[]{:S(2)}, u32[]{:S(2)}) collective-permute-start(bf16[128,2048]{1,0:T(8,128)(2,1)S(1)} %fusion.1), channel_id=1, source_target_pairs={{0,4},{1,5},{4,6},{5,7},{6,2},{7,3},{2,0},{3,1},{8,12},{9,13},{12,... | collective-permute-start | bytes 1572872 | tf_op jit(solution)/shard_map/branch/ppermute | solution.py:65
  253.1 15.3 %collective-permute-start.44 = (bf16[128,2048]{1,0:T(8,128)(2,1)S(1)}, bf16[128,2048]{1,0:T(8,128)(2,1)S(1)}, u32[]{:S(2)}, u32[]{:S(2)}) collective-permute-start(bf16[128,2048]{1,0:T(8,128)(2,1)S(1)} %add_convert_fusion.12), channel_id=1, source_target_pairs={{0,4},{1,5},{4,6},{5,7},{6,2},{7,3},{2,0},{3,1},{8,12},{9,13},{12,... | collective-permute-start | bytes 1572872 | tf_op jit(solution)/shard_map/branch/ppermute | solution.py:65
  268.5 15.3 %collective-permute-start.47 = (bf16[128,2048]{1,0:T(8,128)(2,1)S(1)}, bf16[128,2048]{1,0:T(8,128)(2,1)S(1)}, u32[]{:S(2)}, u32[]{:S(2)}) collective-permute-start(bf16[128,2048]{1,0:T(8,128)(2,1)S(1)} %add_convert_fusion.11), channel_id=1, source_target_pairs={{0,4},{1,5},{4,6},{5,7},{6,2},{7,3},{2,0},{3,1},{8,12},{9,13},{12,... | collective-permute-start | bytes 1572872 | tf_op jit(solution)/shard_map/branch/ppermute | solution.py:65
  269.9 17.9 %collective-permute-start.54 = (bf16[128,2048]{1,0:T(8,128)(2,1)S(1)}, bf16[128,2048]{1,0:T(8,128)(2,1)S(1)}, u32[]{:S(2)}, u32[]{:S(2)}) collective-permute-start(bf16[128,2048]{1,0:T(8,128)(2,1)S(1)} %get-tuple-element.860.refs_4_), channel_id=1, source_target_pairs={{0,8},{8,0},{16,24},{24,16},{1,9},{9,1},{17,25},{25,17},{2,10},{10... | collective-permute-start | bytes 1572872 | tf_op jit(solution)/shard_map/branch/down_weights/ppermute | solution.py:54
  272.8 15.0 %collective-permute-start.55 = (bf16[128,2048]{1,0:T(8,128)(2,1)S(1)}, bf16[128,2048]{1,0:T(8,128)(2,1)S(1)}, u32[]{:S(2)}, u32[]{:S(2)}) collective-permute-start(bf16[128,2048]{1,0:T(8,128)(2,1)S(1)} %get-tuple-element.861.refs_3_), channel_id=1, source_target_pairs={{0,16},{8,24},{16,0},{24,8},{1,17},{9,25},{17,1},{25,9},{2,18},{10... | collective-permute-start | bytes 1572872 | tf_op jit(solution)/shard_map/branch/down_weights/ppermute | solution.py:54
  285.3 15.9 %collective-permute-start.53 = (bf16[128,2048]{1,0:T(8,128)(2,1)}, bf16[128,2048]{1,0:T(8,128)(2,1)S(1)}, u32[]{:S(2)}, u32[]{:S(2)}) collective-permute-start(bf16[128,2048]{1,0:T(8,128)(2,1)} %collective-permute-done.37), channel_id=1, source_target_pairs={{0,1},{1,0},{2,3},{3,2},{4,5},{5,4},{6,7},{7,6},{8,9},{9,8},{10,11... | collective-permute-start | bytes 1572872 | tf_op jit(solution)/shard_map/branch/dy_gather/ppermute | solution.py:54
  299.6 14.9 %collective-permute-start.51 = (bf16[128,2048]{1,0:T(8,128)(2,1)}, bf16[128,2048]{1,0:T(8,128)(2,1)}, u32[]{:S(2)}, u32[]{:S(2)}) collective-permute-start(bf16[128,2048]{1,0:T(8,128)(2,1)} %collective-permute-done.49), channel_id=1, source_target_pairs={{0,4},{1,5},{4,6},{5,7},{6,2},{7,3},{2,0},{3,1},{8,12},{9,13},{12,... | collective-permute-start | bytes 1572872 | tf_op jit(solution)/shard_map/mlp/ppermute | solution.py:65
  299.6 14.9 %collective-permute-start.52 = (bf16[128,2048]{1,0:T(8,128)(2,1)}, bf16[128,2048]{1,0:T(8,128)(2,1)}, u32[]{:S(2)}, u32[]{:S(2)}) collective-permute-start(bf16[128,2048]{1,0:T(8,128)(2,1)} %collective-permute-done.49), channel_id=1, source_target_pairs={{0,1},{1,0},{2,3},{3,2},{4,5},{5,4},{6,7},{7,6},{8,9},{9,8},{10,11... | collective-permute-start | bytes 1572872 | tf_op jit(solution)/shard_map/mlp/ppermute | solution.py:54
  314.5 15.7 %collective-permute-start.56 = (bf16[128,2048]{1,0:T(8,128)(2,1)}, bf16[128,2048]{1,0:T(8,128)(2,1)S(1)}, u32[]{:S(2)}, u32[]{:S(2)}) collective-permute-start(bf16[128,2048]{1,0:T(8,128)(2,1)} %collective-permute-done.51), channel_id=1, source_target_pairs={{0,4},{1,5},{4,6},{5,7},{6,2},{7,3},{2,0},{3,1},{8,12},{9,13},{12,... | collective-permute-start | bytes 1572872 | tf_op jit(solution)/shard_map/mlp/ppermute | solution.py:65
  342.2 15.4 %collective-permute-start.60 = (bf16[128,2048]{1,0:T(8,128)(2,1)S(1)}, bf16[128,2048]{1,0:T(8,128)(2,1)S(1)}, u32[]{:S(2)}, u32[]{:S(2)}) collective-permute-start(bf16[128,2048]{1,0:T(8,128)(2,1)S(1)} %convert_add_fusion.15), channel_id=1, source_target_pairs={{0,4},{1,5},{4,6},{5,7},{6,2},{7,3},{2,0},{3,1},{8,12},{9,13},{12,... | collective-permute-start | bytes 1572872 | tf_op jit(solution)/shard_map/mlp/ppermute | solution.py:65
  358.5 15.6 %collective-permute-start.62 = (bf16[128,2048]{1,0:T(8,128)(2,1)}, bf16[128,2048]{1,0:T(8,128)(2,1)}, u32[]{:S(2)}, u32[]{:S(2)}) collective-permute-start(bf16[128,2048]{1,0:T(8,128)(2,1)} %add_convert_fusion.9), channel_id=1, source_target_pairs={{0,4},{1,5},{4,6},{5,7},{6,2},{7,3},{2,0},{3,1},{8,12},{9,13},{12,... | collective-permute-start | bytes 1572872 | tf_op jit(solution)/shard_map/mlp/ppermute | solution.py:65
  374.1 154.9 %reduce-scatter.6.cloned.1.call-start = ((), (), s32[]{:S(2)}) async-start(), calls=%async_computation.5 | async-start | bytes 5242880 | tf_op jit(solution)/shard_map/down_grad/reduce_scatter | solution.py:818
  376.5 15.9 %collective-permute-start.64 = (bf16[128,2048]{1,0:T(8,128)(2,1)}, bf16[128,2048]{1,0:T(8,128)(2,1)}, u32[]{:S(2)}, u32[]{:S(2)}) collective-permute-start(bf16[128,2048]{1,0:T(8,128)(2,1)} %add_convert_fusion.8), channel_id=1, source_target_pairs={{0,4},{1,5},{4,6},{5,7},{6,2},{7,3},{2,0},{3,1},{8,12},{9,13},{12,... | collective-permute-start | bytes 1572872 | tf_op jit(solution)/shard_map/mlp/ppermute | solution.py:65
  442.1 196.2 %reduce-scatter.8.cloned.1.call-start = ((), (), s32[]{:S(2)}) async-start(), calls=%async_computation.6 | async-start | bytes 1310720 | tf_op jit(solution)/shard_map/out_grad/reduce_scatter | solution.py:818
  448.8 65.1 %collective-permute-start.82 = (bf16[128,2048]{1,0:T(8,128)(2,1)}, bf16[128,2048]{1,0:T(8,128)(2,1)}, u32[]{:S(2)}, u32[]{:S(2)}) collective-permute-start(bf16[128,2048]{1,0:T(8,128)(2,1)} %convolution_convert_fusion.4), channel_id=1, source_target_pairs={{0,1},{1,0},{2,3},{3,2},{4,5},{5,4},{6,7},{7,6},{8,9},{9,8},{10,11... | collective-permute-start | bytes 1572872 | tf_op jit(solution)/shard_map/output/ppermute | solution.py:54
  450.3 32.5 %collective-permute-start.77 = (bf16[128,2048]{1,0:T(8,128)(2,1)S(1)}, bf16[128,2048]{1,0:T(8,128)(2,1)S(1)}, u32[]{:S(2)}, u32[]{:S(2)}) collective-permute-start(bf16[128,2048]{1,0:T(8,128)(2,1)S(1)} %add_convert_fusion.7), channel_id=1, source_target_pairs={{0,4},{1,5},{4,6},{5,7},{6,2},{7,3},{2,0},{3,1},{8,12},{9,13},{12,... | collective-permute-start | bytes 1572872 | tf_op jit(solution)/shard_map/output/ppermute | solution.py:65
  455.8 26.8 %collective-permute-start.78 = (bf16[2,64,2048]{2,1,0:T(8,128)(2,1)S(1)}, bf16[2,64,2048]{2,1,0:T(8,128)(2,1)S(1)}, u32[]{:S(2)}, u32[]{:S(2)}) collective-permute-start(bf16[2,64,2048]{2,1,0:T(8,128)(2,1)S(1)} %dynamic-slice_bitcast_fusion.5), channel_id=1, source_target_pairs={{0,1},{1,0},{2,3},{3,2},{4,5},{5,4},{6,7},{7,6},{8,9},{9,8},{10,11... | collective-permute-start | bytes 1572872 | tf_op jit(solution)/shard_map/out_grad/ppermute | solution.py:54
  472.2 20.9 %collective-permute-start.73 = (bf16[1024,256]{1,0:T(8,128)(2,1)}, bf16[1024,256]{1,0:T(8,128)(2,1)S(1)}, u32[]{:S(2)}, u32[]{:S(2)}) collective-permute-start(bf16[1024,256]{1,0:T(8,128)(2,1)} %get-tuple-element.858), channel_id=1, source_target_pairs={{0,8},{8,0},{16,24},{24,16},{1,9},{9,1},{17,25},{25,17},{2,10},{10... | collective-permute-start | bytes 1572872 | tf_op jit(solution)/shard_map/attention_back/ppermute | solution.py:54
  473.7 21.7 %collective-permute-start.74 = (bf16[1024,256]{1,0:T(8,128)(2,1)S(1)}, bf16[1024,256]{1,0:T(8,128)(2,1)S(1)}, u32[]{:S(2)}, u32[]{:S(2)}) collective-permute-start(bf16[1024,256]{1,0:T(8,128)(2,1)S(1)} %get-tuple-element.857), channel_id=1, source_target_pairs={{0,16},{8,24},{16,0},{24,8},{1,17},{9,25},{17,1},{25,9},{2,18},{10... | collective-permute-start | bytes 1572872 | tf_op jit(solution)/shard_map/attention_back/ppermute | solution.py:54
  482.6 19.3 %collective-permute-start.81 = (bf16[128,2048]{1,0:T(8,128)(2,1)S(1)}, bf16[128,2048]{1,0:T(8,128)(2,1)S(1)}, u32[]{:S(2)}, u32[]{:S(2)}) collective-permute-start(bf16[128,2048]{1,0:T(8,128)(2,1)S(1)} %copy-done.71), channel_id=1, source_target_pairs={{0,1},{1,0},{2,3},{3,2},{4,5},{5,4},{6,7},{7,6},{8,9},{9,8},{10,11... | collective-permute-start | bytes 1572872 | tf_op jit(solution)/shard_map/output/ppermute | solution.py:54
  482.8 29.6 %collective-permute-start.85 = (bf16[4,64,1024]{2,1,0:T(8,128)(2,1)}, bf16[4,64,1024]{2,1,0:T(8,128)(2,1)S(1)}, u32[]{:S(2)}, u32[]{:S(2)}) collective-permute-start(bf16[4,64,1024]{2,1,0:T(8,128)(2,1)} %get-tuple-element.853), channel_id=1, source_target_pairs={{0,1},{1,0},{2,3},{3,2},{4,5},{5,4},{6,7},{7,6},{8,9},{9,8},{10,11... | collective-permute-start | bytes 1572872 | tf_op jit(solution)/shard_map/up_grad/ppermute | solution.py:54
  496.3 17.5 %collective-permute-start.83 = (bf16[128,2048]{1,0:T(8,128)(2,1)}, bf16[128,2048]{1,0:T(8,128)(2,1)}, u32[]{:S(2)}, u32[]{:S(2)}) collective-permute-start(bf16[128,2048]{1,0:T(8,128)(2,1)} %add_convert_fusion.6), channel_id=1, source_target_pairs={{0,4},{1,5},{4,6},{5,7},{6,2},{7,3},{2,0},{3,1},{8,12},{9,13},{12,... | collective-permute-start | bytes 1572872 | tf_op jit(solution)/shard_map/output/ppermute | solution.py:65
  500.3 23.1 %collective-permute-start.79 = (bf16[2,1024,256]{2,1,0:T(8,128)(2,1)}, bf16[2,1024,256]{2,1,0:T(8,128)(2,1)}, u32[]{:S(2)}, u32[]{:S(2)}) collective-permute-start(bf16[2,1024,256]{2,1,0:T(8,128)(2,1)} %pad_maximum_fusion.3), channel_id=1, source_target_pairs={{0,8},{8,0},{16,24},{24,16},{1,9},{9,1},{17,25},{25,17},{2,10},{10... | collective-permute-start | bytes 3145736 | tf_op jit(solution)/shard_map/attention_back/ppermute | solution.py:54
  501.9 23.8 %collective-permute-start.80 = (bf16[2,1024,256]{2,1,0:T(8,128)(2,1)}, bf16[2,1024,256]{2,1,0:T(8,128)(2,1)}, u32[]{:S(2)}, u32[]{:S(2)}) collective-permute-start(bf16[2,1024,256]{2,1,0:T(8,128)(2,1)} %pad_maximum_fusion.4), channel_id=1, source_target_pairs={{0,16},{8,24},{16,0},{24,8},{1,17},{9,25},{17,1},{25,9},{2,18},{10... | collective-permute-start | bytes 3145736 | tf_op jit(solution)/shard_map/attention_back/ppermute | solution.py:54
  529.0 38.3 %collective-permute-start.106 = (bf16[2,64,1024]{2,1,0:T(8,128)(2,1)}, bf16[2,64,1024]{2,1,0:T(8,128)(2,1)S(1)}, u32[]{:S(2)}, u32[]{:S(2)}) collective-permute-start(bf16[2,64,1024]{2,1,0:T(8,128)(2,1)} %get-tuple-element.805), channel_id=1, source_target_pairs={{0,2},{1,3},{2,0},{3,1},{4,6},{5,7},{6,4},{7,5},{8,10},{9,11},{10,... | collective-permute-start | bytes 786440 | tf_op jit(solution)/shard_map/up_grad/ppermute | solution.py:54
  529.0 38.3 %collective-permute-start.107 = (bf16[2,64,1024]{2,1,0:T(8,128)(2,1)}, bf16[2,64,1024]{2,1,0:T(8,128)(2,1)S(1)}, u32[]{:S(2)}, u32[]{:S(2)}) collective-permute-start(bf16[2,64,1024]{2,1,0:T(8,128)(2,1)} %get-tuple-element.806), channel_id=1, source_target_pairs={{0,4},{1,5},{2,6},{3,7},{4,0},{5,1},{6,2},{7,3},{8,12},{9,13},{10,... | collective-permute-start | bytes 786440 | tf_op jit(solution)/shard_map/up_grad/ppermute | solution.py:54
  531.3 36.0 %collective-permute-start.108 = (bf16[2,64,1024]{2,1,0:T(8,128)(2,1)S(1)}, bf16[2,64,1024]{2,1,0:T(8,128)(2,1)S(1)}, u32[]{:S(2)}, u32[]{:S(2)}) collective-permute-start(bf16[2,64,1024]{2,1,0:T(8,128)(2,1)S(1)} %get-tuple-element.807), channel_id=1, source_target_pairs={{0,6},{1,7},{2,4},{3,5},{4,2},{5,3},{6,0},{7,1},{8,14},{9,15},{10,... | collective-permute-start | bytes 786440 | tf_op jit(solution)/shard_map/up_grad/ppermute | solution.py:54
  536.9 37.1 %collective-permute-start.87 = (bf16[128,2048]{1,0:T(8,128)(2,1)}, bf16[128,2048]{1,0:T(8,128)(2,1)}, u32[]{:S(2)}, u32[]{:S(2)}) collective-permute-start(bf16[128,2048]{1,0:T(8,128)(2,1)} %get-tuple-element.849), channel_id=1, source_target_pairs={{0,1},{1,0},{2,3},{3,2},{4,5},{5,4},{6,7},{7,6},{8,9},{9,8},{10,11... | collective-permute-start | bytes 1572872 | tf_op jit(solution)/shard_map/d_normed/ppermute | solution.py:54
  549.4 19.4 %collective-permute-start.86 = (bf16[128,2048]{1,0:T(8,128)(2,1)}, bf16[128,2048]{1,0:T(8,128)(2,1)}, u32[]{:S(2)}, u32[]{:S(2)}) collective-permute-start(bf16[128,2048]{1,0:T(8,128)(2,1)} %get-tuple-element.704), channel_id=1, source_target_pairs={{0,1},{1,0},{2,3},{3,2},{4,5},{5,4},{6,7},{7,6},{8,9},{9,8},{10,11... | collective-permute-start | bytes 1572872 | tf_op jit(solution)/shard_map/d_normed/ppermute | solution.py:54
  570.0 17.2 %collective-permute-start.88 = (bf16[128,2048]{1,0:T(8,128)(2,1)S(1)}, bf16[128,2048]{1,0:T(8,128)(2,1)S(1)}, u32[]{:S(2)}, u32[]{:S(2)}) collective-permute-start(bf16[128,2048]{1,0:T(8,128)(2,1)S(1)} %convert_add_fusion.8), channel_id=1, source_target_pairs={{0,4},{1,5},{4,6},{5,7},{6,2},{7,3},{2,0},{3,1},{8,12},{9,13},{12,... | collective-permute-start | bytes 1572872 | tf_op jit(solution)/shard_map/d_normed/ppermute | solution.py:65
  587.3 19.0 %collective-permute-start.100 = (bf16[512,768]{1,0:T(8,128)(2,1)S(1)}, bf16[512,768]{1,0:T(8,128)(2,1)S(1)}, u32[]{:S(2)}, u32[]{:S(2)}) collective-permute-start(bf16[512,768]{1,0:T(8,128)(2,1)S(1)} %pad_maximum_fusion.5), channel_id=1, source_target_pairs={{0,8},{8,0},{16,24},{24,16},{1,9},{9,1},{17,25},{25,17},{2,10},{10... | collective-permute-start | bytes 2359304 | tf_op jit(solution)/shard_map/qkv_grad/ppermute | solution.py:54
  587.9 15.3 %collective-permute-start.92 = (bf16[128,2048]{1,0:T(8,128)(2,1)S(1)}, bf16[128,2048]{1,0:T(8,128)(2,1)S(1)}, u32[]{:S(2)}, u32[]{:S(2)}) collective-permute-start(bf16[128,2048]{1,0:T(8,128)(2,1)S(1)} %add_convert_fusion.3), channel_id=1, source_target_pairs={{0,4},{1,5},{4,6},{5,7},{6,2},{7,3},{2,0},{3,1},{8,12},{9,13},{12,... | collective-permute-start | bytes 1572872 | tf_op jit(solution)/shard_map/d_normed/ppermute | solution.py:65
  588.6 19.7 %collective-permute-start.101 = (bf16[512,768]{1,0:T(8,128)(2,1)S(1)}, bf16[512,768]{1,0:T(8,128)(2,1)S(1)}, u32[]{:S(2)}, u32[]{:S(2)}) collective-permute-start(bf16[512,768]{1,0:T(8,128)(2,1)S(1)} %pad_maximum_fusion.6), channel_id=1, source_target_pairs={{0,16},{8,24},{16,0},{24,8},{1,17},{9,25},{17,1},{25,9},{2,18},{10... | collective-permute-start | bytes 2359304 | tf_op jit(solution)/shard_map/qkv_grad/ppermute | solution.py:54
  603.3 15.5 %collective-permute-start.94 = (bf16[128,2048]{1,0:T(8,128)(2,1)S(1)}, bf16[128,2048]{1,0:T(8,128)(2,1)S(1)}, u32[]{:S(2)}, u32[]{:S(2)}) collective-permute-start(bf16[128,2048]{1,0:T(8,128)(2,1)S(1)} %add_convert_fusion.2), channel_id=1, source_target_pairs={{0,4},{1,5},{4,6},{5,7},{6,2},{7,3},{2,0},{3,1},{8,12},{9,13},{12,... | collective-permute-start | bytes 1572872 | tf_op jit(solution)/shard_map/d_normed/ppermute | solution.py:65
  620.7 20.0 %collective-permute-start.102 = (bf16[4,64,768]{2,1,0:T(8,128)(2,1)}, bf16[4,64,768]{2,1,0:T(8,128)(2,1)S(1)}, u32[]{:S(2)}, u32[]{:S(2)}) collective-permute-start(bf16[4,64,768]{2,1,0:T(8,128)(2,1)} %get-tuple-element.865), channel_id=1, source_target_pairs={{0,1},{1,0},{2,3},{3,2},{4,5},{5,4},{6,7},{7,6},{8,9},{9,8},{10,11... | collective-permute-start | bytes 1179656 | tf_op jit(solution)/shard_map/qkv_grad/ppermute | solution.py:54
  641.4 15.7 %collective-permute-start.104 = (bf16[2,64,768]{2,1,0:T(8,128)(2,1)S(1)}, bf16[2,64,768]{2,1,0:T(8,128)(2,1)S(1)}, u32[]{:S(2)}, u32[]{:S(2)}) collective-permute-start(bf16[2,64,768]{2,1,0:T(8,128)(2,1)S(1)} %get-tuple-element.798), channel_id=1, source_target_pairs={{0,4},{1,5},{2,6},{3,7},{4,0},{5,1},{6,2},{7,3},{8,12},{9,13},{10,... | collective-permute-start | bytes 589832 | tf_op jit(solution)/shard_map/qkv_grad/ppermute | solution.py:54
  643.4 19.2 %collective-permute-start.105 = (bf16[2,64,768]{2,1,0:T(8,128)(2,1)S(1)}, bf16[2,64,768]{2,1,0:T(8,128)(2,1)S(1)}, u32[]{:S(2)}, u32[]{:S(2)}) collective-permute-start(bf16[2,64,768]{2,1,0:T(8,128)(2,1)S(1)} %get-tuple-element.799), channel_id=1, source_target_pairs={{0,6},{1,7},{2,4},{3,5},{4,2},{5,3},{6,0},{7,1},{8,14},{9,15},{10,... | collective-permute-start | bytes 589832 | tf_op jit(solution)/shard_map/qkv_grad/ppermute | solution.py:54
  (149 other events, 1442.1 us)
Sparse Core Ops, SparseCore 0:
  212.4 66.7 all-gather.1
  374.2 50.8 reduce-scatter.3
  442.3 57.8 reduce-scatter.5
  552.6 30.4 reduce-scatter.7

commit v3 on v1

v3 whole, which is shorter than its diff:
```python
import functools

import jax
import jax.numpy as jnp
from jax import lax
from jax.experimental import pallas as pl
from jax.experimental.pallas import tpu as pltpu
from jax.sharding import PartitionSpec as P

D = 2048
H = 16
DH = 128

norm_epsilon = 1e-05
masked_fill = -1e30
tile = 256
bf16 = jnp.bfloat16
f32 = jnp.float32
log2_e = 1.4426950408889634
vmem_bytes = 48 * 1024 * 1024


def matmul(left, right):
    return jnp.dot(left, right, preferred_element_type=f32)


def cross_rows(left, right):
    return lax.dot_general(left, right, (((0,), (0,)), ((), ())), preferred_element_type=f32)


def times_transposed(left, right):
    return lax.dot_general(left, right, (((1,), (1,)), ((), ())), preferred_element_type=f32)


def norm_parts(values):
    row_mean = jnp.mean(values, axis=-1, keepdims=True)
    centered = values - row_mean
    row_var = jnp.mean(centered * centered, axis=-1, keepdims=True)
    inverse = lax.rsqrt(row_var + norm_epsilon)
    return (centered * inverse, inverse)


def norm_back(grad_out, normal_hat, inverse, gain):
    scaled_grad = grad_out * gain
    return inverse * (
        scaled_grad
        - jnp.mean(scaled_grad, axis=-1, keepdims=True)
        - normal_hat * jnp.mean(scaled_grad * normal_hat, axis=-1, keepdims=True)
    )


def swap(v, axis, mask):
    size = lax.axis_size(axis)
    return lax.ppermute(v, axis, [(i, i ^ mask) for i in range(size)])


def ring_order(chips):
    return list(range(0, chips, 2)) + [k for k in range(chips - 1, 0, -1) if k % 2]


def next_chip(v):
    chips = lax.axis_size("blk") // 2
    order = ring_order(chips)
    moves = [(order[k], order[(k + 1) % chips]) for k in range(chips)]
    return lax.ppermute(v, "blk", [(2 * a + c, 2 * b + c) for a, b in moves for c in range(2)])


def pick(v, index):
    return lax.dynamic_index_in_dim(v, index, 0, keepdims=False)


def put(v, part, index):
    return lax.dynamic_update_index_in_dim(v, part, index, 0)


def bits_of(size):
    return [1 << k for k in range(size.bit_length() - 1)]


def blank(shape, dtype):
    return pl.pallas_call(
        lambda out: None,
        out_shape=jax.ShapeDtypeStruct(shape, dtype),
        out_specs=pl.BlockSpec(memory_space=pl.ANY),
        name="blank",
    )()


def hold(*values):
    return lax.optimization_barrier(values)


def gather_head(v):
    size = lax.axis_size("head")
    if size == 4:
        half = v.shape[0] // 2
        one, two = swap(v, "head", 1), swap(v, "head", 2)
        low = swap(two[:half], "head", 1)
        high = swap(one[half:], "head", 2)
        return [v, one, two, jnp.concatenate([low, high], axis=0)]
    held = [v]
    for bit in bits_of(size):
        held = held + [swap(part, "head", bit) for part in held]
    return held


def scatter_head(chunk):
    size = lax.axis_size("head")
    if size == 4:
        far = chunk(3).astype(bf16)
        half = far.shape[0] // 2
        low = swap(far[:half], "head", 1)
        high = swap(far[half:], "head", 2)
        one, two = chunk(1), chunk(2)
        one = jnp.concatenate([one[:half], one[half:] + high.astype(f32)], axis=0)
        two = jnp.concatenate([two[:half] + low.astype(f32), two[half:]], axis=0)
        one = swap(one.astype(bf16), "head", 1)
        two = swap(two.astype(bf16), "head", 2)
        return chunk(0) + one.astype(f32) + two.astype(f32)
    terms = [chunk(m) for m in range(size)]
    for bit in reversed(bits_of(size)):
        terms = [
            terms[m] + swap(terms[m | bit].astype(bf16), "head", bit).astype(f32) for m in range(bit)
        ]
    return terms[0]


def exchange(pieces, axis, mine, group):
    out = pieces
    for mask in range(1, group):
        out = put(out, swap(pick(pieces, mine ^ mask), axis, mask), mine ^ mask)
    return out


def scalars(*values):
    return jnp.stack([jnp.asarray(v, jnp.int32) for v in values])


def local_call(kernel, out_shapes, scalar, *arrays, name):
    return pl.pallas_call(
        kernel,
        in_specs=[pl.BlockSpec(memory_space=pltpu.SMEM)]
        + [pl.BlockSpec(memory_space=pltpu.VMEM)] * len(arrays),
        out_specs=[pl.BlockSpec(memory_space=pltpu.VMEM)] * len(out_shapes),
        out_shape=[jax.ShapeDtypeStruct(shape, dtype) for shape, dtype in out_shapes],
        compiler_params=pltpu.CompilerParams(vmem_limit_bytes=vmem_bytes),
        name=name,
    )(scalar, *arrays)


def place(blocks, at):
    count = len(blocks)

    def kernel(at_ref, *refs):
        for k in range(count):
            refs[count][at_ref[k]] = refs[k][...]

    shape = ((count,) + blocks[0].shape, blocks[0].dtype)
    return local_call(kernel, [shape], at, *blocks, name="place")[0]


def place_cores(pieces, at):
    count = len(pieces)

    def kernel(at_ref, *refs):
        for k in range(count):
            for c in range(2):
                refs[count + c][at_ref[k]] = refs[k][c]

    shape = ((count,) + pieces[0].shape[1:], pieces[0].dtype)
    return local_call(kernel, [shape, shape], at, *pieces, name="place_cores")


def lanes(start, size):
    return pl.ds(pl.multiple_of(start, DH), size)


def split_columns(arrays, width, columns_of, core, chips, name):
    rows = arrays[0].shape[0]

    def kernel(core_ref, *refs):
        sources, (mine, other) = refs[:-2], refs[-2:]
        me = core_ref[0]
        for chip in range(chips):
            for out, index in ((mine, me), (other, 1 - me)):
                starts, run = columns_of(2 * chip + index)
                for p, source in enumerate(sources):
                    for i, start in enumerate(starts):
                        low = p * width + i * run
                        out[chip, :, low : low + run] = source[:, lanes(start, run)]

    shape = ((chips, rows, len(arrays) * width), arrays[0].dtype)
    return local_call(kernel, [shape, shape], scalars(core), *arrays, name=name)


def pair_up(mine, other, chip, core):
    chips = mine.shape[0]

    def kernel(at, mine_ref, other_ref, *outs):
        for m in range(chips):
            outs[m][at[1]] = mine_ref[at[0] ^ m]
            outs[m][1 - at[1]] = other_ref[at[0] ^ m]

    shape = ((2,) + mine.shape[1:], mine.dtype)
    return local_call(kernel, [shape] * chips, scalars(chip, core), mine, other, name="pair_up")


def swap_chips(pieces):
    return [pieces[0]] + [swap(pieces[m], "blk", 2 * m) for m in range(1, len(pieces))]


def merge_columns(pieces, count, width, columns_of, chip, name, row=None):
    chips = len(pieces)
    rows = pieces[0].shape[1] if row is None else row
    total = 2 * chips * width

    def kernel(at, *refs):
        sources, outs = refs[:chips], refs[chips:]
        sums = None
        for m in range(chips):
            for core in range(2):
                starts, run = columns_of(2 * (at[0] ^ m) + core)
                for p in range(count):
                    for i, start in enumerate(starts):
                        low = p * width + i * run
                        part = sources[m][core, :rows, low : low + run]
                        outs[p][:, lanes(start, run)] = part.astype(f32)
                if row is not None:
                    part = sources[m][core, rows:, :].astype(f32)
                    sums = part if sums is None else sums + part
        if row is not None:
            outs[count][...] = sums

    shapes = [((rows, total), f32)] * count
    if row is not None:
        shapes.append(((pieces[0].shape[1] - row, count * width), f32))
    return local_call(kernel, shapes, scalars(chip), *pieces, name=name)


def attend_tile(t, which, ways, tok, factor, carried, final, refs):
    heads_at, first, query = refs[:3]
    groups = len(which)
    keys = refs[3 : 3 + groups]
    values = refs[3 + groups : 3 + 2 * groups]
    refs = refs[3 + 2 * groups :]
    seen = (t + 1) * tile
    row = t * tile + lax.broadcasted_iota(jnp.int32, (tile, 1), 0)
    column = lax.broadcasted_iota(jnp.int32, (1, seen), 1)
    row = (row // tok * ways + heads_at[0]) * tok + row % tok
    start = jnp.transpose(jnp.broadcast_to(first[...], (DH, tile)))[:, :1]
    if carried:
        acc = refs[0][...]
        high = jnp.transpose(jnp.broadcast_to(refs[1][0, 0:1, :], (DH, tile)))[:, :1]
        total = jnp.transpose(jnp.broadcast_to(refs[1][0, 1:2, :], (DH, tile)))[:, :1]
        refs = refs[2:]
    else:
        high = jnp.full((tile, 1), masked_fill, f32)
        total = jnp.zeros((tile, 1), f32)
        acc = jnp.zeros((tile, DH), f32)
    for k, m in enumerate(which):
        scores = times_transposed(query[...], keys[k][0, :seen, :]) * factor
        pos = (column // tok * ways + heads_at[m]) * tok + column % tok
        keep = pos[:, t * tile :] <= row
        last = jnp.where(keep & (pos[:, t * tile :] >= start), scores[:, t * tile :], masked_fill)
        if t > 0:
            rest = jnp.where(pos[:, : t * tile] >= start, scores[:, : t * tile], masked_fill)
            scores = jnp.concatenate([rest, last], axis=1)
        else:
            scores = last
        new_high = jnp.maximum(high, jnp.max(scores, axis=-1, keepdims=True))
        weights = jnp.exp2(scores - new_high)
        shrink = jnp.exp2(high - new_high)
        total = total * shrink + jnp.sum(weights, axis=-1, keepdims=True)
        acc = acc * shrink + matmul(weights.astype(bf16), values[k][0, :seen, :])
        high = new_high

    def as_row(column):
        return jnp.transpose(jnp.broadcast_to(column, (tile, DH)))[0:1, :]

    if final:
        refs[0][...] = (acc / total).astype(bf16)
        refs[1][0] = as_row(high + jnp.log2(total))
    else:
        refs[0][...] = acc
        refs[1][0, 0:1, :] = as_row(high)
        refs[1][0, 1:2, :] = as_row(total)


def attend_kernel(tiles, which, ways, tok, factor, carried, final, *refs):
    for t in range(tiles):
        pl.when(pl.program_id(1) == t)(
            functools.partial(attend_tile, t, which, ways, tok, factor, carried, final, refs)
        )


def attend(heads_at, which, first, tok, query, keys, values, state, final):
    rows, width = query.shape
    heads = width // DH
    tiles = rows // tile
    line = pl.BlockSpec((1, tile), lambda i, t: (0, t))
    some = pl.BlockSpec((tile, DH), lambda i, t: (t, i))
    pair = pl.BlockSpec((1, 2, tile), lambda i, t: (i, 0, t))
    single = pl.BlockSpec((1, 1, tile), lambda i, t: (i, 0, t))

    def all_rows(index):
        return pl.BlockSpec((1, rows, DH), lambda i, t: (index, 0, i))

    parts = [keys[m] for m in which] + [values[m] for m in which]
    pairs = rows * rows * len(which) * heads // 2
    carried = state is not None
    return pl.pallas_call(
        functools.partial(
            attend_kernel,
            tiles,
            tuple(which),
            heads_at.shape[0],
            tok,
            log2_e * DH**-0.5,
            carried,
            final,
        ),
        grid=(heads, tiles),
        in_specs=[pl.BlockSpec(memory_space=pltpu.SMEM), line, some]
        + [all_rows(index) for _, index in parts]
        + ([some, pair] if carried else []),
        out_specs=[some, single if final else pair],
        out_shape=[
            jax.ShapeDtypeStruct((rows, width), bf16 if final else f32),
            jax.ShapeDtypeStruct((heads, 1 if final else 2, rows), f32),
        ],
        compiler_params=pltpu.CompilerParams(vmem_limit_bytes=vmem_bytes),
        cost_estimate=pl.CostEstimate(
            flops=4 * pairs * DH,
            bytes_accessed=4 * rows * width * len(which),
            transcendentals=pairs,
        ),
        name="attend",
    )(heads_at, first, query, *[array for array, _ in parts], *(state if carried else []))


def attend_back_tile(t, m, ways, tok, factor, scaling, carried, refs):
    heads_at, first, log_total, delta, query, d_out, keys, values = refs[:8]
    dq, dk, dv = refs[-3:]
    rows = query.shape[0]
    ahead = pl.ds(t * tile, rows - t * tile)
    k_tile, v_tile = keys[0], values[0]
    q_part, d_part = query[ahead, :], d_out[ahead, :]
    scores = times_transposed(k_tile, q_part) * factor
    pos = t * tile + lax.broadcasted_iota(jnp.int32, (tile, 1), 0)
    pos = (pos // tok * ways + heads_at[m]) * tok + pos % tok
    row = t * tile + lax.broadcasted_iota(jnp.int32, (1, rows - t * tile), 1)
    row = (row // tok * ways + heads_at[0]) * tok + row % tok
    probs = jnp.exp2(scores - log_total[0, :, ahead])
    start = first[:, ahead]
    keep = (pos >= start[:, :tile]) & (pos <= row[:, :tile])
    near = jnp.where(keep, probs[:, :tile], 0.0)
    if rows > (t + 1) * tile:
        far = jnp.where(pos >= start[:, tile:], probs[:, tile:], 0.0)
        probs = jnp.concatenate([near, far], axis=1)
    else:
        probs = near
    dv[...] = matmul(probs.astype(bf16), d_part).astype(bf16)
    d_probs = times_transposed(v_tile, d_part)
    d_scores = (probs * (d_probs - delta[0, :, ahead])).astype(bf16)
    dk[...] = (scaling * matmul(d_scores, q_part)).astype(bf16)
    term = scaling * cross_rows(d_scores, k_tile)
    if t > 0:
        dq[ahead, :] += term
    elif carried:
        dq[...] = refs[8][...] + term
    else:
        dq[...] = term


def attend_back_kernel(tiles, m, ways, tok, factor, scaling, carried, *refs):
    for t in range(tiles):
        pl.when(pl.program_id(1) == t)(
            functools.partial(attend_back_tile, t, m, ways, tok, factor, scaling, carried, refs)
        )


def attend_back(heads_at, m, first, tok, log_total, delta, query, d_out, key, value, dq_in):
    rows, width = query.shape
    heads = width // DH
    tiles = rows // tile
    line = pl.BlockSpec((1, rows), lambda i, t: (0, 0))
    stat = pl.BlockSpec((1, 1, rows), lambda i, t: (i, 0, 0))
    tile_rows = pl.BlockSpec((tile, DH), lambda i, t: (t, i))
    block = pl.BlockSpec((rows, DH), lambda i, t: (0, i))

    def some(index):
        return pl.BlockSpec((1, tile, DH), lambda i, t: (index, t, i))

    pairs = rows * rows * heads // 2
    carried = dq_in is not None
    return pl.pallas_call(
        functools.partial(
            attend_back_kernel,
            tiles,
            m,
            heads_at.shape[0],
            tok,
            log2_e * DH**-0.5,
            DH**-0.5,
            carried,
        ),
        grid=(heads, tiles),
        in_specs=[pl.BlockSpec(memory_space=pltpu.SMEM), line, stat, stat, block, block]
        + [some(key[1]), some(value[1])]
        + [block] * (1 if carried else 0),
        out_specs=[block, tile_rows, tile_rows],
        out_shape=[
            jax.ShapeDtypeStruct((rows, width), f32),
            jax.ShapeDtypeStruct((rows, width), bf16),
            jax.ShapeDtypeStruct((rows, width), bf16),
        ],
        compiler_params=pltpu.CompilerParams(vmem_limit_bytes=vmem_bytes),
        cost_estimate=pl.CostEstimate(
            flops=10 * pairs * DH, bytes_accessed=20 * rows * width, transcendentals=pairs
        ),
        name="attend_back",
    )(
        heads_at,
        first,
        log_total,
        delta,
        query,
        d_out,
        key[0],
        value[0],
        *([dq_in] if carried else []),
    )


def normalized(values):
    centered = values - jnp.mean(values, axis=-1, keepdims=True)
    return centered * lax.rsqrt(jnp.mean(centered * centered, axis=-1, keepdims=True) + norm_epsilon)


def project_in(at, mine, other, gain, shift, weights, bias):
    chips, count = len(mine), len(weights)
    tok, width = mine[0].shape
    columns = weights[0].shape[2]
    own = columns // 3

    def body(at_ref, *refs):
        mine_refs, other_refs = refs[:chips], refs[chips : 2 * chips]
        gain_ref, shift_ref, bias_ref = refs[2 * chips : 2 * chips + 3]
        weight_refs = refs[2 * chips + 3 : 2 * chips + 3 + count]
        query, key_value, normed, whole = refs[2 * chips + 3 + count :]
        core = at_ref[chips]

        @pl.when(pl.program_id(0) == 0)
        def _():
            for k, part in enumerate(weight_refs):
                for z in range(chips):
                    low = pl.multiple_of(at_ref[chips + 1 + k] + z * 2 * part.shape[1], 16)
                    whole[pl.ds(low, part.shape[1]), :] = part[z]

        for step in range(chips):

            @pl.when(pl.program_id(0) == step)
            def _():
                for part, place in ((mine_refs[step], core), (other_refs[step], 1 - core)):
                    hat = normalized(part[...].astype(f32))
                    low = pl.multiple_of(place * tok, tok)
                    normed[pl.ds(low, tok), :] = (hat * gain_ref[...] + shift_ref[...]).astype(bf16)

        product = matmul(normed[...], whole[...]) + bias_ref[...]
        product = product.astype(bf16)
        query[...] = product[:, :own]
        key_value[0] = product[:, own : 2 * own]
        key_value[1] = product[:, 2 * own :]

    def fixed(shape):
        return pl.BlockSpec(shape, lambda i, at_ref: (0,) * len(shape))

    rows = 2 * tok * chips
    arrays = [*mine, *other, gain, shift, bias, *weights]
    return pl.pallas_call(
        body,
        grid_spec=pltpu.PrefetchScalarGridSpec(
            num_scalar_prefetch=1,
            grid=(chips,),
            in_specs=[fixed(array.shape) for array in arrays],
            out_specs=[
                pl.BlockSpec((2 * tok, own), lambda i, at_ref: (at_ref[i], 0)),
                pl.BlockSpec((2, 2 * tok, own), lambda i, at_ref: (0, at_ref[i], 0)),
                pl.BlockSpec((2 * tok, width), lambda i, at_ref: (at_ref[i], 0)),
                fixed((width, columns)),
            ],
        ),
        out_shape=[
            jax.ShapeDtypeStruct((rows, own), bf16),
            jax.ShapeDtypeStruct((2, rows, own), bf16),
            jax.ShapeDtypeStruct((rows, width), bf16),
            jax.ShapeDtypeStruct((width, columns), bf16),
        ],
        compiler_params=pltpu.CompilerParams(vmem_limit_bytes=vmem_bytes),
        cost_estimate=pl.CostEstimate(
            flops=2 * rows * width * columns, bytes_accessed=8 * rows * width, transcendentals=0
        ),
        name="project_in",
    )(at, *arrays)


def terms_out(at, array, weights, tokens, transposed):
    steps = at.shape[0] // 2
    rows, width = array.shape
    tok = rows // (2 * steps)
    out_width = weights.shape[0] if transposed else weights.shape[1]

    def body(at_ref, *refs):
        parts, whole = refs[:2], refs[2]
        outs = refs[-3:] if tokens else refs[-2:]
        step = pl.program_id(0)
        sums = []
        left = jnp.concatenate([parts[0][...], parts[1][...]], axis=0)
        both = times_transposed(left, whole[...]) if transposed else matmul(left, whole[...])
        for e in (0, 1):
            term = both[e * tok : (e + 1) * tok]
            outs[e][0] = term.astype(bf16)
            if tokens:
                hat = normalized(refs[3 + e][0].astype(f32))
                sums.append(
                    jnp.concatenate(
                        [
                            jnp.sum(term * hat, axis=0, keepdims=True),
                            jnp.sum(term, axis=0, keepdims=True),
                        ],
                        axis=0,
                    )
                )
        if tokens:

            @pl.when(step == 0)
            def _():
                outs[2][...] = sums[0] + sums[1]

            @pl.when(step > 0)
            def _():
                outs[2][...] += sums[0] + sums[1]

    def block(e):
        return pl.BlockSpec((tok, width), lambda i, at_ref: (at_ref[2 * i + e], 0))

    stacked = pl.BlockSpec((1, tok, out_width), lambda i, at_ref: (i, 0, 0))
    shape = jax.ShapeDtypeStruct((steps, tok, out_width), bf16)
    extra = list(tokens) if tokens else []
    return pl.pallas_call(
        body,
        grid_spec=pltpu.PrefetchScalarGridSpec(
            num_scalar_prefetch=1,
            grid=(steps,),
            in_specs=[block(0), block(1), pl.BlockSpec(weights.shape, lambda i, at_ref: (0, 0))]
            + [stacked] * len(extra),
            out_specs=[stacked, stacked]
            + ([pl.BlockSpec((2, out_width), lambda i, at_ref: (0, 0))] if tokens else []),
        ),
        out_shape=[shape, shape]
        + ([jax.ShapeDtypeStruct((2, out_width), f32)] if tokens else []),
        compiler_params=pltpu.CompilerParams(vmem_limit_bytes=vmem_bytes),
        cost_estimate=pl.CostEstimate(
            flops=2 * rows * width * out_width,
            bytes_accessed=4 * rows * out_width,
            transcendentals=0,
        ),
        name="terms_out",
    )(at, array, array, weights, *extra)


def mix_back(at, mine, other, weights, mixed):
    chips = len(mine)
    tok = mine[0].shape[0]
    rows, own = mixed.shape
    heads = own // DH

    def kernel(at_ref, *refs):
        parts = [refs[e * chips + k] for k in range(chips) for e in (0, 1)]
        whole, mixed_ref, d_mixed, delta = refs[2 * chips :]
        for k, part in enumerate(parts):
            here = pl.ds(pl.multiple_of(at_ref[k] * tok, tok), tok)
            d_mixed[here, :] = times_transposed(part[...], whole[...]).astype(bf16)
        products = d_mixed[...].astype(f32) * mixed_ref[...].astype(f32)
        for k in range(heads):
            turned = jnp.transpose(products[:, k * DH : (k + 1) * DH])
            delta[k] = jnp.sum(turned, axis=0, keepdims=True)

    shapes = [((rows, own), bf16), ((heads, 1, rows), f32)]
    return local_call(kernel, shapes, at, *mine, *other, weights, mixed, name="mix_back")


def mix_grad(at, mine, other, mixed, each, team):
    chips = len(mine)
    tok, width = mine[0].shape
    own = mixed.shape[1]
    w_rows = own // (each * team)

    def kernel(at_ref, *refs):
        parts = [refs[e * chips + k] for k in range(chips) for e in (0, 1)]
        mixed_ref, out = refs[2 * chips :]
        total = None
        for k, part in enumerate(parts):
            here = pl.ds(pl.multiple_of(at_ref[k] * tok, tok), tok)
            term = cross_rows(mixed_ref[here, :], part[...])
            total = term if total is None else total + term
        total = total.astype(bf16)
        for i in range(each):
            for j in range(team):
                low = (i * team + j) * w_rows
                out[j, i] = total[low : low + w_rows]

    shape = ((team, each, w_rows, width), bf16)
    return local_call(kernel, [shape], at, *mine, *other, mixed, name="mix_grad")[0]


def reorder(array, at):
    def kernel(at_ref, source, out):
        for k in range(array.shape[0]):
            out[k] = source[at_ref[k]]

    return local_call(kernel, [(array.shape, array.dtype)], at, array, name="reorder")[0]


def local(
    tokens,
    segments,
    cotangent,
    first_gain,
    first_shift,
    query_proj,
    key_proj,
    value_proj,
    query_bias,
    value_bias,
    out_proj,
    out_bias,
    second_gain,
    second_shift,
    up_proj,
    up_bias,
    down_proj,
    down_bias,
):
    n_head, n_blk = lax.axis_size("head"), lax.axis_size("blk")
    head, blk = lax.axis_index("head"), lax.axis_index("blk")
    chips = n_blk // 2
    chip, core = blk // 2, blk % 2
    tok = tokens.shape[0]
    rows = tok * n_blk
    w_rows = query_proj.shape[0]
    ff_rows = down_proj.shape[0]
    team = DH // w_rows
    sets = n_blk // team
    each = n_head // team
    place_in = blk % team
    own_heads = each * DH

    ring = ring_order(chips)
    behind = jnp.array(
        [[ring[(ring.index(z) - k) % chips] for k in range(chips)] for z in range(chips)], jnp.int32
    )
    behind_all = pick(behind, chip)
    behind = [behind_all[k] for k in range(chips)]

    def spot(step, other):
        return (2 * behind[step] + (core ^ other)) * tok

    def fill_pair(buffer, mine, other, step):
        buffer = lax.dynamic_update_slice_in_dim(buffer, mine, spot(step, 0), 0)
        return lax.dynamic_update_slice_in_dim(buffer, other, spot(step, 1), 0)

    square = n_head == 4

    def head_columns(b):
        at = (b % team) * each
        return [((at + i) * sets + b // team) * DH for i in range(each)], DH

    def ff_columns(b):
        return [(h * n_blk + b) * ff_rows for h in range(n_head)], ff_rows

    ways, two_cores = jnp.arange(n_head, dtype=jnp.int32), jnp.arange(2, dtype=jnp.int32)
    heads_at = head ^ ways
    chips_at = chip ^ jnp.arange(chips, dtype=jnp.int32)
    blocks_at = (2 * behind_all[:, None] + (core ^ two_cores)[None, :]).reshape(-1)
    weights_at = (heads_at[:, None] * n_blk + two_cores[None, :]).reshape(-1) * w_rows
    weights_at = jnp.concatenate([behind_all, core[None], weights_at])

    with jax.named_scope("tokens_gather"):
        tok_mine, tok_other = [tokens], []
        tok_mine.append(next_chip(tokens))

    with jax.named_scope("tokens_gather"):
        tok_other.append(swap(tokens, "blk", 1))

    with jax.named_scope("vectors"):
        small = [
            first_gain,
            first_shift,
            query_bias,
            value_bias,
            out_bias,
            second_gain,
            second_shift,
            down_bias,
            up_bias,
            segments.astype(bf16),
        ]
        small = [v.reshape(-1, w_rows).astype(f32) for v in small]
        height = sum(v.shape[0] for v in small)
        above, packed = 0, 0.0
        for v in small:
            packed = packed + lax.pad(
                v, f32(0), ((above, height - above - v.shape[0], 0), (0, 0, 0))
            )
            above += v.shape[0]
        small = packed.astype(bf16)[None]
    with jax.named_scope("qkv_weights"):
        mine, other = split_columns(
            [query_proj, key_proj, value_proj], own_heads, head_columns, core, chips, "split_heads"
        )
        pieces = pair_up(mine, swap(other, "blk", 1), chip, core)

    with jax.named_scope("down_weights"):
        down_w = lax.all_gather(down_proj, "head", axis=0, tiled=True)
    places = (heads_at, chips_at, blocks_at, weights_at)
    pieces, small, up_proj, tok_mine, tok_other, places = hold(
        pieces, small, up_proj, tok_mine, tok_other, places
    )
    heads_at, chips_at, blocks_at, weights_at = places

    with jax.named_scope("qkv_weights"):
        pieces = swap_chips(pieces)
        fused = place_cores(pieces, chips_at)
    with jax.named_scope("vectors"):
        for bit in bits_of(n_head):
            small = jnp.concatenate([small, swap(small, "head", bit)])
        small = jnp.concatenate([small, swap(small, "blk", 1)])
        small_parts = [small]
        small_parts.append(next_chip(small))

    fused, small_parts, tok_mine, tok_other, up_proj = hold(
        fused, small_parts, tok_mine, tok_other, up_proj
    )

    def small_table():
        height, width = small_parts[0].shape[1:]
        source = jnp.concatenate(small_parts).reshape(n_head * n_blk, height * width)
        index = jnp.arange(n_head * n_blk, dtype=jnp.int32)
        from_chip = jnp.repeat(jnp.stack(behind), 2 * n_head)
        from_core = core ^ (index // n_head % 2)
        from_row = (head ^ (index % n_head)) * n_blk + 2 * from_chip + from_core
        select = (from_row[None, :] == index[:, None]).astype(bf16)
        return matmul(select, source).reshape(n_head, n_blk, height * width)

    def vector(index):
        return table[:, :, index * w_rows : (index + 1) * w_rows].reshape(1, D)

    table = None
    for step in range(1, chips - 1):
        with jax.named_scope("tokens_gather"):
            tok_mine.append(next_chip(tok_mine[step]))
        with jax.named_scope("qkv_weights"):
            if step == 1 and square:
                one = [swap(part, "head", 1) for part in fused]
                two = [swap(part, "head", 2) for part in fused]
            if step == 2 and square:
                low, high = swap(two[0], "head", 1), swap(one[1], "head", 2)
            if step == 1 and not square:
                fused_parts = [gather_head(part) for part in fused]
                fused_parts = [part[m] for m in range(n_head) for part in fused_parts]
        with jax.named_scope("vectors"):
            if len(small_parts) < chips:
                small_parts.append(next_chip(small_parts[-1]))
            elif table is None:
                table = small_table()
        if step == 1:
            with jax.named_scope("up_weights"):
                up_mine, up_other = split_columns(
                    [up_proj], n_head * ff_rows, ff_columns, core, chips, "split_up"
                )
        if step == 1:
            tok_mine, tok_other, small_parts, up_mine, up_other = hold(
                tok_mine, tok_other, small_parts, up_mine, up_other
            )
        elif step < chips - 2:
            tok_mine, small_parts = hold(tok_mine, small_parts)
    if square:
        fused_parts = [*fused, *one, *two, low, high]
    if table is None:
        with jax.named_scope("vectors"):
            table = small_table()
    with jax.named_scope("vectors"):

        def own_head_part(full):
            part = full.reshape(n_head, sets, DH)
            part = lax.dynamic_index_in_dim(part, blk // team, 1, keepdims=False)
            return lax.dynamic_slice_in_dim(part, place_in * each, each, 0).reshape(1, own_heads)

        gain_first, shift_first = vector(0), vector(1)
        q_bias, v_bias = own_head_part(vector(2)), own_head_part(vector(3))
        qkv_bias = jnp.concatenate([q_bias, jnp.zeros_like(q_bias), v_bias], axis=1)
    first_vectors = (gain_first, shift_first, qkv_bias)
    fused_parts, tok_mine, cotangent, up_other, out_proj, first_vectors, down_w = hold(
        fused_parts, tok_mine, cotangent, up_other, out_proj, first_vectors, down_w
    )
    gain_first, shift_first, qkv_bias = first_vectors

    with jax.named_scope("tokens_gather"):
        tok_other += [swap(piece, "blk", 1) for piece in tok_mine[1:]]
    with jax.named_scope("qkv"):
        query, kv, normed, qkv_w = project_in(
            weights_at,
            tok_mine,
            tok_other,
            gain_first,
            shift_first,
            fused_parts,
            qkv_bias,
        )
    with jax.named_scope("up_weights"):
        up_pieces = pair_up(up_mine, swap(up_other, "blk", 1), chip, core)
    with jax.named_scope("out_weights"):
        if square:
            out_parts = [out_proj, swap(out_proj, "head", 1), swap(out_proj, "head", 2)]
        else:
            out_parts = gather_head(out_proj)
    query, kv, up_pieces, normed, out_parts, cotangent, qkv_w, table = hold(
        query, kv, up_pieces, normed, out_parts, cotangent, qkv_w, table
    )

    with jax.named_scope("kv_gather"):
        keys, values = [(kv, 0)], [(kv, 1)]
        if square:
            kv_parts = [swap(kv, "head", 1), swap(kv, "head", 2)]
        else:
            kv_parts = gather_head(kv)[1:]
    with jax.named_scope("up_weights"):
        up_pieces = swap_chips(up_pieces)
    with jax.named_scope("vectors"):
        seq = table[:, :, 8 * w_rows + ff_rows :]
        seg_all = seq.transpose(1, 0, 2).reshape(-1)
        seg_rows = pick(seq, head).reshape(rows)
        first_pos = jnp.sum((seg_all[:, None] < seg_rows[None, :]).astype(jnp.int32), axis=0)[None]
    with jax.named_scope("attention"):
        state = attend(heads_at, [0], first_pos, tok, query, keys, values, None, False)
    kv_parts, state, up_pieces, cotangent, out_parts, first_pos = hold(
        kv_parts, state, up_pieces, cotangent, out_parts, first_pos
    )

    with jax.named_scope("dy_gather"):
        dy_all = lax.all_gather(cotangent, "blk", axis=0, tiled=True)
    with jax.named_scope("up_weights"):
        up_part = place(up_pieces, chips_at).reshape(n_blk * w_rows, n_head * ff_rows)
    with jax.named_scope("kv_gather"):
        keys += [(part, 0) for part in kv_parts]
        values += [(part, 1) for part in kv_parts]
        if square:
            low = swap(kv_parts[1][:1], "head", 1)
            high = swap(kv_parts[0][1:], "head", 2)
    with jax.named_scope("out_weights"):
        if square:
            half = w_rows // 2
            out_low = swap(out_parts[2][:half], "head", 1)
            out_high = swap(out_parts[1][half:], "head", 2)
            out_parts = out_parts + [jnp.concatenate([out_low, out_high])]
    if square:
        low, high, out_parts, state, up_part = hold(low, high, out_parts, state, up_part)
        keys.append((low, 0))
        values.append((high, 0))
    else:
        out_parts, state, up_part = hold(out_parts, state, up_part)
    with jax.named_scope("up_weights"):
        up_w = lax.all_gather(up_part, "head", axis=0, tiled=True)

    with jax.named_scope("out_weights"):
        out_w = place(out_parts, heads_at).reshape(team, each, w_rows, D)
        out_w = exchange(out_w, "blk", place_in, team)
        out_w = out_w.transpose(1, 0, 2, 3).reshape(own_heads, D)
    with jax.named_scope("attention"):
        left = list(range(1, n_head))
        mixed, log_total = attend(
            heads_at, left, first_pos, tok, query, keys, values, state, True
        )
    mixed, out_w, table = hold(mixed, out_w, table)

    def cross(term):
        return (term[0], swap(term[1], "blk", 1))

    def onward(pair, moving):
        return next_chip(sum_of(pair, moving).astype(bf16))

    def sum_of(pair, moving):
        total = pair[0].astype(f32) + pair[1].astype(f32)
        return total if moving is None else total + moving.astype(f32)

    def met(own, other):
        crossing = swap(other, "blk", 1)
        return [(own[step], crossing[step]) for step in range(chips)]

    with jax.named_scope("branch"):
        ready = met(*terms_out(blocks_at, mixed, out_w, None, False))
        ready, dy_all = hold(ready, dy_all)
        moving = None
        for step in range(1, chips):
            moving = onward(ready[step], moving)
            with jax.named_scope("vectors"):
                if step == 1:
                    o_bias, gain_second, shift_second, d_bias = [vector(k) for k in range(4, 8)]
                    u_bias = table[:, :, 8 * w_rows : 8 * w_rows + ff_rows]
                    u_bias = lax.dynamic_index_in_dim(u_bias, blk, 1, keepdims=False)
                    vectors = (o_bias, gain_second, shift_second, d_bias, u_bias.reshape(1, -1))
            if step == 1:
                moving, ready, vectors = hold(moving, ready, vectors)
                o_bias, gain_second, shift_second, d_bias, u_bias = vectors
            else:
                moving, ready = hold(moving, ready)
        own = tokens.astype(f32)
        hidden = own + (sum_of(ready[0], moving) + o_bias)
        hat_second, inv_second = norm_parts(hidden)
        second_own = (hat_second * gain_second + shift_second).astype(bf16)
    hidden, second_own, inv_second, up_w = hold(hidden, second_own, inv_second, up_w)

    with jax.named_scope("mlp"):
        second_all = blank((rows, D), bf16)
        active_all = blank((rows, n_head * ff_rows), bf16)
        d_upper_all = blank((rows, n_head * ff_rows), bf16)
        sec_mine, sec_other = [second_own], []
        terms = {}

        def mlp_chunk(step, second_all, active_all, d_upper_all):
            base = 2 * behind[step] * tok

            def chunk_of(array):
                return lax.dynamic_slice_in_dim(array, base, 2 * tok, 0)

            def fill(buffer, chunk):
                return lax.dynamic_update_slice_in_dim(buffer, chunk, base, 0)

            second_all = fill_pair(second_all, sec_mine[step], sec_other[step], step)
            upper = matmul(chunk_of(second_all), up_w) + u_bias
            phi = 0.5 * (1.0 + lax.erf(upper * 0.7071067811865476))
            active = (upper * phi).astype(bf16)
            slope = phi + upper * jnp.exp(-0.5 * upper * upper) * 0.3989422804014327
            d_active = times_transposed(chunk_of(dy_all), down_w)
            d_upper = (d_active * slope).astype(bf16)
            terms[step] = [
                times_transposed(
                    lax.dynamic_slice_in_dim(d_upper, (core ^ other) * tok, tok, 0), up_w
                ).astype(bf16)
                for other in (0, 1)
            ]
            return second_all, fill(active_all, active), fill(d_upper_all, d_upper)

        for step in range(chips):
            if step < chips - 1:
                sec_mine.append(next_chip(sec_mine[step]))
            if step > 0:
                second_all, active_all, d_upper_all = mlp_chunk(
                    step - 1, second_all, active_all, d_upper_all
                )
                if step == chips - 1:
                    ready = cross(terms[1])
            sec_other.append(swap(sec_mine[step], "blk", 1))
            ready, sec_mine, sec_other, terms, second_all, active_all, d_upper_all = hold(
                ready, sec_mine, sec_other, terms, second_all, active_all, d_upper_all
            )
        moving = None
        for step in range(1, chips):
            moving = onward(ready, moving)
            if step == 1:
                second_all, active_all, d_upper_all = mlp_chunk(
                    chips - 1, second_all, active_all, d_upper_all
                )
            ready = cross(terms[(step + 1) % chips])
            if step == 1:
                with jax.named_scope("up_grad"):
                    up_term = cross_rows(second_all, d_upper_all).astype(bf16)
                moving, ready, terms, active_all, d_upper_all, up_term = hold(
                    moving, ready, terms, active_all, d_upper_all, up_term
                )
            elif step == 2:
                with jax.named_scope("down_grad"):
                    down_term = cross_rows(active_all, dy_all).astype(bf16)
                moving, ready, terms, down_term, active_all = hold(
                    moving, ready, terms, down_term, active_all
                )
            elif step == 3:
                with jax.named_scope("output"):
                    out_term = matmul(active_all, down_w).astype(bf16)
                moving, ready, terms, out_term = hold(moving, ready, terms, out_term)
            else:
                moving, ready, terms = hold(moving, ready, terms)
        d_second = sum_of(ready, moving)
        upstream = cotangent.astype(f32)
        d_hidden = upstream + norm_back(d_second, hat_second, inv_second, gain_second)
        d_branch_own = d_hidden.astype(bf16)

    def sum_heads(terms):
        return lax.psum_scatter(terms, "head", scatter_dimension=0, tiled=True)

    with jax.named_scope("up_grad"):
        up_sum = sum_heads(up_term)
    d_hidden, d_branch_own, active_all, d_second = hold(
        d_hidden, d_branch_own, active_all, d_second
    )
    mine, other = [d_branch_own], []

    with jax.named_scope("d_branch_gather"):
        for step in range(chips - 1):
            mine.append(next_chip(mine[step]))
            if step == 1:
                mine, up_sum, down_term = hold(mine, up_sum, down_term)
                with jax.named_scope("down_grad"):
                    down_grad = sum_heads(down_term)
            else:
                (mine,) = hold(mine)
        other = [swap(piece, "blk", 1) for piece in mine]
        d_mixed, delta = mix_back(blocks_at, mine, other, out_w, mixed)
    d_mixed, delta, mine, other, up_sum, out_term = hold(
        d_mixed, delta, mine, other, up_sum, out_term
    )

    dq = None

    def kv_grad(m):
        return attend_back(
            heads_at, m, first_pos, tok, log_total, delta, query, d_mixed, keys[m], values[m], dq
        )

    d_keys, d_values = {}, {}
    for m in reversed(range(n_head)):
        with jax.named_scope("attention_back"):
            if square and m == 2:
                low = swap(d_keys[3], "head", 1)
                high = swap(d_values[3], "head", 2)
            if square and m == 0:
                one = [d_keys[1], (d_values[1].astype(f32) + high.astype(f32)).astype(bf16)]
                two = [(d_keys[2].astype(f32) + low.astype(f32)).astype(bf16), d_values[2]]
                one, two, dq = hold(one, two, dq)
                one[0], two[0] = swap(one[0], "head", 1), swap(two[0], "head", 2)
            dq, d_keys[m], d_values[m] = kv_grad(m)
        if m == n_head - 1:
            with jax.named_scope("up_grad"):
                up_sum = up_sum.reshape(chips, 2, w_rows, n_head * ff_rows)
                up_mine = lax.dynamic_index_in_dim(up_sum, core, 1, keepdims=False)
                up_other = lax.dynamic_index_in_dim(up_sum, 1 - core, 1, keepdims=False)
                up_pieces = pair_up(up_mine, swap(up_other, "blk", 1), chip, core)
            dq, d_keys, d_values, d_mixed, up_pieces = hold(
                dq, d_keys, d_values, d_mixed, up_pieces
            )
        elif m == n_head - 2:
            with jax.named_scope("up_grad"):
                up_pieces = swap_chips(up_pieces)
            dq, d_keys, d_values, d_mixed = hold(dq, d_keys, d_values, d_mixed)
        elif square and m == 1:
            low, high, dq, d_keys, d_values, d_mixed, up_pieces, down_grad, out_term = hold(
                low, high, dq, d_keys, d_values, d_mixed, up_pieces, down_grad, out_term
            )
        elif m > 0:
            dq, d_keys, d_values, d_mixed = hold(dq, d_keys, d_values, d_mixed)
    if square:
        one, two, dq, mine, other, mixed, tok_mine, tok_other = hold(
            one, two, dq, mine, other, mixed, tok_mine, tok_other
        )
        with jax.named_scope("attention_back"):
            one[1], two[1] = swap(one[1], "head", 1), swap(two[1], "head", 2)
    with jax.named_scope("output"):
        out_sum = lax.psum_scatter(out_term, "blk", scatter_dimension=0, tiled=True)
    with jax.named_scope("out_grad"):
        mix_term = mix_grad(blocks_at, mine, other, mixed, each, team)
        mix_term = exchange(mix_term, "blk", place_in, team)
    with jax.named_scope("d_normed"):
        tok_stacks = (jnp.stack(tok_mine), jnp.stack(tok_other))
    with jax.named_scope("attention_back"):
        if square:
            d_keys, d_values = [
                (total[0].astype(f32) + one[k].astype(f32) + two[k].astype(f32)).astype(bf16)
                for k, total in enumerate((d_keys, d_values))
            ]
        else:
            d_keys, d_values = [
                scatter_head(lambda m: total[m].astype(f32)).astype(bf16)
                for total in (d_keys, d_values)
            ]
        d_qkv = jnp.concatenate([dq.astype(bf16), d_keys, d_values], axis=1)
    kept = (d_branch_own, d_second, hat_second, d_upper_all, cotangent, dq, d_values)
    d_qkv, up_pieces, mix_term, tok_stacks = hold(d_qkv, up_pieces, mix_term, tok_stacks)

    slab = n_blk * w_rows
    with jax.named_scope("d_normed"):
        own_terms, other_terms, first_sums = terms_out(
            blocks_at, d_qkv, qkv_w, tok_stacks, True
        )
        ready = met(own_terms, other_terms)
    ready, first_sums, normed, d_qkv, mix_term, out_sum = hold(
        ready, first_sums, normed, d_qkv, mix_term, out_sum
    )
    moving = onward(ready[1], None)
    with jax.named_scope("out_grad"):
        out_grad = sum_heads(mix_term.reshape(n_head * w_rows, D))
    with jax.named_scope("qkv_grad"):
        qkv_term = cross_rows(normed, d_qkv).astype(bf16).reshape(n_head, slab, 3 * own_heads)
    ready, qkv_term, moving, kept, first_sums = hold(ready, qkv_term, moving, kept, first_sums)
    d_branch_own, d_second, hat_second, d_upper_all, cotangent, dq, d_values = kept
    with jax.named_scope("vector_grads"):
        full = [
            first_sums[0],
            first_sums[1],
            jnp.sum(d_branch_own.astype(f32), axis=0),
            jnp.sum(d_second * hat_second, axis=0),
            jnp.sum(d_second, axis=0),
            jnp.sum(cotangent.astype(f32), axis=0),
        ]
        parts = [v.reshape(n_head, n_blk, w_rows) for v in full]
        up_row = jnp.sum(d_upper_all.astype(f32), axis=0)
        up_table = jnp.zeros((n_blk, n_head, ff_rows), f32)
        up_table = put(up_table, up_row.reshape(n_head, ff_rows), blk)
        parts.append(up_table.transpose(1, 0, 2))
        for v in (dq.astype(bf16), d_values):
            bias_sum = jnp.sum(v.astype(f32), axis=0).reshape(each, 1, DH)
            head_table = jnp.zeros((n_head, sets, DH), f32)
            head_table = lax.dynamic_update_slice(
                head_table, bias_sum, (place_in * each, blk // team, 0)
            )
            parts.append(head_table.reshape(n_head, n_blk, w_rows))
        parts = jnp.concatenate(parts, axis=2)
        wide = 3 * own_heads
        deep = -(-parts.shape[2] // wide)
        parts = jnp.pad(parts, ((0, 0), (0, 0), (0, deep * wide - parts.shape[2])))
        parts = parts.reshape(n_head, n_blk * deep, wide).astype(bf16)
    for step in range(2, chips):
        with jax.named_scope("d_normed"):
            moving = onward(ready[step], moving)
        if step == 2 and square:
            with jax.named_scope("qkv_grad"):
                half = slab // 2
                far = pick(qkv_term, head ^ 3)
                low = swap(far[:half], "head", 1)
                high = swap(far[half:], "head", 2)
                one, two = pick(qkv_term, head ^ 1), pick(qkv_term, head ^ 2)
            with jax.named_scope("vector_grads"):
                across = swap(pick(parts, head ^ 3), "head", 1)
            moving, low, high, one, two, parts, across, ready = hold(
                moving, low, high, one, two, parts, across, ready
            )
        elif step == 3 and square:
            with jax.named_scope("qkv_grad"):
                two_parts = pick(parts, head ^ 2) + across
                one = jnp.concatenate([one[:half], one[half:] + high, pick(parts, head ^ 1)])
                two = jnp.concatenate([two[:half] + low, two[half:], two_parts])
                one, two = swap(one, "head", 1), swap(two, "head", 2)
            with jax.named_scope("output"):
                output = (hidden + (out_sum.astype(f32) + d_bias)).astype(bf16)
            with jax.named_scope("up_grad"):
                (up_grad,) = merge_columns(
                    up_pieces, 1, n_head * ff_rows, ff_columns, chip, "merge_up"
                )
            with jax.named_scope("down_grad"):
                down_grad = down_grad.astype(f32)
            moving, one, two, output, up_grad, down_grad, ready = hold(
                moving, one, two, output, up_grad, down_grad, ready
            )
        else:
            moving, ready = hold(moving, ready)
    with jax.named_scope("qkv_grad"):
        whole = jnp.concatenate([qkv_term, parts], axis=1)
        if square:
            qkv_grad = pick(whole, head).astype(f32) + one.astype(f32) + two.astype(f32)
        else:
            qkv_grad = scatter_head(lambda m: pick(whole, head ^ m).astype(f32))
            output = (hidden + (out_sum.astype(f32) + d_bias)).astype(bf16)
            (up_grad,) = merge_columns(up_pieces, 1, n_head * ff_rows, ff_columns, chip, "merge_up")
            down_grad = down_grad.astype(f32)
        qkv_grad = qkv_grad.astype(bf16)
        extra = qkv_grad[slab:].reshape(chips, 2, deep, wide)
        extra = jnp.pad(extra, ((0, 0), (0, 0), (0, -deep % 16), (0, 0)))
        qkv_grad = qkv_grad[:slab].reshape(chips, 2, w_rows, wide)
        qkv_grad = jnp.concatenate([qkv_grad, extra], axis=2)
        qkv_mine = lax.dynamic_index_in_dim(qkv_grad, core, 1, keepdims=False)
        qkv_other = lax.dynamic_index_in_dim(qkv_grad, 1 - core, 1, keepdims=False)
        pieces = pair_up(qkv_mine, swap(qkv_other, "blk", 1), chip, core)
        pieces = swap_chips(pieces)
        *qkv_grad, sums = merge_columns(
            pieces, 3, own_heads, head_columns, chip, "merge_heads", row=w_rows
        )
    with jax.named_scope("vector_grads"):
        sums = sums[:deep].reshape(-1)
        cuts = [sums[i * w_rows : (i + 1) * w_rows] for i in range(6)]
        up_bias_grad = sums[6 * w_rows : 6 * w_rows + ff_rows]
        rest = sums[6 * w_rows + ff_rows : 8 * w_rows + ff_rows]
    with jax.named_scope("d_normed"):
        d_normed = sum_of(ready[0], moving)
        hat_first, inv_first = norm_parts(own)
        tokens_grad = (d_hidden + norm_back(d_normed, hat_first, inv_first, gain_first)).astype(bf16)

    return (
        output,
        tokens_grad,
        cuts[0],
        cuts[1],
        qkv_grad[0],
        qkv_grad[1],
        qkv_grad[2],
        rest[:w_rows],
        rest[w_rows:],
        out_grad.astype(f32),
        cuts[2],
        cuts[3],
        cuts[4],
        up_grad,
        up_bias_grad,
        down_grad,
        cuts[5],
    )


def solution(mesh):
    by_token = P(("blk", "head"), None)
    matrix = P(("head", "blk"), None)
    vector = P(("head", "blk"))
    return jax.shard_map(
        local,
        mesh=mesh,
        in_specs=(
            by_token,
            P(("blk", "head")),
            by_token,
            vector,
            vector,
            matrix,
            matrix,
            matrix,
            vector,
            vector,
            matrix,
            vector,
            vector,
            vector,
            matrix,
            vector,
            matrix,
            vector,
        ),
        out_specs=(
            by_token,
            by_token,
            vector,
            vector,
            matrix,
            matrix,
            matrix,
            vector,
            vector,
            matrix,
            vector,
            vector,
            vector,
            matrix,
            vector,
            matrix,
            vector,
        ),
        check_vma=False,
    )
```

time: 898 us -> 610 us (0.68)
  waiting for transfers between devices: 374 us -> 225 us
  starting transfers between devices: 144 us -> 67.8 us
  matrix products: 131 us -> 66.5 us
  local copies, waits for them, and re-layouts: 130 us -> 71.7 us
  Pallas kernels: 47.3 us -> 99.4 us
  between operations: 3.86 us -> 21.7 us
    ppermute x128 -> x64, waiting for transfers between devices: 247 us -> 97.8 us  [swap(): return lax.ppermute(v, axis, [(i, i ^ mask) for i in range(size)])]
    pallas_call x5 -> x25, Pallas kernels: 47.3 us -> 99.4 us  [the longest x4 32.5 us: attend_back(): pl.pallas_call(functools.partial(attend_back_kernel, tiles, m, heads_at.s...]
    ppermute x128 -> x64, starting transfers between devices: 92.6 us -> 46.3 us  [swap(): return lax.ppermute(v, axis, [(i, i ^ mask) for i in range(size)])]
    dynamic_update_slice x56 -> x3, local copies, waits for them, and re-layouts: 37.1 us -> 0.14 us  [put(): return lax.dynamic_update_index_in_dim(v, part, index, 0)]
    dot_general x13 -> x12, matrix products: 57.7 us -> 26.1 us  [times_transposed(): lax.dot_general(left, right, (((1,), (1,)), ((), ())), preferred_element_...]
    ppermute x36 -> x21, starting transfers between devices: 51.3 us -> 20.6 us  [next_chip(): lax.ppermute(v, 'blk', [(2 * a + c, 2 * b + c) for a, b in moves for c in...]
    unnamed x239 -> x235, local copies, waits for them, and re-layouts: 17.5 us -> 42.5 us
    dot_general x13 -> x6, matrix products: 39.7 us -> 18.7 us  [matmul(): return jnp.dot(left, right, preferred_element_type=f32)]
  transfers between devices with their start and end apart: 164 -> 92, of which waited for: 67 -> 46; matrix products, arithmetic and copies ran while one was open for 30% -> 22% of each run, Pallas kernels for 5% -> 16%
where the time goes in v3:
time: 610 us; the launch traced here: 605 us
  waiting for transfers between devices  225 us (37%)
  Pallas kernels  99.4 us (16%)
  local copies, waits for them, and re-layouts  71.7 us (12%)
  starting transfers between devices  67.8 us (11%)
  matrix products  66.5 us (11%)
  other arithmetic  53.3 us (9%)
  between operations  21.7 us (4%)
    ppermute x21, waiting for transfers between devices, next_chip(): lax.ppermute(v, 'blk', [(2 * a + c, 2 * b + c) for a, b in moves for c in...  125 us
    ppermute x64, waiting for transfers between devices, swap(): return lax.ppermute(v, axis, [(i, i ^ mask) for i in range(size)])  97.8 us
    ppermute x64, starting transfers between devices, swap(): return lax.ppermute(v, axis, [(i, i ^ mask) for i in range(size)])  46.3 us
    unnamed x235, local copies, waits for them, and re-layouts  42.5 us
    pallas_call x4, Pallas kernels, attend_back(): pl.pallas_call(functools.partial(attend_back_kernel, tiles, m, heads_at.s...  32.5 us
    dot_general x12, matrix products, times_transposed(): lax.dot_general(left, right, (((1,), (1,)), ((), ())), preferred_element_...  26.1 us
    pallas_call x2, Pallas kernels, attend(): pl.pallas_call(functools.partial(attend_kernel, tiles, tuple(which), head...  23 us
    dot_general x3, matrix products, cross_rows(): lax.dot_general(left, right, (((0,), (0,)), ((), ())), preferred_element_...  21.7 us
  transfers between devices with their start and end apart: 92, of which 46 were waited for; matrix products, arithmetic and copies ran while one was open for 22% of the time, Pallas kernels for 16%

profile of v3, /device:TPU:8, one launch (start us, length us, event | category | flops | bytes accessed | tf_op | source)
XLA Modules:
  0.0 605.0 jit_solution(10206200485456083937)
XLA Ops:
  16.5 6.3 %collective-permute-done.1.refs_1_ = bf16[128,2048]{1,0:T(8,128)(2,1)S(1)} collective-permute-done((bf16[128,2048]{1,0:T(8,128)(2,1)}, bf16[128,2048]{1,0:T(8,128)(2,1)S(1)}, u32[]{:S(2)}, u32[]{:S(2)}) %collective-permute-start.1) | collective-permute-done | bytes 524320 | tf_op jit(solution)/shard_map/tokens_gather/ppermute | solution.py:65
  24.3 3.0 collective-permute-start.4
  34.0 6.9 %collective-permute-done.4.refs_2_ = bf16[2,64,768]{2,1,0:T(8,128)(2,1)S(1)} collective-permute-done((bf16[2,64,768]{2,1,0:T(8,128)(2,1)S(1)}, bf16[2,64,768]{2,1,0:T(8,128)(2,1)S(1)}, u32[]{:S(2)}, u32[]{:S(2)}) %collective-permute-start.4) | collective-permute-done | bytes 196640 | tf_op jit(solution)/shard_map/qkv_weights/ppermute | solution.py:54
  40.8 3.5 collective-permute-done.5.refs_3_
  48.5 2.7 add_multiply_fusion.6
  51.3 3.0 collective-permute-start.17
  55.3 4.1 collective-permute-done.17
  61.6 5.5 collective-permute-done.12.refs_15_
  69.2 3.1 collective-permute-start.18
  73.2 8.4 %collective-permute-done.10.refs_13_ = bf16[4,64,768]{2,1,0:T(8,128)(2,1)S(1)} collective-permute-done((bf16[4,64,768]{2,1,0:T(8,128)(2,1)}, bf16[4,64,768]{2,1,0:T(8,128)(2,1)S(1)}, u32[]{:S(2)}, u32[]{:S(2)}) %collective-permute-start.10) | collective-permute-done | bytes 393248 | tf_op jit(solution)/shard_map/qkv_weights/ppermute | solution.py:54
  82.3 6.7 %collective-permute-done.14.refs_17_ = bf16[4,64,768]{2,1,0:T(8,128)(2,1)} collective-permute-done((bf16[4,64,768]{2,1,0:T(8,128)(2,1)}, bf16[4,64,768]{2,1,0:T(8,128)(2,1)}, u32[]{:S(2)}, u32[]{:S(2)}) %collective-permute-start.14) | collective-permute-done | bytes 393248 | tf_op jit(solution)/shard_map/qkv_weights/ppermute | solution.py:54
  97.3 12.6 %project_in.1 = (bf16[1024,256]{1,0:T(8,128)(2,1)S(1)}, bf16[2,1024,256]{2,1,0:T(8,128)(2,1)}, bf16[1024,2048]{1,0:T(8,128)(2,1)}, bf16[2048,768]{1,0:T(8,128)(2,1)}) custom-call(s32[13]{0:T(128)S(1)} %pad_add_fusion.1.at_ref, bf16[128,2048]{1,0:T(8,128)(2,1)S(1)} %copy-done, bf16[128,2048]{1,0:T(8,128)(2,1)S(1)} %collective-permute-done.1.refs_1_, ...), custom_call_target="tpu_custom_call" | custom-call | flops 3221225472 | bytes 16777216 | tf_op jit(solution)/shard_map/qkv/project_in/pallas_call | solution.py:480
  113.9 2.3 collective-permute-start.29
  119.9 6.2 %attend.2 = (f32[1024,256]{1,0:T(8,128)S(1)}, f32[2,2,1024]{2,1,0:T(2,128)S(1)}) custom-call(s32[4]{0:T(128)S(1)} %get-tuple-element.388.refs_0_.at_ref, s32[1,1024]{1,0:T(1,128)S(1)} %bitcast.201, bf16[1024,256]{1,0:T(8,128)(2,1)S(1)} %get-tuple-element.449.refs_2_.refs_4_, bf16[2,1024,256]{2,1,0:T(8,128)(2,1)S(1)} %copy-done.3, ...), custom_call_target="tpu_custom_call" | custom-call | flops 536870912 | bytes 1048576 | tf_op jit(solution)/shard_map/attention/attend/pallas_call | solution.py:311
  127.7 6.8 %collective-permute-done.29.refs_2_ = bf16[2,64,1024]{2,1,0:T(8,128)(2,1)S(1)} collective-permute-done((bf16[2,64,1024]{2,1,0:T(8,128)(2,1)}, bf16[2,64,1024]{2,1,0:T(8,128)(2,1)S(1)}, u32[]{:S(2)}, u32[]{:S(2)}) %collective-permute-start.29) | collective-permute-done | bytes 262176 | tf_op jit(solution)/shard_map/up_weights/ppermute | solution.py:54
  135.3 3.9 collective-permute-done.30.refs_3_
  153.8 2.6 collective-permute-done.33
  162.7 16.8 %attend.3 = (bf16[1024,256]{1,0:T(8,128)(2,1)S(1)}, f32[2,1,1024]{2,1,0:T(1,128)S(1)}) custom-call(s32[4]{0:T(128)S(1)} %get-tuple-element.388.refs_0_.at_ref, s32[1,1024]{1,0:T(1,128)S(1)} %bitcast.202, bf16[1024,256]{1,0:T(8,128)(2,1)S(1)} %get-tuple-element.449.refs_2_.refs_4_, bf16[2,1024,256]{2,1,0:T(8,128)(2,1)S(1)} %collective-permute-done.26.refs_3_.refs_6_.refs_7_, ...), custom_call_target="tpu_custom_call" | custom-call | flops 1610612736 | bytes 3145728 | tf_op jit(solution)/shard_map/attention/attend/pallas_call | solution.py:311
  179.6 3.5 terms_out.2
  185.7 2.8 slice_bitcast_fusion.12
  189.9 2.9 slice_bitcast_fusion.4
  195.4 14.8 %collective-permute-done.37 = bf16[128,2048]{1,0:T(8,128)(2,1)} collective-permute-done((bf16[128,2048]{1,0:T(8,128)(2,1)}, bf16[128,2048]{1,0:T(8,128)(2,1)}, u32[]{:S(2)}, u32[]{:S(2)}) %collective-permute-start.37) | collective-permute-done | bytes 524320 | tf_op jit(solution)/shard_map/branch/ppermute | solution.py:65
  211.8 14.1 %collective-permute-done.38 = bf16[128,2048]{1,0:T(8,128)(2,1)S(1)} collective-permute-done((bf16[128,2048]{1,0:T(8,128)(2,1)S(1)}, bf16[128,2048]{1,0:T(8,128)(2,1)S(1)}, u32[]{:S(2)}, u32[]{:S(2)}) %collective-permute-start.38) | collective-permute-done | bytes 524320 | tf_op jit(solution)/shard_map/branch/ppermute | solution.py:65
  227.5 13.0 %collective-permute-done.39 = bf16[128,2048]{1,0:T(8,128)(2,1)S(1)} collective-permute-done((bf16[128,2048]{1,0:T(8,128)(2,1)S(1)}, bf16[128,2048]{1,0:T(8,128)(2,1)S(1)}, u32[]{:S(2)}, u32[]{:S(2)}) %collective-permute-start.39) | collective-permute-done | bytes 524320 | tf_op jit(solution)/shard_map/branch/ppermute | solution.py:65
  249.1 7.3 %collective-permute-done.40 = bf16[128,2048]{1,0:T(8,128)(2,1)} collective-permute-done((bf16[128,2048]{1,0:T(8,128)(2,1)S(1)}, bf16[128,2048]{1,0:T(8,128)(2,1)}, u32[]{:S(2)}, u32[]{:S(2)}) %collective-permute-start.40) | collective-permute-done | bytes 524320 | tf_op jit(solution)/shard_map/mlp/ppermute | solution.py:65
  257.3 2.5 constant_dynamic-update-slice_fusion.10
  259.8 4.8 fusion.44
  266.8 2.3 convolution_convert_fusion.10
  269.1 2.3 convolution_convert_fusion.11
  271.5 3.1 collective-permute-start.44
  281.9 5.2 collective-permute-done.44
  290.6 2.3 convolution_convert_fusion.6
  300.8 6.2 %convolution_convert_fusion.2 = bf16[2048,1024]{1,0:T(8,128)(2,1)} fusion(bf16[1024,2048]{1,0:T(8,128)(2,1)S(1)} %constant_dynamic-update-slice_fusion.1, bf16[1024,1024]{1,0:T(8,128)(2,1)S(1)} %get-tuple-element.701), kind=kOutput, calls=%fused_computation.4 | convolution fusion | flops 4297064448 | bytes 10485760 | tf_op jit(solution)/shard_map/mlp/up_grad/dot_general | solution.py:28
  310.1 4.6 convolution_convert_fusion.4
  317.0 6.0 collective-permute-done.48
  327.9 9.4 %convolution_convert_fusion.1 = bf16[1024,2048]{1,0:T(8,128)(2,1)} fusion(bf16[1024,1024]{1,0:T(8,128)(2,1)} %copy-done.85, bf16[1024,2048]{1,0:T(8,128)(2,1)} %all-gather.6.cloned.1.call-done), kind=kOutput, calls=%fused_computation.3 | convolution fusion | flops 4297064448 | bytes 10485760 | tf_op jit(solution)/shard_map/mlp/down_grad/dot_general | solution.py:28
  337.2 4.0 collective-permute-done.50
  343.5 9.6 %convolution_convert_fusion = bf16[1024,2048]{1,0:T(8,128)(2,1)} fusion(bf16[1024,1024]{1,0:T(8,128)(2,1)} %copy-done.85, bf16[1024,2048]{1,0:T(8,128)(2,1)} %all-gather.4.cloned.1.call-done), kind=kOutput, calls=%fused_computation.2 | convolution fusion | flops 4297064448 | bytes 10485760 | tf_op jit(solution)/shard_map/mlp/output/dot_general | solution.py:24
  353.0 3.8 collective-permute-done.52
  358.8 2.7 fusion.95
  361.9 11.8 %collective-permute-done.54.refs_1_ = bf16[128,2048]{1,0:T(8,128)(2,1)S(1)} collective-permute-done((bf16[128,2048]{1,0:T(8,128)(2,1)S(1)}, bf16[128,2048]{1,0:T(8,128)(2,1)S(1)}, u32[]{:S(2)}, u32[]{:S(2)}) %collective-permute-start.54) | collective-permute-done | bytes 524320 | tf_op jit(solution)/shard_map/d_branch_gather/ppermute | solution.py:65
  376.2 11.1 %collective-permute-done.55.refs_2_ = bf16[128,2048]{1,0:T(8,128)(2,1)} collective-permute-done((bf16[128,2048]{1,0:T(8,128)(2,1)S(1)}, bf16[128,2048]{1,0:T(8,128)(2,1)}, u32[]{:S(2)}, u32[]{:S(2)}) %collective-permute-start.55) | collective-permute-done | bytes 524320 | tf_op jit(solution)/shard_map/d_branch_gather/ppermute | solution.py:65
  389.2 10.4 %collective-permute-done.56.refs_3_ = bf16[128,2048]{1,0:T(8,128)(2,1)} collective-permute-done((bf16[128,2048]{1,0:T(8,128)(2,1)}, bf16[128,2048]{1,0:T(8,128)(2,1)}, u32[]{:S(2)}, u32[]{:S(2)}) %collective-permute-start.56) | collective-permute-done | bytes 524320 | tf_op jit(solution)/shard_map/d_branch_gather/ppermute | solution.py:65
  406.2 5.8 mix_back.1
  412.4 8.3 %attend_back.4 = (f32[1024,256]{1,0:T(8,128)S(1)}, bf16[1024,256]{1,0:T(8,128)(2,1)S(1)}, bf16[1024,256]{1,0:T(8,128)(2,1)S(1)}) custom-call(s32[4]{0:T(128)S(1)} %get-tuple-element.388.refs_0_.at_ref, s32[1,1024]{1,0:T(1,128)S(1)} %bitcast.203, f32[2,1,1024]{2,1,0:T(1,128)S(1)} %get-tuple-element.476.refs_2_, f32[2,1,1024]{2,1,0:T(1,128)S(1)} %get-tuple-element.589.refs_3_, ...), custom_call_target="tpu_custom_call" | custom-call | flops 1342177280 | bytes 5242880 | tf_op jit(solution)/shard_map/attention_back/attend_back/pallas_call | solution.py:396
  426.8 8.1 %attend_back.5 = (f32[1024,256]{1,0:T(8,128)S(1)}, bf16[1024,256]{1,0:T(8,128)(2,1)S(1)}, bf16[1024,256]{1,0:T(8,128)(2,1)S(1)}) custom-call(s32[4]{0:T(128)S(1)} %get-tuple-element.388.refs_0_.at_ref, s32[1,1024]{1,0:T(1,128)S(1)} %bitcast.204, f32[2,1,1024]{2,1,0:T(1,128)S(1)} %get-tuple-element.476.refs_2_, f32[2,1,1024]{2,1,0:T(1,128)S(1)} %get-tuple-element.589.refs_3_, ...), custom_call_target="tpu_custom_call" | custom-call | flops 1342177280 | bytes 5242880 | tf_op jit(solution)/shard_map/attention_back/attend_back/pallas_call | solution.py:396
  435.7 8.1 %attend_back.6 = (f32[1024,256]{1,0:T(8,128)S(1)}, bf16[1024,256]{1,0:T(8,128)(2,1)S(1)}, bf16[1024,256]{1,0:T(8,128)(2,1)S(1)}) custom-call(s32[4]{0:T(128)S(1)} %get-tuple-element.388.refs_0_.at_ref, s32[1,1024]{1,0:T(1,128)S(1)} %bitcast.205, f32[2,1,1024]{2,1,0:T(1,128)S(1)} %get-tuple-element.476.refs_2_, f32[2,1,1024]{2,1,0:T(1,128)S(1)} %get-tuple-element.589.refs_3_, ...), custom_call_target="tpu_custom_call" | custom-call | flops 1342177280 | bytes 5242880 | tf_op jit(solution)/shard_map/attention_back/attend_back/pallas_call | solution.py:396
  459.4 8.1 %attend_back.7 = (f32[1024,256]{1,0:T(8,128)S(1)}, bf16[1024,256]{1,0:T(8,128)(2,1)S(1)}, bf16[1024,256]{1,0:T(8,128)(2,1)S(1)}) custom-call(s32[4]{0:T(128)S(1)} %get-tuple-element.388.refs_0_.at_ref, s32[1,1024]{1,0:T(1,128)S(1)} %bitcast.206, f32[2,1,1024]{2,1,0:T(1,128)S(1)} %get-tuple-element.476.refs_2_, f32[2,1,1024]{2,1,0:T(1,128)S(1)} %get-tuple-element.589.refs_3_, ...), custom_call_target="tpu_custom_call" | custom-call | flops 1342177280 | bytes 5242880 | tf_op jit(solution)/shard_map/attention_back/attend_back/pallas_call | solution.py:396
  467.5 4.3 mix_grad.1
  474.3 2.6 pad_maximum_fusion.1.refs_4_
  478.6 7.8 %collective-permute-done.69 = bf16[1024,256]{1,0:T(8,128)(2,1)S(1)} collective-permute-done((bf16[1024,256]{1,0:T(8,128)(2,1)S(1)}, bf16[1024,256]{1,0:T(8,128)(2,1)S(1)}, u32[]{:S(2)}, u32[]{:S(2)}) %collective-permute-start.69) | collective-permute-done | bytes 524320 | tf_op jit(solution)/shard_map/attention_back/ppermute | solution.py:54
  487.9 9.4 %terms_out.3 = (bf16[4,128,2048]{2,1,0:T(8,128)(2,1)S(1)}, bf16[4,128,2048]{2,1,0:T(8,128)(2,1)}, f32[2,2048]{1,0:T(2,128)S(1)}) custom-call(s32[8]{0:T(128)S(1)} %add.511.at_ref, bf16[1024,768]{1,0:T(8,128)(2,1)S(1)} %pad_maximum_fusion.2.refs_0_.refs_1_, bf16[1024,768]{1,0:T(8,128)(2,1)S(1)} %pad_maximum_fusion.2.refs_0_.refs_1_, ...), custom_call_target="tpu_custom_call" | custom-call | flops 3221225472 | bytes 8388608 | tf_op jit(solution)/shard_map/d_normed/terms_out/pallas_call | solution.py:550
  498.7 2.7 slice_bitcast_fusion.8
  503.2 2.7 slice_bitcast_fusion
  507.0 6.2 %convolution_convert_fusion.3 = bf16[2048,768]{1,0:T(8,128)(2,1)S(1)} fusion(bf16[1024,2048]{1,0:T(8,128)(2,1)} %get-tuple-element.687, bf16[1024,768]{1,0:T(8,128)(2,1)} %copy-done.17), kind=kOutput, calls=%fused_computation.5 | convolution fusion | flops 3222798336 | bytes 8912896 | tf_op jit(solution)/shard_map/qkv_grad/dot_general | solution.py:28
  513.2 8.0 %collective-permute-done.73 = bf16[128,2048]{1,0:T(8,128)(2,1)S(1)} collective-permute-done((bf16[128,2048]{1,0:T(8,128)(2,1)S(1)}, bf16[128,2048]{1,0:T(8,128)(2,1)S(1)}, u32[]{:S(2)}, u32[]{:S(2)}) %collective-permute-start.73) | collective-permute-done | bytes 524320 | tf_op jit(solution)/shard_map/ppermute | solution.py:65
  531.9 3.5 collective-permute-done.77
  543.4 2.5 collective-permute-start.78
  550.9 5.2 collective-permute-done.78
  558.0 7.1 %collective-permute-done.79 = bf16[520,768]{1,0:T(8,128)(2,1)} collective-permute-done((bf16[520,768]{1,0:T(8,128)(2,1)}, bf16[520,768]{1,0:T(8,128)(2,1)}, u32[]{:S(2)}, u32[]{:S(2)}) %collective-permute-start.79) | collective-permute-done | bytes 798752 | tf_op jit(solution)/shard_map/qkv_grad/ppermute | solution.py:54
  573.6 2.8 fusion.15
  578.7 3.2 collective-permute-done.82.refs_1_
  582.0 7.6 %collective-permute-done.83.refs_2_ = bf16[2,80,768]{2,1,0:T(8,128)(2,1)S(1)} collective-permute-done((bf16[2,80,768]{2,1,0:T(8,128)(2,1)S(1)}, bf16[2,80,768]{2,1,0:T(8,128)(2,1)S(1)}, u32[]{:S(2)}, u32[]{:S(2)}) %collective-permute-start.83) | collective-permute-done | bytes 245792 | tf_op jit(solution)/shard_map/qkv_grad/ppermute | solution.py:54
  589.6 5.8 collective-permute-done.84.refs_3_
  (555 shorter events, 198.8 us)
Async XLA Ops:
  7.2 81.8 %all-gather.4.cloned.1.call-start = ((), (), s32[]{:S(2)}) async-start(), calls=%async_computation.4 | async-start | bytes 5242880 | tf_op jit(solution)/shard_map/down_weights/all_gather | solution.py:725
  7.9 184.9 %all-gather.6.cloned.1.call-start = ((), (), s32[]{:S(2)}) async-start(), calls=%async_computation.5 | async-start | bytes 4718592 | tf_op jit(solution)/shard_map/dy_gather/all_gather | solution.py:852
  8.0 14.8 %collective-permute-start.1 = (bf16[128,2048]{1,0:T(8,128)(2,1)}, bf16[128,2048]{1,0:T(8,128)(2,1)S(1)}, u32[]{:S(2)}, u32[]{:S(2)}) collective-permute-start(bf16[128,2048]{1,0:T(8,128)(2,1)} %refs_0_.3), channel_id=1, source_target_pairs={{0,4},{1,5},{4,6},{5,7},{6,2},{7,3},{2,0},{3,1},{8,12},{9,13},{12,... | collective-permute-start | bytes 1572872 | tf_op jit(solution)/shard_map/tokens_gather/ppermute | solution.py:65
  8.1 14.8 %collective-permute-start.2 = (bf16[128,2048]{1,0:T(8,128)(2,1)}, bf16[128,2048]{1,0:T(8,128)(2,1)}, u32[]{:S(2)}, u32[]{:S(2)}) collective-permute-start(bf16[128,2048]{1,0:T(8,128)(2,1)} %refs_0_.3), channel_id=1, source_target_pairs={{0,1},{1,0},{2,3},{3,2},{4,5},{5,4},{6,7},{7,6},{8,9},{9,8},{10,11... | collective-permute-start | bytes 1572872 | tf_op jit(solution)/shard_map/tokens_gather/ppermute | solution.py:54
  24.3 16.5 %collective-permute-start.4 = (bf16[2,64,768]{2,1,0:T(8,128)(2,1)S(1)}, bf16[2,64,768]{2,1,0:T(8,128)(2,1)S(1)}, u32[]{:S(2)}, u32[]{:S(2)}) collective-permute-start(bf16[2,64,768]{2,1,0:T(8,128)(2,1)S(1)} %get-tuple-element.393), channel_id=1, source_target_pairs={{0,4},{1,5},{2,6},{3,7},{4,0},{5,1},{6,2},{7,3},{8,12},{9,13},{10,... | collective-permute-start | bytes 589832 | tf_op jit(solution)/shard_map/qkv_weights/ppermute | solution.py:54
  27.4 17.0 %collective-permute-start.5 = (bf16[2,64,768]{2,1,0:T(8,128)(2,1)S(1)}, bf16[2,64,768]{2,1,0:T(8,128)(2,1)S(1)}, u32[]{:S(2)}, u32[]{:S(2)}) collective-permute-start(bf16[2,64,768]{2,1,0:T(8,128)(2,1)S(1)} %get-tuple-element.394), channel_id=1, source_target_pairs={{0,6},{1,7},{2,4},{3,5},{4,2},{5,3},{6,0},{7,1},{8,14},{9,15},{10,... | collective-permute-start | bytes 589832 | tf_op jit(solution)/shard_map/qkv_weights/ppermute | solution.py:54
  32.9 12.9 %collective-permute-start.9 = (bf16[8,14,64]{2,1,0:T(8,128)(2,1)S(1)}, bf16[8,14,64]{2,1,0:T(8,128)(2,1)S(1)}, u32[]{:S(2)}, u32[]{:S(2)}) collective-permute-start(bf16[8,14,64]{2,1,0:T(8,128)(2,1)S(1)} %constant_dynamic-update-slice_fusion.12), channel_id=1, source_target_pairs={{0,4},{1,5},{4,6},{5,7},{6,2},{7,3},{2,0},{3,1},{8,12},{9,13},{12,... | collective-permute-start | bytes 43016 | tf_op jit(solution)/shard_map/vectors/ppermute | solution.py:65
  45.9 13.5 %collective-permute-start.16 = (bf16[128,2048]{1,0:T(8,128)(2,1)S(1)}, bf16[128,2048]{1,0:T(8,128)(2,1)S(1)}, u32[]{:S(2)}, u32[]{:S(2)}) collective-permute-start(bf16[128,2048]{1,0:T(8,128)(2,1)S(1)} %collective-permute-done.1.refs_1_), channel_id=1, source_target_pairs={{0,4},{1,5},{4,6},{5,7},{6,2},{7,3},{2,0},{3,1},{8,12},{9,13},{12,... | collective-permute-start | bytes 1572872 | tf_op jit(solution)/shard_map/tokens_gather/ppermute | solution.py:65
  46.4 20.7 %collective-permute-start.12 = (bf16[4,64,768]{2,1,0:T(8,128)(2,1)}, bf16[4,64,768]{2,1,0:T(8,128)(2,1)}, u32[]{:S(2)}, u32[]{:S(2)}) collective-permute-start(bf16[4,64,768]{2,1,0:T(8,128)(2,1)} %get-tuple-element.427.refs_11_), channel_id=1, source_target_pairs={{0,16},{8,24},{16,0},{24,8},{1,17},{9,25},{17,1},{25,9},{2,18},{10... | collective-permute-start | bytes 1179656 | tf_op jit(solution)/shard_map/qkv_weights/ppermute | solution.py:54
  48.0 20.7 %collective-permute-start.11 = (bf16[4,64,768]{2,1,0:T(8,128)(2,1)}, bf16[4,64,768]{2,1,0:T(8,128)(2,1)}, u32[]{:S(2)}, u32[]{:S(2)}) collective-permute-start(bf16[4,64,768]{2,1,0:T(8,128)(2,1)} %get-tuple-element.428.refs_12_), channel_id=1, source_target_pairs={{0,8},{8,0},{16,24},{24,16},{1,9},{9,1},{17,25},{25,17},{2,10},{10... | collective-permute-start | bytes 1179656 | tf_op jit(solution)/shard_map/qkv_weights/ppermute | solution.py:54
  59.5 22.0 %collective-permute-start.10 = (bf16[4,64,768]{2,1,0:T(8,128)(2,1)}, bf16[4,64,768]{2,1,0:T(8,128)(2,1)S(1)}, u32[]{:S(2)}, u32[]{:S(2)}) collective-permute-start(bf16[4,64,768]{2,1,0:T(8,128)(2,1)} %get-tuple-element.427.refs_11_), channel_id=1, source_target_pairs={{0,8},{8,0},{16,24},{24,16},{1,9},{9,1},{17,25},{25,17},{2,10},{10... | collective-permute-start | bytes 1179656 | tf_op jit(solution)/shard_map/qkv_weights/ppermute | solution.py:54
  60.1 22.2 %collective-permute-start.13 = (bf16[4,64,768]{2,1,0:T(8,128)(2,1)}, bf16[4,64,768]{2,1,0:T(8,128)(2,1)}, u32[]{:S(2)}, u32[]{:S(2)}) collective-permute-start(bf16[4,64,768]{2,1,0:T(8,128)(2,1)} %get-tuple-element.428.refs_12_), channel_id=1, source_target_pairs={{0,16},{8,24},{16,0},{24,8},{1,17},{9,25},{17,1},{25,9},{2,18},{10... | collective-permute-start | bytes 1179656 | tf_op jit(solution)/shard_map/qkv_weights/ppermute | solution.py:54
  67.1 21.9 %collective-permute-start.14 = (bf16[4,64,768]{2,1,0:T(8,128)(2,1)}, bf16[4,64,768]{2,1,0:T(8,128)(2,1)}, u32[]{:S(2)}, u32[]{:S(2)}) collective-permute-start(bf16[4,64,768]{2,1,0:T(8,128)(2,1)} %collective-permute-done.12.refs_15_), channel_id=1, source_target_pairs={{0,8},{8,0},{16,24},{24,16},{1,9},{9,1},{17,25},{25,17},{2,10},{10... | collective-permute-start | bytes 1179656 | tf_op jit(solution)/shard_map/qkv_weights/ppermute | solution.py:54
  68.7 20.4 %collective-permute-start.15 = (bf16[4,64,768]{2,1,0:T(8,128)(2,1)}, bf16[4,64,768]{2,1,0:T(8,128)(2,1)}, u32[]{:S(2)}, u32[]{:S(2)}) collective-permute-start(bf16[4,64,768]{2,1,0:T(8,128)(2,1)} %collective-permute-done.11.refs_14_), channel_id=1, source_target_pairs={{0,16},{8,24},{16,0},{24,8},{1,17},{9,25},{17,1},{25,9},{2,18},{10... | collective-permute-start | bytes 1179656 | tf_op jit(solution)/shard_map/qkv_weights/ppermute | solution.py:54
  69.2 19.8 %collective-permute-start.18 = (bf16[128,2048]{1,0:T(8,128)(2,1)S(1)}, bf16[128,2048]{1,0:T(8,128)(2,1)S(1)}, u32[]{:S(2)}, u32[]{:S(2)}) collective-permute-start(bf16[128,2048]{1,0:T(8,128)(2,1)S(1)} %collective-permute-done.16.refs_2_), channel_id=1, source_target_pairs={{0,4},{1,5},{4,6},{5,7},{6,2},{7,3},{2,0},{3,1},{8,12},{9,13},{12,... | collective-permute-start | bytes 1572872 | tf_op jit(solution)/shard_map/tokens_gather/ppermute | solution.py:65
  90.1 19.8 %collective-permute-start.24 = (bf16[64,2048]{1,0:T(8,128)(2,1)}, bf16[64,2048]{1,0:T(8,128)(2,1)S(1)}, u32[]{:S(2)}, u32[]{:S(2)}) collective-permute-start(bf16[64,2048]{1,0:T(8,128)(2,1)} %refs_0_.4), channel_id=1, source_target_pairs={{0,8},{8,0},{16,24},{24,16},{1,9},{9,1},{17,25},{25,17},{2,10},{10... | collective-permute-start | bytes 786440 | tf_op jit(solution)/shard_map/out_weights/ppermute | solution.py:54
  91.6 18.4 %collective-permute-start.25 = (bf16[64,2048]{1,0:T(8,128)(2,1)}, bf16[64,2048]{1,0:T(8,128)(2,1)S(1)}, u32[]{:S(2)}, u32[]{:S(2)}) collective-permute-start(bf16[64,2048]{1,0:T(8,128)(2,1)} %refs_0_.4), channel_id=1, source_target_pairs={{0,16},{8,24},{16,0},{24,8},{1,17},{9,25},{17,1},{25,9},{2,18},{10... | collective-permute-start | bytes 786440 | tf_op jit(solution)/shard_map/out_weights/ppermute | solution.py:54
  110.7 29.2 %collective-permute-start.26 = (bf16[2,1024,256]{2,1,0:T(8,128)(2,1)}, bf16[2,1024,256]{2,1,0:T(8,128)(2,1)S(1)}, u32[]{:S(2)}, u32[]{:S(2)}) collective-permute-start(bf16[2,1024,256]{2,1,0:T(8,128)(2,1)} %get-tuple-element.447.refs_3_.refs_4_.refs_6_.refs_7_), channel_id=1, source_target_pairs={{0,8},{8,0},{16,24},{24,16},{1,9},{9,1},{17,25},{25,17},{2,10},{10... | collective-permute-start | bytes 3145736 | tf_op jit(solution)/shard_map/kv_gather/ppermute | solution.py:54
  111.7 28.3 %collective-permute-start.27 = (bf16[2,1024,256]{2,1,0:T(8,128)(2,1)}, bf16[2,1024,256]{2,1,0:T(8,128)(2,1)S(1)}, u32[]{:S(2)}, u32[]{:S(2)}) collective-permute-start(bf16[2,1024,256]{2,1,0:T(8,128)(2,1)} %get-tuple-element.447.refs_3_.refs_4_.refs_6_.refs_7_), channel_id=1, source_target_pairs={{0,16},{8,24},{16,0},{24,8},{1,17},{9,25},{17,1},{25,9},{2,18},{10... | collective-permute-start | bytes 3145736 | tf_op jit(solution)/shard_map/kv_gather/ppermute | solution.py:54
  113.5 13.6 %collective-permute-start.28 = (bf16[2,64,1024]{2,1,0:T(8,128)(2,1)}, bf16[2,64,1024]{2,1,0:T(8,128)(2,1)S(1)}, u32[]{:S(2)}, u32[]{:S(2)}) collective-permute-start(bf16[2,64,1024]{2,1,0:T(8,128)(2,1)} %copy-done.64), channel_id=1, source_target_pairs={{0,2},{1,3},{2,0},{3,1},{4,6},{5,7},{6,4},{7,5},{8,10},{9,11},{10,... | collective-permute-start | bytes 786440 | tf_op jit(solution)/shard_map/up_weights/ppermute | solution.py:54
  113.9 20.7 %collective-permute-start.29 = (bf16[2,64,1024]{2,1,0:T(8,128)(2,1)}, bf16[2,64,1024]{2,1,0:T(8,128)(2,1)S(1)}, u32[]{:S(2)}, u32[]{:S(2)}) collective-permute-start(bf16[2,64,1024]{2,1,0:T(8,128)(2,1)} %copy-done.63), channel_id=1, source_target_pairs={{0,4},{1,5},{2,6},{3,7},{4,0},{5,1},{6,2},{7,3},{8,12},{9,13},{10,... | collective-permute-start | bytes 786440 | tf_op jit(solution)/shard_map/up_weights/ppermute | solution.py:54
  116.3 23.0 %collective-permute-start.30 = (bf16[2,64,1024]{2,1,0:T(8,128)(2,1)}, bf16[2,64,1024]{2,1,0:T(8,128)(2,1)S(1)}, u32[]{:S(2)}, u32[]{:S(2)}) collective-permute-start(bf16[2,64,1024]{2,1,0:T(8,128)(2,1)} %copy-done.62), channel_id=1, source_target_pairs={{0,6},{1,7},{2,4},{3,5},{4,2},{5,3},{6,0},{7,1},{8,14},{9,15},{10,... | collective-permute-start | bytes 786440 | tf_op jit(solution)/shard_map/up_weights/ppermute | solution.py:54
  140.0 103.9 %all-gather.8.cloned.1.call-start = ((), (), s32[]{:S(2)}) async-start(), calls=%async_computation.6 | async-start | bytes 5242880 | tf_op jit(solution)/shard_map/up_weights/all_gather | solution.py:874
  141.3 17.3 %collective-permute-start.31 = (bf16[1,1024,256]{2,1,0:T(8,128)(2,1)}, bf16[1,1024,256]{2,1,0:T(8,128)(2,1)}, u32[]{:S(2)}, u32[]{:S(2)}) collective-permute-start(bf16[1,1024,256]{2,1,0:T(8,128)(2,1)} %slice.232), channel_id=1, source_target_pairs={{0,8},{8,0},{16,24},{24,16},{1,9},{9,1},{17,25},{25,17},{2,10},{10... | collective-permute-start | bytes 1572872 | tf_op jit(solution)/shard_map/kv_gather/ppermute | solution.py:54
  142.9 15.7 %collective-permute-start.32 = (bf16[1,1024,256]{2,1,0:T(8,128)(2,1)}, bf16[1,1024,256]{2,1,0:T(8,128)(2,1)}, u32[]{:S(2)}, u32[]{:S(2)}) collective-permute-start(bf16[1,1024,256]{2,1,0:T(8,128)(2,1)} %slice.233), channel_id=1, source_target_pairs={{0,16},{8,24},{16,0},{24,8},{1,17},{9,25},{17,1},{25,9},{2,18},{10... | collective-permute-start | bytes 1572872 | tf_op jit(solution)/shard_map/kv_gather/ppermute | solution.py:54
  162.2 17.4 %collective-permute-start.35 = (bf16[2,64,2048]{2,1,0:T(8,128)(2,1)S(1)}, bf16[2,64,2048]{2,1,0:T(8,128)(2,1)S(1)}, u32[]{:S(2)}, u32[]{:S(2)}) collective-permute-start(bf16[2,64,2048]{2,1,0:T(8,128)(2,1)S(1)} %dynamic-slice_bitcast_fusion.5), channel_id=1, source_target_pairs={{0,1},{1,0},{2,3},{3,2},{4,5},{5,4},{6,7},{7,6},{8,9},{9,8},{10,11... | collective-permute-start | bytes 1572872 | tf_op jit(solution)/shard_map/out_weights/ppermute | solution.py:54
  185.6 201.6 %reduce-scatter.5.cloned.1.call-start = ((), (), s32[]{:S(2)}) async-start(), calls=%async_computation.7 | async-start | bytes 5242880 | tf_op jit(solution)/shard_map/up_grad/reduce_scatter | solution.py:1000
  194.9 15.2 %collective-permute-start.37 = (bf16[128,2048]{1,0:T(8,128)(2,1)}, bf16[128,2048]{1,0:T(8,128)(2,1)}, u32[]{:S(2)}, u32[]{:S(2)}) collective-permute-start(bf16[128,2048]{1,0:T(8,128)(2,1)} %add_convert_fusion.14), channel_id=1, source_target_pairs={{0,4},{1,5},{4,6},{5,7},{6,2},{7,3},{2,0},{3,1},{8,12},{9,13},{12,... | collective-permute-start | bytes 1572872 | tf_op jit(solution)/shard_map/branch/ppermute | solution.py:65
  211.7 14.1 %collective-permute-start.38 = (bf16[128,2048]{1,0:T(8,128)(2,1)S(1)}, bf16[128,2048]{1,0:T(8,128)(2,1)S(1)}, u32[]{:S(2)}, u32[]{:S(2)}) collective-permute-start(bf16[128,2048]{1,0:T(8,128)(2,1)S(1)} %add_convert_fusion.13), channel_id=1, source_target_pairs={{0,4},{1,5},{4,6},{5,7},{6,2},{7,3},{2,0},{3,1},{8,12},{9,13},{12,... | collective-permute-start | bytes 1572872 | tf_op jit(solution)/shard_map/branch/ppermute | solution.py:65
  227.3 13.2 %collective-permute-start.39 = (bf16[128,2048]{1,0:T(8,128)(2,1)S(1)}, bf16[128,2048]{1,0:T(8,128)(2,1)S(1)}, u32[]{:S(2)}, u32[]{:S(2)}) collective-permute-start(bf16[128,2048]{1,0:T(8,128)(2,1)S(1)} %add_convert_fusion.12), channel_id=1, source_target_pairs={{0,4},{1,5},{4,6},{5,7},{6,2},{7,3},{2,0},{3,1},{8,12},{9,13},{12,... | collective-permute-start | bytes 1572872 | tf_op jit(solution)/shard_map/branch/ppermute | solution.py:65
  243.8 12.6 %collective-permute-start.40 = (bf16[128,2048]{1,0:T(8,128)(2,1)S(1)}, bf16[128,2048]{1,0:T(8,128)(2,1)}, u32[]{:S(2)}, u32[]{:S(2)}) collective-permute-start(bf16[128,2048]{1,0:T(8,128)(2,1)S(1)} %get-tuple-element.517), channel_id=1, source_target_pairs={{0,4},{1,5},{4,6},{5,7},{6,2},{7,3},{2,0},{3,1},{8,12},{9,13},{12,... | collective-permute-start | bytes 1572872 | tf_op jit(solution)/shard_map/mlp/ppermute | solution.py:65
  243.8 12.6 %collective-permute-start.41 = (bf16[128,2048]{1,0:T(8,128)(2,1)S(1)}, bf16[128,2048]{1,0:T(8,128)(2,1)}, u32[]{:S(2)}, u32[]{:S(2)}) collective-permute-start(bf16[128,2048]{1,0:T(8,128)(2,1)S(1)} %get-tuple-element.517), channel_id=1, source_target_pairs={{0,1},{1,0},{2,3},{3,2},{4,5},{5,4},{6,7},{7,6},{8,9},{9,8},{10,11... | collective-permute-start | bytes 1572872 | tf_op jit(solution)/shard_map/mlp/ppermute | solution.py:54
  256.4 15.0 %collective-permute-start.42 = (bf16[128,2048]{1,0:T(8,128)(2,1)}, bf16[128,2048]{1,0:T(8,128)(2,1)S(1)}, u32[]{:S(2)}, u32[]{:S(2)}) collective-permute-start(bf16[128,2048]{1,0:T(8,128)(2,1)} %collective-permute-done.40), channel_id=1, source_target_pairs={{0,4},{1,5},{4,6},{5,7},{6,2},{7,3},{2,0},{3,1},{8,12},{9,13},{12,... | collective-permute-start | bytes 1572872 | tf_op jit(solution)/shard_map/mlp/ppermute | solution.py:65
  256.4 15.0 %collective-permute-start.43 = (bf16[128,2048]{1,0:T(8,128)(2,1)}, bf16[128,2048]{1,0:T(8,128)(2,1)S(1)}, u32[]{:S(2)}, u32[]{:S(2)}) collective-permute-start(bf16[128,2048]{1,0:T(8,128)(2,1)} %collective-permute-done.40), channel_id=1, source_target_pairs={{0,1},{1,0},{2,3},{3,2},{4,5},{5,4},{6,7},{7,6},{8,9},{9,8},{10,11... | collective-permute-start | bytes 1572872 | tf_op jit(solution)/shard_map/mlp/ppermute | solution.py:54
  271.5 15.6 %collective-permute-start.44 = (bf16[128,2048]{1,0:T(8,128)(2,1)S(1)}, bf16[128,2048]{1,0:T(8,128)(2,1)S(1)}, u32[]{:S(2)}, u32[]{:S(2)}) collective-permute-start(bf16[128,2048]{1,0:T(8,128)(2,1)S(1)} %collective-permute-done.42), channel_id=1, source_target_pairs={{0,4},{1,5},{4,6},{5,7},{6,2},{7,3},{2,0},{3,1},{8,12},{9,13},{12,... | collective-permute-start | bytes 1572872 | tf_op jit(solution)/shard_map/mlp/ppermute | solution.py:65
  274.5 12.6 %collective-permute-start.45 = (bf16[128,2048]{1,0:T(8,128)(2,1)S(1)}, bf16[128,2048]{1,0:T(8,128)(2,1)S(1)}, u32[]{:S(2)}, u32[]{:S(2)}) collective-permute-start(bf16[128,2048]{1,0:T(8,128)(2,1)S(1)} %collective-permute-done.42), channel_id=1, source_target_pairs={{0,1},{1,0},{2,3},{3,2},{4,5},{5,4},{6,7},{7,6},{8,9},{9,8},{10,11... | collective-permute-start | bytes 1572872 | tf_op jit(solution)/shard_map/mlp/ppermute | solution.py:54
  308.3 14.8 %collective-permute-start.48 = (bf16[128,2048]{1,0:T(8,128)(2,1)S(1)}, bf16[128,2048]{1,0:T(8,128)(2,1)S(1)}, u32[]{:S(2)}, u32[]{:S(2)}) collective-permute-start(bf16[128,2048]{1,0:T(8,128)(2,1)S(1)} %add_convert_fusion.10), channel_id=1, source_target_pairs={{0,4},{1,5},{4,6},{5,7},{6,2},{7,3},{2,0},{3,1},{8,12},{9,13},{12,... | collective-permute-start | bytes 1572872 | tf_op jit(solution)/shard_map/mlp/ppermute | solution.py:65
  310.1 13.8 %collective-permute-start.49 = (bf16[128,2048]{1,0:T(8,128)(2,1)}, bf16[128,2048]{1,0:T(8,128)(2,1)S(1)}, u32[]{:S(2)}, u32[]{:S(2)}) collective-permute-start(bf16[128,2048]{1,0:T(8,128)(2,1)} %convolution_convert_fusion.6), channel_id=1, source_target_pairs={{0,1},{1,0},{2,3},{3,2},{4,5},{5,4},{6,7},{7,6},{8,9},{9,8},{10,11... | collective-permute-start | bytes 1572872 | tf_op jit(solution)/shard_map/mlp/ppermute | solution.py:54
  324.7 126.2 %reduce-scatter.7.cloned.1.call-start = ((), (), s32[]{:S(2)}) async-start(), calls=%async_computation.8 | async-start | bytes 5242880 | tf_op jit(solution)/shard_map/d_branch_gather/down_grad/reduce_scatter | solution.py:1000
  327.0 14.2 %collective-permute-start.50 = (bf16[128,2048]{1,0:T(8,128)(2,1)}, bf16[128,2048]{1,0:T(8,128)(2,1)}, u32[]{:S(2)}, u32[]{:S(2)}) collective-permute-start(bf16[128,2048]{1,0:T(8,128)(2,1)} %add_convert_fusion.9), channel_id=1, source_target_pairs={{0,4},{1,5},{4,6},{5,7},{6,2},{7,3},{2,0},{3,1},{8,12},{9,13},{12,... | collective-permute-start | bytes 1572872 | tf_op jit(solution)/shard_map/mlp/ppermute | solution.py:65
  327.9 13.3 %collective-permute-start.51 = (bf16[128,2048]{1,0:T(8,128)(2,1)}, bf16[128,2048]{1,0:T(8,128)(2,1)}, u32[]{:S(2)}, u32[]{:S(2)}) collective-permute-start(bf16[128,2048]{1,0:T(8,128)(2,1)} %convolution_convert_fusion.4), channel_id=1, source_target_pairs={{0,1},{1,0},{2,3},{3,2},{4,5},{5,4},{6,7},{7,6},{8,9},{9,8},{10,11... | collective-permute-start | bytes 1572872 | tf_op jit(solution)/shard_map/mlp/ppermute | solution.py:54
  343.4 13.4 %collective-permute-start.52 = (bf16[128,2048]{1,0:T(8,128)(2,1)}, bf16[128,2048]{1,0:T(8,128)(2,1)}, u32[]{:S(2)}, u32[]{:S(2)}) collective-permute-start(bf16[128,2048]{1,0:T(8,128)(2,1)} %add_convert_fusion.8), channel_id=1, source_target_pairs={{0,4},{1,5},{4,6},{5,7},{6,2},{7,3},{2,0},{3,1},{8,12},{9,13},{12,... | collective-permute-start | bytes 1572872 | tf_op jit(solution)/shard_map/mlp/ppermute | solution.py:65
  343.4 13.4 %collective-permute-start.53 = (bf16[128,2048]{1,0:T(8,128)(2,1)}, bf16[128,2048]{1,0:T(8,128)(2,1)}, u32[]{:S(2)}, u32[]{:S(2)}) collective-permute-start(bf16[128,2048]{1,0:T(8,128)(2,1)} %convolution_convert_fusion.10), channel_id=1, source_target_pairs={{0,1},{1,0},{2,3},{3,2},{4,5},{5,4},{6,7},{7,6},{8,9},{9,8},{10,11... | collective-permute-start | bytes 1572872 | tf_op jit(solution)/shard_map/mlp/ppermute | solution.py:54
  374.5 12.7 %collective-permute-start.55 = (bf16[128,2048]{1,0:T(8,128)(2,1)S(1)}, bf16[128,2048]{1,0:T(8,128)(2,1)}, u32[]{:S(2)}, u32[]{:S(2)}) collective-permute-start(bf16[128,2048]{1,0:T(8,128)(2,1)S(1)} %collective-permute-done.54.refs_1_), channel_id=1, source_target_pairs={{0,4},{1,5},{4,6},{5,7},{6,2},{7,3},{2,0},{3,1},{8,12},{9,13},{12,... | collective-permute-start | bytes 1572872 | tf_op jit(solution)/shard_map/d_branch_gather/ppermute | solution.py:65
  387.3 118.6 %reduce-scatter.9.cloned.1.call-start = ((), (), s32[]{:S(2)}) async-start(), calls=%async_computation.9 | async-start | bytes 4718592 | tf_op jit(solution)/shard_map/output/reduce_scatter | solution.py:1069
  387.3 12.3 %collective-permute-start.56 = (bf16[128,2048]{1,0:T(8,128)(2,1)}, bf16[128,2048]{1,0:T(8,128)(2,1)}, u32[]{:S(2)}, u32[]{:S(2)}) collective-permute-start(bf16[128,2048]{1,0:T(8,128)(2,1)} %collective-permute-done.55.refs_2_), channel_id=1, source_target_pairs={{0,4},{1,5},{4,6},{5,7},{6,2},{7,3},{2,0},{3,1},{8,12},{9,13},{12,... | collective-permute-start | bytes 1572872 | tf_op jit(solution)/shard_map/d_branch_gather/ppermute | solution.py:65
  421.3 28.7 %collective-permute-start.62 = (bf16[1024,256]{1,0:T(8,128)(2,1)S(1)}, bf16[1024,256]{1,0:T(8,128)(2,1)S(1)}, u32[]{:S(2)}, u32[]{:S(2)}) collective-permute-start(bf16[1024,256]{1,0:T(8,128)(2,1)S(1)} %get-tuple-element.599), channel_id=1, source_target_pairs={{0,8},{8,0},{16,24},{24,16},{1,9},{9,1},{17,25},{25,17},{2,10},{10... | collective-permute-start | bytes 1572872 | tf_op jit(solution)/shard_map/attention_back/ppermute | solution.py:54
  422.8 28.1 %collective-permute-start.63 = (bf16[1024,256]{1,0:T(8,128)(2,1)S(1)}, bf16[1024,256]{1,0:T(8,128)(2,1)}, u32[]{:S(2)}, u32[]{:S(2)}) collective-permute-start(bf16[1024,256]{1,0:T(8,128)(2,1)S(1)} %get-tuple-element.600), channel_id=1, source_target_pairs={{0,16},{8,24},{16,0},{24,8},{1,17},{9,25},{17,1},{25,9},{2,18},{10... | collective-permute-start | bytes 1572872 | tf_op jit(solution)/shard_map/attention_back/ppermute | solution.py:54
  423.3 23.0 %collective-permute-start.64 = (bf16[2,64,1024]{2,1,0:T(8,128)(2,1)S(1)}, bf16[2,64,1024]{2,1,0:T(8,128)(2,1)S(1)}, u32[]{:S(2)}, u32[]{:S(2)}) collective-permute-start(bf16[2,64,1024]{2,1,0:T(8,128)(2,1)S(1)} %get-tuple-element.614), channel_id=1, source_target_pairs={{0,2},{1,3},{2,0},{3,1},{4,6},{5,7},{6,4},{7,5},{8,10},{9,11},{10,... | collective-permute-start | bytes 786440 | tf_op jit(solution)/shard_map/up_grad/ppermute | solution.py:54
  424.8 22.3 %collective-permute-start.65 = (bf16[2,64,1024]{2,1,0:T(8,128)(2,1)S(1)}, bf16[2,64,1024]{2,1,0:T(8,128)(2,1)S(1)}, u32[]{:S(2)}, u32[]{:S(2)}) collective-permute-start(bf16[2,64,1024]{2,1,0:T(8,128)(2,1)S(1)} %get-tuple-element.615), channel_id=1, source_target_pairs={{0,4},{1,5},{2,6},{3,7},{4,0},{5,1},{6,2},{7,3},{8,12},{9,13},{10,... | collective-permute-start | bytes 786440 | tf_op jit(solution)/shard_map/up_grad/ppermute | solution.py:54
  426.2 23.1 %collective-permute-start.66 = (bf16[2,64,1024]{2,1,0:T(8,128)(2,1)S(1)}, bf16[2,64,1024]{2,1,0:T(8,128)(2,1)S(1)}, u32[]{:S(2)}, u32[]{:S(2)}) collective-permute-start(bf16[2,64,1024]{2,1,0:T(8,128)(2,1)S(1)} %get-tuple-element.616), channel_id=1, source_target_pairs={{0,6},{1,7},{2,4},{3,5},{4,2},{5,3},{6,0},{7,1},{8,14},{9,15},{10,... | collective-permute-start | bytes 786440 | tf_op jit(solution)/shard_map/up_grad/ppermute | solution.py:54
  450.9 126.0 %reduce-scatter.11.cloned.1.call-start = ((), (), s32[]{:S(2)}) async-start(), calls=%async_computation.10 | async-start | bytes 1310720 | tf_op jit(solution)/shard_map/out_grad/reduce_scatter | solution.py:1000
  453.7 13.8 %collective-permute-start.67 = (bf16[1024,256]{1,0:T(8,128)(2,1)}, bf16[1024,256]{1,0:T(8,128)(2,1)S(1)}, u32[]{:S(2)}, u32[]{:S(2)}) collective-permute-start(bf16[1024,256]{1,0:T(8,128)(2,1)} %copy-done.59), channel_id=1, source_target_pairs={{0,8},{8,0},{16,24},{24,16},{1,9},{9,1},{17,25},{25,17},{2,10},{10... | collective-permute-start | bytes 1572872 | tf_op jit(solution)/shard_map/attention_back/ppermute | solution.py:54
  455.2 12.2 %collective-permute-start.68 = (bf16[1024,256]{1,0:T(8,128)(2,1)S(1)}, bf16[1024,256]{1,0:T(8,128)(2,1)S(1)}, u32[]{:S(2)}, u32[]{:S(2)}) collective-permute-start(bf16[1024,256]{1,0:T(8,128)(2,1)S(1)} %add_convert_fusion.6), channel_id=1, source_target_pairs={{0,16},{8,24},{16,0},{24,8},{1,17},{9,25},{17,1},{25,9},{2,18},{10... | collective-permute-start | bytes 1572872 | tf_op jit(solution)/shard_map/attention_back/ppermute | solution.py:54
  472.0 15.9 %collective-permute-start.71 = (bf16[2,64,2048]{2,1,0:T(8,128)(2,1)S(1)}, bf16[2,64,2048]{2,1,0:T(8,128)(2,1)S(1)}, u32[]{:S(2)}, u32[]{:S(2)}) collective-permute-start(bf16[2,64,2048]{2,1,0:T(8,128)(2,1)S(1)} %dynamic-slice_bitcast_fusion.2), channel_id=1, source_target_pairs={{0,1},{1,0},{2,3},{3,2},{4,5},{5,4},{6,7},{7,6},{8,9},{9,8},{10,11... | collective-permute-start | bytes 1572872 | tf_op jit(solution)/shard_map/out_grad/ppermute | solution.py:54
  472.0 14.3 %collective-permute-start.69 = (bf16[1024,256]{1,0:T(8,128)(2,1)S(1)}, bf16[1024,256]{1,0:T(8,128)(2,1)S(1)}, u32[]{:S(2)}, u32[]{:S(2)}) collective-permute-start(bf16[1024,256]{1,0:T(8,128)(2,1)S(1)} %add_convert_fusion.7), channel_id=1, source_target_pairs={{0,8},{8,0},{16,24},{24,16},{1,9},{9,1},{17,25},{25,17},{2,10},{10... | collective-permute-start | bytes 1572872 | tf_op jit(solution)/shard_map/attention_back/ppermute | solution.py:54
  473.5 14.0 %collective-permute-start.70 = (bf16[1024,256]{1,0:T(8,128)(2,1)S(1)}, bf16[1024,256]{1,0:T(8,128)(2,1)S(1)}, u32[]{:S(2)}, u32[]{:S(2)}) collective-permute-start(bf16[1024,256]{1,0:T(8,128)(2,1)S(1)} %copy-done.58), channel_id=1, source_target_pairs={{0,16},{8,24},{16,0},{24,8},{1,17},{9,25},{17,1},{25,9},{2,18},{10... | collective-permute-start | bytes 1572872 | tf_op jit(solution)/shard_map/attention_back/ppermute | solution.py:54
  506.0 15.2 %collective-permute-start.73 = (bf16[128,2048]{1,0:T(8,128)(2,1)S(1)}, bf16[128,2048]{1,0:T(8,128)(2,1)S(1)}, u32[]{:S(2)}, u32[]{:S(2)}) collective-permute-start(bf16[128,2048]{1,0:T(8,128)(2,1)S(1)} %add_convert_fusion.3), channel_id=1, source_target_pairs={{0,4},{1,5},{4,6},{5,7},{6,2},{7,3},{2,0},{3,1},{8,12},{9,13},{12,... | collective-permute-start | bytes 1572872 | tf_op jit(solution)/shard_map/ppermute | solution.py:65
  521.8 14.1 %collective-permute-start.74 = (bf16[128,2048]{1,0:T(8,128)(2,1)S(1)}, bf16[128,2048]{1,0:T(8,128)(2,1)S(1)}, u32[]{:S(2)}, u32[]{:S(2)}) collective-permute-start(bf16[128,2048]{1,0:T(8,128)(2,1)S(1)} %add_convert_fusion.2), channel_id=1, source_target_pairs={{0,4},{1,5},{4,6},{5,7},{6,2},{7,3},{2,0},{3,1},{8,12},{9,13},{12,... | collective-permute-start | bytes 1572872 | tf_op jit(solution)/shard_map/d_normed/ppermute | solution.py:65
  538.4 19.6 %collective-permute-start.80 = (bf16[520,768]{1,0:T(8,128)(2,1)}, bf16[520,768]{1,0:T(8,128)(2,1)}, u32[]{:S(2)}, u32[]{:S(2)}) collective-permute-start(bf16[520,768]{1,0:T(8,128)(2,1)} %pad_maximum_fusion.4), channel_id=1, source_target_pairs={{0,16},{8,24},{16,0},{24,8},{1,17},{9,25},{17,1},{25,9},{2,18},{10... | collective-permute-start | bytes 2396168 | tf_op jit(solution)/shard_map/qkv_grad/ppermute | solution.py:54
  541.7 23.5 %collective-permute-start.79 = (bf16[520,768]{1,0:T(8,128)(2,1)}, bf16[520,768]{1,0:T(8,128)(2,1)}, u32[]{:S(2)}, u32[]{:S(2)}) collective-permute-start(bf16[520,768]{1,0:T(8,128)(2,1)} %pad_maximum_fusion.3), channel_id=1, source_target_pairs={{0,8},{8,0},{16,24},{24,16},{1,9},{9,1},{17,25},{25,17},{2,10},{10... | collective-permute-start | bytes 2396168 | tf_op jit(solution)/shard_map/qkv_grad/ppermute | solution.py:54
  543.4 12.8 %collective-permute-start.78 = (bf16[128,2048]{1,0:T(8,128)(2,1)}, bf16[128,2048]{1,0:T(8,128)(2,1)S(1)}, u32[]{:S(2)}, u32[]{:S(2)}) collective-permute-start(bf16[128,2048]{1,0:T(8,128)(2,1)} %add_convert_fusion.1), channel_id=1, source_target_pairs={{0,4},{1,5},{4,6},{5,7},{6,2},{7,3},{2,0},{3,1},{8,12},{9,13},{12,... | collective-permute-start | bytes 1572872 | tf_op jit(solution)/shard_map/d_normed/ppermute | solution.py:65
  572.0 17.5 %collective-permute-start.83 = (bf16[2,80,768]{2,1,0:T(8,128)(2,1)S(1)}, bf16[2,80,768]{2,1,0:T(8,128)(2,1)S(1)}, u32[]{:S(2)}, u32[]{:S(2)}) collective-permute-start(bf16[2,80,768]{2,1,0:T(8,128)(2,1)S(1)} %get-tuple-element.736), channel_id=1, source_target_pairs={{0,4},{1,5},{2,6},{3,7},{4,0},{5,1},{6,2},{7,3},{8,12},{9,13},{10,... | collective-permute-start | bytes 737288 | tf_op jit(solution)/shard_map/qkv_grad/ppermute | solution.py:54
  572.7 22.7 %collective-permute-start.84 = (bf16[2,80,768]{2,1,0:T(8,128)(2,1)S(1)}, bf16[2,80,768]{2,1,0:T(8,128)(2,1)S(1)}, u32[]{:S(2)}, u32[]{:S(2)}) collective-permute-start(bf16[2,80,768]{2,1,0:T(8,128)(2,1)S(1)} %get-tuple-element.737), channel_id=1, source_target_pairs={{0,6},{1,7},{2,4},{3,5},{4,2},{5,3},{6,0},{7,1},{8,14},{9,15},{10,... | collective-permute-start | bytes 737288 | tf_op jit(solution)/shard_map/qkv_grad/ppermute | solution.py:54
  (145 other events, 1260.5 us)
Sparse Core Ops, SparseCore 0:
  9.9 69.6 all-gather.3
  140.1 44.5 all-gather.5
  186.6 55.1 all-gather.7
  324.8 52.1 reduce-scatter.4
  387.4 61.9 reduce-scatter.6
  451.5 45.0 reduce-scatter.8
  549.0 27.8 reduce-scatter.10

commit v4 on v3

--- a/solution.py
+++ b/solution.py
@@ -17,7 +17,8 @@
 bf16 = jnp.bfloat16
 f32 = jnp.float32
 log2_e = 1.4426950408889634
-vmem_bytes = 48 * 1024 * 1024
+vmem_bytes = 58 * 1024 * 1024
+vmem_small = 20 * 1024 * 1024
 
 
 def matmul(left, right):
@@ -136,14 +137,14 @@
     return jnp.stack([jnp.asarray(v, jnp.int32) for v in values])
 
 
-def local_call(kernel, out_shapes, scalar, *arrays, name):
+def local_call(kernel, out_shapes, scalar, *arrays, name, vmem=None):
     return pl.pallas_call(
         kernel,
         in_specs=[pl.BlockSpec(memory_space=pltpu.SMEM)]
         + [pl.BlockSpec(memory_space=pltpu.VMEM)] * len(arrays),
         out_specs=[pl.BlockSpec(memory_space=pltpu.VMEM)] * len(out_shapes),
         out_shape=[jax.ShapeDtypeStruct(shape, dtype) for shape, dtype in out_shapes],
-        compiler_params=pltpu.CompilerParams(vmem_limit_bytes=vmem_bytes),
+        compiler_params=pltpu.CompilerParams(vmem_limit_bytes=vmem or vmem_small),
         name=name,
     )(scalar, *arrays)
 
@@ -237,97 +238,100 @@
     return local_call(kernel, shapes, scalars(chip), *pieces, name=name)
 
 
-def attend_tile(t, which, ways, tok, factor, carried, final, refs):
-    heads_at, first, query = refs[:3]
-    groups = len(which)
-    keys = refs[3 : 3 + groups]
-    values = refs[3 + groups : 3 + 2 * groups]
-    refs = refs[3 + 2 * groups :]
-    seen = (t + 1) * tile
-    row = t * tile + lax.broadcasted_iota(jnp.int32, (tile, 1), 0)
-    column = lax.broadcasted_iota(jnp.int32, (1, seen), 1)
-    row = (row // tok * ways + heads_at[0]) * tok + row % tok
-    start = jnp.transpose(jnp.broadcast_to(first[...], (DH, tile)))[:, :1]
-    if carried:
-        acc = refs[0][...]
-        high = jnp.transpose(jnp.broadcast_to(refs[1][0, 0:1, :], (DH, tile)))[:, :1]
-        total = jnp.transpose(jnp.broadcast_to(refs[1][0, 1:2, :], (DH, tile)))[:, :1]
-        refs = refs[2:]
-    else:
-        high = jnp.full((tile, 1), masked_fill, f32)
-        total = jnp.zeros((tile, 1), f32)
-        acc = jnp.zeros((tile, DH), f32)
-    for k, m in enumerate(which):
-        scores = times_transposed(query[...], keys[k][0, :seen, :]) * factor
-        pos = (column // tok * ways + heads_at[m]) * tok + column % tok
-        keep = pos[:, t * tile :] <= row
-        last = jnp.where(keep & (pos[:, t * tile :] >= start), scores[:, t * tile :], masked_fill)
-        if t > 0:
-            rest = jnp.where(pos[:, : t * tile] >= start, scores[:, : t * tile], masked_fill)
-            scores = jnp.concatenate([rest, last], axis=1)
-        else:
-            scores = last
-        new_high = jnp.maximum(high, jnp.max(scores, axis=-1, keepdims=True))
-        weights = jnp.exp2(scores - new_high)
-        shrink = jnp.exp2(high - new_high)
-        total = total * shrink + jnp.sum(weights, axis=-1, keepdims=True)
-        acc = acc * shrink + matmul(weights.astype(bf16), values[k][0, :seen, :])
-        high = new_high
-
-    def as_row(column):
-        return jnp.transpose(jnp.broadcast_to(column, (tile, DH)))[0:1, :]
-
-    if final:
-        refs[0][...] = (acc / total).astype(bf16)
-        refs[1][0] = as_row(high + jnp.log2(total))
-    else:
-        refs[0][...] = acc
-        refs[1][0, 0:1, :] = as_row(high)
-        refs[1][0, 1:2, :] = as_row(total)
-
-
-def attend_kernel(tiles, which, ways, tok, factor, carried, final, *refs):
-    for t in range(tiles):
-        pl.when(pl.program_id(1) == t)(
-            functools.partial(attend_tile, t, which, ways, tok, factor, carried, final, refs)
-        )
+def each_tile(heads, tiles, whole, body):
+    for i in range(heads):
+        for t in range(tiles):
+            if whole:
+                body(i, t)
+            else:
+                pl.when(pl.program_id(0) == i * tiles + t)(functools.partial(body, i, t))
+
+
+def fixed_blocks(arrays):
+    return [
+        pl.BlockSpec(array.shape, lambda i, n=len(array.shape): (0,) * n) for array in arrays
+    ]
 
 
 def attend(heads_at, which, first, tok, query, keys, values, state, final):
     rows, width = query.shape
-    heads = width // DH
-    tiles = rows // tile
-    line = pl.BlockSpec((1, tile), lambda i, t: (0, t))
-    some = pl.BlockSpec((tile, DH), lambda i, t: (t, i))
-    pair = pl.BlockSpec((1, 2, tile), lambda i, t: (i, 0, t))
-    single = pl.BlockSpec((1, 1, tile), lambda i, t: (i, 0, t))
-
-    def all_rows(index):
-        return pl.BlockSpec((1, rows, DH), lambda i, t: (index, 0, i))
-
-    parts = [keys[m] for m in which] + [values[m] for m in which]
+    heads, tiles, ways = width // DH, rows // tile, heads_at.shape[0]
+    factor = log2_e * DH**-0.5
+    carried = state is not None
+    arrays = []
+    for array, _ in [keys[m] for m in which] + [values[m] for m in which]:
+        if not any(array is other for other in arrays):
+            arrays.append(array)
+
+    def find(entry):
+        return [array is entry[0] for array in arrays].index(True), entry[1]
+
+    def kernel(heads_ref, first_ref, query_ref, *refs):
+        parts = refs[: len(arrays)]
+        outs = refs[-2:]
+
+        def body(i, t):
+            lane, here = pl.ds(i * DH, DH), pl.ds(t * tile, tile)
+            seen = (t + 1) * tile
+            row = t * tile + lax.broadcasted_iota(jnp.int32, (tile, 1), 0)
+            column = lax.broadcasted_iota(jnp.int32, (1, seen), 1)
+            row = (row // tok * ways + heads_ref[0]) * tok + row % tok
+            start = jnp.transpose(jnp.broadcast_to(first_ref[:, here], (DH, tile)))[:, :1]
+            if carried:
+                stats = refs[len(arrays) + 1]
+                high = jnp.transpose(jnp.broadcast_to(stats[i, 0:1, here], (DH, tile)))[:, :1]
+                total = jnp.transpose(jnp.broadcast_to(stats[i, 1:2, here], (DH, tile)))[:, :1]
+                top = high
+            else:
+                top = jnp.full((tile, 1), masked_fill, f32)
+            scores = []
+            for m in which:
+                k, index = find(keys[m])
+                raw = times_transposed(query_ref[here, lane], parts[k][index, :seen, lane])
+                pos = (column // tok * ways + heads_ref[m]) * tok + column % tok
+                keep = (pos[:, t * tile :] <= row) & (pos[:, t * tile :] >= start)
+                last = jnp.where(keep, raw[:, t * tile :], masked_fill)
+                if t > 0:
+                    rest = jnp.where(pos[:, : t * tile] >= start, raw[:, : t * tile], masked_fill)
+                    last = jnp.concatenate([rest, last], axis=1)
+                scores.append(last)
+                top = jnp.maximum(top, jnp.max(last, axis=-1, keepdims=True))
+            if carried:
+                shrink = jnp.exp2((high - top) * factor)
+                total, acc = total * shrink, refs[len(arrays)][here, lane] * shrink
+            else:
+                total, acc = jnp.zeros((tile, 1), f32), jnp.zeros((tile, DH), f32)
+            for m, part in zip(which, scores):
+                weights = jnp.exp2((part - top) * factor)
+                total = total + jnp.sum(weights, axis=-1, keepdims=True)
+                k, index = find(values[m])
+                acc = acc + matmul(weights.astype(bf16), parts[k][index, :seen, lane])
+
+            def as_row(value):
+                return jnp.transpose(jnp.broadcast_to(value, (tile, DH)))[0:1, :]
+
+            if final:
+                outs[0][here, lane] = (acc / total).astype(bf16)
+                outs[1][i, :, here] = as_row(top * factor + jnp.log2(total))
+            else:
+                outs[0][here, lane] = acc
+                outs[1][i, 0:1, here] = as_row(top)
+                outs[1][i, 1:2, here] = as_row(total)
+
+        each_tile(heads, tiles, rows * len(which) <= 4096, body)
+
     pairs = rows * rows * len(which) * heads // 2
-    carried = state is not None
+    operands = [first, query, *arrays, *(state if carried else [])]
+    shapes = [
+        jax.ShapeDtypeStruct((rows, width), bf16 if final else f32),
+        jax.ShapeDtypeStruct((heads, 1 if final else 2, rows), f32),
+    ]
     return pl.pallas_call(
-        functools.partial(
-            attend_kernel,
-            tiles,
-            tuple(which),
-            heads_at.shape[0],
-            tok,
-            log2_e * DH**-0.5,
-            carried,
-            final,
-        ),
-        grid=(heads, tiles),
-        in_specs=[pl.BlockSpec(memory_space=pltpu.SMEM), line, some]
-        + [all_rows(index) for _, index in parts]
-        + ([some, pair] if carried else []),
-        out_specs=[some, single if final else pair],
-        out_shape=[
-            jax.ShapeDtypeStruct((rows, width), bf16 if final else f32),
-            jax.ShapeDtypeStruct((heads, 1 if final else 2, rows), f32),
-        ],
+        kernel,
+        grid=(1 if rows * len(which) <= 4096 else heads * tiles,),
+        in_specs=[pl.BlockSpec(memory_space=pltpu.SMEM)] + fixed_blocks(operands),
+        out_specs=fixed_blocks(shapes),
+        out_shape=shapes,
         compiler_params=pltpu.CompilerParams(vmem_limit_bytes=vmem_bytes),
         cost_estimate=pl.CostEstimate(
             flops=4 * pairs * DH,
@@ -335,101 +339,68 @@
             transcendentals=pairs,
         ),
         name="attend",
-    )(heads_at, first, query, *[array for array, _ in parts], *(state if carried else []))
-
-
-def attend_back_tile(t, m, ways, tok, factor, scaling, carried, refs):
-    heads_at, first, log_total, delta, query, d_out, keys, values = refs[:8]
-    dq, dk, dv = refs[-3:]
-    rows = query.shape[0]
-    ahead = pl.ds(t * tile, rows - t * tile)
-    k_tile, v_tile = keys[0], values[0]
-    q_part, d_part = query[ahead, :], d_out[ahead, :]
-    scores = times_transposed(k_tile, q_part) * factor
-    pos = t * tile + lax.broadcasted_iota(jnp.int32, (tile, 1), 0)
-    pos = (pos // tok * ways + heads_at[m]) * tok + pos % tok
-    row = t * tile + lax.broadcasted_iota(jnp.int32, (1, rows - t * tile), 1)
-    row = (row // tok * ways + heads_at[0]) * tok + row % tok
-    probs = jnp.exp2(scores - log_total[0, :, ahead])
-    start = first[:, ahead]
-    keep = (pos >= start[:, :tile]) & (pos <= row[:, :tile])
-    near = jnp.where(keep, probs[:, :tile], 0.0)
-    if rows > (t + 1) * tile:
-        far = jnp.where(pos >= start[:, tile:], probs[:, tile:], 0.0)
-        probs = jnp.concatenate([near, far], axis=1)
-    else:
-        probs = near
-    dv[...] = matmul(probs.astype(bf16), d_part).astype(bf16)
-    d_probs = times_transposed(v_tile, d_part)
-    d_scores = (probs * (d_probs - delta[0, :, ahead])).astype(bf16)
-    dk[...] = (scaling * matmul(d_scores, q_part)).astype(bf16)
-    term = scaling * cross_rows(d_scores, k_tile)
-    if t > 0:
-        dq[ahead, :] += term
-    elif carried:
-        dq[...] = refs[8][...] + term
-    else:
-        dq[...] = term
-
-
-def attend_back_kernel(tiles, m, ways, tok, factor, scaling, carried, *refs):
-    for t in range(tiles):
-        pl.when(pl.program_id(1) == t)(
-            functools.partial(attend_back_tile, t, m, ways, tok, factor, scaling, carried, refs)
-        )
+    )(heads_at, *operands)
 
 
 def attend_back(heads_at, m, first, tok, log_total, delta, query, d_out, key, value, dq_in):
     rows, width = query.shape
-    heads = width // DH
-    tiles = rows // tile
-    line = pl.BlockSpec((1, rows), lambda i, t: (0, 0))
-    stat = pl.BlockSpec((1, 1, rows), lambda i, t: (i, 0, 0))
-    tile_rows = pl.BlockSpec((tile, DH), lambda i, t: (t, i))
-    block = pl.BlockSpec((rows, DH), lambda i, t: (0, i))
-
-    def some(index):
-        return pl.BlockSpec((1, tile, DH), lambda i, t: (index, t, i))
+    heads, tiles, ways = width // DH, rows // tile, heads_at.shape[0]
+    factor, scaling = log2_e * DH**-0.5, DH**-0.5
+    carried = dq_in is not None
+    parts = [key[0]] if key[0] is value[0] else [key[0], value[0]]
+
+    def kernel(heads_ref, first_ref, log_ref, delta_ref, query_ref, out_ref, *refs):
+        keys, values = refs[0], refs[len(parts) - 1]
+        dq, dk, dv = refs[-3:]
+
+        def body(i, t):
+            lane, here = pl.ds(i * DH, DH), pl.ds(t * tile, tile)
+            ahead = pl.ds(t * tile, rows - t * tile)
+            k_tile, v_tile = keys[key[1], here, lane], values[value[1], here, lane]
+            q_part, d_part = query_ref[ahead, lane], out_ref[ahead, lane]
+            scores = times_transposed(k_tile, q_part) * factor
+            pos = t * tile + lax.broadcasted_iota(jnp.int32, (tile, 1), 0)
+            pos = (pos // tok * ways + heads_ref[m]) * tok + pos % tok
+            row = t * tile + lax.broadcasted_iota(jnp.int32, (1, tile), 1)
+            row = (row // tok * ways + heads_ref[0]) * tok + row % tok
+            probs = jnp.exp2(scores - log_ref[i, :, ahead])
+            start = first_ref[:, ahead]
+            keep = (pos >= start[:, :tile]) & (pos <= row)
+            near = jnp.where(keep, probs[:, :tile], 0.0)
+            if rows > (t + 1) * tile:
+                far = jnp.where(pos >= start[:, tile:], probs[:, tile:], 0.0)
+                probs = jnp.concatenate([near, far], axis=1)
+            else:
+                probs = near
+            dv[here, lane] = matmul(probs.astype(bf16), d_part).astype(bf16)
+            d_probs = times_transposed(v_tile, d_part)
+            d_scores = (probs * (d_probs - delta_ref[i, :, ahead])).astype(bf16)
+            dk[here, lane] = (scaling * matmul(d_scores, q_part)).astype(bf16)
+            term = scaling * cross_rows(d_scores, k_tile)
+            if t > 0:
+                dq[ahead, lane] += term
+            elif carried:
+                dq[:, lane] = refs[len(parts)][:, lane] + term
+            else:
+                dq[:, lane] = term
+
+        each_tile(heads, tiles, rows <= 1024, body)
 
     pairs = rows * rows * heads // 2
-    carried = dq_in is not None
+    operands = [first, log_total, delta, query, d_out, *parts] + ([dq_in] if carried else [])
+    shapes = [jax.ShapeDtypeStruct((rows, width), kind) for kind in (f32, bf16, bf16)]
     return pl.pallas_call(
-        functools.partial(
-            attend_back_kernel,
-            tiles,
-            m,
-            heads_at.shape[0],
-            tok,
-            log2_e * DH**-0.5,
-            DH**-0.5,
-            carried,
-        ),
-        grid=(heads, tiles),
-        in_specs=[pl.BlockSpec(memory_space=pltpu.SMEM), line, stat, stat, block, block]
-        + [some(key[1]), some(value[1])]
-        + [block] * (1 if carried else 0),
-        out_specs=[block, tile_rows, tile_rows],
-        out_shape=[
-            jax.ShapeDtypeStruct((rows, width), f32),
-            jax.ShapeDtypeStruct((rows, width), bf16),
-            jax.ShapeDtypeStruct((rows, width), bf16),
-        ],
+        kernel,
+        grid=(1 if rows <= 1024 else heads * tiles,),
+        in_specs=[pl.BlockSpec(memory_space=pltpu.SMEM)] + fixed_blocks(operands),
+        out_specs=fixed_blocks(shapes),
+        out_shape=shapes,
         compiler_params=pltpu.CompilerParams(vmem_limit_bytes=vmem_bytes),
         cost_estimate=pl.CostEstimate(
             flops=10 * pairs * DH, bytes_accessed=20 * rows * width, transcendentals=pairs
         ),
         name="attend_back",
-    )(
-        heads_at,
-        first,
-        log_total,
-        delta,
-        query,
-        d_out,
-        key[0],
-        value[0],
-        *([dq_in] if carried else []),
-    )
+    )(heads_at, *operands)
 
 
 def normalized(values):
@@ -504,61 +475,32 @@
     )(at, *arrays)
 
 
-def terms_out(at, array, weights, tokens, transposed):
+def terms_out(at, array, weights, transposed):
     steps = at.shape[0] // 2
     rows, width = array.shape
     tok = rows // (2 * steps)
     out_width = weights.shape[0] if transposed else weights.shape[1]
 
-    def body(at_ref, *refs):
-        parts, whole = refs[:2], refs[2]
-        outs = refs[-3:] if tokens else refs[-2:]
-        step = pl.program_id(0)
-        sums = []
-        left = jnp.concatenate([parts[0][...], parts[1][...]], axis=0)
+    def body(at_ref, mine, other, whole, *outs):
+        left = jnp.concatenate([mine[...], other[...]], axis=0)
         both = times_transposed(left, whole[...]) if transposed else matmul(left, whole[...])
         for e in (0, 1):
-            term = both[e * tok : (e + 1) * tok]
-            outs[e][0] = term.astype(bf16)
-            if tokens:
-                hat = normalized(refs[3 + e][0].astype(f32))
-                sums.append(
-                    jnp.concatenate(
-                        [
-                            jnp.sum(term * hat, axis=0, keepdims=True),
-                            jnp.sum(term, axis=0, keepdims=True),
-                        ],
-                        axis=0,
-                    )
-                )
-        if tokens:
-
-            @pl.when(step == 0)
-            def _():
-                outs[2][...] = sums[0] + sums[1]
-
-            @pl.when(step > 0)
-            def _():
-                outs[2][...] += sums[0] + sums[1]
+            outs[e][0] = both[e * tok : (e + 1) * tok].astype(bf16)
 
     def block(e):
         return pl.BlockSpec((tok, width), lambda i, at_ref: (at_ref[2 * i + e], 0))
 
     stacked = pl.BlockSpec((1, tok, out_width), lambda i, at_ref: (i, 0, 0))
     shape = jax.ShapeDtypeStruct((steps, tok, out_width), bf16)
-    extra = list(tokens) if tokens else []
     return pl.pallas_call(
         body,
         grid_spec=pltpu.PrefetchScalarGridSpec(
             num_scalar_prefetch=1,
             grid=(steps,),
-            in_specs=[block(0), block(1), pl.BlockSpec(weights.shape, lambda i, at_ref: (0, 0))]
-            + [stacked] * len(extra),
-            out_specs=[stacked, stacked]
-            + ([pl.BlockSpec((2, out_width), lambda i, at_ref: (0, 0))] if tokens else []),
+            in_specs=[block(0), block(1), pl.BlockSpec(weights.shape, lambda i, at_ref: (0, 0))],
+            out_specs=[stacked, stacked],
         ),
-        out_shape=[shape, shape]
-        + ([jax.ShapeDtypeStruct((2, out_width), f32)] if tokens else []),
+        out_shape=[shape, shape],
         compiler_params=pltpu.CompilerParams(vmem_limit_bytes=vmem_bytes),
         cost_estimate=pl.CostEstimate(
             flops=2 * rows * width * out_width,
@@ -566,28 +508,70 @@
             transcendentals=0,
         ),
         name="terms_out",
-    )(at, array, array, weights, *extra)
-
-
-def mix_back(at, mine, other, weights, mixed):
-    chips = len(mine)
-    tok = mine[0].shape[0]
+    )(at, array, array, weights)
+
+
+def norm_sums(own, other, mine, others):
+    chips, tok, width = own.shape
+
+    def body(*refs):
+        terms, pieces, out = refs[:2], refs[2 : 2 + 2 * chips], refs[-1]
+        step = pl.program_id(0)
+
+        @pl.when(step == 0)
+        def _():
+            out[...] = jnp.zeros_like(out)
+
+        for k in range(chips):
+
+            @pl.when(step == k)
+            def _():
+                for e in (0, 1):
+                    term = terms[e][0].astype(f32)
+                    hat = normalized(pieces[e * chips + k][...].astype(f32))
+                    out[0:1, :] += jnp.sum(term * hat, axis=0, keepdims=True)
+                    out[1:2, :] += jnp.sum(term, axis=0, keepdims=True)
+
+    stacked = pl.BlockSpec((1, tok, width), lambda i: (i, 0, 0))
+    return pl.pallas_call(
+        body,
+        grid=(chips,),
+        in_specs=[stacked, stacked] + fixed_blocks([*mine, *others]),
+        out_specs=pl.BlockSpec((2, width), lambda i: (0, 0)),
+        out_shape=jax.ShapeDtypeStruct((2, width), f32),
+        compiler_params=pltpu.CompilerParams(vmem_limit_bytes=vmem_bytes),
+        name="norm_sums",
+    )(own, other, *mine, *others)
+
+
+def mix_back(at, parts, weights, mixed, earlier):
+    count = len(parts)
+    tok = parts[0].shape[0]
     rows, own = mixed.shape
     heads = own // DH
 
     def kernel(at_ref, *refs):
-        parts = [refs[e * chips + k] for k in range(chips) for e in (0, 1)]
-        whole, mixed_ref, d_mixed, delta = refs[2 * chips :]
-        for k, part in enumerate(parts):
+        whole, outs = refs[count], refs[count + 1 :]
+        d_mixed = outs[2] if earlier is not None else outs[0]
+        if earlier is not None:
+            mixed_ref, before, _, delta = outs
+            d_mixed[...] = before[...]
+        for k in range(count):
             here = pl.ds(pl.multiple_of(at_ref[k] * tok, tok), tok)
-            d_mixed[here, :] = times_transposed(part[...], whole[...]).astype(bf16)
-        products = d_mixed[...].astype(f32) * mixed_ref[...].astype(f32)
-        for k in range(heads):
-            turned = jnp.transpose(products[:, k * DH : (k + 1) * DH])
-            delta[k] = jnp.sum(turned, axis=0, keepdims=True)
-
-    shapes = [((rows, own), bf16), ((heads, 1, rows), f32)]
-    return local_call(kernel, shapes, at, *mine, *other, weights, mixed, name="mix_back")
+            d_mixed[here, :] = times_transposed(refs[k][...], whole[...]).astype(bf16)
+        if earlier is not None:
+            products = d_mixed[...].astype(f32) * mixed_ref[...].astype(f32)
+            for k in range(heads):
+                turned = jnp.transpose(products[:, k * DH : (k + 1) * DH])
+                delta[k] = jnp.sum(turned, axis=0, keepdims=True)
+
+    shapes = [((rows, own), bf16)]
+    if earlier is None:
+        return local_call(kernel, shapes, at, *parts, weights, name="mix_back", vmem=vmem_bytes)[0]
+    shapes.append(((heads, 1, rows), f32))
+    return local_call(
+        kernel, shapes, at, *parts, weights, mixed, earlier, name="mix_back", vmem=vmem_bytes
+    )
 
 
 def mix_grad(at, mine, other, mixed, each, team):
@@ -611,7 +595,7 @@
                 out[j, i] = total[low : low + w_rows]
 
     shape = ((team, each, w_rows, width), bf16)
-    return local_call(kernel, [shape], at, *mine, *other, mixed, name="mix_grad")[0]
+    return local_call(kernel, [shape], at, *mine, *other, mixed, name="mix_grad", vmem=vmem_bytes)[0]
 
 
 def reorder(array, at):
@@ -721,8 +705,6 @@
         )
         pieces = pair_up(mine, swap(other, "blk", 1), chip, core)
 
-    with jax.named_scope("down_weights"):
-        down_w = lax.all_gather(down_proj, "head", axis=0, tiled=True)
     places = (heads_at, chips_at, blocks_at, weights_at)
     pieces, small, up_proj, tok_mine, tok_other, places = hold(
         pieces, small, up_proj, tok_mine, tok_other, places
@@ -801,8 +783,8 @@
         q_bias, v_bias = own_head_part(vector(2)), own_head_part(vector(3))
         qkv_bias = jnp.concatenate([q_bias, jnp.zeros_like(q_bias), v_bias], axis=1)
     first_vectors = (gain_first, shift_first, qkv_bias)
-    fused_parts, tok_mine, cotangent, up_other, out_proj, first_vectors, down_w = hold(
-        fused_parts, tok_mine, cotangent, up_other, out_proj, first_vectors, down_w
+    fused_parts, tok_mine, cotangent, up_other, out_proj, first_vectors = hold(
+        fused_parts, tok_mine, cotangent, up_other, out_proj, first_vectors
     )
     gain_first, shift_first, qkv_bias = first_vectors
 
@@ -821,10 +803,7 @@
     with jax.named_scope("up_weights"):
         up_pieces = pair_up(up_mine, swap(up_other, "blk", 1), chip, core)
     with jax.named_scope("out_weights"):
-        if square:
-            out_parts = [out_proj, swap(out_proj, "head", 1), swap(out_proj, "head", 2)]
-        else:
-            out_parts = gather_head(out_proj)
+        out_parts = [out_proj] + [swap(out_proj, "head", m) for m in range(1, n_head)]
     query, kv, up_pieces, normed, out_parts, cotangent, qkv_w, table = hold(
         query, kv, up_pieces, normed, out_parts, cotangent, qkv_w, table
     )
@@ -859,30 +838,31 @@
             low = swap(kv_parts[1][:1], "head", 1)
             high = swap(kv_parts[0][1:], "head", 2)
     with jax.named_scope("out_weights"):
-        if square:
-            half = w_rows // 2
-            out_low = swap(out_parts[2][:half], "head", 1)
-            out_high = swap(out_parts[1][half:], "head", 2)
-            out_parts = out_parts + [jnp.concatenate([out_low, out_high])]
+        out_w = place(out_parts, heads_at).reshape(team, each, w_rows, D)
+        out_w = exchange(out_w, "blk", place_in, team)
+        out_w = out_w.transpose(1, 0, 2, 3).reshape(own_heads, D)
     if square:
-        low, high, out_parts, state, up_part = hold(low, high, out_parts, state, up_part)
+        low, high, out_w, state, up_part, down_proj = hold(
+            low, high, out_w, state, up_part, down_proj
+        )
         keys.append((low, 0))
         values.append((high, 0))
     else:
-        out_parts, state, up_part = hold(out_parts, state, up_part)
+        out_w, state, up_part, down_proj = hold(out_w, state, up_part, down_proj)
     with jax.named_scope("up_weights"):
         up_w = lax.all_gather(up_part, "head", axis=0, tiled=True)
 
-    with jax.named_scope("out_weights"):
-        out_w = place(out_parts, heads_at).reshape(team, each, w_rows, D)
-        out_w = exchange(out_w, "blk", place_in, team)
-        out_w = out_w.transpose(1, 0, 2, 3).reshape(own_heads, D)
     with jax.named_scope("attention"):
         left = list(range(1, n_head))
         mixed, log_total = attend(
             heads_at, left, first_pos, tok, query, keys, values, state, True
         )
-    mixed, out_w, table = hold(mixed, out_w, table)
+    with jax.named_scope("down_weights"):
+        if square:
+            downs = [down_proj, swap(down_proj, "head", 1), swap(down_proj, "head", 2)]
+        else:
+            downs = gather_head(down_proj)
+    mixed, out_w, table, downs = hold(mixed, out_w, table, downs)
 
     def cross(term):
         return (term[0], swap(term[1], "blk", 1))
@@ -895,31 +875,50 @@
         return total if moving is None else total + moving.astype(f32)
 
     def met(own, other):
-        crossing = swap(other, "blk", 1)
-        return [(own[step], crossing[step]) for step in range(chips)]
+        return (own, swap(other, "blk", 1))
+
+    def entry(pair, step):
+        return (pair[0][step], pair[1][step])
 
     with jax.named_scope("branch"):
-        ready = met(*terms_out(blocks_at, mixed, out_w, None, False))
+        ready = met(*terms_out(blocks_at, mixed, out_w, False))
         ready, dy_all = hold(ready, dy_all)
         moving = None
         for step in range(1, chips):
-            moving = onward(ready[step], moving)
+            moving = onward(entry(ready, step), moving)
             with jax.named_scope("vectors"):
                 if step == 1:
                     o_bias, gain_second, shift_second, d_bias = [vector(k) for k in range(4, 8)]
                     u_bias = table[:, :, 8 * w_rows : 8 * w_rows + ff_rows]
                     u_bias = lax.dynamic_index_in_dim(u_bias, blk, 1, keepdims=False)
                     vectors = (o_bias, gain_second, shift_second, d_bias, u_bias.reshape(1, -1))
+            with jax.named_scope("down_weights"):
+                if square and step == 2:
+                    half = ff_rows // 2
+                    low = swap(downs[2][:half], "head", 1)
+                    high = swap(downs[1][half:], "head", 2)
+                if not square and step == 1:
+                    down_w = place(downs, heads_at).reshape(n_head * ff_rows, D)
             if step == 1:
                 moving, ready, vectors = hold(moving, ready, vectors)
                 o_bias, gain_second, shift_second, d_bias, u_bias = vectors
+            elif step == 2:
+                moving, ready, downs = hold(moving, ready, downs)
+            elif square and step == 3:
+                moving, ready, low, high = hold(moving, ready, low, high)
             else:
                 moving, ready = hold(moving, ready)
         own = tokens.astype(f32)
-        hidden = own + (sum_of(ready[0], moving) + o_bias)
+        hidden = own + (sum_of(entry(ready, 0), moving) + o_bias)
         hat_second, inv_second = norm_parts(hidden)
         second_own = (hat_second * gain_second + shift_second).astype(bf16)
-    hidden, second_own, inv_second, up_w = hold(hidden, second_own, inv_second, up_w)
+    hidden, second_own, inv_second = hold(hidden, second_own, inv_second)
+
+    with jax.named_scope("down_weights"):
+        if square:
+            blocks = [part.reshape(2, half, D)[k] for part in downs for k in (0, 1)]
+            at = (2 * heads_at[:, None] + two_cores[None, :]).reshape(-1)
+            down_w = place(blocks + [low, high], at).reshape(n_head * ff_rows, D)
 
     with jax.named_scope("mlp"):
         second_all = blank((rows, D), bf16)
@@ -973,24 +972,22 @@
                     chips - 1, second_all, active_all, d_upper_all
                 )
             ready = cross(terms[(step + 1) % chips])
-            if step == 1:
+            if step == 2:
                 with jax.named_scope("up_grad"):
                     up_term = cross_rows(second_all, d_upper_all).astype(bf16)
                 moving, ready, terms, active_all, d_upper_all, up_term = hold(
                     moving, ready, terms, active_all, d_upper_all, up_term
                 )
-            elif step == 2:
+            elif step == 3:
                 with jax.named_scope("down_grad"):
                     down_term = cross_rows(active_all, dy_all).astype(bf16)
                 moving, ready, terms, down_term, active_all = hold(
                     moving, ready, terms, down_term, active_all
                 )
-            elif step == 3:
-                with jax.named_scope("output"):
-                    out_term = matmul(active_all, down_w).astype(bf16)
-                moving, ready, terms, out_term = hold(moving, ready, terms, out_term)
             else:
-                moving, ready, terms = hold(moving, ready, terms)
+                moving, ready, terms, second_all, active_all, d_upper_all = hold(
+                    moving, ready, terms, second_all, active_all, d_upper_all
+                )
         d_second = sum_of(ready, moving)
         upstream = cotangent.astype(f32)
         d_hidden = upstream + norm_back(d_second, hat_second, inv_second, gain_second)
@@ -1007,19 +1004,32 @@
     mine, other = [d_branch_own], []
 
     with jax.named_scope("d_branch_gather"):
+        half = tok // 2
+        halves = [[d_branch_own[:half]], [d_branch_own[half:]]]
+        with jax.named_scope("output"):
+            out_term = matmul(active_all, down_w).astype(bf16)
         for step in range(chips - 1):
-            mine.append(next_chip(mine[step]))
-            if step == 1:
-                mine, up_sum, down_term = hold(mine, up_sum, down_term)
-                with jax.named_scope("down_grad"):
-                    down_grad = sum_heads(down_term)
-            else:
-                (mine,) = hold(mine)
+            for chain in halves:
+                if step > 0:
+                    (held,) = hold(chain[step])
+                    chain[step] = held
+                chain.append(next_chip(chain[step]))
+            if step > 0:
+                mine.append(jnp.concatenate([chain[step] for chain in halves], axis=0))
+        mine.append(jnp.concatenate([chain[-1] for chain in halves], axis=0))
+        mine, up_sum, out_term = hold(mine, up_sum, out_term)
+        with jax.named_scope("output"):
+            out_sum = lax.psum_scatter(out_term, "blk", scatter_dimension=0, tiled=True)
         other = [swap(piece, "blk", 1) for piece in mine]
-        d_mixed, delta = mix_back(blocks_at, mine, other, out_w, mixed)
-    d_mixed, delta, mine, other, up_sum, out_term = hold(
-        d_mixed, delta, mine, other, up_sum, out_term
-    )
+        by_core = blocks_at.reshape(chips, 2)
+        d_mixed = mix_back(by_core[:, 0], mine, out_w, mixed, None)
+        d_mixed, delta = mix_back(by_core[:, 1], other, out_w, mixed, d_mixed)
+    with jax.named_scope("up_grad"):
+        up_sum = up_sum.reshape(chips, 2, w_rows, n_head * ff_rows)
+        up_mine = lax.dynamic_index_in_dim(up_sum, core, 1, keepdims=False)
+        up_other = lax.dynamic_index_in_dim(up_sum, 1 - core, 1, keepdims=False)
+        up_pieces = pair_up(up_mine, swap(up_other, "blk", 1), chip, core)
+    d_mixed, delta, mine, other = hold(d_mixed, delta, mine, other)
 
     dq = None
 
@@ -1037,41 +1047,27 @@
             if square and m == 0:
                 one = [d_keys[1], (d_values[1].astype(f32) + high.astype(f32)).astype(bf16)]
                 two = [(d_keys[2].astype(f32) + low.astype(f32)).astype(bf16), d_values[2]]
-                one, two, dq = hold(one, two, dq)
+                one, two, dq, up_pieces = hold(one, two, dq, up_pieces)
                 one[0], two[0] = swap(one[0], "head", 1), swap(two[0], "head", 2)
             dq, d_keys[m], d_values[m] = kv_grad(m)
-        if m == n_head - 1:
-            with jax.named_scope("up_grad"):
-                up_sum = up_sum.reshape(chips, 2, w_rows, n_head * ff_rows)
-                up_mine = lax.dynamic_index_in_dim(up_sum, core, 1, keepdims=False)
-                up_other = lax.dynamic_index_in_dim(up_sum, 1 - core, 1, keepdims=False)
-                up_pieces = pair_up(up_mine, swap(up_other, "blk", 1), chip, core)
-            dq, d_keys, d_values, d_mixed, up_pieces = hold(
-                dq, d_keys, d_values, d_mixed, up_pieces
-            )
-        elif m == n_head - 2:
-            with jax.named_scope("up_grad"):
-                up_pieces = swap_chips(up_pieces)
-            dq, d_keys, d_values, d_mixed = hold(dq, d_keys, d_values, d_mixed)
-        elif square and m == 1:
-            low, high, dq, d_keys, d_values, d_mixed, up_pieces, down_grad, out_term = hold(
-                low, high, dq, d_keys, d_values, d_mixed, up_pieces, down_grad, out_term
+        if square and m == 1:
+            low, high, dq, d_keys, d_values, d_mixed = hold(
+                low, high, dq, d_keys, d_values, d_mixed
             )
         elif m > 0:
             dq, d_keys, d_values, d_mixed = hold(dq, d_keys, d_values, d_mixed)
+    with jax.named_scope("up_grad"):
+        up_pieces = swap_chips(up_pieces)
     if square:
-        one, two, dq, mine, other, mixed, tok_mine, tok_other = hold(
-            one, two, dq, mine, other, mixed, tok_mine, tok_other
+        one, two, dq, mine, other, mixed, out_sum, down_term = hold(
+            one, two, dq, mine, other, mixed, out_sum, down_term
         )
         with jax.named_scope("attention_back"):
             one[1], two[1] = swap(one[1], "head", 1), swap(two[1], "head", 2)
-    with jax.named_scope("output"):
-        out_sum = lax.psum_scatter(out_term, "blk", scatter_dimension=0, tiled=True)
     with jax.named_scope("out_grad"):
         mix_term = mix_grad(blocks_at, mine, other, mixed, each, team)
-        mix_term = exchange(mix_term, "blk", place_in, team)
-    with jax.named_scope("d_normed"):
-        tok_stacks = (jnp.stack(tok_mine), jnp.stack(tok_other))
+    with jax.named_scope("down_grad"):
+        down_grad = sum_heads(down_term)
     with jax.named_scope("attention_back"):
         if square:
             d_keys, d_values = [
@@ -1085,102 +1081,107 @@
             ]
         d_qkv = jnp.concatenate([dq.astype(bf16), d_keys, d_values], axis=1)
     kept = (d_branch_own, d_second, hat_second, d_upper_all, cotangent, dq, d_values)
-    d_qkv, up_pieces, mix_term, tok_stacks = hold(d_qkv, up_pieces, mix_term, tok_stacks)
-
-    slab = n_blk * w_rows
+    d_qkv, up_pieces, mix_term = hold(d_qkv, up_pieces, mix_term)
+
+    slab, wide = n_blk * w_rows, 3 * own_heads
     with jax.named_scope("d_normed"):
-        own_terms, other_terms, first_sums = terms_out(
-            blocks_at, d_qkv, qkv_w, tok_stacks, True
-        )
+        own_terms, other_terms = terms_out(blocks_at, d_qkv, qkv_w, True)
         ready = met(own_terms, other_terms)
-    ready, first_sums, normed, d_qkv, mix_term, out_sum = hold(
-        ready, first_sums, normed, d_qkv, mix_term, out_sum
-    )
-    moving = onward(ready[1], None)
+    with jax.named_scope("qkv_grad"):
+        qkv_term = cross_rows(normed, d_qkv).astype(bf16).reshape(n_head, slab, wide)
+    ready, qkv_term, mix_term, up_pieces, kept = hold(ready, qkv_term, mix_term, up_pieces, kept)
+    d_branch_own, d_second, hat_second, d_upper_all, cotangent, dq, d_values = kept
+    moving = None
+    for step in range(1, chips):
+        with jax.named_scope("d_normed"):
+            moving = onward(entry(ready, step), moving)
+        if step == 1:
+            with jax.named_scope("qkv_grad"):
+                if square:
+                    half = slab // 2
+                    far = pick(qkv_term, head ^ 3)
+                    low, high = swap(far[:half], "head", 1), swap(far[half:], "head", 2)
+                else:
+                    low = high = qkv_term
+            with jax.named_scope("vector_grads"):
+                full = [
+                    jnp.sum(d_branch_own.astype(f32), axis=0),
+                    jnp.sum(d_second * hat_second, axis=0),
+                    jnp.sum(d_second, axis=0),
+                    jnp.sum(cotangent.astype(f32), axis=0),
+                ]
+                parts = [v.reshape(n_head, n_blk, w_rows) for v in full]
+                up_row = jnp.sum(d_upper_all.astype(f32), axis=0)
+                up_table = jnp.zeros((n_blk, n_head, ff_rows), f32)
+                up_table = put(up_table, up_row.reshape(n_head, ff_rows), blk)
+                parts.append(up_table.transpose(1, 0, 2))
+                for v in (dq.astype(bf16), d_values):
+                    bias_sum = jnp.sum(v.astype(f32), axis=0).reshape(each, 1, DH)
+                    head_table = jnp.zeros((n_head, sets, DH), f32)
+                    head_table = lax.dynamic_update_slice(
+                        head_table, bias_sum, (place_in * each, blk // team, 0)
+                    )
+                    parts.append(head_table.reshape(n_head, n_blk, w_rows))
+            moving, ready, low, high, parts, own_terms, mix_term, tok_mine, tok_other = hold(
+                moving, ready, low, high, parts, own_terms, mix_term, tok_mine, tok_other
+            )
+        elif step == 2:
+            with jax.named_scope("qkv_grad"):
+                if square:
+                    one, two = pick(qkv_term, head ^ 1), pick(qkv_term, head ^ 2)
+                    one = jnp.concatenate([one[:half], one[half:] + high])
+                    two = jnp.concatenate([two[:half] + low, two[half:]])
+                    one, two = swap(one, "head", 1), swap(two, "head", 2)
+            with jax.named_scope("vector_grads"):
+                first_sums = norm_sums(own_terms, other_terms, tok_mine, tok_other)
+            moving, ready, first_sums, down_grad, mix_term = hold(
+                moving, ready, first_sums, down_grad, mix_term
+            )
+        elif step == 3:
+            with jax.named_scope("out_grad"):
+                mix_term = exchange(mix_term, "blk", place_in, team)
+            with jax.named_scope("vector_grads"):
+                parts = [v.reshape(n_head, n_blk, w_rows) for v in first_sums] + parts
+                parts = jnp.concatenate(parts, axis=2)
+                deep = -(-parts.shape[2] // wide)
+                parts = jnp.pad(parts, ((0, 0), (0, 0), (0, deep * wide - parts.shape[2])))
+                parts = parts.reshape(n_head, n_blk * deep, wide)
+            moving, ready, parts, mix_term = hold(moving, ready, parts, mix_term)
+        else:
+            moving, ready = hold(moving, ready)
     with jax.named_scope("out_grad"):
         out_grad = sum_heads(mix_term.reshape(n_head * w_rows, D))
+    with jax.named_scope("vector_grads"):
+        sums = scatter_head(lambda m: pick(parts, head ^ m))
+        sums = sums.astype(bf16)
     with jax.named_scope("qkv_grad"):
-        qkv_term = cross_rows(normed, d_qkv).astype(bf16).reshape(n_head, slab, 3 * own_heads)
-    ready, qkv_term, moving, kept, first_sums = hold(ready, qkv_term, moving, kept, first_sums)
-    d_branch_own, d_second, hat_second, d_upper_all, cotangent, dq, d_values = kept
-    with jax.named_scope("vector_grads"):
-        full = [
-            first_sums[0],
-            first_sums[1],
-            jnp.sum(d_branch_own.astype(f32), axis=0),
-            jnp.sum(d_second * hat_second, axis=0),
-            jnp.sum(d_second, axis=0),
-            jnp.sum(cotangent.astype(f32), axis=0),
-        ]
-        parts = [v.reshape(n_head, n_blk, w_rows) for v in full]
-        up_row = jnp.sum(d_upper_all.astype(f32), axis=0)
-        up_table = jnp.zeros((n_blk, n_head, ff_rows), f32)
-        up_table = put(up_table, up_row.reshape(n_head, ff_rows), blk)
-        parts.append(up_table.transpose(1, 0, 2))
-        for v in (dq.astype(bf16), d_values):
-            bias_sum = jnp.sum(v.astype(f32), axis=0).reshape(each, 1, DH)
-            head_table = jnp.zeros((n_head, sets, DH), f32)
-            head_table = lax.dynamic_update_slice(
-                head_table, bias_sum, (place_in * each, blk // team, 0)
-            )
-            parts.append(head_table.reshape(n_head, n_blk, w_rows))
-        parts = jnp.concatenate(parts, axis=2)
-        wide = 3 * own_heads
-        deep = -(-parts.shape[2] // wide)
-        parts = jnp.pad(parts, ((0, 0), (0, 0), (0, deep * wide - parts.shape[2])))
-        parts = parts.reshape(n_head, n_blk * deep, wide).astype(bf16)
-    for step in range(2, chips):
-        with jax.named_scope("d_normed"):
-            moving = onward(ready[step], moving)
-        if step == 2 and square:
-            with jax.named_scope("qkv_grad"):
-                half = slab // 2
-                far = pick(qkv_term, head ^ 3)
-                low = swap(far[:half], "head", 1)
-                high = swap(far[half:], "head", 2)
-                one, two = pick(qkv_term, head ^ 1), pick(qkv_term, head ^ 2)
-            with jax.named_scope("vector_grads"):
-                across = swap(pick(parts, head ^ 3), "head", 1)
-            moving, low, high, one, two, parts, across, ready = hold(
-                moving, low, high, one, two, parts, across, ready
-            )
-        elif step == 3 and square:
-            with jax.named_scope("qkv_grad"):
-                two_parts = pick(parts, head ^ 2) + across
-                one = jnp.concatenate([one[:half], one[half:] + high, pick(parts, head ^ 1)])
-                two = jnp.concatenate([two[:half] + low, two[half:], two_parts])
-                one, two = swap(one, "head", 1), swap(two, "head", 2)
-            with jax.named_scope("output"):
-                output = (hidden + (out_sum.astype(f32) + d_bias)).astype(bf16)
-            with jax.named_scope("up_grad"):
-                (up_grad,) = merge_columns(
-                    up_pieces, 1, n_head * ff_rows, ff_columns, chip, "merge_up"
-                )
-            with jax.named_scope("down_grad"):
-                down_grad = down_grad.astype(f32)
-            moving, one, two, output, up_grad, down_grad, ready = hold(
-                moving, one, two, output, up_grad, down_grad, ready
-            )
+        if square:
+            qkv_grad = pick(qkv_term, head).astype(f32) + one.astype(f32) + two.astype(f32)
         else:
-            moving, ready = hold(moving, ready)
-    with jax.named_scope("qkv_grad"):
-        whole = jnp.concatenate([qkv_term, parts], axis=1)
-        if square:
-            qkv_grad = pick(whole, head).astype(f32) + one.astype(f32) + two.astype(f32)
-        else:
-            qkv_grad = scatter_head(lambda m: pick(whole, head ^ m).astype(f32))
-            output = (hidden + (out_sum.astype(f32) + d_bias)).astype(bf16)
-            (up_grad,) = merge_columns(up_pieces, 1, n_head * ff_rows, ff_columns, chip, "merge_up")
-            down_grad = down_grad.astype(f32)
-        qkv_grad = qkv_grad.astype(bf16)
-        extra = qkv_grad[slab:].reshape(chips, 2, deep, wide)
+            qkv_grad = scatter_head(lambda m: pick(qkv_term, head ^ m).astype(f32))
+        qkv_grad = qkv_grad.astype(bf16).reshape(chips, 2, w_rows, wide)
+        extra = sums.reshape(chips, 2, deep, wide)
         extra = jnp.pad(extra, ((0, 0), (0, 0), (0, -deep % 16), (0, 0)))
-        qkv_grad = qkv_grad[:slab].reshape(chips, 2, w_rows, wide)
         qkv_grad = jnp.concatenate([qkv_grad, extra], axis=2)
         qkv_mine = lax.dynamic_index_in_dim(qkv_grad, core, 1, keepdims=False)
         qkv_other = lax.dynamic_index_in_dim(qkv_grad, 1 - core, 1, keepdims=False)
         pieces = pair_up(qkv_mine, swap(qkv_other, "blk", 1), chip, core)
+    pieces, up_pieces, down_grad, out_sum, moving = hold(
+        pieces, up_pieces, down_grad, out_sum, moving
+    )
+    with jax.named_scope("qkv_grad"):
         pieces = swap_chips(pieces)
+    with jax.named_scope("d_normed"):
+        d_normed = sum_of(entry(ready, 0), moving)
+        hat_first, inv_first = norm_parts(own)
+        tokens_grad = (d_hidden + norm_back(d_normed, hat_first, inv_first, gain_first)).astype(bf16)
+    with jax.named_scope("output"):
+        output = (hidden + (out_sum.astype(f32) + d_bias)).astype(bf16)
+    with jax.named_scope("up_grad"):
+        (up_grad,) = merge_columns(up_pieces, 1, n_head * ff_rows, ff_columns, chip, "merge_up")
+    with jax.named_scope("down_grad"):
+        down_grad = down_grad.astype(f32)
+    with jax.named_scope("qkv_grad"):
         *qkv_grad, sums = merge_columns(
             pieces, 3, own_heads, head_columns, chip, "merge_heads", row=w_rows
         )
@@ -1189,10 +1190,6 @@
         cuts = [sums[i * w_rows : (i + 1) * w_rows] for i in range(6)]
         up_bias_grad = sums[6 * w_rows : 6 * w_rows + ff_rows]
         rest = sums[6 * w_rows + ff_rows : 8 * w_rows + ff_rows]
-    with jax.named_scope("d_normed"):
-        d_normed = sum_of(ready[0], moving)
-        hat_first, inv_first = norm_parts(own)
-        tokens_grad = (d_hidden + norm_back(d_normed, hat_first, inv_first, gain_first)).astype(bf16)
 
     return (
         output,

time: 610 us -> 578 us (0.948)
  local copies, waits for them, and re-layouts: 71.7 us -> 34.6 us
  waiting for transfers between devices: 225 us -> 208 us
  other arithmetic: 53.3 us -> 62.3 us
  starting transfers between devices: 67.8 us -> 76.4 us
  Pallas kernels: 99.4 us -> 108 us
    unnamed x235 -> x121, local copies, waits for them, and re-layouts: 42.5 us -> 8.57 us
    ppermute x21 -> x24, waiting for transfers between devices: 125 us -> 91.9 us  [next_chip(): lax.ppermute(v, 'blk', [(2 * a + c, 2 * b + c) for a, b in moves for c in...]
    ppermute x64 -> x70, waiting for transfers between devices: 97.8 us -> 115 us  [swap(): return lax.ppermute(v, axis, [(i, i ^ mask) for i in range(size)])]
    squeeze x6 -> x0, local copies, waits for them, and re-layouts: 11.2 us -> none  [the longest x4 11.1 us: met(): return [(own[step], crossing[step]) for step in range(chips)]]
    ppermute x64 -> x70, starting transfers between devices: 46.3 us -> 55.6 us  [swap(): return lax.ppermute(v, axis, [(i, i ^ mask) for i in range(size)])]
    pallas_call x13 -> x15, Pallas kernels: 18.4 us -> 24.5 us  [local_call(): pl.pallas_call(kernel, in_specs=[pl.BlockSpec(memory_space=pltpu.SMEM)] +...]
    ppermute x21 -> x24, starting transfers between devices: 20.6 us -> 19.4 us  [next_chip(): lax.ppermute(v, 'blk', [(2 * a + c, 2 * b + c) for a, b in moves for c in...]
    pallas_call x6 -> x7, Pallas kernels: 55.5 us -> 56 us  [the longest x4 29.7 us: attend_back(): pl.pallas_call(kernel, grid=(1 if rows <= 1024 else heads * tiles,), in_s...]
  transfers between devices with their start and end apart: 92 -> 100, of which waited for: 46 -> 47; matrix products, arithmetic and copies ran while one was open for 22% -> 26% of each run, Pallas kernels for 16% -> 19%
where the time goes in v4:
time: 578 us; the launch traced here: 574 us
  waiting for transfers between devices  208 us (36%)
  Pallas kernels  108 us (19%)
  starting transfers between devices  76.4 us (13%)
  matrix products  64.1 us (11%)
  other arithmetic  62.3 us (11%)
  local copies, waits for them, and re-layouts  34.6 us (6%)
  between operations  20.9 us (4%)
    ppermute x70, waiting for transfers between devices, swap(): return lax.ppermute(v, axis, [(i, i ^ mask) for i in range(size)])  115 us
    ppermute x24, waiting for transfers between devices, next_chip(): lax.ppermute(v, 'blk', [(2 * a + c, 2 * b + c) for a, b in moves for c in...  91.9 us
    ppermute x70, starting transfers between devices, swap(): return lax.ppermute(v, axis, [(i, i ^ mask) for i in range(size)])  55.6 us
    pallas_call x4, Pallas kernels, attend_back(): pl.pallas_call(kernel, grid=(1 if rows <= 1024 else heads * tiles,), in_s...  29.7 us
    pallas_call x15, Pallas kernels, local_call(): pl.pallas_call(kernel, in_specs=[pl.BlockSpec(memory_space=pltpu.SMEM)] +...  24.5 us
    dot_general x3, matrix products, cross_rows(): lax.dot_general(left, right, (((0,), (0,)), ((), ())), preferred_element_...  24.4 us
    dot_general x12, matrix products, times_transposed(): lax.dot_general(left, right, (((1,), (1,)), ((), ())), preferred_element_...  20.4 us
    ppermute x24, starting transfers between devices, next_chip(): lax.ppermute(v, 'blk', [(2 * a + c, 2 * b + c) for a, b in moves for c in...  19.4 us
  transfers between devices with their start and end apart: 100, of which 47 were waited for; matrix products, arithmetic and copies ran while one was open for 26% of the time, Pallas kernels for 19%

profile of v4, /device:TPU:8, one launch (start us, length us, event | category | flops | bytes accessed | tf_op | source)
XLA Modules:
  0.0 573.6 jit_solution(6702400682621227026)
XLA Ops:
  17.3 4.8 collective-permute-done.1.refs_1_.refs_3_
  23.6 3.0 collective-permute-start.4
  33.1 7.0 %collective-permute-done.4.refs_2_ = bf16[2,64,768]{2,1,0:T(8,128)(2,1)S(1)} collective-permute-done((bf16[2,64,768]{2,1,0:T(8,128)(2,1)S(1)}, bf16[2,64,768]{2,1,0:T(8,128)(2,1)S(1)}, u32[]{:S(2)}, u32[]{:S(2)}) %collective-permute-start.4) | collective-permute-done | bytes 196640 | tf_op jit(solution)/shard_map/qkv_weights/ppermute | solution.py:55
  40.2 3.5 collective-permute-done.5.refs_3_
  47.1 2.7 add_multiply_fusion.5
  50.0 2.9 collective-permute-start.17
  54.2 3.3 collective-permute-done.17
  62.4 3.3 collective-permute-start.18
  70.7 4.1 collective-permute-done.14.refs_17_
  82.9 13.4 %project_in.1 = (bf16[1024,256]{1,0:T(8,128)(2,1)}, bf16[2,1024,256]{2,1,0:T(8,128)(2,1)}, bf16[1024,2048]{1,0:T(8,128)(2,1)}, bf16[2048,768]{1,0:T(8,128)(2,1)}) custom-call(s32[13]{0:T(128)} %pad_add_fusion.1.at_ref, bf16[128,2048]{1,0:T(8,128)(2,1)} %refs_2_.2, bf16[128,2048]{1,0:T(8,128)(2,1)} %copy-done.42, ...), custom_call_target="tpu_custom_call" | custom-call | flops 3221225472 | bytes 16777216 | tf_op jit(solution)/shard_map/qkv/project_in/pallas_call | solution.py:451
  99.1 3.6 collective-permute-start.29
  106.5 6.2 %attend.2 = (f32[1024,256]{1,0:T(8,128)}, f32[2,2,1024]{2,1,0:T(2,128)}) custom-call(s32[4]{0:T(128)} %get-tuple-element.374.heads_ref.at_ref, s32[1,1024]{1,0:T(1,128)} %bitcast.252, bf16[1024,256]{1,0:T(8,128)(2,1)} %get-tuple-element.435.query_ref, bf16[2,1024,256]{2,1,0:T(8,128)(2,1)} %get-tuple-element.433.refs_0_), custom_call_target="tpu_custom_call" | custom-call | flops 536870912 | bytes 1048576 | tf_op jit(solution)/shard_map/attention/attend/pallas_call | solution.py:329
  112.7 8.2 %collective-permute-done.30.refs_2_ = bf16[2,64,1024]{2,1,0:T(8,128)(2,1)S(1)} collective-permute-done((bf16[2,64,1024]{2,1,0:T(8,128)(2,1)S(1)}, bf16[2,64,1024]{2,1,0:T(8,128)(2,1)S(1)}, u32[]{:S(2)}, u32[]{:S(2)}) %collective-permute-start.30) | collective-permute-done | bytes 262176 | tf_op jit(solution)/shard_map/up_weights/ppermute | solution.py:55
  120.9 5.0 collective-permute-done.31.refs_3_
  133.1 9.7 %collective-permute-done.32.refs_2_.refs_0_ = bf16[1,1024,256]{2,1,0:T(8,128)(2,1)S(1)} collective-permute-done((bf16[1,1024,256]{2,1,0:T(8,128)(2,1)S(1)}, bf16[1,1024,256]{2,1,0:T(8,128)(2,1)S(1)}, u32[]{:S(2)}, u32[]{:S(2)}) %collective-permute-start.32) | collective-permute-done | bytes 524320 | tf_op jit(solution)/shard_map/kv_gather/ppermute | solution.py:55
  147.0 12.7 %attend.3 = (bf16[1024,256]{1,0:T(8,128)(2,1)}, f32[2,1,1024]{2,1,0:T(1,128)}) custom-call(s32[4]{0:T(128)} %get-tuple-element.374.heads_ref.at_ref, s32[1,1024]{1,0:T(1,128)} %bitcast.253, bf16[1024,256]{1,0:T(8,128)(2,1)} %get-tuple-element.435.query_ref, bf16[2,1024,256]{2,1,0:T(8,128)(2,1)} %collective-permute-done.27.refs_0_, ...), custom_call_target="tpu_custom_call" | custom-call | flops 1610612736 | bytes 3145728 | tf_op jit(solution)/shard_map/attention/attend/pallas_call | solution.py:329
  159.6 10.8 %collective-permute-done.35 = bf16[256,2048]{1,0:T(8,128)(2,1)S(1)} collective-permute-done((bf16[256,2048]{1,0:T(8,128)(2,1)}, bf16[256,2048]{1,0:T(8,128)(2,1)S(1)}, u32[]{:S(2)}, u32[]{:S(2)}) %collective-permute-start.35) | collective-permute-done | bytes 1048608 | tf_op jit(solution)/shard_map/down_weights/ppermute | solution.py:55
  170.9 5.6 terms_out.2
  176.6 4.3 collective-permute-done.37
  180.9 2.4 fusion.48
  189.1 9.4 %collective-permute-done.38 = bf16[128,2048]{1,0:T(8,128)(2,1)} collective-permute-done((bf16[128,2048]{1,0:T(8,128)(2,1)}, bf16[128,2048]{1,0:T(8,128)(2,1)}, u32[]{:S(2)}, u32[]{:S(2)}) %collective-permute-start.38) | collective-permute-done | bytes 524320 | tf_op jit(solution)/shard_map/branch/ppermute | solution.py:66
  203.4 10.9 %collective-permute-done.39 = bf16[128,2048]{1,0:T(8,128)(2,1)S(1)} collective-permute-done((bf16[128,2048]{1,0:T(8,128)(2,1)S(1)}, bf16[128,2048]{1,0:T(8,128)(2,1)S(1)}, u32[]{:S(2)}, u32[]{:S(2)}) %collective-permute-start.39) | collective-permute-done | bytes 524320 | tf_op jit(solution)/shard_map/branch/ppermute | solution.py:66
  218.2 7.9 %collective-permute-done.41.refs_6_ = bf16[128,2048]{1,0:T(8,128)(2,1)S(1)} collective-permute-done((bf16[128,2048]{1,0:T(8,128)(2,1)S(1)}, bf16[128,2048]{1,0:T(8,128)(2,1)S(1)}, u32[]{:S(2)}, u32[]{:S(2)}) %collective-permute-start.41) | collective-permute-done | bytes 524320 | tf_op jit(solution)/shard_map/branch/down_weights/ppermute | solution.py:55
  226.0 2.4 collective-permute-done.42.refs_7_
  236.6 9.0 %collective-permute-done.43 = bf16[128,2048]{1,0:T(8,128)(2,1)S(1)} collective-permute-done((bf16[128,2048]{1,0:T(8,128)(2,1)S(1)}, bf16[128,2048]{1,0:T(8,128)(2,1)S(1)}, u32[]{:S(2)}, u32[]{:S(2)}) %collective-permute-start.43) | collective-permute-done | bytes 524320 | tf_op jit(solution)/shard_map/mlp/ppermute | solution.py:66
  247.3 4.8 fusion.49
  252.1 2.9 constant_dynamic-update-slice_fusion.9
  263.1 2.8 fusion.50
  270.5 4.2 collective-permute-done.47
  276.9 2.6 fusion.51
  287.1 2.6 fusion.52
  294.3 5.0 collective-permute-done.51
  300.4 8.4 %convolution_convert_fusion.2 = bf16[2048,1024]{1,0:T(8,128)(2,1)} fusion(bf16[1024,2048]{1,0:T(8,128)(2,1)} %constant_dynamic-update-slice_fusion.1, bf16[1024,1024]{1,0:T(8,128)(2,1)S(1)} %get-tuple-element.653), kind=kOutput, calls=%fused_computation.4 | convolution fusion | flops 4297064448 | bytes 10485760 | tf_op jit(solution)/shard_map/mlp/up_grad/dot_general | solution.py:29
  308.8 5.7 collective-permute-done.53
  317.2 9.7 %convolution_convert_fusion.1 = bf16[1024,2048]{1,0:T(8,128)(2,1)} fusion(bf16[1024,1024]{1,0:T(8,128)(2,1)} %copy-done.35, bf16[1024,2048]{1,0:T(8,128)(2,1)} %all-gather.3.cloned.1.call-done), kind=kOutput, calls=%fused_computation.3 | convolution fusion | flops 4297064448 | bytes 10485760 | tf_op jit(solution)/shard_map/mlp/down_grad/dot_general | solution.py:29
  327.0 3.5 collective-permute-done.55
  333.8 2.8 collective-permute-start.58
  336.6 7.3 %collective-permute-done.57 = bf16[64,2048]{1,0:T(8,128)(2,1)S(1)} collective-permute-done((bf16[64,2048]{1,0:T(8,128)(2,1)S(1)}, bf16[64,2048]{1,0:T(8,128)(2,1)S(1)}, u32[]{:S(2)}, u32[]{:S(2)}) %collective-permute-start.57) | collective-permute-done | bytes 262176 | tf_op jit(solution)/shard_map/d_branch_gather/ppermute | solution.py:66
  343.9 5.6 collective-permute-done.58
  349.5 6.1 %convolution_convert_fusion = bf16[1024,2048]{1,0:T(8,128)(2,1)} fusion(bf16[1024,1024]{1,0:T(8,128)(2,1)S(1)} %copy-done.36, bf16[1024,2048]{1,0:T(8,128)(2,1)S(1)} %bitcast.215), kind=kOutput, calls=%fused_computation.2 | convolution fusion | flops 4297064448 | bytes 10485760 | tf_op jit(solution)/shard_map/d_branch_gather/output/dot_general | solution.py:25
  355.6 2.8 collective-permute-start.61
  362.0 3.7 collective-permute-done.61
  365.7 2.8 collective-permute-done.62
  373.0 4.2 mix_back.2.refs_6_
  377.1 4.7 mix_back.3
  381.8 7.1 %attend_back.4 = (f32[1024,256]{1,0:T(8,128)}, bf16[1024,256]{1,0:T(8,128)(2,1)}, bf16[1024,256]{1,0:T(8,128)(2,1)}) custom-call(s32[4]{0:T(128)} %get-tuple-element.374.heads_ref.at_ref, s32[1,1024]{1,0:T(1,128)} %bitcast.254, f32[2,1,1024]{2,1,0:T(1,128)} %get-tuple-element.491.log_ref, f32[2,1,1024]{2,1,0:T(1,128)} %get-tuple-element.566.delta_ref, ...), custom_call_target="tpu_custom_call" | custom-call | flops 1342177280 | bytes 5242880 | tf_op jit(solution)/shard_map/attention_back/attend_back/pallas_call | solution.py:392
  390.3 7.4 %attend_back.5 = (f32[1024,256]{1,0:T(8,128)}, bf16[1024,256]{1,0:T(8,128)(2,1)}, bf16[1024,256]{1,0:T(8,128)(2,1)}) custom-call(s32[4]{0:T(128)} %get-tuple-element.374.heads_ref.at_ref, s32[1,1024]{1,0:T(1,128)} %bitcast.255, f32[2,1,1024]{2,1,0:T(1,128)} %get-tuple-element.491.log_ref, f32[2,1,1024]{2,1,0:T(1,128)} %get-tuple-element.566.delta_ref, ...), custom_call_target="tpu_custom_call" | custom-call | flops 1342177280 | bytes 5242880 | tf_op jit(solution)/shard_map/attention_back/attend_back/pallas_call | solution.py:392
  398.4 7.7 %attend_back.6 = (f32[1024,256]{1,0:T(8,128)}, bf16[1024,256]{1,0:T(8,128)(2,1)}, bf16[1024,256]{1,0:T(8,128)(2,1)}) custom-call(s32[4]{0:T(128)} %get-tuple-element.374.heads_ref.at_ref, s32[1,1024]{1,0:T(1,128)} %bitcast.256, f32[2,1,1024]{2,1,0:T(1,128)} %get-tuple-element.491.log_ref, f32[2,1,1024]{2,1,0:T(1,128)} %get-tuple-element.566.delta_ref, ...), custom_call_target="tpu_custom_call" | custom-call | flops 1342177280 | bytes 5242880 | tf_op jit(solution)/shard_map/attention_back/attend_back/pallas_call | solution.py:392
  410.9 7.5 %attend_back.7 = (f32[1024,256]{1,0:T(8,128)}, bf16[1024,256]{1,0:T(8,128)(2,1)}, bf16[1024,256]{1,0:T(8,128)(2,1)}) custom-call(s32[4]{0:T(128)} %get-tuple-element.374.heads_ref.at_ref, s32[1,1024]{1,0:T(1,128)} %bitcast.257, f32[2,1,1024]{2,1,0:T(1,128)} %get-tuple-element.491.log_ref, f32[2,1,1024]{2,1,0:T(1,128)} %get-tuple-element.566.delta_ref, ...), custom_call_target="tpu_custom_call" | custom-call | flops 1342177280 | bytes 5242880 | tf_op jit(solution)/shard_map/attention_back/attend_back/pallas_call | solution.py:392
  418.4 3.9 collective-permute-done.70
  431.2 5.7 mix_grad.1
  438.2 4.4 collective-permute-done.72
  447.7 2.7 collective-permute-done.76.refs_3_
  450.5 8.3 %terms_out.3 = (bf16[4,128,2048]{2,1,0:T(8,128)(2,1)}, bf16[4,128,2048]{2,1,0:T(8,128)(2,1)}) custom-call(s32[8]{0:T(128)} %add.557.at_ref, bf16[1024,768]{1,0:T(8,128)(2,1)} %pad_maximum_fusion.mine.other, bf16[1024,768]{1,0:T(8,128)(2,1)} %pad_maximum_fusion.mine.other, bf16[2048,768]{1,0:T(8,128)(2,1)} %get-tuple-element.635.whole), custom_call_target="tpu_custom_call" | custom-call | flops 3221225472 | bytes 8388608 | tf_op jit(solution)/shard_map/d_normed/terms_out/pallas_call | solution.py:495
  458.8 6.3 %convolution_convert_fusion.3 = bf16[2048,768]{1,0:T(8,128)(2,1)S(1)} fusion(bf16[1024,2048]{1,0:T(8,128)(2,1)} %get-tuple-element.638, bf16[1024,768]{1,0:T(8,128)(2,1)} %pad_maximum_fusion.mine.other), kind=kOutput, calls=%fused_computation.5 | convolution fusion | flops 3222798336 | bytes 8912896 | tf_op jit(solution)/shard_map/qkv_grad/dot_general | solution.py:29
  467.6 2.6 fusion.53
  474.2 12.6 %collective-permute-done.79 = bf16[256,768]{1,0:T(8,128)(2,1)} collective-permute-done((bf16[256,768]{1,0:T(8,128)(2,1)}, bf16[256,768]{1,0:T(8,128)(2,1)}, u32[]{:S(2)}, u32[]{:S(2)}) %collective-permute-start.79) | collective-permute-done | bytes 393248 | tf_op jit(solution)/shard_map/qkv_grad/ppermute | solution.py:55
  495.4 7.4 %norm_sums.1 = f32[2,2048]{1,0:T(2,128)} custom-call(bf16[4,128,2048]{2,1,0:T(8,128)(2,1)} %get-tuple-element.700.refs_0_, bf16[4,128,2048]{2,1,0:T(8,128)(2,1)} %get-tuple-element.637.refs_1_, bf16[128,2048]{1,0:T(8,128)(2,1)} %refs_2_.2, bf16[128,2048]{1,0:T(8,128)(2,1)} %copy-done.42, bf16[128,2048]{1,0:T(8,128)(2,1)} %collective-permute-done.16.refs_2_.refs_4_, ...), custom_call_target="tpu_custom_call" | custom-call | tf_op jit(solution)/shard_map/vector_grads/norm_sums/pallas_call | solution.py:536
  504.6 2.4 fusion.34
  509.6 12.9 %collective-permute-done.84 = bf16[128,2048]{1,0:T(8,128)(2,1)} collective-permute-done((bf16[128,2048]{1,0:T(8,128)(2,1)}, bf16[128,2048]{1,0:T(8,128)(2,1)}, u32[]{:S(2)}, u32[]{:S(2)}) %collective-permute-start.84) | collective-permute-done | bytes 524320 | tf_op jit(solution)/shard_map/d_normed/ppermute | solution.py:66
  529.6 2.8 fusion.2
  542.8 3.3 fusion.15
  550.0 6.1 %collective-permute-done.92.refs_2_ = bf16[2,80,768]{2,1,0:T(8,128)(2,1)S(1)} collective-permute-done((bf16[2,80,768]{2,1,0:T(8,128)(2,1)S(1)}, bf16[2,80,768]{2,1,0:T(8,128)(2,1)S(1)}, u32[]{:S(2)}, u32[]{:S(2)}) %collective-permute-start.92) | collective-permute-done | bytes 245792 | tf_op jit(solution)/shard_map/qkv_grad/ppermute | solution.py:55
  556.2 6.1 %collective-permute-done.93.refs_3_ = bf16[2,80,768]{2,1,0:T(8,128)(2,1)S(1)} collective-permute-done((bf16[2,80,768]{2,1,0:T(8,128)(2,1)S(1)}, bf16[2,80,768]{2,1,0:T(8,128)(2,1)S(1)}, u32[]{:S(2)}, u32[]{:S(2)}) %collective-permute-start.93) | collective-permute-done | bytes 245792 | tf_op jit(solution)/shard_map/qkv_grad/ppermute | solution.py:55
  (462 shorter events, 186.9 us)
Async XLA Ops:
  7.2 173.7 %all-gather.3.cloned.1.call-start = ((), (), s32[]{:S(2)}) async-start(), calls=%async_computation.4 | async-start | bytes 4718592 | tf_op jit(solution)/shard_map/dy_gather/all_gather | solution.py:831
  7.2 14.8 %collective-permute-start.1 = (bf16[128,2048]{1,0:T(8,128)(2,1)}, bf16[128,2048]{1,0:T(8,128)(2,1)S(1)}, u32[]{:S(2)}, u32[]{:S(2)}) collective-permute-start(bf16[128,2048]{1,0:T(8,128)(2,1)} %refs_2_.2), channel_id=1, source_target_pairs={{0,4},{1,5},{4,6},{5,7},{6,2},{7,3},{2,0},{3,1},{8,12},{9,13},{12,... | collective-permute-start | bytes 1572872 | tf_op jit(solution)/shard_map/tokens_gather/ppermute | solution.py:66
  7.3 14.8 %collective-permute-start.2 = (bf16[128,2048]{1,0:T(8,128)(2,1)}, bf16[128,2048]{1,0:T(8,128)(2,1)S(1)}, u32[]{:S(2)}, u32[]{:S(2)}) collective-permute-start(bf16[128,2048]{1,0:T(8,128)(2,1)} %refs_2_.2), channel_id=1, source_target_pairs={{0,1},{1,0},{2,3},{3,2},{4,5},{5,4},{6,7},{7,6},{8,9},{9,8},{10,11... | collective-permute-start | bytes 1572872 | tf_op jit(solution)/shard_map/tokens_gather/ppermute | solution.py:55
  23.6 16.5 %collective-permute-start.4 = (bf16[2,64,768]{2,1,0:T(8,128)(2,1)S(1)}, bf16[2,64,768]{2,1,0:T(8,128)(2,1)S(1)}, u32[]{:S(2)}, u32[]{:S(2)}) collective-permute-start(bf16[2,64,768]{2,1,0:T(8,128)(2,1)S(1)} %get-tuple-element.379), channel_id=1, source_target_pairs={{0,4},{1,5},{2,6},{3,7},{4,0},{5,1},{6,2},{7,3},{8,12},{9,13},{10,... | collective-permute-start | bytes 589832 | tf_op jit(solution)/shard_map/qkv_weights/ppermute | solution.py:55
  26.7 17.0 %collective-permute-start.5 = (bf16[2,64,768]{2,1,0:T(8,128)(2,1)S(1)}, bf16[2,64,768]{2,1,0:T(8,128)(2,1)S(1)}, u32[]{:S(2)}, u32[]{:S(2)}) collective-permute-start(bf16[2,64,768]{2,1,0:T(8,128)(2,1)S(1)} %get-tuple-element.380), channel_id=1, source_target_pairs={{0,6},{1,7},{2,4},{3,5},{4,2},{5,3},{6,0},{7,1},{8,14},{9,15},{10,... | collective-permute-start | bytes 589832 | tf_op jit(solution)/shard_map/qkv_weights/ppermute | solution.py:55
  44.3 13.2 %collective-permute-start.16 = (bf16[128,2048]{1,0:T(8,128)(2,1)S(1)}, bf16[128,2048]{1,0:T(8,128)(2,1)}, u32[]{:S(2)}, u32[]{:S(2)}) collective-permute-start(bf16[128,2048]{1,0:T(8,128)(2,1)S(1)} %collective-permute-done.1.refs_1_.refs_3_), channel_id=1, source_target_pairs={{0,4},{1,5},{4,6},{5,7},{6,2},{7,3},{2,0},{3,1},{8,12},{9,13},{12,... | collective-permute-start | bytes 1572872 | tf_op jit(solution)/shard_map/tokens_gather/ppermute | solution.py:66
  45.1 15.0 %collective-permute-start.12 = (bf16[4,64,768]{2,1,0:T(8,128)(2,1)S(1)}, bf16[4,64,768]{2,1,0:T(8,128)(2,1)}, u32[]{:S(2)}, u32[]{:S(2)}) collective-permute-start(bf16[4,64,768]{2,1,0:T(8,128)(2,1)S(1)} %get-tuple-element.413.refs_11_), channel_id=1, source_target_pairs={{0,16},{8,24},{16,0},{24,8},{1,17},{9,25},{17,1},{25,9},{2,18},{10... | collective-permute-start | bytes 1179656 | tf_op jit(solution)/shard_map/qkv_weights/ppermute | solution.py:55
  46.6 14.9 %collective-permute-start.11 = (bf16[4,64,768]{2,1,0:T(8,128)(2,1)S(1)}, bf16[4,64,768]{2,1,0:T(8,128)(2,1)}, u32[]{:S(2)}, u32[]{:S(2)}) collective-permute-start(bf16[4,64,768]{2,1,0:T(8,128)(2,1)S(1)} %get-tuple-element.414.refs_12_), channel_id=1, source_target_pairs={{0,8},{8,0},{16,24},{24,16},{1,9},{9,1},{17,25},{25,17},{2,10},{10... | collective-permute-start | bytes 1179656 | tf_op jit(solution)/shard_map/qkv_weights/ppermute | solution.py:55
  60.0 14.8 %collective-permute-start.14 = (bf16[4,64,768]{2,1,0:T(8,128)(2,1)}, bf16[4,64,768]{2,1,0:T(8,128)(2,1)}, u32[]{:S(2)}, u32[]{:S(2)}) collective-permute-start(bf16[4,64,768]{2,1,0:T(8,128)(2,1)} %collective-permute-done.12.refs_15_), channel_id=1, source_target_pairs={{0,8},{8,0},{16,24},{24,16},{1,9},{9,1},{17,25},{25,17},{2,10},{10... | collective-permute-start | bytes 1179656 | tf_op jit(solution)/shard_map/qkv_weights/ppermute | solution.py:55
  61.5 13.5 %collective-permute-start.15 = (bf16[4,64,768]{2,1,0:T(8,128)(2,1)}, bf16[4,64,768]{2,1,0:T(8,128)(2,1)}, u32[]{:S(2)}, u32[]{:S(2)}) collective-permute-start(bf16[4,64,768]{2,1,0:T(8,128)(2,1)} %collective-permute-done.11.refs_14_), channel_id=1, source_target_pairs={{0,16},{8,24},{16,0},{24,8},{1,17},{9,25},{17,1},{25,9},{2,18},{10... | collective-permute-start | bytes 1179656 | tf_op jit(solution)/shard_map/qkv_weights/ppermute | solution.py:55
  62.4 12.7 %collective-permute-start.18 = (bf16[128,2048]{1,0:T(8,128)(2,1)}, bf16[128,2048]{1,0:T(8,128)(2,1)}, u32[]{:S(2)}, u32[]{:S(2)}) collective-permute-start(bf16[128,2048]{1,0:T(8,128)(2,1)} %collective-permute-done.16.refs_2_.refs_4_), channel_id=1, source_target_pairs={{0,4},{1,5},{4,6},{5,7},{6,2},{7,3},{2,0},{3,1},{8,12},{9,13},{12,... | collective-permute-start | bytes 1572872 | tf_op jit(solution)/shard_map/tokens_gather/ppermute | solution.py:66
  76.1 20.2 %collective-permute-start.24 = (bf16[64,2048]{1,0:T(8,128)(2,1)S(1)}, bf16[64,2048]{1,0:T(8,128)(2,1)S(1)}, u32[]{:S(2)}, u32[]{:S(2)}) collective-permute-start(bf16[64,2048]{1,0:T(8,128)(2,1)S(1)} %copy-done.4), channel_id=1, source_target_pairs={{0,8},{8,0},{16,24},{24,16},{1,9},{9,1},{17,25},{25,17},{2,10},{10... | collective-permute-start | bytes 786440 | tf_op jit(solution)/shard_map/out_weights/ppermute | solution.py:55
  77.6 18.7 %collective-permute-start.25 = (bf16[64,2048]{1,0:T(8,128)(2,1)S(1)}, bf16[64,2048]{1,0:T(8,128)(2,1)S(1)}, u32[]{:S(2)}, u32[]{:S(2)}) collective-permute-start(bf16[64,2048]{1,0:T(8,128)(2,1)S(1)} %copy-done.4), channel_id=1, source_target_pairs={{0,16},{8,24},{16,0},{24,8},{1,17},{9,25},{17,1},{25,9},{2,18},{10... | collective-permute-start | bytes 786440 | tf_op jit(solution)/shard_map/out_weights/ppermute | solution.py:55
  80.4 15.9 %collective-permute-start.26 = (bf16[64,2048]{1,0:T(8,128)(2,1)S(1)}, bf16[64,2048]{1,0:T(8,128)(2,1)S(1)}, u32[]{:S(2)}, u32[]{:S(2)}) collective-permute-start(bf16[64,2048]{1,0:T(8,128)(2,1)S(1)} %copy-done.4), channel_id=1, source_target_pairs={{0,24},{8,16},{16,8},{24,0},{1,25},{9,17},{17,9},{25,1},{2,26},{10... | collective-permute-start | bytes 786440 | tf_op jit(solution)/shard_map/out_weights/ppermute | solution.py:55
  96.3 29.6 %collective-permute-start.27 = (bf16[2,1024,256]{2,1,0:T(8,128)(2,1)}, bf16[2,1024,256]{2,1,0:T(8,128)(2,1)}, u32[]{:S(2)}, u32[]{:S(2)}) collective-permute-start(bf16[2,1024,256]{2,1,0:T(8,128)(2,1)} %get-tuple-element.433.refs_0_), channel_id=1, source_target_pairs={{0,8},{8,0},{16,24},{24,16},{1,9},{9,1},{17,25},{25,17},{2,10},{10... | collective-permute-start | bytes 3145736 | tf_op jit(solution)/shard_map/kv_gather/ppermute | solution.py:55
  97.6 28.4 %collective-permute-start.28 = (bf16[2,1024,256]{2,1,0:T(8,128)(2,1)}, bf16[2,1024,256]{2,1,0:T(8,128)(2,1)}, u32[]{:S(2)}, u32[]{:S(2)}) collective-permute-start(bf16[2,1024,256]{2,1,0:T(8,128)(2,1)} %get-tuple-element.433.refs_0_), channel_id=1, source_target_pairs={{0,16},{8,24},{16,0},{24,8},{1,17},{9,25},{17,1},{25,9},{2,18},{10... | collective-permute-start | bytes 3145736 | tf_op jit(solution)/shard_map/kv_gather/ppermute | solution.py:55
  99.1 13.6 %collective-permute-start.29 = (bf16[2,64,1024]{2,1,0:T(8,128)(2,1)}, bf16[2,64,1024]{2,1,0:T(8,128)(2,1)S(1)}, u32[]{:S(2)}, u32[]{:S(2)}) collective-permute-start(bf16[2,64,1024]{2,1,0:T(8,128)(2,1)} %get-tuple-element.439), channel_id=1, source_target_pairs={{0,2},{1,3},{2,0},{3,1},{4,6},{5,7},{6,4},{7,5},{8,10},{9,11},{10,... | collective-permute-start | bytes 786440 | tf_op jit(solution)/shard_map/up_weights/ppermute | solution.py:55
  102.7 18.3 %collective-permute-start.30 = (bf16[2,64,1024]{2,1,0:T(8,128)(2,1)S(1)}, bf16[2,64,1024]{2,1,0:T(8,128)(2,1)S(1)}, u32[]{:S(2)}, u32[]{:S(2)}) collective-permute-start(bf16[2,64,1024]{2,1,0:T(8,128)(2,1)S(1)} %get-tuple-element.440), channel_id=1, source_target_pairs={{0,4},{1,5},{2,6},{3,7},{4,0},{5,1},{6,2},{7,3},{8,12},{9,13},{10,... | collective-permute-start | bytes 786440 | tf_op jit(solution)/shard_map/up_weights/ppermute | solution.py:55
  102.9 23.0 %collective-permute-start.31 = (bf16[2,64,1024]{2,1,0:T(8,128)(2,1)S(1)}, bf16[2,64,1024]{2,1,0:T(8,128)(2,1)S(1)}, u32[]{:S(2)}, u32[]{:S(2)}) collective-permute-start(bf16[2,64,1024]{2,1,0:T(8,128)(2,1)S(1)} %get-tuple-element.441), channel_id=1, source_target_pairs={{0,6},{1,7},{2,4},{3,5},{4,2},{5,3},{6,0},{7,1},{8,14},{9,15},{10,... | collective-permute-start | bytes 786440 | tf_op jit(solution)/shard_map/up_weights/ppermute | solution.py:55
  126.0 121.3 %all-gather.5.cloned.1.call-start = ((), (), s32[]{:S(2)}) async-start(), calls=%async_computation.5 | async-start | bytes 5242880 | tf_op jit(solution)/shard_map/up_weights/all_gather | solution.py:853
  128.4 14.4 %collective-permute-start.32 = (bf16[1,1024,256]{2,1,0:T(8,128)(2,1)S(1)}, bf16[1,1024,256]{2,1,0:T(8,128)(2,1)S(1)}, u32[]{:S(2)}, u32[]{:S(2)}) collective-permute-start(bf16[1,1024,256]{2,1,0:T(8,128)(2,1)S(1)} %slice.304), channel_id=1, source_target_pairs={{0,8},{8,0},{16,24},{24,16},{1,9},{9,1},{17,25},{25,17},{2,10},{10... | collective-permute-start | bytes 1572872 | tf_op jit(solution)/shard_map/kv_gather/ppermute | solution.py:55
  130.8 14.1 %collective-permute-start.33 = (bf16[1,1024,256]{2,1,0:T(8,128)(2,1)S(1)}, bf16[1,1024,256]{2,1,0:T(8,128)(2,1)S(1)}, u32[]{:S(2)}, u32[]{:S(2)}) collective-permute-start(bf16[1,1024,256]{2,1,0:T(8,128)(2,1)S(1)} %slice.305), channel_id=1, source_target_pairs={{0,16},{8,24},{16,0},{24,8},{1,17},{9,25},{17,1},{25,9},{2,18},{10... | collective-permute-start | bytes 1572872 | tf_op jit(solution)/shard_map/kv_gather/ppermute | solution.py:55
  145.7 24.8 %collective-permute-start.35 = (bf16[256,2048]{1,0:T(8,128)(2,1)}, bf16[256,2048]{1,0:T(8,128)(2,1)S(1)}, u32[]{:S(2)}, u32[]{:S(2)}) collective-permute-start(bf16[256,2048]{1,0:T(8,128)(2,1)} %param.35), channel_id=1, source_target_pairs={{0,8},{8,0},{16,24},{24,16},{1,9},{9,1},{17,25},{25,17},{2,10},{10... | collective-permute-start | bytes 3145736 | tf_op jit(solution)/shard_map/down_weights/ppermute | solution.py:55
  146.5 24.4 %collective-permute-start.36 = (bf16[256,2048]{1,0:T(8,128)(2,1)}, bf16[256,2048]{1,0:T(8,128)(2,1)S(1)}, u32[]{:S(2)}, u32[]{:S(2)}) collective-permute-start(bf16[256,2048]{1,0:T(8,128)(2,1)} %param.35), channel_id=1, source_target_pairs={{0,16},{8,24},{16,0},{24,8},{1,17},{9,25},{17,1},{25,9},{2,18},{10... | collective-permute-start | bytes 3145736 | tf_op jit(solution)/shard_map/down_weights/ppermute | solution.py:55
  176.5 192.9 %reduce-scatter.5.cloned.1.call-start = ((), (), s32[]{:S(2)}) async-start(), calls=%async_computation.6 | async-start | bytes 5242880 | tf_op jit(solution)/shard_map/up_grad/reduce_scatter | solution.py:997
  183.3 15.2 %collective-permute-start.38 = (bf16[128,2048]{1,0:T(8,128)(2,1)}, bf16[128,2048]{1,0:T(8,128)(2,1)}, u32[]{:S(2)}, u32[]{:S(2)}) collective-permute-start(bf16[128,2048]{1,0:T(8,128)(2,1)} %fusion.48), channel_id=1, source_target_pairs={{0,4},{1,5},{4,6},{5,7},{6,2},{7,3},{2,0},{3,1},{8,12},{9,13},{12,... | collective-permute-start | bytes 1572872 | tf_op jit(solution)/shard_map/branch/ppermute | solution.py:66
  200.1 14.3 %collective-permute-start.39 = (bf16[128,2048]{1,0:T(8,128)(2,1)S(1)}, bf16[128,2048]{1,0:T(8,128)(2,1)S(1)}, u32[]{:S(2)}, u32[]{:S(2)}) collective-permute-start(bf16[128,2048]{1,0:T(8,128)(2,1)S(1)} %fusion.38), channel_id=1, source_target_pairs={{0,4},{1,5},{4,6},{5,7},{6,2},{7,3},{2,0},{3,1},{8,12},{9,13},{12,... | collective-permute-start | bytes 1572872 | tf_op jit(solution)/shard_map/branch/ppermute | solution.py:66
  201.6 24.4 %collective-permute-start.41 = (bf16[128,2048]{1,0:T(8,128)(2,1)S(1)}, bf16[128,2048]{1,0:T(8,128)(2,1)S(1)}, u32[]{:S(2)}, u32[]{:S(2)}) collective-permute-start(bf16[128,2048]{1,0:T(8,128)(2,1)S(1)} %slice.317), channel_id=1, source_target_pairs={{0,8},{8,0},{16,24},{24,16},{1,9},{9,1},{17,25},{25,17},{2,10},{10... | collective-permute-start | bytes 1572872 | tf_op jit(solution)/shard_map/branch/down_weights/ppermute | solution.py:55
  203.0 25.4 %collective-permute-start.42 = (bf16[128,2048]{1,0:T(8,128)(2,1)S(1)}, bf16[128,2048]{1,0:T(8,128)(2,1)S(1)}, u32[]{:S(2)}, u32[]{:S(2)}) collective-permute-start(bf16[128,2048]{1,0:T(8,128)(2,1)S(1)} %slice.318), channel_id=1, source_target_pairs={{0,16},{8,24},{16,0},{24,8},{1,17},{9,25},{17,1},{25,9},{2,18},{10... | collective-permute-start | bytes 1572872 | tf_op jit(solution)/shard_map/branch/down_weights/ppermute | solution.py:55
  216.6 13.3 %collective-permute-start.40 = (bf16[128,2048]{1,0:T(8,128)(2,1)}, bf16[128,2048]{1,0:T(8,128)(2,1)S(1)}, u32[]{:S(2)}, u32[]{:S(2)}) collective-permute-start(bf16[128,2048]{1,0:T(8,128)(2,1)} %fusion.37), channel_id=1, source_target_pairs={{0,4},{1,5},{4,6},{5,7},{6,2},{7,3},{2,0},{3,1},{8,12},{9,13},{12,... | collective-permute-start | bytes 1572872 | tf_op jit(solution)/shard_map/branch/ppermute | solution.py:66
  245.6 13.3 %collective-permute-start.45 = (bf16[128,2048]{1,0:T(8,128)(2,1)S(1)}, bf16[128,2048]{1,0:T(8,128)(2,1)S(1)}, u32[]{:S(2)}, u32[]{:S(2)}) collective-permute-start(bf16[128,2048]{1,0:T(8,128)(2,1)S(1)} %collective-permute-done.43), channel_id=1, source_target_pairs={{0,4},{1,5},{4,6},{5,7},{6,2},{7,3},{2,0},{3,1},{8,12},{9,13},{12,... | collective-permute-start | bytes 1572872 | tf_op jit(solution)/shard_map/mlp/ppermute | solution.py:66
  245.6 13.4 %collective-permute-start.46 = (bf16[128,2048]{1,0:T(8,128)(2,1)S(1)}, bf16[128,2048]{1,0:T(8,128)(2,1)S(1)}, u32[]{:S(2)}, u32[]{:S(2)}) collective-permute-start(bf16[128,2048]{1,0:T(8,128)(2,1)S(1)} %collective-permute-done.43), channel_id=1, source_target_pairs={{0,1},{1,0},{2,3},{3,2},{4,5},{5,4},{6,7},{7,6},{8,9},{9,8},{10,11... | collective-permute-start | bytes 1572872 | tf_op jit(solution)/shard_map/mlp/ppermute | solution.py:55
  258.9 15.7 %collective-permute-start.47 = (bf16[128,2048]{1,0:T(8,128)(2,1)S(1)}, bf16[128,2048]{1,0:T(8,128)(2,1)S(1)}, u32[]{:S(2)}, u32[]{:S(2)}) collective-permute-start(bf16[128,2048]{1,0:T(8,128)(2,1)S(1)} %collective-permute-done.45), channel_id=1, source_target_pairs={{0,4},{1,5},{4,6},{5,7},{6,2},{7,3},{2,0},{3,1},{8,12},{9,13},{12,... | collective-permute-start | bytes 1572872 | tf_op jit(solution)/shard_map/mlp/ppermute | solution.py:66
  261.2 13.5 %collective-permute-start.48 = (bf16[128,2048]{1,0:T(8,128)(2,1)S(1)}, bf16[128,2048]{1,0:T(8,128)(2,1)S(1)}, u32[]{:S(2)}, u32[]{:S(2)}) collective-permute-start(bf16[128,2048]{1,0:T(8,128)(2,1)S(1)} %collective-permute-done.45), channel_id=1, source_target_pairs={{0,1},{1,0},{2,3},{3,2},{4,5},{5,4},{6,7},{7,6},{8,9},{9,8},{10,11... | collective-permute-start | bytes 1572872 | tf_op jit(solution)/shard_map/mlp/ppermute | solution.py:55
  284.3 15.0 %collective-permute-start.51 = (bf16[128,2048]{1,0:T(8,128)(2,1)S(1)}, bf16[128,2048]{1,0:T(8,128)(2,1)S(1)}, u32[]{:S(2)}, u32[]{:S(2)}) collective-permute-start(bf16[128,2048]{1,0:T(8,128)(2,1)S(1)} %add_convert_fusion.8), channel_id=1, source_target_pairs={{0,4},{1,5},{4,6},{5,7},{6,2},{7,3},{2,0},{3,1},{8,12},{9,13},{12,... | collective-permute-start | bytes 1572872 | tf_op jit(solution)/shard_map/mlp/ppermute | solution.py:66
  285.4 14.0 %collective-permute-start.52 = (bf16[128,2048]{1,0:T(8,128)(2,1)S(1)}, bf16[128,2048]{1,0:T(8,128)(2,1)S(1)}, u32[]{:S(2)}, u32[]{:S(2)}) collective-permute-start(bf16[128,2048]{1,0:T(8,128)(2,1)S(1)} %convolution_convert_fusion.6), channel_id=1, source_target_pairs={{0,1},{1,0},{2,3},{3,2},{4,5},{5,4},{6,7},{7,6},{8,9},{9,8},{10,11... | collective-permute-start | bytes 1572872 | tf_op jit(solution)/shard_map/mlp/ppermute | solution.py:55
  300.4 14.1 %collective-permute-start.53 = (bf16[128,2048]{1,0:T(8,128)(2,1)}, bf16[128,2048]{1,0:T(8,128)(2,1)S(1)}, u32[]{:S(2)}, u32[]{:S(2)}) collective-permute-start(bf16[128,2048]{1,0:T(8,128)(2,1)} %add_convert_fusion.7), channel_id=1, source_target_pairs={{0,4},{1,5},{4,6},{5,7},{6,2},{7,3},{2,0},{3,1},{8,12},{9,13},{12,... | collective-permute-start | bytes 1572872 | tf_op jit(solution)/shard_map/mlp/ppermute | solution.py:66
  300.4 14.1 %collective-permute-start.54 = (bf16[128,2048]{1,0:T(8,128)(2,1)S(1)}, bf16[128,2048]{1,0:T(8,128)(2,1)}, u32[]{:S(2)}, u32[]{:S(2)}) collective-permute-start(bf16[128,2048]{1,0:T(8,128)(2,1)S(1)} %convolution_convert_fusion.4), channel_id=1, source_target_pairs={{0,1},{1,0},{2,3},{3,2},{4,5},{5,4},{6,7},{7,6},{8,9},{9,8},{10,11... | collective-permute-start | bytes 1572872 | tf_op jit(solution)/shard_map/mlp/ppermute | solution.py:55
  314.5 108.1 %reduce-scatter.7.cloned.1.call-start = ((), (), s32[]{:S(2)}) async-start(), calls=%async_computation.7 | async-start | bytes 4718592 | tf_op jit(solution)/shard_map/d_branch_gather/output/reduce_scatter | solution.py:1022
  316.7 13.7 %collective-permute-start.55 = (bf16[128,2048]{1,0:T(8,128)(2,1)}, bf16[128,2048]{1,0:T(8,128)(2,1)}, u32[]{:S(2)}, u32[]{:S(2)}) collective-permute-start(bf16[128,2048]{1,0:T(8,128)(2,1)} %add_convert_fusion.6), channel_id=1, source_target_pairs={{0,4},{1,5},{4,6},{5,7},{6,2},{7,3},{2,0},{3,1},{8,12},{9,13},{12,... | collective-permute-start | bytes 1572872 | tf_op jit(solution)/shard_map/mlp/ppermute | solution.py:66
  317.1 13.3 %collective-permute-start.56 = (bf16[128,2048]{1,0:T(8,128)(2,1)}, bf16[128,2048]{1,0:T(8,128)(2,1)}, u32[]{:S(2)}, u32[]{:S(2)}) collective-permute-start(bf16[128,2048]{1,0:T(8,128)(2,1)} %convolution_convert_fusion.10), channel_id=1, source_target_pairs={{0,1},{1,0},{2,3},{3,2},{4,5},{5,4},{6,7},{7,6},{8,9},{9,8},{10,11... | collective-permute-start | bytes 1572872 | tf_op jit(solution)/shard_map/mlp/ppermute | solution.py:55
  333.8 15.7 %collective-permute-start.58 = (bf16[64,2048]{1,0:T(8,128)(2,1)S(1)}, bf16[64,2048]{1,0:T(8,128)(2,1)S(1)}, u32[]{:S(2)}, u32[]{:S(2)}) collective-permute-start(bf16[64,2048]{1,0:T(8,128)(2,1)S(1)} %get-tuple-element.752), channel_id=1, source_target_pairs={{0,4},{1,5},{4,6},{5,7},{6,2},{7,3},{2,0},{3,1},{8,12},{9,13},{12,... | collective-permute-start | bytes 786440 | tf_op jit(solution)/shard_map/d_branch_gather/ppermute | solution.py:66
  369.4 134.3 %reduce-scatter.9.cloned.1.call-start = ((), (), s32[]{:S(2)}) async-start(), calls=%async_computation.8 | async-start | bytes 5242880 | tf_op jit(solution)/shard_map/down_grad/reduce_scatter | solution.py:997
  372.8 25.0 %collective-permute-start.69 = (bf16[4,64,1024]{2,1,0:T(8,128)(2,1)S(1)}, bf16[4,64,1024]{2,1,0:T(8,128)(2,1)S(1)}, u32[]{:S(2)}, u32[]{:S(2)}) collective-permute-start(bf16[4,64,1024]{2,1,0:T(8,128)(2,1)S(1)} %get-tuple-element.740), channel_id=1, source_target_pairs={{0,1},{1,0},{2,3},{3,2},{4,5},{5,4},{6,7},{7,6},{8,9},{9,8},{10,11... | collective-permute-start | bytes 1572872 | tf_op jit(solution)/shard_map/up_grad/ppermute | solution.py:55
  388.9 17.1 %collective-permute-start.67 = (bf16[1024,256]{1,0:T(8,128)(2,1)}, bf16[1024,256]{1,0:T(8,128)(2,1)S(1)}, u32[]{:S(2)}, u32[]{:S(2)}) collective-permute-start(bf16[1024,256]{1,0:T(8,128)(2,1)} %get-tuple-element.571), channel_id=1, source_target_pairs={{0,8},{8,0},{16,24},{24,16},{1,9},{9,1},{17,25},{25,17},{2,10},{10... | collective-permute-start | bytes 1572872 | tf_op jit(solution)/shard_map/attention_back/ppermute | solution.py:55
  390.3 15.8 %collective-permute-start.68 = (bf16[1024,256]{1,0:T(8,128)(2,1)}, bf16[1024,256]{1,0:T(8,128)(2,1)S(1)}, u32[]{:S(2)}, u32[]{:S(2)}) collective-permute-start(bf16[1024,256]{1,0:T(8,128)(2,1)} %get-tuple-element.572), channel_id=1, source_target_pairs={{0,16},{8,24},{16,0},{24,8},{1,17},{9,25},{17,1},{25,9},{2,18},{10... | collective-permute-start | bytes 1572872 | tf_op jit(solution)/shard_map/attention_back/ppermute | solution.py:55
  408.2 14.0 %collective-permute-start.70 = (bf16[1024,256]{1,0:T(8,128)(2,1)}, bf16[1024,256]{1,0:T(8,128)(2,1)S(1)}, u32[]{:S(2)}, u32[]{:S(2)}) collective-permute-start(bf16[1024,256]{1,0:T(8,128)(2,1)} %get-tuple-element.597), channel_id=1, source_target_pairs={{0,8},{8,0},{16,24},{24,16},{1,9},{9,1},{17,25},{25,17},{2,10},{10... | collective-permute-start | bytes 1572872 | tf_op jit(solution)/shard_map/attention_back/ppermute | solution.py:55
  409.0 13.6 %collective-permute-start.71 = (bf16[1024,256]{1,0:T(8,128)(2,1)S(1)}, bf16[1024,256]{1,0:T(8,128)(2,1)}, u32[]{:S(2)}, u32[]{:S(2)}) collective-permute-start(bf16[1024,256]{1,0:T(8,128)(2,1)S(1)} %add_convert_fusion.4), channel_id=1, source_target_pairs={{0,16},{8,24},{16,0},{24,8},{1,17},{9,25},{17,1},{25,9},{2,18},{10... | collective-permute-start | bytes 1572872 | tf_op jit(solution)/shard_map/attention_back/ppermute | solution.py:55
  422.6 142.2 %reduce-scatter.11.cloned.1.call-start = ((), (), s32[]{:S(2)}) async-start(), calls=%async_computation.9 | async-start | bytes 1310720 | tf_op jit(solution)/shard_map/out_grad/reduce_scatter | solution.py:997
  423.1 19.5 %collective-permute-start.72 = (bf16[1024,256]{1,0:T(8,128)(2,1)}, bf16[1024,256]{1,0:T(8,128)(2,1)}, u32[]{:S(2)}, u32[]{:S(2)}) collective-permute-start(bf16[1024,256]{1,0:T(8,128)(2,1)} %add_convert_fusion.5), channel_id=1, source_target_pairs={{0,8},{8,0},{16,24},{24,16},{1,9},{9,1},{17,25},{25,17},{2,10},{10... | collective-permute-start | bytes 1572872 | tf_op jit(solution)/shard_map/attention_back/ppermute | solution.py:55
  424.5 20.5 %collective-permute-start.73 = (bf16[1024,256]{1,0:T(8,128)(2,1)}, bf16[1024,256]{1,0:T(8,128)(2,1)}, u32[]{:S(2)}, u32[]{:S(2)}) collective-permute-start(bf16[1024,256]{1,0:T(8,128)(2,1)} %get-tuple-element.620), channel_id=1, source_target_pairs={{0,16},{8,24},{16,0},{24,8},{1,17},{9,25},{17,1},{25,9},{2,18},{10... | collective-permute-start | bytes 1572872 | tf_op jit(solution)/shard_map/attention_back/ppermute | solution.py:55
  426.2 21.5 %collective-permute-start.74 = (bf16[2,64,1024]{2,1,0:T(8,128)(2,1)S(1)}, bf16[2,64,1024]{2,1,0:T(8,128)(2,1)S(1)}, u32[]{:S(2)}, u32[]{:S(2)}) collective-permute-start(bf16[2,64,1024]{2,1,0:T(8,128)(2,1)S(1)} %get-tuple-element.622), channel_id=1, source_target_pairs={{0,2},{1,3},{2,0},{3,1},{4,6},{5,7},{6,4},{7,5},{8,10},{9,11},{10,... | collective-permute-start | bytes 786440 | tf_op jit(solution)/shard_map/up_grad/ppermute | solution.py:55
  426.9 20.8 %collective-permute-start.75 = (bf16[2,64,1024]{2,1,0:T(8,128)(2,1)S(1)}, bf16[2,64,1024]{2,1,0:T(8,128)(2,1)S(1)}, u32[]{:S(2)}, u32[]{:S(2)}) collective-permute-start(bf16[2,64,1024]{2,1,0:T(8,128)(2,1)S(1)} %get-tuple-element.623), channel_id=1, source_target_pairs={{0,4},{1,5},{2,6},{3,7},{4,0},{5,1},{6,2},{7,3},{8,12},{9,13},{10,... | collective-permute-start | bytes 786440 | tf_op jit(solution)/shard_map/up_grad/ppermute | solution.py:55
  428.0 22.5 %collective-permute-start.76 = (bf16[2,64,1024]{2,1,0:T(8,128)(2,1)S(1)}, bf16[2,64,1024]{2,1,0:T(8,128)(2,1)S(1)}, u32[]{:S(2)}, u32[]{:S(2)}) collective-permute-start(bf16[2,64,1024]{2,1,0:T(8,128)(2,1)S(1)} %get-tuple-element.624), channel_id=1, source_target_pairs={{0,6},{1,7},{2,4},{3,5},{4,2},{5,3},{6,0},{7,1},{8,14},{9,15},{10,... | collective-permute-start | bytes 786440 | tf_op jit(solution)/shard_map/up_grad/ppermute | solution.py:55
  466.4 20.5 %collective-permute-start.79 = (bf16[256,768]{1,0:T(8,128)(2,1)}, bf16[256,768]{1,0:T(8,128)(2,1)}, u32[]{:S(2)}, u32[]{:S(2)}) collective-permute-start(bf16[256,768]{1,0:T(8,128)(2,1)} %get-tuple-element.735), channel_id=1, source_target_pairs={{0,8},{8,0},{16,24},{24,16},{1,9},{9,1},{17,25},{25,17},{2,10},{10... | collective-permute-start | bytes 1179656 | tf_op jit(solution)/shard_map/qkv_grad/ppermute | solution.py:55
  467.2 20.4 %collective-permute-start.80 = (bf16[256,768]{1,0:T(8,128)(2,1)}, bf16[256,768]{1,0:T(8,128)(2,1)}, u32[]{:S(2)}, u32[]{:S(2)}) collective-permute-start(bf16[256,768]{1,0:T(8,128)(2,1)} %get-tuple-element.737), channel_id=1, source_target_pairs={{0,16},{8,24},{16,0},{24,8},{1,17},{9,25},{17,1},{25,9},{2,18},{10... | collective-permute-start | bytes 1179656 | tf_op jit(solution)/shard_map/qkv_grad/ppermute | solution.py:55
  470.3 17.4 %collective-permute-start.78 = (bf16[128,2048]{1,0:T(8,128)(2,1)}, bf16[128,2048]{1,0:T(8,128)(2,1)}, u32[]{:S(2)}, u32[]{:S(2)}) collective-permute-start(bf16[128,2048]{1,0:T(8,128)(2,1)} %fusion.53), channel_id=1, source_target_pairs={{0,4},{1,5},{4,6},{5,7},{6,2},{7,3},{2,0},{3,1},{8,12},{9,13},{12,... | collective-permute-start | bytes 1572872 | tf_op jit(solution)/shard_map/d_normed/ppermute | solution.py:66
  489.2 14.5 %collective-permute-start.83 = (bf16[128,2048]{1,0:T(8,128)(2,1)S(1)}, bf16[128,2048]{1,0:T(8,128)(2,1)}, u32[]{:S(2)}, u32[]{:S(2)}) collective-permute-start(bf16[128,2048]{1,0:T(8,128)(2,1)S(1)} %fusion.35), channel_id=1, source_target_pairs={{0,4},{1,5},{4,6},{5,7},{6,2},{7,3},{2,0},{3,1},{8,12},{9,13},{12,... | collective-permute-start | bytes 1572872 | tf_op jit(solution)/shard_map/d_normed/ppermute | solution.py:66
  492.0 37.6 %collective-permute-start.81 = (bf16[512,768]{1,0:T(8,128)(2,1)}, bf16[512,768]{1,0:T(8,128)(2,1)}, u32[]{:S(2)}, u32[]{:S(2)}) collective-permute-start(bf16[512,768]{1,0:T(8,128)(2,1)} %pad_maximum_fusion.1), channel_id=1, source_target_pairs={{0,8},{8,0},{16,24},{24,16},{1,9},{9,1},{17,25},{25,17},{2,10},{10... | collective-permute-start | bytes 2359304 | tf_op jit(solution)/shard_map/qkv_grad/ppermute | solution.py:55
  494.1 35.4 %collective-permute-start.82 = (bf16[512,768]{1,0:T(8,128)(2,1)}, bf16[512,768]{1,0:T(8,128)(2,1)}, u32[]{:S(2)}, u32[]{:S(2)}) collective-permute-start(bf16[512,768]{1,0:T(8,128)(2,1)} %pad_maximum_fusion.2), channel_id=1, source_target_pairs={{0,16},{8,24},{16,0},{24,8},{1,17},{9,25},{17,1},{25,9},{2,18},{10... | collective-permute-start | bytes 2359304 | tf_op jit(solution)/shard_map/qkv_grad/ppermute | solution.py:55
  507.0 15.6 %collective-permute-start.84 = (bf16[128,2048]{1,0:T(8,128)(2,1)}, bf16[128,2048]{1,0:T(8,128)(2,1)}, u32[]{:S(2)}, u32[]{:S(2)}) collective-permute-start(bf16[128,2048]{1,0:T(8,128)(2,1)} %fusion.34), channel_id=1, source_target_pairs={{0,4},{1,5},{4,6},{5,7},{6,2},{7,3},{2,0},{3,1},{8,12},{9,13},{12,... | collective-permute-start | bytes 1572872 | tf_op jit(solution)/shard_map/d_normed/ppermute | solution.py:66
  537.2 12.9 %collective-permute-start.91 = (bf16[2,80,768]{2,1,0:T(8,128)(2,1)S(1)}, bf16[2,80,768]{2,1,0:T(8,128)(2,1)S(1)}, u32[]{:S(2)}, u32[]{:S(2)}) collective-permute-start(bf16[2,80,768]{2,1,0:T(8,128)(2,1)S(1)} %get-tuple-element.704), channel_id=1, source_target_pairs={{0,2},{1,3},{2,0},{3,1},{4,6},{5,7},{6,4},{7,5},{8,10},{9,11},{10,... | collective-permute-start | bytes 737288 | tf_op jit(solution)/shard_map/qkv_grad/ppermute | solution.py:55
  537.4 18.8 %collective-permute-start.92 = (bf16[2,80,768]{2,1,0:T(8,128)(2,1)S(1)}, bf16[2,80,768]{2,1,0:T(8,128)(2,1)S(1)}, u32[]{:S(2)}, u32[]{:S(2)}) collective-permute-start(bf16[2,80,768]{2,1,0:T(8,128)(2,1)S(1)} %get-tuple-element.705), channel_id=1, source_target_pairs={{0,4},{1,5},{2,6},{3,7},{4,0},{5,1},{6,2},{7,3},{8,12},{9,13},{10,... | collective-permute-start | bytes 737288 | tf_op jit(solution)/shard_map/qkv_grad/ppermute | solution.py:55
  539.3 23.0 %collective-permute-start.93 = (bf16[2,80,768]{2,1,0:T(8,128)(2,1)S(1)}, bf16[2,80,768]{2,1,0:T(8,128)(2,1)S(1)}, u32[]{:S(2)}, u32[]{:S(2)}) collective-permute-start(bf16[2,80,768]{2,1,0:T(8,128)(2,1)S(1)} %get-tuple-element.706), channel_id=1, source_target_pairs={{0,6},{1,7},{2,4},{3,5},{4,2},{5,3},{6,0},{7,1},{8,14},{9,15},{10,... | collective-permute-start | bytes 737288 | tf_op jit(solution)/shard_map/qkv_grad/ppermute | solution.py:55
  (95 other events, 1045.0 us)
Sparse Core Ops, SparseCore 0:
  126.1 43.5 all-gather.2
  176.7 62.0 all-gather.4
  314.7 50.8 reduce-scatter.4
  369.5 45.2 reduce-scatter.6
  422.8 66.4 reduce-scatter.8
  534.6 26.3 reduce-scatter.10

commit v5 on v4

--- a/solution.py
+++ b/solution.py
@@ -158,6 +158,61 @@
 
     shape = ((count,) + blocks[0].shape, blocks[0].dtype)
     return local_call(kernel, [shape], at, *blocks, name="place")[0]
+
+
+def place_halves(first, parts, low, high, at):
+    count, rows, width = first.shape
+
+    def kernel(at_ref, first_ref, *refs):
+        out = refs[-1]
+        for k in range(count):
+            out[k, 0] = first_ref[k]
+        for m in range(count - 1):
+            out[at_ref[m], 1] = refs[m][...]
+        out[at_ref[count - 1], 1, : rows // 2] = refs[count - 1][...]
+        out[at_ref[count - 1], 1, rows // 2 :] = refs[count][...]
+
+    shape = ((count, 2, rows, width), first.dtype)
+    return local_call(kernel, [shape], at, first, *parts, low, high, name="place_halves")[0]
+
+
+def pack_sums(at, first, early, up_row, d_query, d_values, n_head, n_blk, wide, w_rows):
+    ff = up_row.shape[1] // n_head
+    own = d_query.shape[1]
+    each = own // DH
+
+    team = DH // w_rows
+
+    def kernel(at_ref, first_ref, *refs):
+        earlies, up_ref, query_ref, value_ref, out = refs[:-4], *refs[-4:]
+        vectors = [first_ref[0:1, :], first_ref[1:2, :]] + [ref[...] for ref in earlies]
+        totals = [
+            jnp.sum(ref[...].astype(bf16).astype(f32), axis=0, keepdims=True)
+            for ref in (query_ref, value_ref)
+        ]
+        for h in range(n_head):
+            for b in range(n_blk):
+                low = (h * n_blk + b) * w_rows
+                row = [v[:, low : low + w_rows] for v in vectors]
+                mine = jnp.where(at_ref[0] == b, 1.0, 0.0)
+                row.append(up_ref[:, h * ff : (h + 1) * ff] * mine)
+                for total in totals:
+                    part = jnp.zeros((1, w_rows), f32)
+                    for i in range(each):
+                        for k in range(team):
+                            here = (at_ref[1] + i == h) & (at_ref[2] + k == b)
+                            low = i * DH + k * w_rows
+                            part += total[:, low : low + w_rows] * jnp.where(here, 1.0, 0.0)
+                    row.append(part)
+                used = sum(part.shape[1] for part in row)
+                if used < wide:
+                    row.append(jnp.zeros((1, wide - used), f32))
+                out[h, b : b + 1, :] = jnp.concatenate(row, axis=1)
+
+    shape = ((n_head, n_blk, wide), f32)
+    return local_call(
+        kernel, [shape], at, first, *early, up_row, d_query, d_values, name="pack_sums"
+    )[0]
 
 
 def place_cores(pieces, at):
@@ -703,6 +758,14 @@
         mine, other = split_columns(
             [query_proj, key_proj, value_proj], own_heads, head_columns, core, chips, "split_heads"
         )
+    other, down_late = hold(other, down_proj)
+    with jax.named_scope("down_weights"):
+        half = ff_rows // 2
+        if square:
+            down_first = lax.all_gather(down_late[:half], "head", axis=0, tiled=False)
+        else:
+            down_first = down_proj
+    with jax.named_scope("qkv_weights"):
         pieces = pair_up(mine, swap(other, "blk", 1), chip, core)
 
     places = (heads_at, chips_at, blocks_at, weights_at)
@@ -721,8 +784,8 @@
         small_parts = [small]
         small_parts.append(next_chip(small))
 
-    fused, small_parts, tok_mine, tok_other, up_proj = hold(
-        fused, small_parts, tok_mine, tok_other, up_proj
+    fused, small_parts, tok_mine, tok_other, up_proj, down_first = hold(
+        fused, small_parts, tok_mine, tok_other, up_proj, down_first
     )
 
     def small_table():
@@ -859,7 +922,8 @@
         )
     with jax.named_scope("down_weights"):
         if square:
-            downs = [down_proj, swap(down_proj, "head", 1), swap(down_proj, "head", 2)]
+            downs = down_proj[half:]
+            downs = [downs, swap(downs, "head", 1), swap(downs, "head", 2)]
         else:
             downs = gather_head(down_proj)
     mixed, out_w, table, downs = hold(mixed, out_w, table, downs)
@@ -894,17 +958,14 @@
                     vectors = (o_bias, gain_second, shift_second, d_bias, u_bias.reshape(1, -1))
             with jax.named_scope("down_weights"):
                 if square and step == 2:
-                    half = ff_rows // 2
-                    low = swap(downs[2][:half], "head", 1)
-                    high = swap(downs[1][half:], "head", 2)
+                    low = swap(downs[2][: half // 2], "head", 1)
+                    high = swap(downs[1][half // 2 :], "head", 2)
                 if not square and step == 1:
                     down_w = place(downs, heads_at).reshape(n_head * ff_rows, D)
             if step == 1:
                 moving, ready, vectors = hold(moving, ready, vectors)
                 o_bias, gain_second, shift_second, d_bias, u_bias = vectors
-            elif step == 2:
-                moving, ready, downs = hold(moving, ready, downs)
-            elif square and step == 3:
+            elif square and step == 2:
                 moving, ready, low, high = hold(moving, ready, low, high)
             else:
                 moving, ready = hold(moving, ready)
@@ -916,9 +977,8 @@
 
     with jax.named_scope("down_weights"):
         if square:
-            blocks = [part.reshape(2, half, D)[k] for part in downs for k in (0, 1)]
-            at = (2 * heads_at[:, None] + two_cores[None, :]).reshape(-1)
-            down_w = place(blocks + [low, high], at).reshape(n_head * ff_rows, D)
+            down_w = place_halves(down_first, downs, low, high, heads_at)
+            down_w = down_w.reshape(n_head * ff_rows, D)
 
     with jax.named_scope("mlp"):
         second_all = blank((rows, D), bf16)
@@ -998,8 +1058,8 @@
 
     with jax.named_scope("up_grad"):
         up_sum = sum_heads(up_term)
-    d_hidden, d_branch_own, active_all, d_second = hold(
-        d_hidden, d_branch_own, active_all, d_second
+    d_hidden, d_branch_own, active_all, d_second, d_upper_all, hat_second, cotangent = hold(
+        d_hidden, d_branch_own, active_all, d_second, d_upper_all, hat_second, cotangent
     )
     mine, other = [d_branch_own], []
 
@@ -1017,7 +1077,15 @@
             if step > 0:
                 mine.append(jnp.concatenate([chain[step] for chain in halves], axis=0))
         mine.append(jnp.concatenate([chain[-1] for chain in halves], axis=0))
-        mine, up_sum, out_term = hold(mine, up_sum, out_term)
+        with jax.named_scope("vector_grads"):
+            early = [
+                jnp.sum(d_branch_own.astype(f32), axis=0, keepdims=True),
+                jnp.sum(d_second * hat_second, axis=0, keepdims=True),
+                jnp.sum(d_second, axis=0, keepdims=True),
+                jnp.sum(cotangent.astype(f32), axis=0, keepdims=True),
+                jnp.sum(d_upper_all.astype(f32), axis=0, keepdims=True),
+            ]
+        mine, up_sum, out_term, early = hold(mine, up_sum, out_term, early)
         with jax.named_scope("output"):
             out_sum = lax.psum_scatter(out_term, "blk", scatter_dimension=0, tiled=True)
         other = [swap(piece, "blk", 1) for piece in mine]
@@ -1080,22 +1148,24 @@
                 for total in (d_keys, d_values)
             ]
         d_qkv = jnp.concatenate([dq.astype(bf16), d_keys, d_values], axis=1)
-    kept = (d_branch_own, d_second, hat_second, d_upper_all, cotangent, dq, d_values)
     d_qkv, up_pieces, mix_term = hold(d_qkv, up_pieces, mix_term)
 
     slab, wide = n_blk * w_rows, 3 * own_heads
     with jax.named_scope("d_normed"):
         own_terms, other_terms = terms_out(blocks_at, d_qkv, qkv_w, True)
         ready = met(own_terms, other_terms)
-    with jax.named_scope("qkv_grad"):
-        qkv_term = cross_rows(normed, d_qkv).astype(bf16).reshape(n_head, slab, wide)
-    ready, qkv_term, mix_term, up_pieces, kept = hold(ready, qkv_term, mix_term, up_pieces, kept)
-    d_branch_own, d_second, hat_second, d_upper_all, cotangent, dq, d_values = kept
+    ready, normed, d_qkv, mix_term, up_pieces = hold(ready, normed, d_qkv, mix_term, up_pieces)
     moving = None
     for step in range(1, chips):
         with jax.named_scope("d_normed"):
             moving = onward(entry(ready, step), moving)
         if step == 1:
+            with jax.named_scope("qkv_grad"):
+                qkv_term = cross_rows(normed, d_qkv).astype(bf16).reshape(n_head, slab, wide)
+            late = (other_terms, mix_term, tok_mine, tok_other, dq, d_values)
+            moving, ready, qkv_term, late = hold(moving, ready, qkv_term, late)
+            other_terms, mix_term, tok_mine, tok_other, dq, d_values = late
+        elif step == 2:
             with jax.named_scope("qkv_grad"):
                 if square:
                     half = slab // 2
@@ -1103,29 +1173,10 @@
                     low, high = swap(far[:half], "head", 1), swap(far[half:], "head", 2)
                 else:
                     low = high = qkv_term
-            with jax.named_scope("vector_grads"):
-                full = [
-                    jnp.sum(d_branch_own.astype(f32), axis=0),
-                    jnp.sum(d_second * hat_second, axis=0),
-                    jnp.sum(d_second, axis=0),
-                    jnp.sum(cotangent.astype(f32), axis=0),
-                ]
-                parts = [v.reshape(n_head, n_blk, w_rows) for v in full]
-                up_row = jnp.sum(d_upper_all.astype(f32), axis=0)
-                up_table = jnp.zeros((n_blk, n_head, ff_rows), f32)
-                up_table = put(up_table, up_row.reshape(n_head, ff_rows), blk)
-                parts.append(up_table.transpose(1, 0, 2))
-                for v in (dq.astype(bf16), d_values):
-                    bias_sum = jnp.sum(v.astype(f32), axis=0).reshape(each, 1, DH)
-                    head_table = jnp.zeros((n_head, sets, DH), f32)
-                    head_table = lax.dynamic_update_slice(
-                        head_table, bias_sum, (place_in * each, blk // team, 0)
-                    )
-                    parts.append(head_table.reshape(n_head, n_blk, w_rows))
-            moving, ready, low, high, parts, own_terms, mix_term, tok_mine, tok_other = hold(
-                moving, ready, low, high, parts, own_terms, mix_term, tok_mine, tok_other
-            )
-        elif step == 2:
+            with jax.named_scope("out_grad"):
+                mix_term = exchange(mix_term, "blk", place_in, team)
+            moving, ready, low, high, mix_term = hold(moving, ready, low, high, mix_term)
+        elif step == 3:
             with jax.named_scope("qkv_grad"):
                 if square:
                     one, two = pick(qkv_term, head ^ 1), pick(qkv_term, head ^ 2)
@@ -1133,22 +1184,25 @@
                     two = jnp.concatenate([two[:half] + low, two[half:]])
                     one, two = swap(one, "head", 1), swap(two, "head", 2)
             with jax.named_scope("vector_grads"):
-                first_sums = norm_sums(own_terms, other_terms, tok_mine, tok_other)
-            moving, ready, first_sums, down_grad, mix_term = hold(
-                moving, ready, first_sums, down_grad, mix_term
+                first_sums = norm_sums(ready[0], other_terms, tok_mine, tok_other)
+                parts = pack_sums(
+                    scalars(blk, place_in * each, blk - place_in),
+                    first_sums,
+                    early[:4],
+                    early[4],
+                    dq,
+                    d_values,
+                    n_head,
+                    n_blk,
+                    wide,
+                    w_rows,
+                )
+            moving, ready, parts, mix_term, down_grad = hold(
+                moving, ready, parts, mix_term, down_grad
             )
-        elif step == 3:
-            with jax.named_scope("out_grad"):
-                mix_term = exchange(mix_term, "blk", place_in, team)
-            with jax.named_scope("vector_grads"):
-                parts = [v.reshape(n_head, n_blk, w_rows) for v in first_sums] + parts
-                parts = jnp.concatenate(parts, axis=2)
-                deep = -(-parts.shape[2] // wide)
-                parts = jnp.pad(parts, ((0, 0), (0, 0), (0, deep * wide - parts.shape[2])))
-                parts = parts.reshape(n_head, n_blk * deep, wide)
-            moving, ready, parts, mix_term = hold(moving, ready, parts, mix_term)
         else:
             moving, ready = hold(moving, ready)
+    deep = 1
     with jax.named_scope("out_grad"):
         out_grad = sum_heads(mix_term.reshape(n_head * w_rows, D))
     with jax.named_scope("vector_grads"):

time: 578 us -> 567 us (0.981)
  other arithmetic: 62.3 us -> 48 us
    ppermute x24, waiting for transfers between devices: 91.9 us -> 97.9 us  [next_chip(): lax.ppermute(v, 'blk', [(2 * a + c, 2 * b + c) for a, b in moves for c in...]
    unnamed x121 -> x125, local copies, waits for them, and re-layouts: 8.57 us -> 11.7 us
    pallas_call x15 -> x16, Pallas kernels: 24.5 us -> 26.7 us  [local_call(): pl.pallas_call(kernel, in_specs=[pl.BlockSpec(memory_space=pltpu.SMEM)] +...]
  transfers between devices with their start and end apart: 100 -> 101, of which waited for: 47 -> 49; matrix products, arithmetic and copies ran while one was open for 26% -> 23% of each run, Pallas kernels for 19% -> 20%
where the time goes in v5:
time: 567 us; the launch traced here: 563 us
  waiting for transfers between devices  208 us (37%)
  Pallas kernels  110 us (19%)
  starting transfers between devices  74.8 us (13%)
  matrix products  63 us (11%)
  other arithmetic  48 us (8%)
  local copies, waits for them, and re-layouts  37.2 us (7%)
  between operations  21 us (4%)
    ppermute x70, waiting for transfers between devices, swap(): return lax.ppermute(v, axis, [(i, i ^ mask) for i in range(size)])  110 us
    ppermute x24, waiting for transfers between devices, next_chip(): lax.ppermute(v, 'blk', [(2 * a + c, 2 * b + c) for a, b in moves for c in...  97.9 us
    ppermute x70, starting transfers between devices, swap(): return lax.ppermute(v, axis, [(i, i ^ mask) for i in range(size)])  57 us
    pallas_call x4, Pallas kernels, attend_back(): pl.pallas_call(kernel, grid=(1 if rows <= 1024 else heads * tiles,), in_s...  29.9 us
    pallas_call x16, Pallas kernels, local_call(): pl.pallas_call(kernel, in_specs=[pl.BlockSpec(memory_space=pltpu.SMEM)] +...  26.7 us
    dot_general x3, matrix products, cross_rows(): lax.dot_general(left, right, (((0,), (0,)), ((), ())), preferred_element_...  24.5 us
    dot_general x12, matrix products, times_transposed(): lax.dot_general(left, right, (((1,), (1,)), ((), ())), preferred_element_...  19.6 us
    pallas_call x2, Pallas kernels, attend(): pl.pallas_call(kernel, grid=(1 if rows * len(which) <= 4096 else heads *...  19 us
  transfers between devices with their start and end apart: 101, of which 49 were waited for; matrix products, arithmetic and copies ran while one was open for 23% of the time, Pallas kernels for 20%

profile of v5, /device:TPU:8, one launch (start us, length us, event | category | flops | bytes accessed | tf_op | source)
XLA Modules:
  0.0 562.6 jit_solution(266612328566173112)
XLA Ops:
  19.3 8.0 %collective-permute-done.1.refs_1_.refs_3_ = bf16[128,2048]{1,0:T(8,128)(2,1)} collective-permute-done((bf16[128,2048]{1,0:T(8,128)(2,1)}, bf16[128,2048]{1,0:T(8,128)(2,1)}, u32[]{:S(2)}, u32[]{:S(2)}) %collective-permute-start.1) | collective-permute-done | bytes 524320 | tf_op jit(solution)/shard_map/tokens_gather/ppermute | solution.py:66
  28.8 3.0 collective-permute-start.4
  38.3 7.0 %collective-permute-done.4.refs_2_ = bf16[2,64,768]{2,1,0:T(8,128)(2,1)S(1)} collective-permute-done((bf16[2,64,768]{2,1,0:T(8,128)(2,1)S(1)}, bf16[2,64,768]{2,1,0:T(8,128)(2,1)S(1)}, u32[]{:S(2)}, u32[]{:S(2)}) %collective-permute-start.4) | collective-permute-done | bytes 196640 | tf_op jit(solution)/shard_map/qkv_weights/ppermute | solution.py:55
  45.4 3.5 collective-permute-done.5.refs_3_
  53.0 2.7 add_multiply_fusion.5
  55.8 3.0 collective-permute-start.17
  58.9 5.5 collective-permute-done.17
  69.3 2.8 collective-permute-start.18
  78.3 4.2 collective-permute-done.14.refs_17_
  91.0 13.4 %project_in.1 = (bf16[1024,256]{1,0:T(8,128)(2,1)}, bf16[2,1024,256]{2,1,0:T(8,128)(2,1)}, bf16[1024,2048]{1,0:T(8,128)(2,1)}, bf16[2048,768]{1,0:T(8,128)(2,1)}) custom-call(s32[13]{0:T(128)} %pad_add_fusion.1.at_ref, bf16[128,2048]{1,0:T(8,128)(2,1)} %refs_2_.2, bf16[128,2048]{1,0:T(8,128)(2,1)} %collective-permute-done.1.refs_1_.refs_3_, ...), custom_call_target="tpu_custom_call" | custom-call | flops 3221225472 | bytes 16777216 | tf_op jit(solution)/shard_map/qkv/project_in/pallas_call | solution.py:506
  106.4 2.7 collective-permute-start.29
  110.6 2.3 convert_reduce_fusion
  112.9 6.2 %attend.2 = (f32[1024,256]{1,0:T(8,128)}, f32[2,2,1024]{2,1,0:T(2,128)}) custom-call(s32[4]{0:T(128)} %get-tuple-element.372.heads_ref.at_ref, s32[1,1024]{1,0:T(1,128)} %bitcast.259, bf16[1024,256]{1,0:T(8,128)(2,1)} %get-tuple-element.434.query_ref, bf16[2,1024,256]{2,1,0:T(8,128)(2,1)} %get-tuple-element.432.refs_0_), custom_call_target="tpu_custom_call" | custom-call | flops 536870912 | bytes 1048576 | tf_op jit(solution)/shard_map/attention/attend/pallas_call | solution.py:384
  119.1 9.2 %collective-permute-done.30.refs_2_ = bf16[2,64,1024]{2,1,0:T(8,128)(2,1)S(1)} collective-permute-done((bf16[2,64,1024]{2,1,0:T(8,128)(2,1)S(1)}, bf16[2,64,1024]{2,1,0:T(8,128)(2,1)S(1)}, u32[]{:S(2)}, u32[]{:S(2)}) %collective-permute-start.30) | collective-permute-done | bytes 262176 | tf_op jit(solution)/shard_map/up_weights/ppermute | solution.py:55
  128.4 4.3 collective-permute-done.31.refs_3_
  139.9 9.3 %collective-permute-done.32.refs_2_.refs_0_ = bf16[1,1024,256]{2,1,0:T(8,128)(2,1)S(1)} collective-permute-done((bf16[1,1024,256]{2,1,0:T(8,128)(2,1)S(1)}, bf16[1,1024,256]{2,1,0:T(8,128)(2,1)S(1)}, u32[]{:S(2)}, u32[]{:S(2)}) %collective-permute-start.32) | collective-permute-done | bytes 524320 | tf_op jit(solution)/shard_map/kv_gather/ppermute | solution.py:55
  155.8 12.8 %attend.3 = (bf16[1024,256]{1,0:T(8,128)(2,1)}, f32[2,1,1024]{2,1,0:T(1,128)}) custom-call(s32[4]{0:T(128)} %get-tuple-element.372.heads_ref.at_ref, s32[1,1024]{1,0:T(1,128)} %bitcast.260, bf16[1024,256]{1,0:T(8,128)(2,1)} %get-tuple-element.434.query_ref, bf16[2,1024,256]{2,1,0:T(8,128)(2,1)} %collective-permute-done.27.refs_0_, ...), custom_call_target="tpu_custom_call" | custom-call | flops 1610612736 | bytes 3145728 | tf_op jit(solution)/shard_map/attention/attend/pallas_call | solution.py:384
  168.6 5.6 terms_out.2
  174.3 4.4 collective-permute-done.37
  181.5 13.6 %collective-permute-done.38 = bf16[128,2048]{1,0:T(8,128)(2,1)S(1)} collective-permute-done((bf16[128,2048]{1,0:T(8,128)(2,1)S(1)}, bf16[128,2048]{1,0:T(8,128)(2,1)S(1)}, u32[]{:S(2)}, u32[]{:S(2)}) %collective-permute-start.38) | collective-permute-done | bytes 524320 | tf_op jit(solution)/shard_map/branch/ppermute | solution.py:66
  199.8 7.3 %collective-permute-done.40.refs_3_ = bf16[64,2048]{1,0:T(8,128)(2,1)S(1)} collective-permute-done((bf16[64,2048]{1,0:T(8,128)(2,1)S(1)}, bf16[64,2048]{1,0:T(8,128)(2,1)S(1)}, u32[]{:S(2)}, u32[]{:S(2)}) %collective-permute-start.40) | collective-permute-done | bytes 262176 | tf_op jit(solution)/shard_map/branch/down_weights/ppermute | solution.py:55
  207.6 3.1 collective-permute-done.39
  212.9 12.7 %collective-permute-done.42 = bf16[128,2048]{1,0:T(8,128)(2,1)S(1)} collective-permute-done((bf16[128,2048]{1,0:T(8,128)(2,1)S(1)}, bf16[128,2048]{1,0:T(8,128)(2,1)S(1)}, u32[]{:S(2)}, u32[]{:S(2)}) %collective-permute-start.42) | collective-permute-done | bytes 524320 | tf_op jit(solution)/shard_map/branch/ppermute | solution.py:66
  225.7 2.4 fusion.112
  246.4 4.8 fusion.49
  251.2 2.9 constant_dynamic-update-slice_fusion.9
  262.3 2.7 fusion.50
  269.6 2.9 collective-permute-done.47
  274.8 2.6 fusion.51
  285.3 2.6 fusion.52
  292.5 4.8 collective-permute-done.51
  298.6 8.4 %convolution_convert_fusion.2 = bf16[2048,1024]{1,0:T(8,128)(2,1)} fusion(bf16[1024,2048]{1,0:T(8,128)(2,1)} %constant_dynamic-update-slice_fusion.1, bf16[1024,1024]{1,0:T(8,128)(2,1)S(1)} %get-tuple-element.561), kind=kOutput, calls=%fused_computation.4 | convolution fusion | flops 4297064448 | bytes 10485760 | tf_op jit(solution)/shard_map/mlp/up_grad/dot_general | solution.py:29
  307.0 5.4 collective-permute-done.53
  313.8 9.6 %convolution_convert_fusion.1 = bf16[1024,2048]{1,0:T(8,128)(2,1)} fusion(bf16[1024,1024]{1,0:T(8,128)(2,1)} %copy-done.38, bf16[1024,2048]{1,0:T(8,128)(2,1)} %all-gather.5.cloned.1.call-done), kind=kOutput, calls=%fused_computation.3 | convolution fusion | flops 4297064448 | bytes 10485760 | tf_op jit(solution)/shard_map/mlp/down_grad/dot_general | solution.py:29
  323.4 3.5 collective-permute-done.55
  331.7 2.6 collective-permute-start.58
  334.3 6.0 %convolution_convert_fusion = bf16[1024,2048]{1,0:T(8,128)(2,1)} fusion(bf16[1024,1024]{1,0:T(8,128)(2,1)S(1)} %copy-done.39, bf16[1024,2048]{1,0:T(8,128)(2,1)S(1)} %bitcast.220), kind=kOutput, calls=%fused_computation.2 | convolution fusion | flops 4297064448 | bytes 10485760 | tf_op jit(solution)/shard_map/d_branch_gather/output/dot_general | solution.py:25
  341.2 5.7 %collective-permute-done.58 = bf16[64,2048]{1,0:T(8,128)(2,1)} collective-permute-done((bf16[64,2048]{1,0:T(8,128)(2,1)}, bf16[64,2048]{1,0:T(8,128)(2,1)}, u32[]{:S(2)}, u32[]{:S(2)}) %collective-permute-start.58) | collective-permute-done | bytes 262176 | tf_op jit(solution)/shard_map/d_branch_gather/ppermute | solution.py:66
  347.4 5.0 collective-permute-done.59
  352.4 5.6 collective-permute-done.60
  359.1 4.4 collective-permute-done.61
  363.6 2.8 collective-permute-done.62
  370.1 4.2 mix_back.2.refs_6_
  375.0 4.7 mix_back.3
  379.7 7.1 %attend_back.4 = (f32[1024,256]{1,0:T(8,128)}, bf16[1024,256]{1,0:T(8,128)(2,1)}, bf16[1024,256]{1,0:T(8,128)(2,1)}) custom-call(s32[4]{0:T(128)} %get-tuple-element.372.heads_ref.at_ref, s32[1,1024]{1,0:T(1,128)} %bitcast.261, f32[2,1,1024]{2,1,0:T(1,128)} %get-tuple-element.489.log_ref, f32[2,1,1024]{2,1,0:T(1,128)} %get-tuple-element.568.delta_ref, ...), custom_call_target="tpu_custom_call" | custom-call | flops 1342177280 | bytes 5242880 | tf_op jit(solution)/shard_map/attention_back/attend_back/pallas_call | solution.py:447
  389.3 7.4 %attend_back.5 = (f32[1024,256]{1,0:T(8,128)}, bf16[1024,256]{1,0:T(8,128)(2,1)}, bf16[1024,256]{1,0:T(8,128)(2,1)}) custom-call(s32[4]{0:T(128)} %get-tuple-element.372.heads_ref.at_ref, s32[1,1024]{1,0:T(1,128)} %bitcast.262, f32[2,1,1024]{2,1,0:T(1,128)} %get-tuple-element.489.log_ref, f32[2,1,1024]{2,1,0:T(1,128)} %get-tuple-element.568.delta_ref, ...), custom_call_target="tpu_custom_call" | custom-call | flops 1342177280 | bytes 5242880 | tf_op jit(solution)/shard_map/attention_back/attend_back/pallas_call | solution.py:447
  398.1 7.9 %attend_back.6 = (f32[1024,256]{1,0:T(8,128)}, bf16[1024,256]{1,0:T(8,128)(2,1)}, bf16[1024,256]{1,0:T(8,128)(2,1)}) custom-call(s32[4]{0:T(128)} %get-tuple-element.372.heads_ref.at_ref, s32[1,1024]{1,0:T(1,128)} %bitcast.263, f32[2,1,1024]{2,1,0:T(1,128)} %get-tuple-element.489.log_ref, f32[2,1,1024]{2,1,0:T(1,128)} %get-tuple-element.568.delta_ref, ...), custom_call_target="tpu_custom_call" | custom-call | flops 1342177280 | bytes 5242880 | tf_op jit(solution)/shard_map/attention_back/attend_back/pallas_call | solution.py:447
  409.0 7.4 %attend_back.7 = (f32[1024,256]{1,0:T(8,128)}, bf16[1024,256]{1,0:T(8,128)(2,1)}, bf16[1024,256]{1,0:T(8,128)(2,1)}) custom-call(s32[4]{0:T(128)} %get-tuple-element.372.heads_ref.at_ref, s32[1,1024]{1,0:T(1,128)} %bitcast.264, f32[2,1,1024]{2,1,0:T(1,128)} %get-tuple-element.489.log_ref, f32[2,1,1024]{2,1,0:T(1,128)} %get-tuple-element.568.delta_ref, ...), custom_call_target="tpu_custom_call" | custom-call | flops 1342177280 | bytes 5242880 | tf_op jit(solution)/shard_map/attention_back/attend_back/pallas_call | solution.py:447
  416.4 5.0 collective-permute-done.70
  427.3 6.1 %mix_grad.1 = bf16[2,2,64,2048]{3,2,1,0:T(8,128)(2,1)} custom-call(s32[8]{0:T(128)} %add.534.at_ref, bf16[128,2048]{1,0:T(8,128)(2,1)} %copy-done.23, bf16[128,2048]{1,0:T(8,128)(2,1)} %copy-done.32, bf16[128,2048]{1,0:T(8,128)(2,1)} %copy-done.33, bf16[128,2048]{1,0:T(8,128)(2,1)} %copy-done.34, bf16[128,2048]{1,0:T(8,128)(2,1)} %copy-done.36, ...), custom_call_target="tpu_custom_call" | custom-call | tf_op jit(solution)/shard_map/out_grad/mix_grad/pallas_call | solution.py:141
  434.6 7.0 %collective-permute-done.72 = bf16[1024,256]{1,0:T(8,128)(2,1)} collective-permute-done((bf16[1024,256]{1,0:T(8,128)(2,1)S(1)}, bf16[1024,256]{1,0:T(8,128)(2,1)}, u32[]{:S(2)}, u32[]{:S(2)}) %collective-permute-start.72) | collective-permute-done | bytes 524320 | tf_op jit(solution)/shard_map/attention_back/ppermute | solution.py:55
  441.6 2.8 collective-permute-done.73
  448.1 8.3 %terms_out.3 = (bf16[4,128,2048]{2,1,0:T(8,128)(2,1)}, bf16[4,128,2048]{2,1,0:T(8,128)(2,1)}) custom-call(s32[8]{0:T(128)} %add.534.at_ref, bf16[1024,768]{1,0:T(8,128)(2,1)} %pad_maximum_fusion.mine.other, bf16[1024,768]{1,0:T(8,128)(2,1)} %pad_maximum_fusion.mine.other, bf16[2048,768]{1,0:T(8,128)(2,1)} %get-tuple-element.637.whole), custom_call_target="tpu_custom_call" | custom-call | flops 3221225472 | bytes 8388608 | tf_op jit(solution)/shard_map/d_normed/terms_out/pallas_call | solution.py:550
  456.4 4.4 collective-permute-done.77
  463.6 6.5 %convolution_convert_fusion.3 = bf16[2048,768]{1,0:T(8,128)(2,1)S(1)} fusion(bf16[1024,2048]{1,0:T(8,128)(2,1)} %get-tuple-element.648, bf16[1024,768]{1,0:T(8,128)(2,1)} %pad_maximum_fusion.mine.other), kind=kOutput, calls=%fused_computation.5 | convolution fusion | flops 3222798336 | bytes 8912896 | tf_op jit(solution)/shard_map/qkv_grad/dot_general | solution.py:29
  470.1 7.2 %collective-permute-done.78 = bf16[128,2048]{1,0:T(8,128)(2,1)S(1)} collective-permute-done((bf16[128,2048]{1,0:T(8,128)(2,1)S(1)}, bf16[128,2048]{1,0:T(8,128)(2,1)S(1)}, u32[]{:S(2)}, u32[]{:S(2)}) %collective-permute-start.78) | collective-permute-done | bytes 524320 | tf_op jit(solution)/shard_map/d_normed/ppermute | solution.py:66
  481.5 9.0 %collective-permute-done.80 = bf16[256,768]{1,0:T(8,128)(2,1)S(1)} collective-permute-done((bf16[256,768]{1,0:T(8,128)(2,1)S(1)}, bf16[256,768]{1,0:T(8,128)(2,1)S(1)}, u32[]{:S(2)}, u32[]{:S(2)}) %collective-permute-start.80) | collective-permute-done | bytes 393248 | tf_op jit(solution)/shard_map/qkv_grad/ppermute | solution.py:55
  491.4 2.6 collective-permute-done.79
  499.1 7.4 %norm_sums.1.first_ref = f32[2,2048]{1,0:T(2,128)} custom-call(bf16[4,128,2048]{2,1,0:T(8,128)(2,1)} %get-tuple-element.694.refs_0_, bf16[4,128,2048]{2,1,0:T(8,128)(2,1)} %get-tuple-element.661.refs_1_, bf16[128,2048]{1,0:T(8,128)(2,1)} %refs_2_.2, bf16[128,2048]{1,0:T(8,128)(2,1)} %collective-permute-done.1.refs_1_.refs_3_, ...), custom_call_target="tpu_custom_call" | custom-call | tf_op jit(solution)/shard_map/vector_grads/norm_sums/pallas_call | solution.py:591
  512.4 4.6 collective-permute-done.86
  525.5 2.4 collective-permute-start.91
  531.7 3.2 fusion.15
  538.9 6.2 %collective-permute-done.92.refs_2_ = bf16[2,80,768]{2,1,0:T(8,128)(2,1)S(1)} collective-permute-done((bf16[2,80,768]{2,1,0:T(8,128)(2,1)S(1)}, bf16[2,80,768]{2,1,0:T(8,128)(2,1)S(1)}, u32[]{:S(2)}, u32[]{:S(2)}) %collective-permute-start.92) | collective-permute-done | bytes 245792 | tf_op jit(solution)/shard_map/qkv_grad/ppermute | solution.py:55
  545.1 6.1 %collective-permute-done.93.refs_3_ = bf16[2,80,768]{2,1,0:T(8,128)(2,1)S(1)} collective-permute-done((bf16[2,80,768]{2,1,0:T(8,128)(2,1)S(1)}, bf16[2,80,768]{2,1,0:T(8,128)(2,1)S(1)}, u32[]{:S(2)}, u32[]{:S(2)}) %collective-permute-start.93) | collective-permute-done | bytes 245792 | tf_op jit(solution)/shard_map/qkv_grad/ppermute | solution.py:55
  (449 shorter events, 182.3 us)
Async XLA Ops:
  7.2 43.0 %all-gather.9.cloned.1.call-start = ((), (), s32[]{:S(2)}) async-start(), calls=%async_computation.10 | async-start | bytes 2621440 | tf_op jit(solution)/shard_map/down_weights/all_gather | solution.py:765
  12.4 166.3 %all-gather.5.cloned.1.call-start = ((), (), s32[]{:S(2)}) async-start(), calls=%async_computation.4 | async-start | bytes 4718592 | tf_op jit(solution)/shard_map/dy_gather/all_gather | solution.py:894
  12.4 14.9 %collective-permute-start.1 = (bf16[128,2048]{1,0:T(8,128)(2,1)}, bf16[128,2048]{1,0:T(8,128)(2,1)}, u32[]{:S(2)}, u32[]{:S(2)}) collective-permute-start(bf16[128,2048]{1,0:T(8,128)(2,1)} %refs_2_.2), channel_id=1, source_target_pairs={{0,4},{1,5},{4,6},{5,7},{6,2},{7,3},{2,0},{3,1},{8,12},{9,13},{12,... | collective-permute-start | bytes 1572872 | tf_op jit(solution)/shard_map/tokens_gather/ppermute | solution.py:66
  12.5 14.9 %collective-permute-start.2 = (bf16[128,2048]{1,0:T(8,128)(2,1)}, bf16[128,2048]{1,0:T(8,128)(2,1)S(1)}, u32[]{:S(2)}, u32[]{:S(2)}) collective-permute-start(bf16[128,2048]{1,0:T(8,128)(2,1)} %refs_2_.2), channel_id=1, source_target_pairs={{0,1},{1,0},{2,3},{3,2},{4,5},{5,4},{6,7},{7,6},{8,9},{9,8},{10,11... | collective-permute-start | bytes 1572872 | tf_op jit(solution)/shard_map/tokens_gather/ppermute | solution.py:55
  28.8 16.5 %collective-permute-start.4 = (bf16[2,64,768]{2,1,0:T(8,128)(2,1)S(1)}, bf16[2,64,768]{2,1,0:T(8,128)(2,1)S(1)}, u32[]{:S(2)}, u32[]{:S(2)}) collective-permute-start(bf16[2,64,768]{2,1,0:T(8,128)(2,1)S(1)} %get-tuple-element.377), channel_id=1, source_target_pairs={{0,4},{1,5},{2,6},{3,7},{4,0},{5,1},{6,2},{7,3},{8,12},{9,13},{10,... | collective-permute-start | bytes 589832 | tf_op jit(solution)/shard_map/qkv_weights/ppermute | solution.py:55
  31.9 17.0 %collective-permute-start.5 = (bf16[2,64,768]{2,1,0:T(8,128)(2,1)S(1)}, bf16[2,64,768]{2,1,0:T(8,128)(2,1)S(1)}, u32[]{:S(2)}, u32[]{:S(2)}) collective-permute-start(bf16[2,64,768]{2,1,0:T(8,128)(2,1)S(1)} %get-tuple-element.378), channel_id=1, source_target_pairs={{0,6},{1,7},{2,4},{3,5},{4,2},{5,3},{6,0},{7,1},{8,14},{9,15},{10,... | collective-permute-start | bytes 589832 | tf_op jit(solution)/shard_map/qkv_weights/ppermute | solution.py:55
  37.3 12.9 %collective-permute-start.9 = (bf16[8,14,64]{2,1,0:T(8,128)(2,1)S(1)}, bf16[8,14,64]{2,1,0:T(8,128)(2,1)S(1)}, u32[]{:S(2)}, u32[]{:S(2)}) collective-permute-start(bf16[8,14,64]{2,1,0:T(8,128)(2,1)S(1)} %constant_dynamic-update-slice_fusion.12), channel_id=1, source_target_pairs={{0,4},{1,5},{4,6},{5,7},{6,2},{7,3},{2,0},{3,1},{8,12},{9,13},{12,... | collective-permute-start | bytes 43016 | tf_op jit(solution)/shard_map/vectors/ppermute | solution.py:66
  50.2 14.2 %collective-permute-start.16 = (bf16[128,2048]{1,0:T(8,128)(2,1)}, bf16[128,2048]{1,0:T(8,128)(2,1)}, u32[]{:S(2)}, u32[]{:S(2)}) collective-permute-start(bf16[128,2048]{1,0:T(8,128)(2,1)} %collective-permute-done.1.refs_1_.refs_3_), channel_id=1, source_target_pairs={{0,4},{1,5},{4,6},{5,7},{6,2},{7,3},{2,0},{3,1},{8,12},{9,13},{12,... | collective-permute-start | bytes 1572872 | tf_op jit(solution)/shard_map/tokens_gather/ppermute | solution.py:66
  50.9 15.7 %collective-permute-start.12 = (bf16[4,64,768]{2,1,0:T(8,128)(2,1)S(1)}, bf16[4,64,768]{2,1,0:T(8,128)(2,1)}, u32[]{:S(2)}, u32[]{:S(2)}) collective-permute-start(bf16[4,64,768]{2,1,0:T(8,128)(2,1)S(1)} %get-tuple-element.412.refs_11_), channel_id=1, source_target_pairs={{0,16},{8,24},{16,0},{24,8},{1,17},{9,25},{17,1},{25,9},{2,18},{10... | collective-permute-start | bytes 1179656 | tf_op jit(solution)/shard_map/qkv_weights/ppermute | solution.py:55
  52.4 15.7 %collective-permute-start.11 = (bf16[4,64,768]{2,1,0:T(8,128)(2,1)}, bf16[4,64,768]{2,1,0:T(8,128)(2,1)}, u32[]{:S(2)}, u32[]{:S(2)}) collective-permute-start(bf16[4,64,768]{2,1,0:T(8,128)(2,1)} %get-tuple-element.413.refs_12_), channel_id=1, source_target_pairs={{0,8},{8,0},{16,24},{24,16},{1,9},{9,1},{17,25},{25,17},{2,10},{10... | collective-permute-start | bytes 1179656 | tf_op jit(solution)/shard_map/qkv_weights/ppermute | solution.py:55
  66.6 15.9 %collective-permute-start.14 = (bf16[4,64,768]{2,1,0:T(8,128)(2,1)}, bf16[4,64,768]{2,1,0:T(8,128)(2,1)}, u32[]{:S(2)}, u32[]{:S(2)}) collective-permute-start(bf16[4,64,768]{2,1,0:T(8,128)(2,1)} %collective-permute-done.12.refs_15_), channel_id=1, source_target_pairs={{0,8},{8,0},{16,24},{24,16},{1,9},{9,1},{17,25},{25,17},{2,10},{10... | collective-permute-start | bytes 1179656 | tf_op jit(solution)/shard_map/qkv_weights/ppermute | solution.py:55
  68.1 16.1 %collective-permute-start.15 = (bf16[4,64,768]{2,1,0:T(8,128)(2,1)}, bf16[4,64,768]{2,1,0:T(8,128)(2,1)}, u32[]{:S(2)}, u32[]{:S(2)}) collective-permute-start(bf16[4,64,768]{2,1,0:T(8,128)(2,1)} %collective-permute-done.11.refs_14_), channel_id=1, source_target_pairs={{0,16},{8,24},{16,0},{24,8},{1,17},{9,25},{17,1},{25,9},{2,18},{10... | collective-permute-start | bytes 1179656 | tf_op jit(solution)/shard_map/qkv_weights/ppermute | solution.py:55
  69.3 14.9 %collective-permute-start.18 = (bf16[128,2048]{1,0:T(8,128)(2,1)}, bf16[128,2048]{1,0:T(8,128)(2,1)}, u32[]{:S(2)}, u32[]{:S(2)}) collective-permute-start(bf16[128,2048]{1,0:T(8,128)(2,1)} %collective-permute-done.16.refs_2_.refs_4_), channel_id=1, source_target_pairs={{0,4},{1,5},{4,6},{5,7},{6,2},{7,3},{2,0},{3,1},{8,12},{9,13},{12,... | collective-permute-start | bytes 1572872 | tf_op jit(solution)/shard_map/tokens_gather/ppermute | solution.py:66
  85.2 19.2 %collective-permute-start.24 = (bf16[64,2048]{1,0:T(8,128)(2,1)S(1)}, bf16[64,2048]{1,0:T(8,128)(2,1)S(1)}, u32[]{:S(2)}, u32[]{:S(2)}) collective-permute-start(bf16[64,2048]{1,0:T(8,128)(2,1)S(1)} %copy-done.8), channel_id=1, source_target_pairs={{0,8},{8,0},{16,24},{24,16},{1,9},{9,1},{17,25},{25,17},{2,10},{10... | collective-permute-start | bytes 786440 | tf_op jit(solution)/shard_map/out_weights/ppermute | solution.py:55
  86.8 17.6 %collective-permute-start.25 = (bf16[64,2048]{1,0:T(8,128)(2,1)S(1)}, bf16[64,2048]{1,0:T(8,128)(2,1)S(1)}, u32[]{:S(2)}, u32[]{:S(2)}) collective-permute-start(bf16[64,2048]{1,0:T(8,128)(2,1)S(1)} %copy-done.8), channel_id=1, source_target_pairs={{0,16},{8,24},{16,0},{24,8},{1,17},{9,25},{17,1},{25,9},{2,18},{10... | collective-permute-start | bytes 786440 | tf_op jit(solution)/shard_map/out_weights/ppermute | solution.py:55
  87.7 16.7 %collective-permute-start.26 = (bf16[64,2048]{1,0:T(8,128)(2,1)S(1)}, bf16[64,2048]{1,0:T(8,128)(2,1)S(1)}, u32[]{:S(2)}, u32[]{:S(2)}) collective-permute-start(bf16[64,2048]{1,0:T(8,128)(2,1)S(1)} %copy-done.8), channel_id=1, source_target_pairs={{0,24},{8,16},{16,8},{24,0},{1,25},{9,17},{17,9},{25,1},{2,26},{10... | collective-permute-start | bytes 786440 | tf_op jit(solution)/shard_map/out_weights/ppermute | solution.py:55
  104.4 28.3 %collective-permute-start.27 = (bf16[2,1024,256]{2,1,0:T(8,128)(2,1)}, bf16[2,1024,256]{2,1,0:T(8,128)(2,1)}, u32[]{:S(2)}, u32[]{:S(2)}) collective-permute-start(bf16[2,1024,256]{2,1,0:T(8,128)(2,1)} %get-tuple-element.432.refs_0_), channel_id=1, source_target_pairs={{0,8},{8,0},{16,24},{24,16},{1,9},{9,1},{17,25},{25,17},{2,10},{10... | collective-permute-start | bytes 3145736 | tf_op jit(solution)/shard_map/kv_gather/ppermute | solution.py:55
  106.1 26.6 %collective-permute-start.28 = (bf16[2,1024,256]{2,1,0:T(8,128)(2,1)}, bf16[2,1024,256]{2,1,0:T(8,128)(2,1)}, u32[]{:S(2)}, u32[]{:S(2)}) collective-permute-start(bf16[2,1024,256]{2,1,0:T(8,128)(2,1)} %get-tuple-element.432.refs_0_), channel_id=1, source_target_pairs={{0,16},{8,24},{16,0},{24,8},{1,17},{9,25},{17,1},{25,9},{2,18},{10... | collective-permute-start | bytes 3145736 | tf_op jit(solution)/shard_map/kv_gather/ppermute | solution.py:55
  106.4 12.8 %collective-permute-start.29 = (bf16[2,64,1024]{2,1,0:T(8,128)(2,1)S(1)}, bf16[2,64,1024]{2,1,0:T(8,128)(2,1)S(1)}, u32[]{:S(2)}, u32[]{:S(2)}) collective-permute-start(bf16[2,64,1024]{2,1,0:T(8,128)(2,1)S(1)} %get-tuple-element.438), channel_id=1, source_target_pairs={{0,2},{1,3},{2,0},{3,1},{4,6},{5,7},{6,4},{7,5},{8,10},{9,11},{10,... | collective-permute-start | bytes 786440 | tf_op jit(solution)/shard_map/up_weights/ppermute | solution.py:55
  109.1 19.3 %collective-permute-start.30 = (bf16[2,64,1024]{2,1,0:T(8,128)(2,1)S(1)}, bf16[2,64,1024]{2,1,0:T(8,128)(2,1)S(1)}, u32[]{:S(2)}, u32[]{:S(2)}) collective-permute-start(bf16[2,64,1024]{2,1,0:T(8,128)(2,1)S(1)} %get-tuple-element.439), channel_id=1, source_target_pairs={{0,4},{1,5},{2,6},{3,7},{4,0},{5,1},{6,2},{7,3},{8,12},{9,13},{10,... | collective-permute-start | bytes 786440 | tf_op jit(solution)/shard_map/up_weights/ppermute | solution.py:55
  110.4 22.3 %collective-permute-start.31 = (bf16[2,64,1024]{2,1,0:T(8,128)(2,1)S(1)}, bf16[2,64,1024]{2,1,0:T(8,128)(2,1)S(1)}, u32[]{:S(2)}, u32[]{:S(2)}) collective-permute-start(bf16[2,64,1024]{2,1,0:T(8,128)(2,1)S(1)} %get-tuple-element.440), channel_id=1, source_target_pairs={{0,6},{1,7},{2,4},{3,5},{4,2},{5,3},{6,0},{7,1},{8,14},{9,15},{10,... | collective-permute-start | bytes 786440 | tf_op jit(solution)/shard_map/up_weights/ppermute | solution.py:55
  132.7 113.7 %all-gather.7.cloned.1.call-start = ((), (), s32[]{:S(2)}) async-start(), calls=%async_computation.5 | async-start | bytes 5242880 | tf_op jit(solution)/shard_map/up_weights/all_gather | solution.py:916
  134.8 14.4 %collective-permute-start.32 = (bf16[1,1024,256]{2,1,0:T(8,128)(2,1)S(1)}, bf16[1,1024,256]{2,1,0:T(8,128)(2,1)S(1)}, u32[]{:S(2)}, u32[]{:S(2)}) collective-permute-start(bf16[1,1024,256]{2,1,0:T(8,128)(2,1)S(1)} %slice.287), channel_id=1, source_target_pairs={{0,8},{8,0},{16,24},{24,16},{1,9},{9,1},{17,25},{25,17},{2,10},{10... | collective-permute-start | bytes 1572872 | tf_op jit(solution)/shard_map/kv_gather/ppermute | solution.py:55
  137.0 14.1 %collective-permute-start.33 = (bf16[1,1024,256]{2,1,0:T(8,128)(2,1)S(1)}, bf16[1,1024,256]{2,1,0:T(8,128)(2,1)S(1)}, u32[]{:S(2)}, u32[]{:S(2)}) collective-permute-start(bf16[1,1024,256]{2,1,0:T(8,128)(2,1)S(1)} %slice.288), channel_id=1, source_target_pairs={{0,16},{8,24},{16,0},{24,8},{1,17},{9,25},{17,1},{25,9},{2,18},{10... | collective-permute-start | bytes 1572872 | tf_op jit(solution)/shard_map/kv_gather/ppermute | solution.py:55
  153.0 15.5 %collective-permute-start.35 = (bf16[128,2048]{1,0:T(8,128)(2,1)S(1)}, bf16[128,2048]{1,0:T(8,128)(2,1)S(1)}, u32[]{:S(2)}, u32[]{:S(2)}) collective-permute-start(bf16[128,2048]{1,0:T(8,128)(2,1)S(1)} %slice.289.refs_0_), channel_id=1, source_target_pairs={{0,8},{8,0},{16,24},{24,16},{1,9},{9,1},{17,25},{25,17},{2,10},{10... | collective-permute-start | bytes 1572872 | tf_op jit(solution)/shard_map/down_weights/ppermute | solution.py:55
  154.0 14.5 %collective-permute-start.36 = (bf16[128,2048]{1,0:T(8,128)(2,1)S(1)}, bf16[128,2048]{1,0:T(8,128)(2,1)S(1)}, u32[]{:S(2)}, u32[]{:S(2)}) collective-permute-start(bf16[128,2048]{1,0:T(8,128)(2,1)S(1)} %slice.289.refs_0_), channel_id=1, source_target_pairs={{0,16},{8,24},{16,0},{24,8},{1,17},{9,25},{17,1},{25,9},{2,18},{10... | collective-permute-start | bytes 1572872 | tf_op jit(solution)/shard_map/down_weights/ppermute | solution.py:55
  174.2 192.2 %reduce-scatter.5.cloned.1.call-start = ((), (), s32[]{:S(2)}) async-start(), calls=%async_computation.6 | async-start | bytes 5242880 | tf_op jit(solution)/shard_map/up_grad/reduce_scatter | solution.py:1057
  180.0 15.0 %collective-permute-start.38 = (bf16[128,2048]{1,0:T(8,128)(2,1)S(1)}, bf16[128,2048]{1,0:T(8,128)(2,1)S(1)}, u32[]{:S(2)}, u32[]{:S(2)}) collective-permute-start(bf16[128,2048]{1,0:T(8,128)(2,1)S(1)} %fusion.48), channel_id=1, source_target_pairs={{0,4},{1,5},{4,6},{5,7},{6,2},{7,3},{2,0},{3,1},{8,12},{9,13},{12,... | collective-permute-start | bytes 1572872 | tf_op jit(solution)/shard_map/branch/ppermute | solution.py:66
  196.5 14.2 %collective-permute-start.39 = (bf16[128,2048]{1,0:T(8,128)(2,1)S(1)}, bf16[128,2048]{1,0:T(8,128)(2,1)S(1)}, u32[]{:S(2)}, u32[]{:S(2)}) collective-permute-start(bf16[128,2048]{1,0:T(8,128)(2,1)S(1)} %fusion.38), channel_id=1, source_target_pairs={{0,4},{1,5},{4,6},{5,7},{6,2},{7,3},{2,0},{3,1},{8,12},{9,13},{12,... | collective-permute-start | bytes 1572872 | tf_op jit(solution)/shard_map/branch/ppermute | solution.py:66
  212.5 13.2 %collective-permute-start.42 = (bf16[128,2048]{1,0:T(8,128)(2,1)S(1)}, bf16[128,2048]{1,0:T(8,128)(2,1)S(1)}, u32[]{:S(2)}, u32[]{:S(2)}) collective-permute-start(bf16[128,2048]{1,0:T(8,128)(2,1)S(1)} %fusion.37), channel_id=1, source_target_pairs={{0,4},{1,5},{4,6},{5,7},{6,2},{7,3},{2,0},{3,1},{8,12},{9,13},{12,... | collective-permute-start | bytes 1572872 | tf_op jit(solution)/shard_map/branch/ppermute | solution.py:66
  229.8 12.4 %collective-permute-start.43 = (bf16[128,2048]{1,0:T(8,128)(2,1)}, bf16[128,2048]{1,0:T(8,128)(2,1)}, u32[]{:S(2)}, u32[]{:S(2)}) collective-permute-start(bf16[128,2048]{1,0:T(8,128)(2,1)} %get-tuple-element.492), channel_id=1, source_target_pairs={{0,4},{1,5},{4,6},{5,7},{6,2},{7,3},{2,0},{3,1},{8,12},{9,13},{12,... | collective-permute-start | bytes 1572872 | tf_op jit(solution)/shard_map/mlp/ppermute | solution.py:66
  229.8 12.3 %collective-permute-start.44 = (bf16[128,2048]{1,0:T(8,128)(2,1)}, bf16[128,2048]{1,0:T(8,128)(2,1)}, u32[]{:S(2)}, u32[]{:S(2)}) collective-permute-start(bf16[128,2048]{1,0:T(8,128)(2,1)} %get-tuple-element.492), channel_id=1, source_target_pairs={{0,1},{1,0},{2,3},{3,2},{4,5},{5,4},{6,7},{7,6},{8,9},{9,8},{10,11... | collective-permute-start | bytes 1572872 | tf_op jit(solution)/shard_map/mlp/ppermute | solution.py:55
  242.1 15.1 %collective-permute-start.45 = (bf16[128,2048]{1,0:T(8,128)(2,1)}, bf16[128,2048]{1,0:T(8,128)(2,1)S(1)}, u32[]{:S(2)}, u32[]{:S(2)}) collective-permute-start(bf16[128,2048]{1,0:T(8,128)(2,1)} %collective-permute-done.43), channel_id=1, source_target_pairs={{0,4},{1,5},{4,6},{5,7},{6,2},{7,3},{2,0},{3,1},{8,12},{9,13},{12,... | collective-permute-start | bytes 1572872 | tf_op jit(solution)/shard_map/mlp/ppermute | solution.py:66
  242.3 14.9 %collective-permute-start.46 = (bf16[128,2048]{1,0:T(8,128)(2,1)}, bf16[128,2048]{1,0:T(8,128)(2,1)S(1)}, u32[]{:S(2)}, u32[]{:S(2)}) collective-permute-start(bf16[128,2048]{1,0:T(8,128)(2,1)} %collective-permute-done.43), channel_id=1, source_target_pairs={{0,1},{1,0},{2,3},{3,2},{4,5},{5,4},{6,7},{7,6},{8,9},{9,8},{10,11... | collective-permute-start | bytes 1572872 | tf_op jit(solution)/shard_map/mlp/ppermute | solution.py:55
  257.2 15.3 %collective-permute-start.47 = (bf16[128,2048]{1,0:T(8,128)(2,1)S(1)}, bf16[128,2048]{1,0:T(8,128)(2,1)S(1)}, u32[]{:S(2)}, u32[]{:S(2)}) collective-permute-start(bf16[128,2048]{1,0:T(8,128)(2,1)S(1)} %collective-permute-done.45), channel_id=1, source_target_pairs={{0,4},{1,5},{4,6},{5,7},{6,2},{7,3},{2,0},{3,1},{8,12},{9,13},{12,... | collective-permute-start | bytes 1572872 | tf_op jit(solution)/shard_map/mlp/ppermute | solution.py:66
  259.3 13.2 %collective-permute-start.48 = (bf16[128,2048]{1,0:T(8,128)(2,1)S(1)}, bf16[128,2048]{1,0:T(8,128)(2,1)S(1)}, u32[]{:S(2)}, u32[]{:S(2)}) collective-permute-start(bf16[128,2048]{1,0:T(8,128)(2,1)S(1)} %collective-permute-done.45), channel_id=1, source_target_pairs={{0,1},{1,0},{2,3},{3,2},{4,5},{5,4},{6,7},{7,6},{8,9},{9,8},{10,11... | collective-permute-start | bytes 1572872 | tf_op jit(solution)/shard_map/mlp/ppermute | solution.py:55
  282.1 15.2 %collective-permute-start.51 = (bf16[128,2048]{1,0:T(8,128)(2,1)S(1)}, bf16[128,2048]{1,0:T(8,128)(2,1)S(1)}, u32[]{:S(2)}, u32[]{:S(2)}) collective-permute-start(bf16[128,2048]{1,0:T(8,128)(2,1)S(1)} %add_convert_fusion.8), channel_id=1, source_target_pairs={{0,4},{1,5},{4,6},{5,7},{6,2},{7,3},{2,0},{3,1},{8,12},{9,13},{12,... | collective-permute-start | bytes 1572872 | tf_op jit(solution)/shard_map/mlp/ppermute | solution.py:66
  283.7 13.6 %collective-permute-start.52 = (bf16[128,2048]{1,0:T(8,128)(2,1)S(1)}, bf16[128,2048]{1,0:T(8,128)(2,1)S(1)}, u32[]{:S(2)}, u32[]{:S(2)}) collective-permute-start(bf16[128,2048]{1,0:T(8,128)(2,1)S(1)} %convolution_convert_fusion.6), channel_id=1, source_target_pairs={{0,1},{1,0},{2,3},{3,2},{4,5},{5,4},{6,7},{7,6},{8,9},{9,8},{10,11... | collective-permute-start | bytes 1572872 | tf_op jit(solution)/shard_map/mlp/ppermute | solution.py:55
  298.4 14.1 %collective-permute-start.53 = (bf16[128,2048]{1,0:T(8,128)(2,1)}, bf16[128,2048]{1,0:T(8,128)(2,1)S(1)}, u32[]{:S(2)}, u32[]{:S(2)}) collective-permute-start(bf16[128,2048]{1,0:T(8,128)(2,1)} %add_convert_fusion.7), channel_id=1, source_target_pairs={{0,4},{1,5},{4,6},{5,7},{6,2},{7,3},{2,0},{3,1},{8,12},{9,13},{12,... | collective-permute-start | bytes 1572872 | tf_op jit(solution)/shard_map/mlp/ppermute | solution.py:66
  298.6 13.9 %collective-permute-start.54 = (bf16[128,2048]{1,0:T(8,128)(2,1)S(1)}, bf16[128,2048]{1,0:T(8,128)(2,1)S(1)}, u32[]{:S(2)}, u32[]{:S(2)}) collective-permute-start(bf16[128,2048]{1,0:T(8,128)(2,1)S(1)} %convolution_convert_fusion.4), channel_id=1, source_target_pairs={{0,1},{1,0},{2,3},{3,2},{4,5},{5,4},{6,7},{7,6},{8,9},{9,8},{10,11... | collective-permute-start | bytes 1572872 | tf_op jit(solution)/shard_map/mlp/ppermute | solution.py:55
  312.5 109.0 %reduce-scatter.7.cloned.1.call-start = ((), (), s32[]{:S(2)}) async-start(), calls=%async_computation.7 | async-start | bytes 4718592 | tf_op jit(solution)/shard_map/d_branch_gather/output/reduce_scatter | solution.py:1090
  313.6 13.3 %collective-permute-start.55 = (bf16[128,2048]{1,0:T(8,128)(2,1)}, bf16[128,2048]{1,0:T(8,128)(2,1)S(1)}, u32[]{:S(2)}, u32[]{:S(2)}) collective-permute-start(bf16[128,2048]{1,0:T(8,128)(2,1)} %add_convert_fusion.6), channel_id=1, source_target_pairs={{0,4},{1,5},{4,6},{5,7},{6,2},{7,3},{2,0},{3,1},{8,12},{9,13},{12,... | collective-permute-start | bytes 1572872 | tf_op jit(solution)/shard_map/mlp/ppermute | solution.py:66
  313.7 13.2 %collective-permute-start.56 = (bf16[128,2048]{1,0:T(8,128)(2,1)S(1)}, bf16[128,2048]{1,0:T(8,128)(2,1)}, u32[]{:S(2)}, u32[]{:S(2)}) collective-permute-start(bf16[128,2048]{1,0:T(8,128)(2,1)S(1)} %convolution_convert_fusion.10), channel_id=1, source_target_pairs={{0,1},{1,0},{2,3},{3,2},{4,5},{5,4},{6,7},{7,6},{8,9},{9,8},{10,11... | collective-permute-start | bytes 1572872 | tf_op jit(solution)/shard_map/mlp/ppermute | solution.py:55
  331.7 15.2 %collective-permute-start.58 = (bf16[64,2048]{1,0:T(8,128)(2,1)}, bf16[64,2048]{1,0:T(8,128)(2,1)}, u32[]{:S(2)}, u32[]{:S(2)}) collective-permute-start(bf16[64,2048]{1,0:T(8,128)(2,1)} %get-tuple-element.738), channel_id=1, source_target_pairs={{0,4},{1,5},{4,6},{5,7},{6,2},{7,3},{2,0},{3,1},{8,12},{9,13},{12,... | collective-permute-start | bytes 786440 | tf_op jit(solution)/shard_map/d_branch_gather/ppermute | solution.py:66
  366.5 143.4 %reduce-scatter.9.cloned.1.call-start = ((), (), s32[]{:S(2)}) async-start(), calls=%async_computation.8 | async-start | bytes 5242880 | tf_op jit(solution)/shard_map/down_grad/reduce_scatter | solution.py:1057
  369.9 26.8 %collective-permute-start.69 = (bf16[4,64,1024]{2,1,0:T(8,128)(2,1)S(1)}, bf16[4,64,1024]{2,1,0:T(8,128)(2,1)S(1)}, u32[]{:S(2)}, u32[]{:S(2)}) collective-permute-start(bf16[4,64,1024]{2,1,0:T(8,128)(2,1)S(1)} %get-tuple-element.732), channel_id=1, source_target_pairs={{0,1},{1,0},{2,3},{3,2},{4,5},{5,4},{6,7},{7,6},{8,9},{9,8},{10,11... | collective-permute-start | bytes 1572872 | tf_op jit(solution)/shard_map/up_grad/ppermute | solution.py:55
  386.8 19.2 %collective-permute-start.67 = (bf16[1024,256]{1,0:T(8,128)(2,1)}, bf16[1024,256]{1,0:T(8,128)(2,1)S(1)}, u32[]{:S(2)}, u32[]{:S(2)}) collective-permute-start(bf16[1024,256]{1,0:T(8,128)(2,1)} %get-tuple-element.573), channel_id=1, source_target_pairs={{0,8},{8,0},{16,24},{24,16},{1,9},{9,1},{17,25},{25,17},{2,10},{10... | collective-permute-start | bytes 1572872 | tf_op jit(solution)/shard_map/attention_back/ppermute | solution.py:55
  387.9 18.1 %collective-permute-start.68 = (bf16[1024,256]{1,0:T(8,128)(2,1)}, bf16[1024,256]{1,0:T(8,128)(2,1)S(1)}, u32[]{:S(2)}, u32[]{:S(2)}) collective-permute-start(bf16[1024,256]{1,0:T(8,128)(2,1)} %get-tuple-element.574), channel_id=1, source_target_pairs={{0,16},{8,24},{16,0},{24,8},{1,17},{9,25},{17,1},{25,9},{2,18},{10... | collective-permute-start | bytes 1572872 | tf_op jit(solution)/shard_map/attention_back/ppermute | solution.py:55
  407.4 14.0 %collective-permute-start.70 = (bf16[1024,256]{1,0:T(8,128)(2,1)}, bf16[1024,256]{1,0:T(8,128)(2,1)S(1)}, u32[]{:S(2)}, u32[]{:S(2)}) collective-permute-start(bf16[1024,256]{1,0:T(8,128)(2,1)} %get-tuple-element.599), channel_id=1, source_target_pairs={{0,8},{8,0},{16,24},{24,16},{1,9},{9,1},{17,25},{25,17},{2,10},{10... | collective-permute-start | bytes 1572872 | tf_op jit(solution)/shard_map/attention_back/ppermute | solution.py:55
  408.0 13.5 %collective-permute-start.71 = (bf16[1024,256]{1,0:T(8,128)(2,1)S(1)}, bf16[1024,256]{1,0:T(8,128)(2,1)}, u32[]{:S(2)}, u32[]{:S(2)}) collective-permute-start(bf16[1024,256]{1,0:T(8,128)(2,1)S(1)} %add_convert_fusion.4), channel_id=1, source_target_pairs={{0,16},{8,24},{16,0},{24,8},{1,17},{9,25},{17,1},{25,9},{2,18},{10... | collective-permute-start | bytes 1572872 | tf_op jit(solution)/shard_map/attention_back/ppermute | solution.py:55
  421.6 132.3 %reduce-scatter.11.cloned.1.call-start = ((), (), s32[]{:S(2)}) async-start(), calls=%async_computation.9 | async-start | bytes 1310720 | tf_op jit(solution)/shard_map/out_grad/reduce_scatter | solution.py:1057
  421.6 20.0 %collective-permute-start.72 = (bf16[1024,256]{1,0:T(8,128)(2,1)S(1)}, bf16[1024,256]{1,0:T(8,128)(2,1)}, u32[]{:S(2)}, u32[]{:S(2)}) collective-permute-start(bf16[1024,256]{1,0:T(8,128)(2,1)S(1)} %add_convert_fusion.5), channel_id=1, source_target_pairs={{0,8},{8,0},{16,24},{24,16},{1,9},{9,1},{17,25},{25,17},{2,10},{10... | collective-permute-start | bytes 1572872 | tf_op jit(solution)/shard_map/attention_back/ppermute | solution.py:55
  423.2 21.3 %collective-permute-start.73 = (bf16[1024,256]{1,0:T(8,128)(2,1)}, bf16[1024,256]{1,0:T(8,128)(2,1)}, u32[]{:S(2)}, u32[]{:S(2)}) collective-permute-start(bf16[1024,256]{1,0:T(8,128)(2,1)} %get-tuple-element.622), channel_id=1, source_target_pairs={{0,16},{8,24},{16,0},{24,8},{1,17},{9,25},{17,1},{25,9},{2,18},{10... | collective-permute-start | bytes 1572872 | tf_op jit(solution)/shard_map/attention_back/ppermute | solution.py:55
  423.7 23.5 %collective-permute-start.74 = (bf16[2,64,1024]{2,1,0:T(8,128)(2,1)}, bf16[2,64,1024]{2,1,0:T(8,128)(2,1)S(1)}, u32[]{:S(2)}, u32[]{:S(2)}) collective-permute-start(bf16[2,64,1024]{2,1,0:T(8,128)(2,1)} %get-tuple-element.624), channel_id=1, source_target_pairs={{0,2},{1,3},{2,0},{3,1},{4,6},{5,7},{6,4},{7,5},{8,10},{9,11},{10,... | collective-permute-start | bytes 786440 | tf_op jit(solution)/shard_map/up_grad/ppermute | solution.py:55
  425.0 22.3 %collective-permute-start.75 = (bf16[2,64,1024]{2,1,0:T(8,128)(2,1)S(1)}, bf16[2,64,1024]{2,1,0:T(8,128)(2,1)S(1)}, u32[]{:S(2)}, u32[]{:S(2)}) collective-permute-start(bf16[2,64,1024]{2,1,0:T(8,128)(2,1)S(1)} %get-tuple-element.625), channel_id=1, source_target_pairs={{0,4},{1,5},{2,6},{3,7},{4,0},{5,1},{6,2},{7,3},{8,12},{9,13},{10,... | collective-permute-start | bytes 786440 | tf_op jit(solution)/shard_map/up_grad/ppermute | solution.py:55
  426.3 21.8 %collective-permute-start.76 = (bf16[2,64,1024]{2,1,0:T(8,128)(2,1)S(1)}, bf16[2,64,1024]{2,1,0:T(8,128)(2,1)S(1)}, u32[]{:S(2)}, u32[]{:S(2)}) collective-permute-start(bf16[2,64,1024]{2,1,0:T(8,128)(2,1)S(1)} %get-tuple-element.626), channel_id=1, source_target_pairs={{0,6},{1,7},{2,4},{3,5},{4,2},{5,3},{6,0},{7,1},{8,14},{9,15},{10,... | collective-permute-start | bytes 786440 | tf_op jit(solution)/shard_map/up_grad/ppermute | solution.py:55
  462.2 15.1 %collective-permute-start.78 = (bf16[128,2048]{1,0:T(8,128)(2,1)S(1)}, bf16[128,2048]{1,0:T(8,128)(2,1)S(1)}, u32[]{:S(2)}, u32[]{:S(2)}) collective-permute-start(bf16[128,2048]{1,0:T(8,128)(2,1)S(1)} %fusion.53), channel_id=1, source_target_pairs={{0,4},{1,5},{4,6},{5,7},{6,2},{7,3},{2,0},{3,1},{8,12},{9,13},{12,... | collective-permute-start | bytes 1572872 | tf_op jit(solution)/shard_map/d_normed/ppermute | solution.py:66
  478.8 15.2 %collective-permute-start.79 = (bf16[128,2048]{1,0:T(8,128)(2,1)S(1)}, bf16[128,2048]{1,0:T(8,128)(2,1)S(1)}, u32[]{:S(2)}, u32[]{:S(2)}) collective-permute-start(bf16[128,2048]{1,0:T(8,128)(2,1)S(1)} %fusion.35), channel_id=1, source_target_pairs={{0,4},{1,5},{4,6},{5,7},{6,2},{7,3},{2,0},{3,1},{8,12},{9,13},{12,... | collective-permute-start | bytes 1572872 | tf_op jit(solution)/shard_map/d_normed/ppermute | solution.py:66
  495.3 14.6 %collective-permute-start.85 = (bf16[128,2048]{1,0:T(8,128)(2,1)S(1)}, bf16[128,2048]{1,0:T(8,128)(2,1)}, u32[]{:S(2)}, u32[]{:S(2)}) collective-permute-start(bf16[128,2048]{1,0:T(8,128)(2,1)S(1)} %fusion.34), channel_id=1, source_target_pairs={{0,4},{1,5},{4,6},{5,7},{6,2},{7,3},{2,0},{3,1},{8,12},{9,13},{12,... | collective-permute-start | bytes 1572872 | tf_op jit(solution)/shard_map/d_normed/ppermute | solution.py:66
  495.7 24.1 %collective-permute-start.83 = (bf16[512,768]{1,0:T(8,128)(2,1)S(1)}, bf16[512,768]{1,0:T(8,128)(2,1)}, u32[]{:S(2)}, u32[]{:S(2)}) collective-permute-start(bf16[512,768]{1,0:T(8,128)(2,1)S(1)} %pad_maximum_fusion.1), channel_id=1, source_target_pairs={{0,8},{8,0},{16,24},{24,16},{1,9},{9,1},{17,25},{25,17},{2,10},{10... | collective-permute-start | bytes 2359304 | tf_op jit(solution)/shard_map/qkv_grad/ppermute | solution.py:55
  497.8 21.9 %collective-permute-start.84 = (bf16[512,768]{1,0:T(8,128)(2,1)}, bf16[512,768]{1,0:T(8,128)(2,1)}, u32[]{:S(2)}, u32[]{:S(2)}) collective-permute-start(bf16[512,768]{1,0:T(8,128)(2,1)} %pad_maximum_fusion.2), channel_id=1, source_target_pairs={{0,16},{8,24},{16,0},{24,8},{1,17},{9,25},{17,1},{25,9},{2,18},{10... | collective-permute-start | bytes 2359304 | tf_op jit(solution)/shard_map/qkv_grad/ppermute | solution.py:55
  525.5 13.4 %collective-permute-start.91 = (bf16[2,80,768]{2,1,0:T(8,128)(2,1)S(1)}, bf16[2,80,768]{2,1,0:T(8,128)(2,1)S(1)}, u32[]{:S(2)}, u32[]{:S(2)}) collective-permute-start(bf16[2,80,768]{2,1,0:T(8,128)(2,1)S(1)} %get-tuple-element.698), channel_id=1, source_target_pairs={{0,2},{1,3},{2,0},{3,1},{4,6},{5,7},{6,4},{7,5},{8,10},{9,11},{10,... | collective-permute-start | bytes 737288 | tf_op jit(solution)/shard_map/qkv_grad/ppermute | solution.py:55
  527.9 17.2 %collective-permute-start.92 = (bf16[2,80,768]{2,1,0:T(8,128)(2,1)S(1)}, bf16[2,80,768]{2,1,0:T(8,128)(2,1)S(1)}, u32[]{:S(2)}, u32[]{:S(2)}) collective-permute-start(bf16[2,80,768]{2,1,0:T(8,128)(2,1)S(1)} %get-tuple-element.699), channel_id=1, source_target_pairs={{0,4},{1,5},{2,6},{3,7},{4,0},{5,1},{6,2},{7,3},{8,12},{9,13},{10,... | collective-permute-start | bytes 737288 | tf_op jit(solution)/shard_map/qkv_grad/ppermute | solution.py:55
  528.2 23.0 %collective-permute-start.93 = (bf16[2,80,768]{2,1,0:T(8,128)(2,1)S(1)}, bf16[2,80,768]{2,1,0:T(8,128)(2,1)S(1)}, u32[]{:S(2)}, u32[]{:S(2)}) collective-permute-start(bf16[2,80,768]{2,1,0:T(8,128)(2,1)S(1)} %get-tuple-element.700), channel_id=1, source_target_pairs={{0,6},{1,7},{2,4},{3,5},{4,2},{5,3},{6,0},{7,1},{8,14},{9,15},{10,... | collective-permute-start | bytes 737288 | tf_op jit(solution)/shard_map/qkv_grad/ppermute | solution.py:55
  (98 other events, 1037.8 us)
Sparse Core Ops, SparseCore 0:
  12.5 36.4 all-gather.8
  132.9 45.7 all-gather.4
  180.5 54.6 all-gather.6
  312.6 51.9 reduce-scatter.4
  366.8 46.1 reduce-scatter.6
  421.7 56.5 reduce-scatter.8
  522.9 28.5 reduce-scatter.10

commit v6 on v5

--- a/solution.py
+++ b/solution.py
@@ -535,25 +535,35 @@
     rows, width = array.shape
     tok = rows // (2 * steps)
     out_width = weights.shape[0] if transposed else weights.shape[1]
-
-    def body(at_ref, mine, other, whole, *outs):
-        left = jnp.concatenate([mine[...], other[...]], axis=0)
-        both = times_transposed(left, whole[...]) if transposed else matmul(left, whole[...])
-        for e in (0, 1):
-            outs[e][0] = both[e * tok : (e + 1) * tok].astype(bf16)
-
-    def block(e):
-        return pl.BlockSpec((tok, width), lambda i, at_ref: (at_ref[2 * i + e], 0))
-
-    stacked = pl.BlockSpec((1, tok, out_width), lambda i, at_ref: (i, 0, 0))
+    run = out_width // 4
+
+    def body(at_ref, source, part, mine, other, held):
+        @pl.when(pl.program_id(0) == 0)
+        def _():
+            for k in range(2 * steps):
+                low = pl.multiple_of(at_ref[k] * tok, tok)
+                row = (k % 2) * (rows // 2) + (k // 2) * tok
+                held[row : row + tok, :] = source[pl.ds(low, tok), :]
+
+        for e, out in ((1, other), (0, mine)):
+            left = held[e * (rows // 2) : (e + 1) * (rows // 2), :]
+            term = (times_transposed if transposed else matmul)(left, part[...])
+            out[...] = term.astype(bf16).reshape(steps, tok, run)
+
+    stacked = pl.BlockSpec((steps, tok, run), lambda i, at_ref: (0, 0, i))
     shape = jax.ShapeDtypeStruct((steps, tok, out_width), bf16)
+    if transposed:
+        part = pl.BlockSpec((run, width), lambda i, at_ref: (i, 0))
+    else:
+        part = pl.BlockSpec((width, run), lambda i, at_ref: (0, i))
     return pl.pallas_call(
         body,
         grid_spec=pltpu.PrefetchScalarGridSpec(
             num_scalar_prefetch=1,
-            grid=(steps,),
-            in_specs=[block(0), block(1), pl.BlockSpec(weights.shape, lambda i, at_ref: (0, 0))],
+            grid=(4,),
+            in_specs=[pl.BlockSpec((rows, width), lambda i, at_ref: (0, 0)), part],
             out_specs=[stacked, stacked],
+            scratch_shapes=[pltpu.VMEM((rows, width), bf16)],
         ),
         out_shape=[shape, shape],
         compiler_params=pltpu.CompilerParams(vmem_limit_bytes=vmem_bytes),
@@ -563,7 +573,7 @@
             transcendentals=0,
         ),
         name="terms_out",
-    )(at, array, array, weights)
+    )(at, array, weights)
 
 
 def norm_sums(own, other, mine, others):
@@ -781,18 +791,18 @@
         for bit in bits_of(n_head):
             small = jnp.concatenate([small, swap(small, "head", bit)])
         small = jnp.concatenate([small, swap(small, "blk", 1)])
-        small_parts = [small]
-        small_parts.append(next_chip(small))
-
-    fused, small_parts, tok_mine, tok_other, up_proj, down_first = hold(
-        fused, small_parts, tok_mine, tok_other, up_proj, down_first
+        for bit in bits_of(chips)[:1]:
+            small = jnp.concatenate([small, swap(small, "blk", 2 * bit)])
+
+    fused, small, tok_mine, tok_other, up_proj, down_first = hold(
+        fused, small, tok_mine, tok_other, up_proj, down_first
     )
 
     def small_table():
-        height, width = small_parts[0].shape[1:]
-        source = jnp.concatenate(small_parts).reshape(n_head * n_blk, height * width)
+        height, width = small.shape[1:]
+        source = small.reshape(n_head * n_blk, height * width)
         index = jnp.arange(n_head * n_blk, dtype=jnp.int32)
-        from_chip = jnp.repeat(jnp.stack(behind), 2 * n_head)
+        from_chip = chip ^ (index // (2 * n_head))
         from_core = core ^ (index // n_head % 2)
         from_row = (head ^ (index % n_head)) * n_blk + 2 * from_chip + from_core
         select = (from_row[None, :] == index[:, None]).astype(bf16)
@@ -801,10 +811,10 @@
     def vector(index):
         return table[:, :, index * w_rows : (index + 1) * w_rows].reshape(1, D)
 
-    table = None
     for step in range(1, chips - 1):
         with jax.named_scope("tokens_gather"):
             tok_mine.append(next_chip(tok_mine[step]))
+            tok_other.append(swap(tok_mine[step], "blk", 1))
         with jax.named_scope("qkv_weights"):
             if step == 1 and square:
                 one = [swap(part, "head", 1) for part in fused]
@@ -814,27 +824,25 @@
             if step == 1 and not square:
                 fused_parts = [gather_head(part) for part in fused]
                 fused_parts = [part[m] for m in range(n_head) for part in fused_parts]
-        with jax.named_scope("vectors"):
-            if len(small_parts) < chips:
-                small_parts.append(next_chip(small_parts[-1]))
-            elif table is None:
-                table = small_table()
+        if step == chips - 2:
+            with jax.named_scope("vectors"):
+                for bit in bits_of(chips)[1:]:
+                    small = jnp.concatenate([small, swap(small, "blk", 2 * bit)])
         if step == 1:
             with jax.named_scope("up_weights"):
                 up_mine, up_other = split_columns(
                     [up_proj], n_head * ff_rows, ff_columns, core, chips, "split_up"
                 )
         if step == 1:
-            tok_mine, tok_other, small_parts, up_mine, up_other = hold(
-                tok_mine, tok_other, small_parts, up_mine, up_other
+            tok_mine, tok_other, up_mine, up_other, small = hold(
+                tok_mine, tok_other, up_mine, up_other, small
             )
         elif step < chips - 2:
-            tok_mine, small_parts = hold(tok_mine, small_parts)
+            tok_mine, small = hold(tok_mine, small)
     if square:
         fused_parts = [*fused, *one, *two, low, high]
-    if table is None:
-        with jax.named_scope("vectors"):
-            table = small_table()
+    with jax.named_scope("vectors"):
+        table = small_table()
     with jax.named_scope("vectors"):
 
         def own_head_part(full):
@@ -846,13 +854,13 @@
         q_bias, v_bias = own_head_part(vector(2)), own_head_part(vector(3))
         qkv_bias = jnp.concatenate([q_bias, jnp.zeros_like(q_bias), v_bias], axis=1)
     first_vectors = (gain_first, shift_first, qkv_bias)
-    fused_parts, tok_mine, cotangent, up_other, out_proj, first_vectors = hold(
-        fused_parts, tok_mine, cotangent, up_other, out_proj, first_vectors
+    fused_parts, tok_mine, tok_other, cotangent, up_other, out_proj, first_vectors = hold(
+        fused_parts, tok_mine, tok_other, cotangent, up_other, out_proj, first_vectors
     )
     gain_first, shift_first, qkv_bias = first_vectors
 
     with jax.named_scope("tokens_gather"):
-        tok_other += [swap(piece, "blk", 1) for piece in tok_mine[1:]]
+        tok_other.append(swap(tok_mine[chips - 1], "blk", 1))
     with jax.named_scope("qkv"):
         query, kv, normed, qkv_w = project_in(
             weights_at,
@@ -886,8 +894,12 @@
         first_pos = jnp.sum((seg_all[:, None] < seg_rows[None, :]).astype(jnp.int32), axis=0)[None]
     with jax.named_scope("attention"):
         state = attend(heads_at, [0], first_pos, tok, query, keys, values, None, False)
-    kv_parts, state, up_pieces, cotangent, out_parts, first_pos = hold(
-        kv_parts, state, up_pieces, cotangent, out_parts, first_pos
+    if square:
+        down_second = down_proj[half:]
+    else:
+        down_second = down_proj
+    kv_parts, state, up_pieces, cotangent, out_parts, first_pos, down_second = hold(
+        kv_parts, state, up_pieces, cotangent, out_parts, first_pos, down_second
     )
 
     with jax.named_scope("dy_gather"):
@@ -905,13 +917,13 @@
         out_w = exchange(out_w, "blk", place_in, team)
         out_w = out_w.transpose(1, 0, 2, 3).reshape(own_heads, D)
     if square:
-        low, high, out_w, state, up_part, down_proj = hold(
-            low, high, out_w, state, up_part, down_proj
+        low, high, out_w, state, up_part, down_second = hold(
+            low, high, out_w, state, up_part, down_second
         )
         keys.append((low, 0))
         values.append((high, 0))
     else:
-        out_w, state, up_part, down_proj = hold(out_w, state, up_part, down_proj)
+        out_w, state, up_part, down_second = hold(out_w, state, up_part, down_second)
     with jax.named_scope("up_weights"):
         up_w = lax.all_gather(up_part, "head", axis=0, tiled=True)
 
@@ -922,10 +934,9 @@
         )
     with jax.named_scope("down_weights"):
         if square:
-            downs = down_proj[half:]
-            downs = [downs, swap(downs, "head", 1), swap(downs, "head", 2)]
+            downs = [down_second, swap(down_second, "head", 1), swap(down_second, "head", 2)]
         else:
-            downs = gather_head(down_proj)
+            downs = gather_head(down_second)
     mixed, out_w, table, downs = hold(mixed, out_w, table, downs)
 
     def cross(term):
@@ -946,7 +957,7 @@
 
     with jax.named_scope("branch"):
         ready = met(*terms_out(blocks_at, mixed, out_w, False))
-        ready, dy_all = hold(ready, dy_all)
+        (ready,) = hold(ready)
         moving = None
         for step in range(1, chips):
             moving = onward(entry(ready, step), moving)
@@ -963,7 +974,7 @@
                 if not square and step == 1:
                     down_w = place(downs, heads_at).reshape(n_head * ff_rows, D)
             if step == 1:
-                moving, ready, vectors = hold(moving, ready, vectors)
+                moving, ready, vectors, dy_all = hold(moving, ready, vectors, dy_all)
                 o_bias, gain_second, shift_second, d_bias, u_bias = vectors
             elif square and step == 2:
                 moving, ready, low, high = hold(moving, ready, low, high)
@@ -1092,11 +1103,6 @@
         by_core = blocks_at.reshape(chips, 2)
         d_mixed = mix_back(by_core[:, 0], mine, out_w, mixed, None)
         d_mixed, delta = mix_back(by_core[:, 1], other, out_w, mixed, d_mixed)
-    with jax.named_scope("up_grad"):
-        up_sum = up_sum.reshape(chips, 2, w_rows, n_head * ff_rows)
-        up_mine = lax.dynamic_index_in_dim(up_sum, core, 1, keepdims=False)
-        up_other = lax.dynamic_index_in_dim(up_sum, 1 - core, 1, keepdims=False)
-        up_pieces = pair_up(up_mine, swap(up_other, "blk", 1), chip, core)
     d_mixed, delta, mine, other = hold(d_mixed, delta, mine, other)
 
     dq = None
@@ -1115,7 +1121,7 @@
             if square and m == 0:
                 one = [d_keys[1], (d_values[1].astype(f32) + high.astype(f32)).astype(bf16)]
                 two = [(d_keys[2].astype(f32) + low.astype(f32)).astype(bf16), d_values[2]]
-                one, two, dq, up_pieces = hold(one, two, dq, up_pieces)
+                one, two, dq, up_sum = hold(one, two, dq, up_sum)
                 one[0], two[0] = swap(one[0], "head", 1), swap(two[0], "head", 2)
             dq, d_keys[m], d_values[m] = kv_grad(m)
         if square and m == 1:
@@ -1125,11 +1131,17 @@
         elif m > 0:
             dq, d_keys, d_values, d_mixed = hold(dq, d_keys, d_values, d_mixed)
     with jax.named_scope("up_grad"):
+        up_sum = up_sum.reshape(chips, 2, w_rows, n_head * ff_rows)
+        up_mine = lax.dynamic_index_in_dim(up_sum, core, 1, keepdims=False)
+        up_other = lax.dynamic_index_in_dim(up_sum, 1 - core, 1, keepdims=False)
+        up_pieces = pair_up(up_mine, swap(up_other, "blk", 1), chip, core)
+    if square:
+        one, two, dq, mine, other, mixed, out_sum, down_term, up_pieces = hold(
+            one, two, dq, mine, other, mixed, out_sum, down_term, up_pieces
+        )
+    with jax.named_scope("up_grad"):
         up_pieces = swap_chips(up_pieces)
     if square:
-        one, two, dq, mine, other, mixed, out_sum, down_term = hold(
-            one, two, dq, mine, other, mixed, out_sum, down_term
-        )
         with jax.named_scope("attention_back"):
             one[1], two[1] = swap(one[1], "head", 1), swap(two[1], "head", 2)
     with jax.named_scope("out_grad"):

time: 567 us -> 567 us (level)
  waiting for transfers between devices: 208 us -> 216 us
  starting transfers between devices: 74.8 us -> 67.7 us
    ppermute x24 -> x21, starting transfers between devices: 17.1 us -> 11.4 us  [next_chip(): lax.ppermute(v, 'blk', [(2 * a + c, 2 * b + c) for a, b in moves for c in...]
    ppermute x24 -> x21, waiting for transfers between devices: 97.9 us -> 103 us  [next_chip(): lax.ppermute(v, 'blk', [(2 * a + c, 2 * b + c) for a, b in moves for c in...]
    ppermute x70 -> x72, waiting for transfers between devices: 110 us -> 113 us  [swap(): return lax.ppermute(v, axis, [(i, i ^ mask) for i in range(size)])]
    unnamed x125 -> x126, local copies, waits for them, and re-layouts: 11.7 us -> 13.4 us
    ppermute x70 -> x72, starting transfers between devices: 57 us -> 55.6 us  [swap(): return lax.ppermute(v, axis, [(i, i ^ mask) for i in range(size)])]
  transfers between devices with their start and end apart: 101 -> 100, of which waited for: 49 -> 50; matrix products, arithmetic and copies ran while one was open for 23% -> 23% of each run, Pallas kernels for 20% -> 20%
where the time goes in v6:
time: 567 us; the launch traced here: 562 us
  waiting for transfers between devices  216 us (38%)
  Pallas kernels  110 us (19%)
  starting transfers between devices  67.7 us (12%)
  matrix products  63.6 us (11%)
  other arithmetic  44.6 us (8%)
  local copies, waits for them, and re-layouts  39.4 us (7%)
  between operations  20.8 us (4%)
    ppermute x72, waiting for transfers between devices, swap(): return lax.ppermute(v, axis, [(i, i ^ mask) for i in range(size)])  113 us
    ppermute x21, waiting for transfers between devices, next_chip(): lax.ppermute(v, 'blk', [(2 * a + c, 2 * b + c) for a, b in moves for c in...  103 us
    ppermute x72, starting transfers between devices, swap(): return lax.ppermute(v, axis, [(i, i ^ mask) for i in range(size)])  55.6 us
    pallas_call x4, Pallas kernels, attend_back(): pl.pallas_call(kernel, grid=(1 if rows <= 1024 else heads * tiles,), in_s...  30 us
    pallas_call x16, Pallas kernels, local_call(): pl.pallas_call(kernel, in_specs=[pl.BlockSpec(memory_space=pltpu.SMEM)] +...  27.4 us
    dot_general x3, matrix products, cross_rows(): lax.dot_general(left, right, (((0,), (0,)), ((), ())), preferred_element_...  25.1 us
    dot_general x12, matrix products, times_transposed(): lax.dot_general(left, right, (((1,), (1,)), ((), ())), preferred_element_...  19.6 us
    dot_general x6, matrix products, matmul(): return jnp.dot(left, right, preferred_element_type=f32)  19 us
  transfers between devices with their start and end apart: 100, of which 50 were waited for; matrix products, arithmetic and copies ran while one was open for 23% of the time, Pallas kernels for 20%

profile of v6, /device:TPU:8, one launch (start us, length us, event | category | flops | bytes accessed | tf_op | source)
XLA Modules:
  0.0 562.4 jit_solution(14673439145401032529)
XLA Ops:
  19.3 7.9 %collective-permute-done.1.refs_1_.refs_3_ = bf16[128,2048]{1,0:T(8,128)(2,1)S(1)} collective-permute-done((bf16[128,2048]{1,0:T(8,128)(2,1)}, bf16[128,2048]{1,0:T(8,128)(2,1)S(1)}, u32[]{:S(2)}, u32[]{:S(2)}) %collective-permute-start.1) | collective-permute-done | bytes 524320 | tf_op jit(solution)/shard_map/tokens_gather/ppermute | solution.py:66
  28.7 3.0 collective-permute-start.4
  38.3 5.0 collective-permute-done.9
  44.5 3.5 collective-permute-done.5.refs_3_
  53.3 10.3 %collective-permute-done.16.refs_2_.refs_4_ = bf16[128,2048]{1,0:T(8,128)(2,1)S(1)} collective-permute-done((bf16[128,2048]{1,0:T(8,128)(2,1)S(1)}, bf16[128,2048]{1,0:T(8,128)(2,1)S(1)}, u32[]{:S(2)}, u32[]{:S(2)}) %collective-permute-start.16) | collective-permute-done | bytes 524320 | tf_op jit(solution)/shard_map/tokens_gather/ppermute | solution.py:66
  74.8 4.2 collective-permute-done.13.refs_16_
  79.4 5.8 %collective-permute-done.15.refs_18_ = bf16[4,64,768]{2,1,0:T(8,128)(2,1)} collective-permute-done((bf16[4,64,768]{2,1,0:T(8,128)(2,1)}, bf16[4,64,768]{2,1,0:T(8,128)(2,1)}, u32[]{:S(2)}, u32[]{:S(2)}) %collective-permute-start.15) | collective-permute-done | bytes 393248 | tf_op jit(solution)/shard_map/qkv_weights/ppermute | solution.py:55
  91.8 13.4 %project_in.1 = (bf16[1024,256]{1,0:T(8,128)(2,1)}, bf16[2,1024,256]{2,1,0:T(8,128)(2,1)}, bf16[1024,2048]{1,0:T(8,128)(2,1)}, bf16[2048,768]{1,0:T(8,128)(2,1)}) custom-call(s32[13]{0:T(128)} %pad_add_fusion.1.at_ref, bf16[128,2048]{1,0:T(8,128)(2,1)} %refs_2_.2, bf16[128,2048]{1,0:T(8,128)(2,1)} %copy-done.42, bf16[128,2048]{1,0:T(8,128)(2,1)} %copy-done.43, ...), custom_call_target="tpu_custom_call" | custom-call | flops 3221225472 | bytes 16777216 | tf_op jit(solution)/shard_map/qkv/project_in/pallas_call | solution.py:506
  111.9 2.3 convert_reduce_fusion
  114.2 6.3 %attend.2 = (f32[1024,256]{1,0:T(8,128)}, f32[2,2,1024]{2,1,0:T(2,128)}) custom-call(s32[4]{0:T(128)} %get-tuple-element.375.heads_ref.at_ref, s32[1,1024]{1,0:T(1,128)} %bitcast.252, bf16[1024,256]{1,0:T(8,128)(2,1)} %get-tuple-element.438.query_ref, bf16[2,1024,256]{2,1,0:T(8,128)(2,1)} %get-tuple-element.436.refs_0_), custom_call_target="tpu_custom_call" | custom-call | flops 536870912 | bytes 1048576 | tf_op jit(solution)/shard_map/attention/attend/pallas_call | solution.py:384
  120.5 7.4 %collective-permute-done.29.refs_2_ = bf16[2,64,1024]{2,1,0:T(8,128)(2,1)S(1)} collective-permute-done((bf16[2,64,1024]{2,1,0:T(8,128)(2,1)S(1)}, bf16[2,64,1024]{2,1,0:T(8,128)(2,1)S(1)}, u32[]{:S(2)}, u32[]{:S(2)}) %collective-permute-start.29) | collective-permute-done | bytes 262176 | tf_op jit(solution)/shard_map/up_weights/ppermute | solution.py:55
  127.8 5.9 %collective-permute-done.30.refs_3_ = bf16[2,64,1024]{2,1,0:T(8,128)(2,1)S(1)} collective-permute-done((bf16[2,64,1024]{2,1,0:T(8,128)(2,1)S(1)}, bf16[2,64,1024]{2,1,0:T(8,128)(2,1)S(1)}, u32[]{:S(2)}, u32[]{:S(2)}) %collective-permute-start.30) | collective-permute-done | bytes 262176 | tf_op jit(solution)/shard_map/up_weights/ppermute | solution.py:55
  142.6 7.7 %collective-permute-done.31.refs_2_.refs_0_ = bf16[1,1024,256]{2,1,0:T(8,128)(2,1)S(1)} collective-permute-done((bf16[1,1024,256]{2,1,0:T(8,128)(2,1)S(1)}, bf16[1,1024,256]{2,1,0:T(8,128)(2,1)S(1)}, u32[]{:S(2)}, u32[]{:S(2)}) %collective-permute-start.31) | collective-permute-done | bytes 524320 | tf_op jit(solution)/shard_map/kv_gather/ppermute | solution.py:55
  150.3 2.3 collective-permute-done.32.refs_3_.refs_1_
  155.4 12.7 %attend.3 = (bf16[1024,256]{1,0:T(8,128)(2,1)}, f32[2,1,1024]{2,1,0:T(1,128)}) custom-call(s32[4]{0:T(128)} %get-tuple-element.375.heads_ref.at_ref, s32[1,1024]{1,0:T(1,128)} %bitcast.253, bf16[1024,256]{1,0:T(8,128)(2,1)} %get-tuple-element.438.query_ref, bf16[2,1024,256]{2,1,0:T(8,128)(2,1)} %collective-permute-done.26.refs_0_, ...), custom_call_target="tpu_custom_call" | custom-call | flops 1610612736 | bytes 3145728 | tf_op jit(solution)/shard_map/attention/attend/pallas_call | solution.py:384
  168.2 5.4 terms_out.2
  173.6 4.4 collective-permute-done.36
  179.9 14.6 %collective-permute-done.37 = bf16[128,2048]{1,0:T(8,128)(2,1)} collective-permute-done((bf16[128,2048]{1,0:T(8,128)(2,1)S(1)}, bf16[128,2048]{1,0:T(8,128)(2,1)}, u32[]{:S(2)}, u32[]{:S(2)}) %collective-permute-start.37) | collective-permute-done | bytes 524320 | tf_op jit(solution)/shard_map/branch/ppermute | solution.py:66
  198.4 8.7 %collective-permute-done.39.refs_3_ = bf16[64,2048]{1,0:T(8,128)(2,1)S(1)} collective-permute-done((bf16[64,2048]{1,0:T(8,128)(2,1)S(1)}, bf16[64,2048]{1,0:T(8,128)(2,1)S(1)}, u32[]{:S(2)}, u32[]{:S(2)}) %collective-permute-start.39) | collective-permute-done | bytes 262176 | tf_op jit(solution)/shard_map/branch/down_weights/ppermute | solution.py:55
  207.7 2.4 collective-permute-done.38
  212.1 13.0 %collective-permute-done.41 = bf16[128,2048]{1,0:T(8,128)(2,1)S(1)} collective-permute-done((bf16[128,2048]{1,0:T(8,128)(2,1)S(1)}, bf16[128,2048]{1,0:T(8,128)(2,1)S(1)}, u32[]{:S(2)}, u32[]{:S(2)}) %collective-permute-start.41) | collective-permute-done | bytes 524320 | tf_op jit(solution)/shard_map/branch/ppermute | solution.py:66
  225.1 2.3 fusion.114
  245.6 4.8 fusion.49
  250.5 2.9 constant_dynamic-update-slice_fusion.9
  261.2 2.8 fusion.50
  268.6 3.6 collective-permute-done.46
  274.4 2.6 fusion.51
  284.3 2.6 fusion.52
  291.5 5.4 collective-permute-done.50
  298.0 8.4 %convolution_convert_fusion.2 = bf16[2048,1024]{1,0:T(8,128)(2,1)} fusion(bf16[1024,2048]{1,0:T(8,128)(2,1)} %constant_dynamic-update-slice_fusion.1, bf16[1024,1024]{1,0:T(8,128)(2,1)S(1)} %get-tuple-element.566), kind=kOutput, calls=%fused_computation.4 | convolution fusion | flops 4297064448 | bytes 10485760 | tf_op jit(solution)/shard_map/mlp/up_grad/dot_general | solution.py:29
  306.4 5.6 %collective-permute-done.52 = bf16[128,2048]{1,0:T(8,128)(2,1)S(1)} collective-permute-done((bf16[128,2048]{1,0:T(8,128)(2,1)}, bf16[128,2048]{1,0:T(8,128)(2,1)S(1)}, u32[]{:S(2)}, u32[]{:S(2)}) %collective-permute-start.52) | collective-permute-done | bytes 524320 | tf_op jit(solution)/shard_map/mlp/ppermute | solution.py:66
  313.4 9.6 %convolution_convert_fusion.1 = bf16[1024,2048]{1,0:T(8,128)(2,1)} fusion(bf16[1024,1024]{1,0:T(8,128)(2,1)} %copy-done.38, bf16[1024,2048]{1,0:T(8,128)(2,1)} %all-gather.5.cloned.1.call-done), kind=kOutput, calls=%fused_computation.3 | convolution fusion | flops 4297064448 | bytes 10485760 | tf_op jit(solution)/shard_map/mlp/down_grad/dot_general | solution.py:29
  323.0 3.5 collective-permute-done.54
  331.3 2.8 collective-permute-start.57
  334.1 6.0 %convolution_convert_fusion = bf16[1024,2048]{1,0:T(8,128)(2,1)} fusion(bf16[1024,1024]{1,0:T(8,128)(2,1)S(1)} %copy-done.39, bf16[1024,2048]{1,0:T(8,128)(2,1)S(1)} %bitcast.216), kind=kOutput, calls=%fused_computation.2 | convolution fusion | flops 4297064448 | bytes 10485760 | tf_op jit(solution)/shard_map/d_branch_gather/output/dot_general | solution.py:25
  341.2 4.7 collective-permute-done.57
  347.1 4.3 collective-permute-done.58
  352.1 4.8 collective-permute-done.59
  358.9 3.6 collective-permute-done.60
  362.6 3.4 collective-permute-done.61
  368.2 4.2 mix_back.2.refs_6_
  373.4 4.6 mix_back.3
  378.0 7.1 %attend_back.4 = (f32[1024,256]{1,0:T(8,128)}, bf16[1024,256]{1,0:T(8,128)(2,1)}, bf16[1024,256]{1,0:T(8,128)(2,1)}) custom-call(s32[4]{0:T(128)} %get-tuple-element.375.heads_ref.at_ref, s32[1,1024]{1,0:T(1,128)} %bitcast.254, f32[2,1,1024]{2,1,0:T(1,128)} %get-tuple-element.494.log_ref, f32[2,1,1024]{2,1,0:T(1,128)} %get-tuple-element.573.delta_ref, ...), custom_call_target="tpu_custom_call" | custom-call | flops 1342177280 | bytes 5242880 | tf_op jit(solution)/shard_map/attention_back/attend_back/pallas_call | solution.py:447
  387.2 7.4 %attend_back.5 = (f32[1024,256]{1,0:T(8,128)}, bf16[1024,256]{1,0:T(8,128)(2,1)}, bf16[1024,256]{1,0:T(8,128)(2,1)}) custom-call(s32[4]{0:T(128)} %get-tuple-element.375.heads_ref.at_ref, s32[1,1024]{1,0:T(1,128)} %bitcast.255, f32[2,1,1024]{2,1,0:T(1,128)} %get-tuple-element.494.log_ref, f32[2,1,1024]{2,1,0:T(1,128)} %get-tuple-element.573.delta_ref, ...), custom_call_target="tpu_custom_call" | custom-call | flops 1342177280 | bytes 5242880 | tf_op jit(solution)/shard_map/attention_back/attend_back/pallas_call | solution.py:447
  394.6 8.0 %attend_back.6 = (f32[1024,256]{1,0:T(8,128)}, bf16[1024,256]{1,0:T(8,128)(2,1)}, bf16[1024,256]{1,0:T(8,128)(2,1)}) custom-call(s32[4]{0:T(128)} %get-tuple-element.375.heads_ref.at_ref, s32[1,1024]{1,0:T(1,128)} %bitcast.256, f32[2,1,1024]{2,1,0:T(1,128)} %get-tuple-element.494.log_ref, f32[2,1,1024]{2,1,0:T(1,128)} %get-tuple-element.573.delta_ref, ...), custom_call_target="tpu_custom_call" | custom-call | flops 1342177280 | bytes 5242880 | tf_op jit(solution)/shard_map/attention_back/attend_back/pallas_call | solution.py:447
  407.0 7.4 %attend_back.7 = (f32[1024,256]{1,0:T(8,128)}, bf16[1024,256]{1,0:T(8,128)(2,1)}, bf16[1024,256]{1,0:T(8,128)(2,1)}) custom-call(s32[4]{0:T(128)} %get-tuple-element.375.heads_ref.at_ref, s32[1,1024]{1,0:T(1,128)} %bitcast.257, f32[2,1,1024]{2,1,0:T(1,128)} %get-tuple-element.494.log_ref, f32[2,1,1024]{2,1,0:T(1,128)} %get-tuple-element.573.delta_ref, ...), custom_call_target="tpu_custom_call" | custom-call | flops 1342177280 | bytes 5242880 | tf_op jit(solution)/shard_map/attention_back/attend_back/pallas_call | solution.py:447
  415.8 3.6 collective-permute-done.68
  426.3 6.1 %mix_grad.1 = bf16[2,2,64,2048]{3,2,1,0:T(8,128)(2,1)} custom-call(s32[8]{0:T(128)} %add.539.at_ref, bf16[128,2048]{1,0:T(8,128)(2,1)} %copy-done.23, bf16[128,2048]{1,0:T(8,128)(2,1)} %copy-done.31, bf16[128,2048]{1,0:T(8,128)(2,1)} %copy-done.32, bf16[128,2048]{1,0:T(8,128)(2,1)} %copy-done.33, bf16[128,2048]{1,0:T(8,128)(2,1)} %copy-done.35, ...), custom_call_target="tpu_custom_call" | custom-call | tf_op jit(solution)/shard_map/out_grad/mix_grad/pallas_call | solution.py:141
  433.8 5.9 %collective-permute-done.71 = bf16[1024,256]{1,0:T(8,128)(2,1)S(1)} collective-permute-done((bf16[1024,256]{1,0:T(8,128)(2,1)}, bf16[1024,256]{1,0:T(8,128)(2,1)S(1)}, u32[]{:S(2)}, u32[]{:S(2)}) %collective-permute-start.71) | collective-permute-done | bytes 524320 | tf_op jit(solution)/shard_map/attention_back/ppermute | solution.py:55
  439.7 2.6 collective-permute-done.72
  443.9 4.2 collective-permute-done.75.refs_3_
  448.1 7.8 %terms_out.3 = (bf16[4,128,2048]{2,1,0:T(8,128)(2,1)}, bf16[4,128,2048]{2,1,0:T(8,128)(2,1)}) custom-call(s32[8]{0:T(128)} %add.539.at_ref, bf16[1024,768]{1,0:T(8,128)(2,1)} %pad_maximum_fusion.source, bf16[2048,768]{1,0:T(8,128)(2,1)} %get-tuple-element.643.part), custom_call_target="tpu_custom_call" | custom-call | flops 3221225472 | bytes 8388608 | tf_op jit(solution)/shard_map/d_normed/terms_out/pallas_call | solution.py:559
  456.0 4.4 collective-permute-done.76
  462.0 7.0 %convolution_convert_fusion.3 = bf16[2048,768]{1,0:T(8,128)(2,1)S(1)} fusion(bf16[1024,2048]{1,0:T(8,128)(2,1)} %get-tuple-element.654, bf16[1024,768]{1,0:T(8,128)(2,1)} %pad_maximum_fusion.source), kind=kOutput, calls=%fused_computation.5 | convolution fusion | flops 3222798336 | bytes 8912896 | tf_op jit(solution)/shard_map/qkv_grad/dot_general | solution.py:29
  469.1 7.8 %collective-permute-done.77 = bf16[128,2048]{1,0:T(8,128)(2,1)S(1)} collective-permute-done((bf16[128,2048]{1,0:T(8,128)(2,1)S(1)}, bf16[128,2048]{1,0:T(8,128)(2,1)S(1)}, u32[]{:S(2)}, u32[]{:S(2)}) %collective-permute-start.77) | collective-permute-done | bytes 524320 | tf_op jit(solution)/shard_map/d_normed/ppermute | solution.py:66
  480.0 10.1 %collective-permute-done.79 = bf16[256,768]{1,0:T(8,128)(2,1)S(1)} collective-permute-done((bf16[256,768]{1,0:T(8,128)(2,1)S(1)}, bf16[256,768]{1,0:T(8,128)(2,1)S(1)}, u32[]{:S(2)}, u32[]{:S(2)}) %collective-permute-start.79) | collective-permute-done | bytes 393248 | tf_op jit(solution)/shard_map/qkv_grad/ppermute | solution.py:55
  490.6 2.9 collective-permute-done.78
  497.6 7.4 %norm_sums.1.first_ref = f32[2,2048]{1,0:T(2,128)} custom-call(bf16[4,128,2048]{2,1,0:T(8,128)(2,1)} %get-tuple-element.700.refs_0_, bf16[4,128,2048]{2,1,0:T(8,128)(2,1)} %get-tuple-element.667.refs_1_, bf16[128,2048]{1,0:T(8,128)(2,1)} %refs_2_.2, bf16[128,2048]{1,0:T(8,128)(2,1)} %copy-done.42, bf16[128,2048]{1,0:T(8,128)(2,1)} %copy-done.43, ...), custom_call_target="tpu_custom_call" | custom-call | tf_op jit(solution)/shard_map/vector_grads/norm_sums/pallas_call | solution.py:601
  506.8 2.6 collective-permute-done.84
  510.9 5.4 collective-permute-done.85
  525.0 2.6 collective-permute-start.90
  531.2 3.3 fusion.15
  538.5 6.4 %collective-permute-done.91.refs_2_ = bf16[2,80,768]{2,1,0:T(8,128)(2,1)S(1)} collective-permute-done((bf16[2,80,768]{2,1,0:T(8,128)(2,1)S(1)}, bf16[2,80,768]{2,1,0:T(8,128)(2,1)S(1)}, u32[]{:S(2)}, u32[]{:S(2)}) %collective-permute-start.91) | collective-permute-done | bytes 245792 | tf_op jit(solution)/shard_map/qkv_grad/ppermute | solution.py:55
  544.9 6.2 %collective-permute-done.92.refs_3_ = bf16[2,80,768]{2,1,0:T(8,128)(2,1)S(1)} collective-permute-done((bf16[2,80,768]{2,1,0:T(8,128)(2,1)S(1)}, bf16[2,80,768]{2,1,0:T(8,128)(2,1)S(1)}, u32[]{:S(2)}, u32[]{:S(2)}) %collective-permute-start.92) | collective-permute-done | bytes 245792 | tf_op jit(solution)/shard_map/qkv_grad/ppermute | solution.py:55
  (446 shorter events, 176.5 us)
Async XLA Ops:
  7.2 42.2 %all-gather.9.cloned.1.call-start = ((), (), s32[]{:S(2)}) async-start(), calls=%async_computation.10 | async-start | bytes 2621440 | tf_op jit(solution)/shard_map/down_weights/all_gather | solution.py:775
  12.4 182.1 %all-gather.5.cloned.1.call-start = ((), (), s32[]{:S(2)}) async-start(), calls=%async_computation.4 | async-start | bytes 4718592 | tf_op jit(solution)/shard_map/dy_gather/all_gather | solution.py:906
  12.4 14.8 %collective-permute-start.1 = (bf16[128,2048]{1,0:T(8,128)(2,1)}, bf16[128,2048]{1,0:T(8,128)(2,1)S(1)}, u32[]{:S(2)}, u32[]{:S(2)}) collective-permute-start(bf16[128,2048]{1,0:T(8,128)(2,1)} %refs_2_.2), channel_id=1, source_target_pairs={{0,4},{1,5},{4,6},{5,7},{6,2},{7,3},{2,0},{3,1},{8,12},{9,13},{12,... | collective-permute-start | bytes 1572872 | tf_op jit(solution)/shard_map/tokens_gather/ppermute | solution.py:66
  12.5 14.8 %collective-permute-start.2 = (bf16[128,2048]{1,0:T(8,128)(2,1)}, bf16[128,2048]{1,0:T(8,128)(2,1)}, u32[]{:S(2)}, u32[]{:S(2)}) collective-permute-start(bf16[128,2048]{1,0:T(8,128)(2,1)} %refs_2_.2), channel_id=1, source_target_pairs={{0,1},{1,0},{2,3},{3,2},{4,5},{5,4},{6,7},{7,6},{8,9},{9,8},{10,11... | collective-permute-start | bytes 1572872 | tf_op jit(solution)/shard_map/tokens_gather/ppermute | solution.py:55
  28.7 14.6 %collective-permute-start.3 = (bf16[2,64,768]{2,1,0:T(8,128)(2,1)S(1)}, bf16[2,64,768]{2,1,0:T(8,128)(2,1)S(1)}, u32[]{:S(2)}, u32[]{:S(2)}) collective-permute-start(bf16[2,64,768]{2,1,0:T(8,128)(2,1)S(1)} %get-tuple-element.379), channel_id=1, source_target_pairs={{0,2},{1,3},{2,0},{3,1},{4,6},{5,7},{6,4},{7,5},{8,10},{9,11},{10,... | collective-permute-start | bytes 589832 | tf_op jit(solution)/shard_map/qkv_weights/ppermute | solution.py:55
  28.7 15.8 %collective-permute-start.4 = (bf16[2,64,768]{2,1,0:T(8,128)(2,1)S(1)}, bf16[2,64,768]{2,1,0:T(8,128)(2,1)S(1)}, u32[]{:S(2)}, u32[]{:S(2)}) collective-permute-start(bf16[2,64,768]{2,1,0:T(8,128)(2,1)S(1)} %get-tuple-element.380), channel_id=1, source_target_pairs={{0,4},{1,5},{2,6},{3,7},{4,0},{5,1},{6,2},{7,3},{8,12},{9,13},{10,... | collective-permute-start | bytes 589832 | tf_op jit(solution)/shard_map/qkv_weights/ppermute | solution.py:55
  31.8 16.3 %collective-permute-start.5 = (bf16[2,64,768]{2,1,0:T(8,128)(2,1)S(1)}, bf16[2,64,768]{2,1,0:T(8,128)(2,1)S(1)}, u32[]{:S(2)}, u32[]{:S(2)}) collective-permute-start(bf16[2,64,768]{2,1,0:T(8,128)(2,1)S(1)} %get-tuple-element.381), channel_id=1, source_target_pairs={{0,6},{1,7},{2,4},{3,5},{4,2},{5,3},{6,0},{7,1},{8,14},{9,15},{10,... | collective-permute-start | bytes 589832 | tf_op jit(solution)/shard_map/qkv_weights/ppermute | solution.py:55
  49.4 14.1 %collective-permute-start.16 = (bf16[128,2048]{1,0:T(8,128)(2,1)S(1)}, bf16[128,2048]{1,0:T(8,128)(2,1)S(1)}, u32[]{:S(2)}, u32[]{:S(2)}) collective-permute-start(bf16[128,2048]{1,0:T(8,128)(2,1)S(1)} %collective-permute-done.1.refs_1_.refs_3_), channel_id=1, source_target_pairs={{0,4},{1,5},{4,6},{5,7},{6,2},{7,3},{2,0},{3,1},{8,12},{9,13},{12,... | collective-permute-start | bytes 1572872 | tf_op jit(solution)/shard_map/tokens_gather/ppermute | solution.py:66
  49.5 14.0 %collective-permute-start.17 = (bf16[128,2048]{1,0:T(8,128)(2,1)S(1)}, bf16[128,2048]{1,0:T(8,128)(2,1)S(1)}, u32[]{:S(2)}, u32[]{:S(2)}) collective-permute-start(bf16[128,2048]{1,0:T(8,128)(2,1)S(1)} %collective-permute-done.1.refs_1_.refs_3_), channel_id=1, source_target_pairs={{0,1},{1,0},{2,3},{3,2},{4,5},{5,4},{6,7},{7,6},{8,9},{9,8},{10,11... | collective-permute-start | bytes 1572872 | tf_op jit(solution)/shard_map/tokens_gather/ppermute | solution.py:55
  49.5 18.7 %collective-permute-start.12 = (bf16[4,64,768]{2,1,0:T(8,128)(2,1)S(1)}, bf16[4,64,768]{2,1,0:T(8,128)(2,1)}, u32[]{:S(2)}, u32[]{:S(2)}) collective-permute-start(bf16[4,64,768]{2,1,0:T(8,128)(2,1)S(1)} %get-tuple-element.416.refs_11_), channel_id=1, source_target_pairs={{0,16},{8,24},{16,0},{24,8},{1,17},{9,25},{17,1},{25,9},{2,18},{10... | collective-permute-start | bytes 1179656 | tf_op jit(solution)/shard_map/qkv_weights/ppermute | solution.py:55
  51.1 17.7 %collective-permute-start.11 = (bf16[4,64,768]{2,1,0:T(8,128)(2,1)}, bf16[4,64,768]{2,1,0:T(8,128)(2,1)}, u32[]{:S(2)}, u32[]{:S(2)}) collective-permute-start(bf16[4,64,768]{2,1,0:T(8,128)(2,1)} %get-tuple-element.417.refs_12_), channel_id=1, source_target_pairs={{0,8},{8,0},{16,24},{24,16},{1,9},{9,1},{17,25},{25,17},{2,10},{10... | collective-permute-start | bytes 1179656 | tf_op jit(solution)/shard_map/qkv_weights/ppermute | solution.py:55
  51.6 20.9 %collective-permute-start.10 = (bf16[4,64,768]{2,1,0:T(8,128)(2,1)S(1)}, bf16[4,64,768]{2,1,0:T(8,128)(2,1)}, u32[]{:S(2)}, u32[]{:S(2)}) collective-permute-start(bf16[4,64,768]{2,1,0:T(8,128)(2,1)S(1)} %get-tuple-element.416.refs_11_), channel_id=1, source_target_pairs={{0,8},{8,0},{16,24},{24,16},{1,9},{9,1},{17,25},{25,17},{2,10},{10... | collective-permute-start | bytes 1179656 | tf_op jit(solution)/shard_map/qkv_weights/ppermute | solution.py:55
  68.8 16.5 %collective-permute-start.15 = (bf16[4,64,768]{2,1,0:T(8,128)(2,1)}, bf16[4,64,768]{2,1,0:T(8,128)(2,1)}, u32[]{:S(2)}, u32[]{:S(2)}) collective-permute-start(bf16[4,64,768]{2,1,0:T(8,128)(2,1)} %collective-permute-done.11.refs_14_), channel_id=1, source_target_pairs={{0,16},{8,24},{16,0},{24,8},{1,17},{9,25},{17,1},{25,9},{2,18},{10... | collective-permute-start | bytes 1179656 | tf_op jit(solution)/shard_map/qkv_weights/ppermute | solution.py:55
  70.3 15.0 %collective-permute-start.18 = (bf16[128,2048]{1,0:T(8,128)(2,1)}, bf16[128,2048]{1,0:T(8,128)(2,1)}, u32[]{:S(2)}, u32[]{:S(2)}) collective-permute-start(bf16[128,2048]{1,0:T(8,128)(2,1)} %copy-done.43), channel_id=1, source_target_pairs={{0,4},{1,5},{4,6},{5,7},{6,2},{7,3},{2,0},{3,1},{8,12},{9,13},{12,... | collective-permute-start | bytes 1572872 | tf_op jit(solution)/shard_map/tokens_gather/ppermute | solution.py:66
  72.5 12.8 %collective-permute-start.19 = (bf16[128,2048]{1,0:T(8,128)(2,1)}, bf16[128,2048]{1,0:T(8,128)(2,1)S(1)}, u32[]{:S(2)}, u32[]{:S(2)}) collective-permute-start(bf16[128,2048]{1,0:T(8,128)(2,1)} %copy-done.43), channel_id=1, source_target_pairs={{0,1},{1,0},{2,3},{3,2},{4,5},{5,4},{6,7},{7,6},{8,9},{9,8},{10,11... | collective-permute-start | bytes 1572872 | tf_op jit(solution)/shard_map/tokens_gather/ppermute | solution.py:55
  86.1 19.1 %collective-permute-start.23 = (bf16[64,2048]{1,0:T(8,128)(2,1)S(1)}, bf16[64,2048]{1,0:T(8,128)(2,1)S(1)}, u32[]{:S(2)}, u32[]{:S(2)}) collective-permute-start(bf16[64,2048]{1,0:T(8,128)(2,1)S(1)} %copy-done.8), channel_id=1, source_target_pairs={{0,8},{8,0},{16,24},{24,16},{1,9},{9,1},{17,25},{25,17},{2,10},{10... | collective-permute-start | bytes 786440 | tf_op jit(solution)/shard_map/out_weights/ppermute | solution.py:55
  87.6 17.5 %collective-permute-start.24 = (bf16[64,2048]{1,0:T(8,128)(2,1)S(1)}, bf16[64,2048]{1,0:T(8,128)(2,1)S(1)}, u32[]{:S(2)}, u32[]{:S(2)}) collective-permute-start(bf16[64,2048]{1,0:T(8,128)(2,1)S(1)} %copy-done.8), channel_id=1, source_target_pairs={{0,16},{8,24},{16,0},{24,8},{1,17},{9,25},{17,1},{25,9},{2,18},{10... | collective-permute-start | bytes 786440 | tf_op jit(solution)/shard_map/out_weights/ppermute | solution.py:55
  88.2 17.0 %collective-permute-start.25 = (bf16[64,2048]{1,0:T(8,128)(2,1)S(1)}, bf16[64,2048]{1,0:T(8,128)(2,1)S(1)}, u32[]{:S(2)}, u32[]{:S(2)}) collective-permute-start(bf16[64,2048]{1,0:T(8,128)(2,1)S(1)} %copy-done.8), channel_id=1, source_target_pairs={{0,24},{8,16},{16,8},{24,0},{1,25},{9,17},{17,9},{25,1},{2,26},{10... | collective-permute-start | bytes 786440 | tf_op jit(solution)/shard_map/out_weights/ppermute | solution.py:55
  105.2 28.6 %collective-permute-start.26 = (bf16[2,1024,256]{2,1,0:T(8,128)(2,1)}, bf16[2,1024,256]{2,1,0:T(8,128)(2,1)}, u32[]{:S(2)}, u32[]{:S(2)}) collective-permute-start(bf16[2,1024,256]{2,1,0:T(8,128)(2,1)} %get-tuple-element.436.refs_0_), channel_id=1, source_target_pairs={{0,8},{8,0},{16,24},{24,16},{1,9},{9,1},{17,25},{25,17},{2,10},{10... | collective-permute-start | bytes 3145736 | tf_op jit(solution)/shard_map/kv_gather/ppermute | solution.py:55
  106.7 27.1 %collective-permute-start.27 = (bf16[2,1024,256]{2,1,0:T(8,128)(2,1)}, bf16[2,1024,256]{2,1,0:T(8,128)(2,1)}, u32[]{:S(2)}, u32[]{:S(2)}) collective-permute-start(bf16[2,1024,256]{2,1,0:T(8,128)(2,1)} %get-tuple-element.436.refs_0_), channel_id=1, source_target_pairs={{0,16},{8,24},{16,0},{24,8},{1,17},{9,25},{17,1},{25,9},{2,18},{10... | collective-permute-start | bytes 3145736 | tf_op jit(solution)/shard_map/kv_gather/ppermute | solution.py:55
  109.5 18.3 %collective-permute-start.29 = (bf16[2,64,1024]{2,1,0:T(8,128)(2,1)S(1)}, bf16[2,64,1024]{2,1,0:T(8,128)(2,1)S(1)}, u32[]{:S(2)}, u32[]{:S(2)}) collective-permute-start(bf16[2,64,1024]{2,1,0:T(8,128)(2,1)S(1)} %get-tuple-element.443), channel_id=1, source_target_pairs={{0,4},{1,5},{2,6},{3,7},{4,0},{5,1},{6,2},{7,3},{8,12},{9,13},{10,... | collective-permute-start | bytes 786440 | tf_op jit(solution)/shard_map/up_weights/ppermute | solution.py:55
  109.8 23.9 %collective-permute-start.30 = (bf16[2,64,1024]{2,1,0:T(8,128)(2,1)S(1)}, bf16[2,64,1024]{2,1,0:T(8,128)(2,1)S(1)}, u32[]{:S(2)}, u32[]{:S(2)}) collective-permute-start(bf16[2,64,1024]{2,1,0:T(8,128)(2,1)S(1)} %get-tuple-element.444), channel_id=1, source_target_pairs={{0,6},{1,7},{2,4},{3,5},{4,2},{5,3},{6,0},{7,1},{8,14},{9,15},{10,... | collective-permute-start | bytes 786440 | tf_op jit(solution)/shard_map/up_weights/ppermute | solution.py:55
  133.8 111.8 %all-gather.7.cloned.1.call-start = ((), (), s32[]{:S(2)}) async-start(), calls=%async_computation.5 | async-start | bytes 5242880 | tf_op jit(solution)/shard_map/up_weights/all_gather | solution.py:928
  135.9 14.4 %collective-permute-start.31 = (bf16[1,1024,256]{2,1,0:T(8,128)(2,1)S(1)}, bf16[1,1024,256]{2,1,0:T(8,128)(2,1)S(1)}, u32[]{:S(2)}, u32[]{:S(2)}) collective-permute-start(bf16[1,1024,256]{2,1,0:T(8,128)(2,1)S(1)} %slice.272), channel_id=1, source_target_pairs={{0,8},{8,0},{16,24},{24,16},{1,9},{9,1},{17,25},{25,17},{2,10},{10... | collective-permute-start | bytes 1572872 | tf_op jit(solution)/shard_map/kv_gather/ppermute | solution.py:55
  138.5 14.1 %collective-permute-start.32 = (bf16[1,1024,256]{2,1,0:T(8,128)(2,1)S(1)}, bf16[1,1024,256]{2,1,0:T(8,128)(2,1)S(1)}, u32[]{:S(2)}, u32[]{:S(2)}) collective-permute-start(bf16[1,1024,256]{2,1,0:T(8,128)(2,1)S(1)} %slice.273), channel_id=1, source_target_pairs={{0,16},{8,24},{16,0},{24,8},{1,17},{9,25},{17,1},{25,9},{2,18},{10... | collective-permute-start | bytes 1572872 | tf_op jit(solution)/shard_map/kv_gather/ppermute | solution.py:55
  153.4 14.8 %collective-permute-start.34 = (bf16[128,2048]{1,0:T(8,128)(2,1)S(1)}, bf16[128,2048]{1,0:T(8,128)(2,1)S(1)}, u32[]{:S(2)}, u32[]{:S(2)}) collective-permute-start(bf16[128,2048]{1,0:T(8,128)(2,1)S(1)} %slice.271.refs_0_), channel_id=1, source_target_pairs={{0,8},{8,0},{16,24},{24,16},{1,9},{9,1},{17,25},{25,17},{2,10},{10... | collective-permute-start | bytes 1572872 | tf_op jit(solution)/shard_map/down_weights/ppermute | solution.py:55
  154.0 14.2 %collective-permute-start.35 = (bf16[128,2048]{1,0:T(8,128)(2,1)S(1)}, bf16[128,2048]{1,0:T(8,128)(2,1)S(1)}, u32[]{:S(2)}, u32[]{:S(2)}) collective-permute-start(bf16[128,2048]{1,0:T(8,128)(2,1)S(1)} %slice.271.refs_0_), channel_id=1, source_target_pairs={{0,16},{8,24},{16,0},{24,8},{1,17},{9,25},{17,1},{25,9},{2,18},{10... | collective-permute-start | bytes 1572872 | tf_op jit(solution)/shard_map/down_weights/ppermute | solution.py:55
  173.6 192.5 %reduce-scatter.5.cloned.1.call-start = ((), (), s32[]{:S(2)}) async-start(), calls=%async_computation.6 | async-start | bytes 5242880 | tf_op jit(solution)/shard_map/up_grad/reduce_scatter | solution.py:1068
  179.4 15.1 %collective-permute-start.37 = (bf16[128,2048]{1,0:T(8,128)(2,1)S(1)}, bf16[128,2048]{1,0:T(8,128)(2,1)}, u32[]{:S(2)}, u32[]{:S(2)}) collective-permute-start(bf16[128,2048]{1,0:T(8,128)(2,1)S(1)} %fusion.48), channel_id=1, source_target_pairs={{0,4},{1,5},{4,6},{5,7},{6,2},{7,3},{2,0},{3,1},{8,12},{9,13},{12,... | collective-permute-start | bytes 1572872 | tf_op jit(solution)/shard_map/branch/ppermute | solution.py:66
  196.0 14.1 %collective-permute-start.38 = (bf16[128,2048]{1,0:T(8,128)(2,1)S(1)}, bf16[128,2048]{1,0:T(8,128)(2,1)S(1)}, u32[]{:S(2)}, u32[]{:S(2)}) collective-permute-start(bf16[128,2048]{1,0:T(8,128)(2,1)S(1)} %fusion.38), channel_id=1, source_target_pairs={{0,4},{1,5},{4,6},{5,7},{6,2},{7,3},{2,0},{3,1},{8,12},{9,13},{12,... | collective-permute-start | bytes 1572872 | tf_op jit(solution)/shard_map/branch/ppermute | solution.py:66
  211.7 13.4 %collective-permute-start.41 = (bf16[128,2048]{1,0:T(8,128)(2,1)S(1)}, bf16[128,2048]{1,0:T(8,128)(2,1)S(1)}, u32[]{:S(2)}, u32[]{:S(2)}) collective-permute-start(bf16[128,2048]{1,0:T(8,128)(2,1)S(1)} %fusion.37), channel_id=1, source_target_pairs={{0,4},{1,5},{4,6},{5,7},{6,2},{7,3},{2,0},{3,1},{8,12},{9,13},{12,... | collective-permute-start | bytes 1572872 | tf_op jit(solution)/shard_map/branch/ppermute | solution.py:66
  229.1 12.6 %collective-permute-start.42 = (bf16[128,2048]{1,0:T(8,128)(2,1)}, bf16[128,2048]{1,0:T(8,128)(2,1)}, u32[]{:S(2)}, u32[]{:S(2)}) collective-permute-start(bf16[128,2048]{1,0:T(8,128)(2,1)} %get-tuple-element.497), channel_id=1, source_target_pairs={{0,4},{1,5},{4,6},{5,7},{6,2},{7,3},{2,0},{3,1},{8,12},{9,13},{12,... | collective-permute-start | bytes 1572872 | tf_op jit(solution)/shard_map/mlp/ppermute | solution.py:66
  229.2 12.6 %collective-permute-start.43 = (bf16[128,2048]{1,0:T(8,128)(2,1)}, bf16[128,2048]{1,0:T(8,128)(2,1)}, u32[]{:S(2)}, u32[]{:S(2)}) collective-permute-start(bf16[128,2048]{1,0:T(8,128)(2,1)} %get-tuple-element.497), channel_id=1, source_target_pairs={{0,1},{1,0},{2,3},{3,2},{4,5},{5,4},{6,7},{7,6},{8,9},{9,8},{10,11... | collective-permute-start | bytes 1572872 | tf_op jit(solution)/shard_map/mlp/ppermute | solution.py:55
  241.7 14.7 %collective-permute-start.44 = (bf16[128,2048]{1,0:T(8,128)(2,1)}, bf16[128,2048]{1,0:T(8,128)(2,1)S(1)}, u32[]{:S(2)}, u32[]{:S(2)}) collective-permute-start(bf16[128,2048]{1,0:T(8,128)(2,1)} %collective-permute-done.42), channel_id=1, source_target_pairs={{0,4},{1,5},{4,6},{5,7},{6,2},{7,3},{2,0},{3,1},{8,12},{9,13},{12,... | collective-permute-start | bytes 1572872 | tf_op jit(solution)/shard_map/mlp/ppermute | solution.py:66
  241.8 14.7 %collective-permute-start.45 = (bf16[128,2048]{1,0:T(8,128)(2,1)}, bf16[128,2048]{1,0:T(8,128)(2,1)S(1)}, u32[]{:S(2)}, u32[]{:S(2)}) collective-permute-start(bf16[128,2048]{1,0:T(8,128)(2,1)} %collective-permute-done.42), channel_id=1, source_target_pairs={{0,1},{1,0},{2,3},{3,2},{4,5},{5,4},{6,7},{7,6},{8,9},{9,8},{10,11... | collective-permute-start | bytes 1572872 | tf_op jit(solution)/shard_map/mlp/ppermute | solution.py:55
  256.5 15.7 %collective-permute-start.46 = (bf16[128,2048]{1,0:T(8,128)(2,1)S(1)}, bf16[128,2048]{1,0:T(8,128)(2,1)S(1)}, u32[]{:S(2)}, u32[]{:S(2)}) collective-permute-start(bf16[128,2048]{1,0:T(8,128)(2,1)S(1)} %collective-permute-done.44), channel_id=1, source_target_pairs={{0,4},{1,5},{4,6},{5,7},{6,2},{7,3},{2,0},{3,1},{8,12},{9,13},{12,... | collective-permute-start | bytes 1572872 | tf_op jit(solution)/shard_map/mlp/ppermute | solution.py:66
  258.3 13.9 %collective-permute-start.47 = (bf16[128,2048]{1,0:T(8,128)(2,1)S(1)}, bf16[128,2048]{1,0:T(8,128)(2,1)S(1)}, u32[]{:S(2)}, u32[]{:S(2)}) collective-permute-start(bf16[128,2048]{1,0:T(8,128)(2,1)S(1)} %collective-permute-done.44), channel_id=1, source_target_pairs={{0,1},{1,0},{2,3},{3,2},{4,5},{5,4},{6,7},{7,6},{8,9},{9,8},{10,11... | collective-permute-start | bytes 1572872 | tf_op jit(solution)/shard_map/mlp/ppermute | solution.py:55
  281.7 15.2 %collective-permute-start.50 = (bf16[128,2048]{1,0:T(8,128)(2,1)S(1)}, bf16[128,2048]{1,0:T(8,128)(2,1)S(1)}, u32[]{:S(2)}, u32[]{:S(2)}) collective-permute-start(bf16[128,2048]{1,0:T(8,128)(2,1)S(1)} %add_convert_fusion.8), channel_id=1, source_target_pairs={{0,4},{1,5},{4,6},{5,7},{6,2},{7,3},{2,0},{3,1},{8,12},{9,13},{12,... | collective-permute-start | bytes 1572872 | tf_op jit(solution)/shard_map/mlp/ppermute | solution.py:66
  282.6 14.3 %collective-permute-start.51 = (bf16[128,2048]{1,0:T(8,128)(2,1)S(1)}, bf16[128,2048]{1,0:T(8,128)(2,1)S(1)}, u32[]{:S(2)}, u32[]{:S(2)}) collective-permute-start(bf16[128,2048]{1,0:T(8,128)(2,1)S(1)} %convolution_convert_fusion.6), channel_id=1, source_target_pairs={{0,1},{1,0},{2,3},{3,2},{4,5},{5,4},{6,7},{7,6},{8,9},{9,8},{10,11... | collective-permute-start | bytes 1572872 | tf_op jit(solution)/shard_map/mlp/ppermute | solution.py:55
  298.0 14.1 %collective-permute-start.52 = (bf16[128,2048]{1,0:T(8,128)(2,1)}, bf16[128,2048]{1,0:T(8,128)(2,1)S(1)}, u32[]{:S(2)}, u32[]{:S(2)}) collective-permute-start(bf16[128,2048]{1,0:T(8,128)(2,1)} %add_convert_fusion.7), channel_id=1, source_target_pairs={{0,4},{1,5},{4,6},{5,7},{6,2},{7,3},{2,0},{3,1},{8,12},{9,13},{12,... | collective-permute-start | bytes 1572872 | tf_op jit(solution)/shard_map/mlp/ppermute | solution.py:66
  298.0 14.1 %collective-permute-start.53 = (bf16[128,2048]{1,0:T(8,128)(2,1)S(1)}, bf16[128,2048]{1,0:T(8,128)(2,1)S(1)}, u32[]{:S(2)}, u32[]{:S(2)}) collective-permute-start(bf16[128,2048]{1,0:T(8,128)(2,1)S(1)} %convolution_convert_fusion.4), channel_id=1, source_target_pairs={{0,1},{1,0},{2,3},{3,2},{4,5},{5,4},{6,7},{7,6},{8,9},{9,8},{10,11... | collective-permute-start | bytes 1572872 | tf_op jit(solution)/shard_map/mlp/ppermute | solution.py:55
  312.1 107.6 %reduce-scatter.7.cloned.1.call-start = ((), (), s32[]{:S(2)}) async-start(), calls=%async_computation.7 | async-start | bytes 4718592 | tf_op jit(solution)/shard_map/d_branch_gather/output/reduce_scatter | solution.py:1101
  313.2 13.3 %collective-permute-start.54 = (bf16[128,2048]{1,0:T(8,128)(2,1)}, bf16[128,2048]{1,0:T(8,128)(2,1)S(1)}, u32[]{:S(2)}, u32[]{:S(2)}) collective-permute-start(bf16[128,2048]{1,0:T(8,128)(2,1)} %add_convert_fusion.6), channel_id=1, source_target_pairs={{0,4},{1,5},{4,6},{5,7},{6,2},{7,3},{2,0},{3,1},{8,12},{9,13},{12,... | collective-permute-start | bytes 1572872 | tf_op jit(solution)/shard_map/mlp/ppermute | solution.py:66
  313.3 13.2 %collective-permute-start.55 = (bf16[128,2048]{1,0:T(8,128)(2,1)S(1)}, bf16[128,2048]{1,0:T(8,128)(2,1)}, u32[]{:S(2)}, u32[]{:S(2)}) collective-permute-start(bf16[128,2048]{1,0:T(8,128)(2,1)S(1)} %convolution_convert_fusion.10), channel_id=1, source_target_pairs={{0,1},{1,0},{2,3},{3,2},{4,5},{5,4},{6,7},{7,6},{8,9},{9,8},{10,11... | collective-permute-start | bytes 1572872 | tf_op jit(solution)/shard_map/mlp/ppermute | solution.py:55
  331.3 14.6 %collective-permute-start.57 = (bf16[64,2048]{1,0:T(8,128)(2,1)}, bf16[64,2048]{1,0:T(8,128)(2,1)}, u32[]{:S(2)}, u32[]{:S(2)}) collective-permute-start(bf16[64,2048]{1,0:T(8,128)(2,1)} %get-tuple-element.744), channel_id=1, source_target_pairs={{0,4},{1,5},{4,6},{5,7},{6,2},{7,3},{2,0},{3,1},{8,12},{9,13},{12,... | collective-permute-start | bytes 786440 | tf_op jit(solution)/shard_map/d_branch_gather/ppermute | solution.py:66
  366.1 143.4 %reduce-scatter.9.cloned.1.call-start = ((), (), s32[]{:S(2)}) async-start(), calls=%async_computation.8 | async-start | bytes 5242880 | tf_op jit(solution)/shard_map/down_grad/reduce_scatter | solution.py:1068
  385.1 17.6 %collective-permute-start.66 = (bf16[1024,256]{1,0:T(8,128)(2,1)}, bf16[1024,256]{1,0:T(8,128)(2,1)S(1)}, u32[]{:S(2)}, u32[]{:S(2)}) collective-permute-start(bf16[1024,256]{1,0:T(8,128)(2,1)} %get-tuple-element.578), channel_id=1, source_target_pairs={{0,8},{8,0},{16,24},{24,16},{1,9},{9,1},{17,25},{25,17},{2,10},{10... | collective-permute-start | bytes 1572872 | tf_op jit(solution)/shard_map/attention_back/ppermute | solution.py:55
  386.2 16.4 %collective-permute-start.67 = (bf16[1024,256]{1,0:T(8,128)(2,1)}, bf16[1024,256]{1,0:T(8,128)(2,1)S(1)}, u32[]{:S(2)}, u32[]{:S(2)}) collective-permute-start(bf16[1024,256]{1,0:T(8,128)(2,1)} %get-tuple-element.579), channel_id=1, source_target_pairs={{0,16},{8,24},{16,0},{24,8},{1,17},{9,25},{17,1},{25,9},{2,18},{10... | collective-permute-start | bytes 1572872 | tf_op jit(solution)/shard_map/attention_back/ppermute | solution.py:55
  405.0 14.4 %collective-permute-start.68 = (bf16[1024,256]{1,0:T(8,128)(2,1)S(1)}, bf16[1024,256]{1,0:T(8,128)(2,1)}, u32[]{:S(2)}, u32[]{:S(2)}) collective-permute-start(bf16[1024,256]{1,0:T(8,128)(2,1)S(1)} %copy-done.59), channel_id=1, source_target_pairs={{0,8},{8,0},{16,24},{24,16},{1,9},{9,1},{17,25},{25,17},{2,10},{10... | collective-permute-start | bytes 1572872 | tf_op jit(solution)/shard_map/attention_back/ppermute | solution.py:55
  405.6 14.1 %collective-permute-start.69 = (bf16[1024,256]{1,0:T(8,128)(2,1)S(1)}, bf16[1024,256]{1,0:T(8,128)(2,1)}, u32[]{:S(2)}, u32[]{:S(2)}) collective-permute-start(bf16[1024,256]{1,0:T(8,128)(2,1)S(1)} %add_convert_fusion.4), channel_id=1, source_target_pairs={{0,16},{8,24},{16,0},{24,8},{1,17},{9,25},{17,1},{25,9},{2,18},{10... | collective-permute-start | bytes 1572872 | tf_op jit(solution)/shard_map/attention_back/ppermute | solution.py:55
  419.8 133.8 %reduce-scatter.11.cloned.1.call-start = ((), (), s32[]{:S(2)}) async-start(), calls=%async_computation.9 | async-start | bytes 1310720 | tf_op jit(solution)/shard_map/out_grad/reduce_scatter | solution.py:1068
  419.8 19.8 %collective-permute-start.71 = (bf16[1024,256]{1,0:T(8,128)(2,1)}, bf16[1024,256]{1,0:T(8,128)(2,1)S(1)}, u32[]{:S(2)}, u32[]{:S(2)}) collective-permute-start(bf16[1024,256]{1,0:T(8,128)(2,1)} %add_convert_fusion.5), channel_id=1, source_target_pairs={{0,8},{8,0},{16,24},{24,16},{1,9},{9,1},{17,25},{25,17},{2,10},{10... | collective-permute-start | bytes 1572872 | tf_op jit(solution)/shard_map/attention_back/ppermute | solution.py:55
  421.3 20.9 %collective-permute-start.72 = (bf16[1024,256]{1,0:T(8,128)(2,1)}, bf16[1024,256]{1,0:T(8,128)(2,1)S(1)}, u32[]{:S(2)}, u32[]{:S(2)}) collective-permute-start(bf16[1024,256]{1,0:T(8,128)(2,1)} %get-tuple-element.628), channel_id=1, source_target_pairs={{0,16},{8,24},{16,0},{24,8},{1,17},{9,25},{17,1},{25,9},{2,18},{10... | collective-permute-start | bytes 1572872 | tf_op jit(solution)/shard_map/attention_back/ppermute | solution.py:55
  422.5 21.2 %collective-permute-start.73 = (bf16[2,64,1024]{2,1,0:T(8,128)(2,1)}, bf16[2,64,1024]{2,1,0:T(8,128)(2,1)S(1)}, u32[]{:S(2)}, u32[]{:S(2)}) collective-permute-start(bf16[2,64,1024]{2,1,0:T(8,128)(2,1)} %get-tuple-element.630), channel_id=1, source_target_pairs={{0,2},{1,3},{2,0},{3,1},{4,6},{5,7},{6,4},{7,5},{8,10},{9,11},{10,... | collective-permute-start | bytes 786440 | tf_op jit(solution)/shard_map/up_grad/ppermute | solution.py:55
  424.8 19.2 %collective-permute-start.74 = (bf16[2,64,1024]{2,1,0:T(8,128)(2,1)S(1)}, bf16[2,64,1024]{2,1,0:T(8,128)(2,1)S(1)}, u32[]{:S(2)}, u32[]{:S(2)}) collective-permute-start(bf16[2,64,1024]{2,1,0:T(8,128)(2,1)S(1)} %get-tuple-element.631), channel_id=1, source_target_pairs={{0,4},{1,5},{2,6},{3,7},{4,0},{5,1},{6,2},{7,3},{8,12},{9,13},{10,... | collective-permute-start | bytes 786440 | tf_op jit(solution)/shard_map/up_grad/ppermute | solution.py:55
  425.9 22.2 %collective-permute-start.75 = (bf16[2,64,1024]{2,1,0:T(8,128)(2,1)S(1)}, bf16[2,64,1024]{2,1,0:T(8,128)(2,1)S(1)}, u32[]{:S(2)}, u32[]{:S(2)}) collective-permute-start(bf16[2,64,1024]{2,1,0:T(8,128)(2,1)S(1)} %get-tuple-element.632), channel_id=1, source_target_pairs={{0,6},{1,7},{2,4},{3,5},{4,2},{5,3},{6,0},{7,1},{8,14},{9,15},{10,... | collective-permute-start | bytes 786440 | tf_op jit(solution)/shard_map/up_grad/ppermute | solution.py:55
  461.8 15.1 %collective-permute-start.77 = (bf16[128,2048]{1,0:T(8,128)(2,1)S(1)}, bf16[128,2048]{1,0:T(8,128)(2,1)S(1)}, u32[]{:S(2)}, u32[]{:S(2)}) collective-permute-start(bf16[128,2048]{1,0:T(8,128)(2,1)S(1)} %fusion.53), channel_id=1, source_target_pairs={{0,4},{1,5},{4,6},{5,7},{6,2},{7,3},{2,0},{3,1},{8,12},{9,13},{12,... | collective-permute-start | bytes 1572872 | tf_op jit(solution)/shard_map/d_normed/ppermute | solution.py:66
  478.3 15.2 %collective-permute-start.78 = (bf16[128,2048]{1,0:T(8,128)(2,1)S(1)}, bf16[128,2048]{1,0:T(8,128)(2,1)S(1)}, u32[]{:S(2)}, u32[]{:S(2)}) collective-permute-start(bf16[128,2048]{1,0:T(8,128)(2,1)S(1)} %fusion.35), channel_id=1, source_target_pairs={{0,4},{1,5},{4,6},{5,7},{6,2},{7,3},{2,0},{3,1},{8,12},{9,13},{12,... | collective-permute-start | bytes 1572872 | tf_op jit(solution)/shard_map/d_normed/ppermute | solution.py:66
  494.9 14.6 %collective-permute-start.84 = (bf16[128,2048]{1,0:T(8,128)(2,1)S(1)}, bf16[128,2048]{1,0:T(8,128)(2,1)}, u32[]{:S(2)}, u32[]{:S(2)}) collective-permute-start(bf16[128,2048]{1,0:T(8,128)(2,1)S(1)} %fusion.34), channel_id=1, source_target_pairs={{0,4},{1,5},{4,6},{5,7},{6,2},{7,3},{2,0},{3,1},{8,12},{9,13},{12,... | collective-permute-start | bytes 1572872 | tf_op jit(solution)/shard_map/d_normed/ppermute | solution.py:66
  495.2 22.9 %collective-permute-start.82 = (bf16[512,768]{1,0:T(8,128)(2,1)S(1)}, bf16[512,768]{1,0:T(8,128)(2,1)}, u32[]{:S(2)}, u32[]{:S(2)}) collective-permute-start(bf16[512,768]{1,0:T(8,128)(2,1)S(1)} %pad_maximum_fusion.1), channel_id=1, source_target_pairs={{0,8},{8,0},{16,24},{24,16},{1,9},{9,1},{17,25},{25,17},{2,10},{10... | collective-permute-start | bytes 2359304 | tf_op jit(solution)/shard_map/qkv_grad/ppermute | solution.py:55
  497.1 21.0 %collective-permute-start.83 = (bf16[512,768]{1,0:T(8,128)(2,1)}, bf16[512,768]{1,0:T(8,128)(2,1)}, u32[]{:S(2)}, u32[]{:S(2)}) collective-permute-start(bf16[512,768]{1,0:T(8,128)(2,1)} %pad_maximum_fusion.2), channel_id=1, source_target_pairs={{0,16},{8,24},{16,0},{24,8},{1,17},{9,25},{17,1},{25,9},{2,18},{10... | collective-permute-start | bytes 2359304 | tf_op jit(solution)/shard_map/qkv_grad/ppermute | solution.py:55
  525.0 13.4 %collective-permute-start.90 = (bf16[2,80,768]{2,1,0:T(8,128)(2,1)S(1)}, bf16[2,80,768]{2,1,0:T(8,128)(2,1)S(1)}, u32[]{:S(2)}, u32[]{:S(2)}) collective-permute-start(bf16[2,80,768]{2,1,0:T(8,128)(2,1)S(1)} %get-tuple-element.704), channel_id=1, source_target_pairs={{0,2},{1,3},{2,0},{3,1},{4,6},{5,7},{6,4},{7,5},{8,10},{9,11},{10,... | collective-permute-start | bytes 737288 | tf_op jit(solution)/shard_map/qkv_grad/ppermute | solution.py:55
  527.7 17.2 %collective-permute-start.91 = (bf16[2,80,768]{2,1,0:T(8,128)(2,1)S(1)}, bf16[2,80,768]{2,1,0:T(8,128)(2,1)S(1)}, u32[]{:S(2)}, u32[]{:S(2)}) collective-permute-start(bf16[2,80,768]{2,1,0:T(8,128)(2,1)S(1)} %get-tuple-element.705), channel_id=1, source_target_pairs={{0,4},{1,5},{2,6},{3,7},{4,0},{5,1},{6,2},{7,3},{8,12},{9,13},{10,... | collective-permute-start | bytes 737288 | tf_op jit(solution)/shard_map/qkv_grad/ppermute | solution.py:55
  528.0 23.1 %collective-permute-start.92 = (bf16[2,80,768]{2,1,0:T(8,128)(2,1)S(1)}, bf16[2,80,768]{2,1,0:T(8,128)(2,1)S(1)}, u32[]{:S(2)}, u32[]{:S(2)}) collective-permute-start(bf16[2,80,768]{2,1,0:T(8,128)(2,1)S(1)} %get-tuple-element.706), channel_id=1, source_target_pairs={{0,6},{1,7},{2,4},{3,5},{4,2},{5,3},{6,0},{7,1},{8,14},{9,15},{10,... | collective-permute-start | bytes 737288 | tf_op jit(solution)/shard_map/qkv_grad/ppermute | solution.py:55
  (97 other events, 1004.7 us)
Sparse Core Ops, SparseCore 0:
  12.5 36.4 all-gather.8
  133.9 44.0 all-gather.4
  179.9 56.5 all-gather.6
  312.2 51.6 reduce-scatter.4
  366.2 46.0 reduce-scatter.6
  419.9 57.9 reduce-scatter.8
  522.5 27.5 reduce-scatter.10

commit v7 on v6

--- a/solution.py
+++ b/solution.py
@@ -246,7 +246,9 @@
                         out[chip, :, low : low + run] = source[:, lanes(start, run)]
 
     shape = ((chips, rows, len(arrays) * width), arrays[0].dtype)
-    return local_call(kernel, [shape, shape], scalars(core), *arrays, name=name)
+    return local_call(
+        kernel, [shape, shape], scalars(core), *arrays, name=name, vmem=vmem_bytes
+    )
 
 
 def pair_up(mine, other, chip, core):
@@ -768,11 +770,10 @@
         mine, other = split_columns(
             [query_proj, key_proj, value_proj], own_heads, head_columns, core, chips, "split_heads"
         )
-    other, down_late = hold(other, down_proj)
     with jax.named_scope("down_weights"):
         half = ff_rows // 2
         if square:
-            down_first = lax.all_gather(down_late[:half], "head", axis=0, tiled=False)
+            down_first = lax.all_gather(down_proj[:half], "head", axis=0, tiled=False)
         else:
             down_first = down_proj
     with jax.named_scope("qkv_weights"):

time: 567 us -> 563 us (level)
    ppermute x21, waiting for transfers between devices: 103 us -> 96.9 us  [next_chip(): lax.ppermute(v, 'blk', [(2 * a + c, 2 * b + c) for a, b in moves for c in...]
    unnamed x126 -> x124, local copies, waits for them, and re-layouts: 13.4 us -> 11.1 us
where the time goes in v7:
time: 563 us; the launch traced here: 559 us
  waiting for transfers between devices  213 us (38%)
  Pallas kernels  112 us (20%)
  starting transfers between devices  69.1 us (12%)
  matrix products  63.8 us (11%)
  other arithmetic  45.3 us (8%)
  local copies, waits for them, and re-layouts  34.4 us (6%)
  between operations  20.8 us (4%)
    ppermute x72, waiting for transfers between devices, swap(): return lax.ppermute(v, axis, [(i, i ^ mask) for i in range(size)])  115 us
    ppermute x21, waiting for transfers between devices, next_chip(): lax.ppermute(v, 'blk', [(2 * a + c, 2 * b + c) for a, b in moves for c in...  96.9 us
    ppermute x72, starting transfers between devices, swap(): return lax.ppermute(v, axis, [(i, i ^ mask) for i in range(size)])  55.9 us
    pallas_call x4, Pallas kernels, attend_back(): pl.pallas_call(kernel, grid=(1 if rows <= 1024 else heads * tiles,), in_s...  30 us
    pallas_call x16, Pallas kernels, local_call(): pl.pallas_call(kernel, in_specs=[pl.BlockSpec(memory_space=pltpu.SMEM)] +...  29.4 us
    dot_general x3, matrix products, cross_rows(): lax.dot_general(left, right, (((0,), (0,)), ((), ())), preferred_element_...  25.1 us
    dot_general x12, matrix products, times_transposed(): lax.dot_general(left, right, (((1,), (1,)), ((), ())), preferred_element_...  19.6 us
    dot_general x6, matrix products, matmul(): return jnp.dot(left, right, preferred_element_type=f32)  19.1 us
  transfers between devices with their start and end apart: 100, of which 50 were waited for; matrix products, arithmetic and copies ran while one was open for 23% of the time, Pallas kernels for 20%

profile of v7, /device:TPU:8, one launch (start us, length us, event | category | flops | bytes accessed | tf_op | source)
XLA Modules:
  0.0 558.8 jit_solution(8570558994088942892)
XLA Ops:
  19.6 4.7 collective-permute-done.1.refs_1_.refs_3_
  25.8 3.0 collective-permute-start.4
  35.4 5.0 collective-permute-done.9
  41.6 3.5 collective-permute-done.5.refs_3_
  51.0 2.3 split_up.1
  53.3 8.2 %collective-permute-done.16.refs_2_.refs_4_ = bf16[128,2048]{1,0:T(8,128)(2,1)S(1)} collective-permute-done((bf16[128,2048]{1,0:T(8,128)(2,1)S(1)}, bf16[128,2048]{1,0:T(8,128)(2,1)S(1)}, u32[]{:S(2)}, u32[]{:S(2)}) %collective-permute-start.16) | collective-permute-done | bytes 524320 | tf_op jit(solution)/shard_map/tokens_gather/ppermute | solution.py:66
  72.0 4.1 collective-permute-done.13.refs_16_
  77.2 5.1 collective-permute-done.15.refs_18_
  88.8 13.4 %project_in.1 = (bf16[1024,256]{1,0:T(8,128)(2,1)}, bf16[2,1024,256]{2,1,0:T(8,128)(2,1)}, bf16[1024,2048]{1,0:T(8,128)(2,1)}, bf16[2048,768]{1,0:T(8,128)(2,1)}) custom-call(s32[13]{0:T(128)} %pad_add_fusion.1.at_ref, bf16[128,2048]{1,0:T(8,128)(2,1)} %refs_2_.2, bf16[128,2048]{1,0:T(8,128)(2,1)} %copy-done.42, bf16[128,2048]{1,0:T(8,128)(2,1)} %copy-done.44, ...), custom_call_target="tpu_custom_call" | custom-call | flops 3221225472 | bytes 16777216 | tf_op jit(solution)/shard_map/qkv/project_in/pallas_call | solution.py:508
  107.9 2.3 convert_reduce_fusion
  110.2 6.3 %attend.2 = (f32[1024,256]{1,0:T(8,128)}, f32[2,2,1024]{2,1,0:T(2,128)}) custom-call(s32[4]{0:T(128)} %get-tuple-element.372.heads_ref.at_ref, s32[1,1024]{1,0:T(1,128)} %bitcast.255, bf16[1024,256]{1,0:T(8,128)(2,1)} %get-tuple-element.434.query_ref, bf16[2,1024,256]{2,1,0:T(8,128)(2,1)} %get-tuple-element.432.refs_0_), custom_call_target="tpu_custom_call" | custom-call | flops 536870912 | bytes 1048576 | tf_op jit(solution)/shard_map/attention/attend/pallas_call | solution.py:386
  116.4 7.6 %collective-permute-done.29.refs_2_ = bf16[2,64,1024]{2,1,0:T(8,128)(2,1)S(1)} collective-permute-done((bf16[2,64,1024]{2,1,0:T(8,128)(2,1)S(1)}, bf16[2,64,1024]{2,1,0:T(8,128)(2,1)S(1)}, u32[]{:S(2)}, u32[]{:S(2)}) %collective-permute-start.29) | collective-permute-done | bytes 262176 | tf_op jit(solution)/shard_map/up_weights/ppermute | solution.py:55
  124.1 5.3 collective-permute-done.30.refs_3_
  136.5 9.4 %collective-permute-done.31.refs_2_.refs_0_ = bf16[1,1024,256]{2,1,0:T(8,128)(2,1)S(1)} collective-permute-done((bf16[1,1024,256]{2,1,0:T(8,128)(2,1)S(1)}, bf16[1,1024,256]{2,1,0:T(8,128)(2,1)S(1)}, u32[]{:S(2)}, u32[]{:S(2)}) %collective-permute-start.31) | collective-permute-done | bytes 524320 | tf_op jit(solution)/shard_map/kv_gather/ppermute | solution.py:55
  145.9 2.3 collective-permute-done.32.refs_3_.refs_1_
  151.0 12.7 %attend.3 = (bf16[1024,256]{1,0:T(8,128)(2,1)}, f32[2,1,1024]{2,1,0:T(1,128)}) custom-call(s32[4]{0:T(128)} %get-tuple-element.372.heads_ref.at_ref, s32[1,1024]{1,0:T(1,128)} %bitcast.256, bf16[1024,256]{1,0:T(8,128)(2,1)} %get-tuple-element.434.query_ref, bf16[2,1024,256]{2,1,0:T(8,128)(2,1)} %collective-permute-done.26.refs_0_, ...), custom_call_target="tpu_custom_call" | custom-call | flops 1610612736 | bytes 3145728 | tf_op jit(solution)/shard_map/attention/attend/pallas_call | solution.py:386
  163.8 5.4 terms_out.2
  169.2 4.4 collective-permute-done.36
  175.5 14.5 %collective-permute-done.37 = bf16[128,2048]{1,0:T(8,128)(2,1)S(1)} collective-permute-done((bf16[128,2048]{1,0:T(8,128)(2,1)S(1)}, bf16[128,2048]{1,0:T(8,128)(2,1)S(1)}, u32[]{:S(2)}, u32[]{:S(2)}) %collective-permute-start.37) | collective-permute-done | bytes 524320 | tf_op jit(solution)/shard_map/branch/ppermute | solution.py:66
  193.8 8.9 %collective-permute-done.39.refs_3_ = bf16[64,2048]{1,0:T(8,128)(2,1)S(1)} collective-permute-done((bf16[64,2048]{1,0:T(8,128)(2,1)S(1)}, bf16[64,2048]{1,0:T(8,128)(2,1)S(1)}, u32[]{:S(2)}, u32[]{:S(2)}) %collective-permute-start.39) | collective-permute-done | bytes 262176 | tf_op jit(solution)/shard_map/branch/down_weights/ppermute | solution.py:55
  207.5 13.0 %collective-permute-done.41 = bf16[128,2048]{1,0:T(8,128)(2,1)S(1)} collective-permute-done((bf16[128,2048]{1,0:T(8,128)(2,1)S(1)}, bf16[128,2048]{1,0:T(8,128)(2,1)S(1)}, u32[]{:S(2)}, u32[]{:S(2)}) %collective-permute-start.41) | collective-permute-done | bytes 524320 | tf_op jit(solution)/shard_map/branch/ppermute | solution.py:66
  220.5 2.3 fusion.114
  241.0 4.8 fusion.49
  245.8 2.9 constant_dynamic-update-slice_fusion.9
  256.9 2.8 fusion.50
  264.3 3.2 collective-permute-done.46
  269.7 2.6 fusion.51
  280.1 2.6 fusion.52
  287.3 5.0 collective-permute-done.50
  293.4 8.5 %convolution_convert_fusion.2 = bf16[2048,1024]{1,0:T(8,128)(2,1)} fusion(bf16[1024,2048]{1,0:T(8,128)(2,1)} %constant_dynamic-update-slice_fusion.1, bf16[1024,1024]{1,0:T(8,128)(2,1)S(1)} %get-tuple-element.562), kind=kOutput, calls=%fused_computation.4 | convolution fusion | flops 4297064448 | bytes 10485760 | tf_op jit(solution)/shard_map/mlp/up_grad/dot_general | solution.py:29
  301.9 5.6 %collective-permute-done.52 = bf16[128,2048]{1,0:T(8,128)(2,1)S(1)} collective-permute-done((bf16[128,2048]{1,0:T(8,128)(2,1)}, bf16[128,2048]{1,0:T(8,128)(2,1)S(1)}, u32[]{:S(2)}, u32[]{:S(2)}) %collective-permute-start.52) | collective-permute-done | bytes 524320 | tf_op jit(solution)/shard_map/mlp/ppermute | solution.py:66
  308.9 9.6 %convolution_convert_fusion.1 = bf16[1024,2048]{1,0:T(8,128)(2,1)} fusion(bf16[1024,1024]{1,0:T(8,128)(2,1)} %copy-done.38, bf16[1024,2048]{1,0:T(8,128)(2,1)} %all-gather.5.cloned.1.call-done), kind=kOutput, calls=%fused_computation.3 | convolution fusion | flops 4297064448 | bytes 10485760 | tf_op jit(solution)/shard_map/mlp/down_grad/dot_general | solution.py:29
  318.4 3.5 collective-permute-done.54
  326.7 2.8 collective-permute-start.57
  329.5 6.0 %convolution_convert_fusion = bf16[1024,2048]{1,0:T(8,128)(2,1)} fusion(bf16[1024,1024]{1,0:T(8,128)(2,1)S(1)} %copy-done.39, bf16[1024,2048]{1,0:T(8,128)(2,1)S(1)} %bitcast.216), kind=kOutput, calls=%fused_computation.2 | convolution fusion | flops 4297064448 | bytes 10485760 | tf_op jit(solution)/shard_map/d_branch_gather/output/dot_general | solution.py:25
  336.6 4.7 collective-permute-done.57
  342.6 4.2 collective-permute-done.58
  347.6 4.8 collective-permute-done.59
  354.4 3.6 collective-permute-done.60
  358.1 3.4 collective-permute-done.61
  363.7 4.2 mix_back.2.refs_6_
  368.8 4.6 mix_back.3
  373.5 7.1 %attend_back.4 = (f32[1024,256]{1,0:T(8,128)}, bf16[1024,256]{1,0:T(8,128)(2,1)}, bf16[1024,256]{1,0:T(8,128)(2,1)}) custom-call(s32[4]{0:T(128)} %get-tuple-element.372.heads_ref.at_ref, s32[1,1024]{1,0:T(1,128)} %bitcast.257, f32[2,1,1024]{2,1,0:T(1,128)} %get-tuple-element.490.log_ref, f32[2,1,1024]{2,1,0:T(1,128)} %get-tuple-element.569.delta_ref, ...), custom_call_target="tpu_custom_call" | custom-call | flops 1342177280 | bytes 5242880 | tf_op jit(solution)/shard_map/attention_back/attend_back/pallas_call | solution.py:449
  382.6 7.4 %attend_back.5 = (f32[1024,256]{1,0:T(8,128)}, bf16[1024,256]{1,0:T(8,128)(2,1)}, bf16[1024,256]{1,0:T(8,128)(2,1)}) custom-call(s32[4]{0:T(128)} %get-tuple-element.372.heads_ref.at_ref, s32[1,1024]{1,0:T(1,128)} %bitcast.258, f32[2,1,1024]{2,1,0:T(1,128)} %get-tuple-element.490.log_ref, f32[2,1,1024]{2,1,0:T(1,128)} %get-tuple-element.569.delta_ref, ...), custom_call_target="tpu_custom_call" | custom-call | flops 1342177280 | bytes 5242880 | tf_op jit(solution)/shard_map/attention_back/attend_back/pallas_call | solution.py:449
  390.0 8.0 %attend_back.6 = (f32[1024,256]{1,0:T(8,128)}, bf16[1024,256]{1,0:T(8,128)(2,1)}, bf16[1024,256]{1,0:T(8,128)(2,1)}) custom-call(s32[4]{0:T(128)} %get-tuple-element.372.heads_ref.at_ref, s32[1,1024]{1,0:T(1,128)} %bitcast.259, f32[2,1,1024]{2,1,0:T(1,128)} %get-tuple-element.490.log_ref, f32[2,1,1024]{2,1,0:T(1,128)} %get-tuple-element.569.delta_ref, ...), custom_call_target="tpu_custom_call" | custom-call | flops 1342177280 | bytes 5242880 | tf_op jit(solution)/shard_map/attention_back/attend_back/pallas_call | solution.py:449
  402.5 7.4 %attend_back.7 = (f32[1024,256]{1,0:T(8,128)}, bf16[1024,256]{1,0:T(8,128)(2,1)}, bf16[1024,256]{1,0:T(8,128)(2,1)}) custom-call(s32[4]{0:T(128)} %get-tuple-element.372.heads_ref.at_ref, s32[1,1024]{1,0:T(1,128)} %bitcast.260, f32[2,1,1024]{2,1,0:T(1,128)} %get-tuple-element.490.log_ref, f32[2,1,1024]{2,1,0:T(1,128)} %get-tuple-element.569.delta_ref, ...), custom_call_target="tpu_custom_call" | custom-call | flops 1342177280 | bytes 5242880 | tf_op jit(solution)/shard_map/attention_back/attend_back/pallas_call | solution.py:449
  410.6 4.3 collective-permute-done.68
  422.1 6.1 %mix_grad.1 = bf16[2,2,64,2048]{3,2,1,0:T(8,128)(2,1)} custom-call(s32[8]{0:T(128)} %add.539.at_ref, bf16[128,2048]{1,0:T(8,128)(2,1)} %copy-done.22, bf16[128,2048]{1,0:T(8,128)(2,1)} %copy-done.31, bf16[128,2048]{1,0:T(8,128)(2,1)} %copy-done.32, bf16[128,2048]{1,0:T(8,128)(2,1)} %copy-done.33, bf16[128,2048]{1,0:T(8,128)(2,1)} %copy-done.35, ...), custom_call_target="tpu_custom_call" | custom-call | tf_op jit(solution)/shard_map/out_grad/mix_grad/pallas_call | solution.py:141
  429.6 5.2 collective-permute-done.71
  434.8 2.5 collective-permute-done.72
  439.7 4.2 collective-permute-done.75.refs_3_
  443.9 7.7 %terms_out.3 = (bf16[4,128,2048]{2,1,0:T(8,128)(2,1)}, bf16[4,128,2048]{2,1,0:T(8,128)(2,1)}) custom-call(s32[8]{0:T(128)} %add.539.at_ref, bf16[1024,768]{1,0:T(8,128)(2,1)} %pad_maximum_fusion.source, bf16[2048,768]{1,0:T(8,128)(2,1)} %get-tuple-element.639.part), custom_call_target="tpu_custom_call" | custom-call | flops 3221225472 | bytes 8388608 | tf_op jit(solution)/shard_map/d_normed/terms_out/pallas_call | solution.py:561
  451.7 4.4 collective-permute-done.76
  457.8 7.0 %convolution_convert_fusion.3 = bf16[2048,768]{1,0:T(8,128)(2,1)S(1)} fusion(bf16[1024,2048]{1,0:T(8,128)(2,1)} %get-tuple-element.650, bf16[1024,768]{1,0:T(8,128)(2,1)} %pad_maximum_fusion.source), kind=kOutput, calls=%fused_computation.5 | convolution fusion | flops 3222798336 | bytes 8912896 | tf_op jit(solution)/shard_map/qkv_grad/dot_general | solution.py:29
  464.8 7.8 %collective-permute-done.77 = bf16[128,2048]{1,0:T(8,128)(2,1)S(1)} collective-permute-done((bf16[128,2048]{1,0:T(8,128)(2,1)S(1)}, bf16[128,2048]{1,0:T(8,128)(2,1)S(1)}, u32[]{:S(2)}, u32[]{:S(2)}) %collective-permute-start.77) | collective-permute-done | bytes 524320 | tf_op jit(solution)/shard_map/d_normed/ppermute | solution.py:66
  475.4 10.4 %collective-permute-done.79 = bf16[256,768]{1,0:T(8,128)(2,1)S(1)} collective-permute-done((bf16[256,768]{1,0:T(8,128)(2,1)S(1)}, bf16[256,768]{1,0:T(8,128)(2,1)S(1)}, u32[]{:S(2)}, u32[]{:S(2)}) %collective-permute-start.79) | collective-permute-done | bytes 393248 | tf_op jit(solution)/shard_map/qkv_grad/ppermute | solution.py:55
  486.1 3.2 collective-permute-done.78
  493.9 7.4 %norm_sums.1.first_ref = f32[2,2048]{1,0:T(2,128)} custom-call(bf16[4,128,2048]{2,1,0:T(8,128)(2,1)} %get-tuple-element.696.refs_0_, bf16[4,128,2048]{2,1,0:T(8,128)(2,1)} %get-tuple-element.663.refs_1_, bf16[128,2048]{1,0:T(8,128)(2,1)} %refs_2_.2, bf16[128,2048]{1,0:T(8,128)(2,1)} %copy-done.42, bf16[128,2048]{1,0:T(8,128)(2,1)} %copy-done.44, ...), custom_call_target="tpu_custom_call" | custom-call | tf_op jit(solution)/shard_map/vector_grads/norm_sums/pallas_call | solution.py:603
  503.1 3.0 collective-permute-done.84
  507.3 5.2 collective-permute-done.85
  521.5 2.7 collective-permute-start.90
  527.7 3.3 fusion.15
  535.0 6.3 %collective-permute-done.91.refs_2_ = bf16[2,80,768]{2,1,0:T(8,128)(2,1)S(1)} collective-permute-done((bf16[2,80,768]{2,1,0:T(8,128)(2,1)S(1)}, bf16[2,80,768]{2,1,0:T(8,128)(2,1)S(1)}, u32[]{:S(2)}, u32[]{:S(2)}) %collective-permute-start.91) | collective-permute-done | bytes 245792 | tf_op jit(solution)/shard_map/qkv_grad/ppermute | solution.py:55
  541.3 6.2 %collective-permute-done.92.refs_3_ = bf16[2,80,768]{2,1,0:T(8,128)(2,1)S(1)} collective-permute-done((bf16[2,80,768]{2,1,0:T(8,128)(2,1)S(1)}, bf16[2,80,768]{2,1,0:T(8,128)(2,1)S(1)}, u32[]{:S(2)}, u32[]{:S(2)}) %collective-permute-start.92) | collective-permute-done | bytes 245792 | tf_op jit(solution)/shard_map/qkv_grad/ppermute | solution.py:55
  (443 shorter events, 177.6 us)
Async XLA Ops:
  7.2 39.8 %all-gather.9.cloned.1.call-start = ((), (), s32[]{:S(2)}) async-start(), calls=%async_computation.10 | async-start | bytes 2621440 | tf_op jit(solution)/shard_map/down_weights/all_gather | solution.py:776
  9.4 180.6 %all-gather.5.cloned.1.call-start = ((), (), s32[]{:S(2)}) async-start(), calls=%async_computation.4 | async-start | bytes 4718592 | tf_op jit(solution)/shard_map/dy_gather/all_gather | solution.py:907
  9.4 14.8 %collective-permute-start.1 = (bf16[128,2048]{1,0:T(8,128)(2,1)}, bf16[128,2048]{1,0:T(8,128)(2,1)S(1)}, u32[]{:S(2)}, u32[]{:S(2)}) collective-permute-start(bf16[128,2048]{1,0:T(8,128)(2,1)} %refs_2_.2), channel_id=1, source_target_pairs={{0,4},{1,5},{4,6},{5,7},{6,2},{7,3},{2,0},{3,1},{8,12},{9,13},{12,... | collective-permute-start | bytes 1572872 | tf_op jit(solution)/shard_map/tokens_gather/ppermute | solution.py:66
  9.5 14.8 %collective-permute-start.2 = (bf16[128,2048]{1,0:T(8,128)(2,1)}, bf16[128,2048]{1,0:T(8,128)(2,1)S(1)}, u32[]{:S(2)}, u32[]{:S(2)}) collective-permute-start(bf16[128,2048]{1,0:T(8,128)(2,1)} %refs_2_.2), channel_id=1, source_target_pairs={{0,1},{1,0},{2,3},{3,2},{4,5},{5,4},{6,7},{7,6},{8,9},{9,8},{10,11... | collective-permute-start | bytes 1572872 | tf_op jit(solution)/shard_map/tokens_gather/ppermute | solution.py:55
  25.8 14.6 %collective-permute-start.3 = (bf16[2,64,768]{2,1,0:T(8,128)(2,1)S(1)}, bf16[2,64,768]{2,1,0:T(8,128)(2,1)S(1)}, u32[]{:S(2)}, u32[]{:S(2)}) collective-permute-start(bf16[2,64,768]{2,1,0:T(8,128)(2,1)S(1)} %get-tuple-element.376), channel_id=1, source_target_pairs={{0,2},{1,3},{2,0},{3,1},{4,6},{5,7},{6,4},{7,5},{8,10},{9,11},{10,... | collective-permute-start | bytes 589832 | tf_op jit(solution)/shard_map/qkv_weights/ppermute | solution.py:55
  25.8 15.8 %collective-permute-start.4 = (bf16[2,64,768]{2,1,0:T(8,128)(2,1)S(1)}, bf16[2,64,768]{2,1,0:T(8,128)(2,1)S(1)}, u32[]{:S(2)}, u32[]{:S(2)}) collective-permute-start(bf16[2,64,768]{2,1,0:T(8,128)(2,1)S(1)} %get-tuple-element.377), channel_id=1, source_target_pairs={{0,4},{1,5},{2,6},{3,7},{4,0},{5,1},{6,2},{7,3},{8,12},{9,13},{10,... | collective-permute-start | bytes 589832 | tf_op jit(solution)/shard_map/qkv_weights/ppermute | solution.py:55
  28.9 16.3 %collective-permute-start.5 = (bf16[2,64,768]{2,1,0:T(8,128)(2,1)S(1)}, bf16[2,64,768]{2,1,0:T(8,128)(2,1)S(1)}, u32[]{:S(2)}, u32[]{:S(2)}) collective-permute-start(bf16[2,64,768]{2,1,0:T(8,128)(2,1)S(1)} %get-tuple-element.378), channel_id=1, source_target_pairs={{0,6},{1,7},{2,4},{3,5},{4,2},{5,3},{6,0},{7,1},{8,14},{9,15},{10,... | collective-permute-start | bytes 589832 | tf_op jit(solution)/shard_map/qkv_weights/ppermute | solution.py:55
  47.0 14.6 %collective-permute-start.16 = (bf16[128,2048]{1,0:T(8,128)(2,1)S(1)}, bf16[128,2048]{1,0:T(8,128)(2,1)S(1)}, u32[]{:S(2)}, u32[]{:S(2)}) collective-permute-start(bf16[128,2048]{1,0:T(8,128)(2,1)S(1)} %collective-permute-done.1.refs_1_.refs_3_), channel_id=1, source_target_pairs={{0,4},{1,5},{4,6},{5,7},{6,2},{7,3},{2,0},{3,1},{8,12},{9,13},{12,... | collective-permute-start | bytes 1572872 | tf_op jit(solution)/shard_map/tokens_gather/ppermute | solution.py:66
  47.5 14.0 %collective-permute-start.17 = (bf16[128,2048]{1,0:T(8,128)(2,1)S(1)}, bf16[128,2048]{1,0:T(8,128)(2,1)S(1)}, u32[]{:S(2)}, u32[]{:S(2)}) collective-permute-start(bf16[128,2048]{1,0:T(8,128)(2,1)S(1)} %collective-permute-done.1.refs_1_.refs_3_), channel_id=1, source_target_pairs={{0,1},{1,0},{2,3},{3,2},{4,5},{5,4},{6,7},{7,6},{8,9},{9,8},{10,11... | collective-permute-start | bytes 1572872 | tf_op jit(solution)/shard_map/tokens_gather/ppermute | solution.py:55
  47.5 17.9 %collective-permute-start.12 = (bf16[4,64,768]{2,1,0:T(8,128)(2,1)S(1)}, bf16[4,64,768]{2,1,0:T(8,128)(2,1)}, u32[]{:S(2)}, u32[]{:S(2)}) collective-permute-start(bf16[4,64,768]{2,1,0:T(8,128)(2,1)S(1)} %get-tuple-element.412.refs_11_), channel_id=1, source_target_pairs={{0,16},{8,24},{16,0},{24,8},{1,17},{9,25},{17,1},{25,9},{2,18},{10... | collective-permute-start | bytes 1179656 | tf_op jit(solution)/shard_map/qkv_weights/ppermute | solution.py:55
  49.0 17.0 %collective-permute-start.11 = (bf16[4,64,768]{2,1,0:T(8,128)(2,1)S(1)}, bf16[4,64,768]{2,1,0:T(8,128)(2,1)}, u32[]{:S(2)}, u32[]{:S(2)}) collective-permute-start(bf16[4,64,768]{2,1,0:T(8,128)(2,1)S(1)} %get-tuple-element.413.refs_12_), channel_id=1, source_target_pairs={{0,8},{8,0},{16,24},{24,16},{1,9},{9,1},{17,25},{25,17},{2,10},{10... | collective-permute-start | bytes 1179656 | tf_op jit(solution)/shard_map/qkv_weights/ppermute | solution.py:55
  49.5 20.2 %collective-permute-start.10 = (bf16[4,64,768]{2,1,0:T(8,128)(2,1)S(1)}, bf16[4,64,768]{2,1,0:T(8,128)(2,1)}, u32[]{:S(2)}, u32[]{:S(2)}) collective-permute-start(bf16[4,64,768]{2,1,0:T(8,128)(2,1)S(1)} %get-tuple-element.412.refs_11_), channel_id=1, source_target_pairs={{0,8},{8,0},{16,24},{24,16},{1,9},{9,1},{17,25},{25,17},{2,10},{10... | collective-permute-start | bytes 1179656 | tf_op jit(solution)/shard_map/qkv_weights/ppermute | solution.py:55
  66.0 16.3 %collective-permute-start.15 = (bf16[4,64,768]{2,1,0:T(8,128)(2,1)}, bf16[4,64,768]{2,1,0:T(8,128)(2,1)}, u32[]{:S(2)}, u32[]{:S(2)}) collective-permute-start(bf16[4,64,768]{2,1,0:T(8,128)(2,1)} %collective-permute-done.11.refs_14_), channel_id=1, source_target_pairs={{0,16},{8,24},{16,0},{24,8},{1,17},{9,25},{17,1},{25,9},{2,18},{10... | collective-permute-start | bytes 1179656 | tf_op jit(solution)/shard_map/qkv_weights/ppermute | solution.py:55
  67.5 14.8 %collective-permute-start.18 = (bf16[128,2048]{1,0:T(8,128)(2,1)S(1)}, bf16[128,2048]{1,0:T(8,128)(2,1)}, u32[]{:S(2)}, u32[]{:S(2)}) collective-permute-start(bf16[128,2048]{1,0:T(8,128)(2,1)S(1)} %collective-permute-done.16.refs_2_.refs_4_), channel_id=1, source_target_pairs={{0,4},{1,5},{4,6},{5,7},{6,2},{7,3},{2,0},{3,1},{8,12},{9,13},{12,... | collective-permute-start | bytes 1572872 | tf_op jit(solution)/shard_map/tokens_gather/ppermute | solution.py:66
  69.7 12.6 %collective-permute-start.19 = (bf16[128,2048]{1,0:T(8,128)(2,1)S(1)}, bf16[128,2048]{1,0:T(8,128)(2,1)}, u32[]{:S(2)}, u32[]{:S(2)}) collective-permute-start(bf16[128,2048]{1,0:T(8,128)(2,1)S(1)} %collective-permute-done.16.refs_2_.refs_4_), channel_id=1, source_target_pairs={{0,1},{1,0},{2,3},{3,2},{4,5},{5,4},{6,7},{7,6},{8,9},{9,8},{10,11... | collective-permute-start | bytes 1572872 | tf_op jit(solution)/shard_map/tokens_gather/ppermute | solution.py:55
  82.8 19.4 %collective-permute-start.23 = (bf16[64,2048]{1,0:T(8,128)(2,1)S(1)}, bf16[64,2048]{1,0:T(8,128)(2,1)S(1)}, u32[]{:S(2)}, u32[]{:S(2)}) collective-permute-start(bf16[64,2048]{1,0:T(8,128)(2,1)S(1)} %copy-done.9), channel_id=1, source_target_pairs={{0,8},{8,0},{16,24},{24,16},{1,9},{9,1},{17,25},{25,17},{2,10},{10... | collective-permute-start | bytes 786440 | tf_op jit(solution)/shard_map/out_weights/ppermute | solution.py:55
  84.3 17.9 %collective-permute-start.24 = (bf16[64,2048]{1,0:T(8,128)(2,1)S(1)}, bf16[64,2048]{1,0:T(8,128)(2,1)S(1)}, u32[]{:S(2)}, u32[]{:S(2)}) collective-permute-start(bf16[64,2048]{1,0:T(8,128)(2,1)S(1)} %copy-done.9), channel_id=1, source_target_pairs={{0,16},{8,24},{16,0},{24,8},{1,17},{9,25},{17,1},{25,9},{2,18},{10... | collective-permute-start | bytes 786440 | tf_op jit(solution)/shard_map/out_weights/ppermute | solution.py:55
  84.8 17.4 %collective-permute-start.25 = (bf16[64,2048]{1,0:T(8,128)(2,1)S(1)}, bf16[64,2048]{1,0:T(8,128)(2,1)S(1)}, u32[]{:S(2)}, u32[]{:S(2)}) collective-permute-start(bf16[64,2048]{1,0:T(8,128)(2,1)S(1)} %copy-done.9), channel_id=1, source_target_pairs={{0,24},{8,16},{16,8},{24,0},{1,25},{9,17},{17,9},{25,1},{2,26},{10... | collective-permute-start | bytes 786440 | tf_op jit(solution)/shard_map/out_weights/ppermute | solution.py:55
  102.2 27.1 %collective-permute-start.26 = (bf16[2,1024,256]{2,1,0:T(8,128)(2,1)}, bf16[2,1024,256]{2,1,0:T(8,128)(2,1)}, u32[]{:S(2)}, u32[]{:S(2)}) collective-permute-start(bf16[2,1024,256]{2,1,0:T(8,128)(2,1)} %get-tuple-element.432.refs_0_), channel_id=1, source_target_pairs={{0,8},{8,0},{16,24},{24,16},{1,9},{9,1},{17,25},{25,17},{2,10},{10... | collective-permute-start | bytes 3145736 | tf_op jit(solution)/shard_map/kv_gather/ppermute | solution.py:55
  103.8 25.6 %collective-permute-start.27 = (bf16[2,1024,256]{2,1,0:T(8,128)(2,1)}, bf16[2,1024,256]{2,1,0:T(8,128)(2,1)}, u32[]{:S(2)}, u32[]{:S(2)}) collective-permute-start(bf16[2,1024,256]{2,1,0:T(8,128)(2,1)} %get-tuple-element.432.refs_0_), channel_id=1, source_target_pairs={{0,16},{8,24},{16,0},{24,8},{1,17},{9,25},{17,1},{25,9},{2,18},{10... | collective-permute-start | bytes 3145736 | tf_op jit(solution)/shard_map/kv_gather/ppermute | solution.py:55
  105.8 18.3 %collective-permute-start.29 = (bf16[2,64,1024]{2,1,0:T(8,128)(2,1)S(1)}, bf16[2,64,1024]{2,1,0:T(8,128)(2,1)S(1)}, u32[]{:S(2)}, u32[]{:S(2)}) collective-permute-start(bf16[2,64,1024]{2,1,0:T(8,128)(2,1)S(1)} %get-tuple-element.439), channel_id=1, source_target_pairs={{0,4},{1,5},{2,6},{3,7},{4,0},{5,1},{6,2},{7,3},{8,12},{9,13},{10,... | collective-permute-start | bytes 786440 | tf_op jit(solution)/shard_map/up_weights/ppermute | solution.py:55
  106.1 23.3 %collective-permute-start.30 = (bf16[2,64,1024]{2,1,0:T(8,128)(2,1)S(1)}, bf16[2,64,1024]{2,1,0:T(8,128)(2,1)S(1)}, u32[]{:S(2)}, u32[]{:S(2)}) collective-permute-start(bf16[2,64,1024]{2,1,0:T(8,128)(2,1)S(1)} %get-tuple-element.440), channel_id=1, source_target_pairs={{0,6},{1,7},{2,4},{3,5},{4,2},{5,3},{6,0},{7,1},{8,14},{9,15},{10,... | collective-permute-start | bytes 786440 | tf_op jit(solution)/shard_map/up_weights/ppermute | solution.py:55
  129.4 111.6 %all-gather.7.cloned.1.call-start = ((), (), s32[]{:S(2)}) async-start(), calls=%async_computation.5 | async-start | bytes 5242880 | tf_op jit(solution)/shard_map/up_weights/all_gather | solution.py:929
  131.5 14.4 %collective-permute-start.31 = (bf16[1,1024,256]{2,1,0:T(8,128)(2,1)S(1)}, bf16[1,1024,256]{2,1,0:T(8,128)(2,1)S(1)}, u32[]{:S(2)}, u32[]{:S(2)}) collective-permute-start(bf16[1,1024,256]{2,1,0:T(8,128)(2,1)S(1)} %slice.272), channel_id=1, source_target_pairs={{0,8},{8,0},{16,24},{24,16},{1,9},{9,1},{17,25},{25,17},{2,10},{10... | collective-permute-start | bytes 1572872 | tf_op jit(solution)/shard_map/kv_gather/ppermute | solution.py:55
  134.1 14.1 %collective-permute-start.32 = (bf16[1,1024,256]{2,1,0:T(8,128)(2,1)S(1)}, bf16[1,1024,256]{2,1,0:T(8,128)(2,1)S(1)}, u32[]{:S(2)}, u32[]{:S(2)}) collective-permute-start(bf16[1,1024,256]{2,1,0:T(8,128)(2,1)S(1)} %slice.273), channel_id=1, source_target_pairs={{0,16},{8,24},{16,0},{24,8},{1,17},{9,25},{17,1},{25,9},{2,18},{10... | collective-permute-start | bytes 1572872 | tf_op jit(solution)/shard_map/kv_gather/ppermute | solution.py:55
  149.0 14.8 %collective-permute-start.34 = (bf16[128,2048]{1,0:T(8,128)(2,1)S(1)}, bf16[128,2048]{1,0:T(8,128)(2,1)S(1)}, u32[]{:S(2)}, u32[]{:S(2)}) collective-permute-start(bf16[128,2048]{1,0:T(8,128)(2,1)S(1)} %get-tuple-element.498.refs_0_), channel_id=1, source_target_pairs={{0,8},{8,0},{16,24},{24,16},{1,9},{9,1},{17,25},{25,17},{2,10},{10... | collective-permute-start | bytes 1572872 | tf_op jit(solution)/shard_map/down_weights/ppermute | solution.py:55
  149.6 14.2 %collective-permute-start.35 = (bf16[128,2048]{1,0:T(8,128)(2,1)S(1)}, bf16[128,2048]{1,0:T(8,128)(2,1)S(1)}, u32[]{:S(2)}, u32[]{:S(2)}) collective-permute-start(bf16[128,2048]{1,0:T(8,128)(2,1)S(1)} %get-tuple-element.498.refs_0_), channel_id=1, source_target_pairs={{0,16},{8,24},{16,0},{24,8},{1,17},{9,25},{17,1},{25,9},{2,18},{10... | collective-permute-start | bytes 1572872 | tf_op jit(solution)/shard_map/down_weights/ppermute | solution.py:55
  169.2 192.3 %reduce-scatter.5.cloned.1.call-start = ((), (), s32[]{:S(2)}) async-start(), calls=%async_computation.6 | async-start | bytes 5242880 | tf_op jit(solution)/shard_map/up_grad/reduce_scatter | solution.py:1069
  175.0 15.0 %collective-permute-start.37 = (bf16[128,2048]{1,0:T(8,128)(2,1)S(1)}, bf16[128,2048]{1,0:T(8,128)(2,1)S(1)}, u32[]{:S(2)}, u32[]{:S(2)}) collective-permute-start(bf16[128,2048]{1,0:T(8,128)(2,1)S(1)} %fusion.48), channel_id=1, source_target_pairs={{0,4},{1,5},{4,6},{5,7},{6,2},{7,3},{2,0},{3,1},{8,12},{9,13},{12,... | collective-permute-start | bytes 1572872 | tf_op jit(solution)/shard_map/branch/ppermute | solution.py:66
  191.4 14.1 %collective-permute-start.38 = (bf16[128,2048]{1,0:T(8,128)(2,1)S(1)}, bf16[128,2048]{1,0:T(8,128)(2,1)S(1)}, u32[]{:S(2)}, u32[]{:S(2)}) collective-permute-start(bf16[128,2048]{1,0:T(8,128)(2,1)S(1)} %fusion.38), channel_id=1, source_target_pairs={{0,4},{1,5},{4,6},{5,7},{6,2},{7,3},{2,0},{3,1},{8,12},{9,13},{12,... | collective-permute-start | bytes 1572872 | tf_op jit(solution)/shard_map/branch/ppermute | solution.py:66
  207.0 13.4 %collective-permute-start.41 = (bf16[128,2048]{1,0:T(8,128)(2,1)S(1)}, bf16[128,2048]{1,0:T(8,128)(2,1)S(1)}, u32[]{:S(2)}, u32[]{:S(2)}) collective-permute-start(bf16[128,2048]{1,0:T(8,128)(2,1)S(1)} %fusion.37), channel_id=1, source_target_pairs={{0,4},{1,5},{4,6},{5,7},{6,2},{7,3},{2,0},{3,1},{8,12},{9,13},{12,... | collective-permute-start | bytes 1572872 | tf_op jit(solution)/shard_map/branch/ppermute | solution.py:66
  224.5 12.6 %collective-permute-start.42 = (bf16[128,2048]{1,0:T(8,128)(2,1)}, bf16[128,2048]{1,0:T(8,128)(2,1)}, u32[]{:S(2)}, u32[]{:S(2)}) collective-permute-start(bf16[128,2048]{1,0:T(8,128)(2,1)} %get-tuple-element.493), channel_id=1, source_target_pairs={{0,4},{1,5},{4,6},{5,7},{6,2},{7,3},{2,0},{3,1},{8,12},{9,13},{12,... | collective-permute-start | bytes 1572872 | tf_op jit(solution)/shard_map/mlp/ppermute | solution.py:66
  224.5 12.6 %collective-permute-start.43 = (bf16[128,2048]{1,0:T(8,128)(2,1)}, bf16[128,2048]{1,0:T(8,128)(2,1)}, u32[]{:S(2)}, u32[]{:S(2)}) collective-permute-start(bf16[128,2048]{1,0:T(8,128)(2,1)} %get-tuple-element.493), channel_id=1, source_target_pairs={{0,1},{1,0},{2,3},{3,2},{4,5},{5,4},{6,7},{7,6},{8,9},{9,8},{10,11... | collective-permute-start | bytes 1572872 | tf_op jit(solution)/shard_map/mlp/ppermute | solution.py:55
  237.1 14.7 %collective-permute-start.44 = (bf16[128,2048]{1,0:T(8,128)(2,1)}, bf16[128,2048]{1,0:T(8,128)(2,1)S(1)}, u32[]{:S(2)}, u32[]{:S(2)}) collective-permute-start(bf16[128,2048]{1,0:T(8,128)(2,1)} %collective-permute-done.42), channel_id=1, source_target_pairs={{0,4},{1,5},{4,6},{5,7},{6,2},{7,3},{2,0},{3,1},{8,12},{9,13},{12,... | collective-permute-start | bytes 1572872 | tf_op jit(solution)/shard_map/mlp/ppermute | solution.py:66
  237.1 14.7 %collective-permute-start.45 = (bf16[128,2048]{1,0:T(8,128)(2,1)}, bf16[128,2048]{1,0:T(8,128)(2,1)S(1)}, u32[]{:S(2)}, u32[]{:S(2)}) collective-permute-start(bf16[128,2048]{1,0:T(8,128)(2,1)} %collective-permute-done.42), channel_id=1, source_target_pairs={{0,1},{1,0},{2,3},{3,2},{4,5},{5,4},{6,7},{7,6},{8,9},{9,8},{10,11... | collective-permute-start | bytes 1572872 | tf_op jit(solution)/shard_map/mlp/ppermute | solution.py:55
  251.8 15.7 %collective-permute-start.46 = (bf16[128,2048]{1,0:T(8,128)(2,1)S(1)}, bf16[128,2048]{1,0:T(8,128)(2,1)S(1)}, u32[]{:S(2)}, u32[]{:S(2)}) collective-permute-start(bf16[128,2048]{1,0:T(8,128)(2,1)S(1)} %collective-permute-done.44), channel_id=1, source_target_pairs={{0,4},{1,5},{4,6},{5,7},{6,2},{7,3},{2,0},{3,1},{8,12},{9,13},{12,... | collective-permute-start | bytes 1572872 | tf_op jit(solution)/shard_map/mlp/ppermute | solution.py:66
  254.0 13.6 %collective-permute-start.47 = (bf16[128,2048]{1,0:T(8,128)(2,1)S(1)}, bf16[128,2048]{1,0:T(8,128)(2,1)S(1)}, u32[]{:S(2)}, u32[]{:S(2)}) collective-permute-start(bf16[128,2048]{1,0:T(8,128)(2,1)S(1)} %collective-permute-done.44), channel_id=1, source_target_pairs={{0,1},{1,0},{2,3},{3,2},{4,5},{5,4},{6,7},{7,6},{8,9},{9,8},{10,11... | collective-permute-start | bytes 1572872 | tf_op jit(solution)/shard_map/mlp/ppermute | solution.py:55
  277.1 15.2 %collective-permute-start.50 = (bf16[128,2048]{1,0:T(8,128)(2,1)S(1)}, bf16[128,2048]{1,0:T(8,128)(2,1)S(1)}, u32[]{:S(2)}, u32[]{:S(2)}) collective-permute-start(bf16[128,2048]{1,0:T(8,128)(2,1)S(1)} %add_convert_fusion.8), channel_id=1, source_target_pairs={{0,4},{1,5},{4,6},{5,7},{6,2},{7,3},{2,0},{3,1},{8,12},{9,13},{12,... | collective-permute-start | bytes 1572872 | tf_op jit(solution)/shard_map/mlp/ppermute | solution.py:66
  278.4 14.0 %collective-permute-start.51 = (bf16[128,2048]{1,0:T(8,128)(2,1)S(1)}, bf16[128,2048]{1,0:T(8,128)(2,1)S(1)}, u32[]{:S(2)}, u32[]{:S(2)}) collective-permute-start(bf16[128,2048]{1,0:T(8,128)(2,1)S(1)} %convolution_convert_fusion.6), channel_id=1, source_target_pairs={{0,1},{1,0},{2,3},{3,2},{4,5},{5,4},{6,7},{7,6},{8,9},{9,8},{10,11... | collective-permute-start | bytes 1572872 | tf_op jit(solution)/shard_map/mlp/ppermute | solution.py:55
  293.4 14.1 %collective-permute-start.52 = (bf16[128,2048]{1,0:T(8,128)(2,1)}, bf16[128,2048]{1,0:T(8,128)(2,1)S(1)}, u32[]{:S(2)}, u32[]{:S(2)}) collective-permute-start(bf16[128,2048]{1,0:T(8,128)(2,1)} %add_convert_fusion.7), channel_id=1, source_target_pairs={{0,4},{1,5},{4,6},{5,7},{6,2},{7,3},{2,0},{3,1},{8,12},{9,13},{12,... | collective-permute-start | bytes 1572872 | tf_op jit(solution)/shard_map/mlp/ppermute | solution.py:66
  293.4 14.1 %collective-permute-start.53 = (bf16[128,2048]{1,0:T(8,128)(2,1)S(1)}, bf16[128,2048]{1,0:T(8,128)(2,1)S(1)}, u32[]{:S(2)}, u32[]{:S(2)}) collective-permute-start(bf16[128,2048]{1,0:T(8,128)(2,1)S(1)} %convolution_convert_fusion.4), channel_id=1, source_target_pairs={{0,1},{1,0},{2,3},{3,2},{4,5},{5,4},{6,7},{7,6},{8,9},{9,8},{10,11... | collective-permute-start | bytes 1572872 | tf_op jit(solution)/shard_map/mlp/ppermute | solution.py:55
  307.5 107.7 %reduce-scatter.7.cloned.1.call-start = ((), (), s32[]{:S(2)}) async-start(), calls=%async_computation.7 | async-start | bytes 4718592 | tf_op jit(solution)/shard_map/d_branch_gather/output/reduce_scatter | solution.py:1102
  308.6 13.3 %collective-permute-start.54 = (bf16[128,2048]{1,0:T(8,128)(2,1)}, bf16[128,2048]{1,0:T(8,128)(2,1)S(1)}, u32[]{:S(2)}, u32[]{:S(2)}) collective-permute-start(bf16[128,2048]{1,0:T(8,128)(2,1)} %add_convert_fusion.6), channel_id=1, source_target_pairs={{0,4},{1,5},{4,6},{5,7},{6,2},{7,3},{2,0},{3,1},{8,12},{9,13},{12,... | collective-permute-start | bytes 1572872 | tf_op jit(solution)/shard_map/mlp/ppermute | solution.py:66
  308.8 13.2 %collective-permute-start.55 = (bf16[128,2048]{1,0:T(8,128)(2,1)S(1)}, bf16[128,2048]{1,0:T(8,128)(2,1)}, u32[]{:S(2)}, u32[]{:S(2)}) collective-permute-start(bf16[128,2048]{1,0:T(8,128)(2,1)S(1)} %convolution_convert_fusion.10), channel_id=1, source_target_pairs={{0,1},{1,0},{2,3},{3,2},{4,5},{5,4},{6,7},{7,6},{8,9},{9,8},{10,11... | collective-permute-start | bytes 1572872 | tf_op jit(solution)/shard_map/mlp/ppermute | solution.py:55
  326.7 14.6 %collective-permute-start.57 = (bf16[64,2048]{1,0:T(8,128)(2,1)}, bf16[64,2048]{1,0:T(8,128)(2,1)}, u32[]{:S(2)}, u32[]{:S(2)}) collective-permute-start(bf16[64,2048]{1,0:T(8,128)(2,1)} %get-tuple-element.742), channel_id=1, source_target_pairs={{0,4},{1,5},{4,6},{5,7},{6,2},{7,3},{2,0},{3,1},{8,12},{9,13},{12,... | collective-permute-start | bytes 786440 | tf_op jit(solution)/shard_map/d_branch_gather/ppermute | solution.py:66
  361.5 144.5 %reduce-scatter.9.cloned.1.call-start = ((), (), s32[]{:S(2)}) async-start(), calls=%async_computation.8 | async-start | bytes 5242880 | tf_op jit(solution)/shard_map/down_grad/reduce_scatter | solution.py:1069
  380.5 17.5 %collective-permute-start.66 = (bf16[1024,256]{1,0:T(8,128)(2,1)}, bf16[1024,256]{1,0:T(8,128)(2,1)S(1)}, u32[]{:S(2)}, u32[]{:S(2)}) collective-permute-start(bf16[1024,256]{1,0:T(8,128)(2,1)} %get-tuple-element.574), channel_id=1, source_target_pairs={{0,8},{8,0},{16,24},{24,16},{1,9},{9,1},{17,25},{25,17},{2,10},{10... | collective-permute-start | bytes 1572872 | tf_op jit(solution)/shard_map/attention_back/ppermute | solution.py:55
  382.0 16.1 %collective-permute-start.67 = (bf16[1024,256]{1,0:T(8,128)(2,1)}, bf16[1024,256]{1,0:T(8,128)(2,1)S(1)}, u32[]{:S(2)}, u32[]{:S(2)}) collective-permute-start(bf16[1024,256]{1,0:T(8,128)(2,1)} %get-tuple-element.575), channel_id=1, source_target_pairs={{0,16},{8,24},{16,0},{24,8},{1,17},{9,25},{17,1},{25,9},{2,18},{10... | collective-permute-start | bytes 1572872 | tf_op jit(solution)/shard_map/attention_back/ppermute | solution.py:55
  400.4 14.4 %collective-permute-start.68 = (bf16[1024,256]{1,0:T(8,128)(2,1)S(1)}, bf16[1024,256]{1,0:T(8,128)(2,1)}, u32[]{:S(2)}, u32[]{:S(2)}) collective-permute-start(bf16[1024,256]{1,0:T(8,128)(2,1)S(1)} %copy-done.59), channel_id=1, source_target_pairs={{0,8},{8,0},{16,24},{24,16},{1,9},{9,1},{17,25},{25,17},{2,10},{10... | collective-permute-start | bytes 1572872 | tf_op jit(solution)/shard_map/attention_back/ppermute | solution.py:55
  401.1 14.1 %collective-permute-start.69 = (bf16[1024,256]{1,0:T(8,128)(2,1)S(1)}, bf16[1024,256]{1,0:T(8,128)(2,1)}, u32[]{:S(2)}, u32[]{:S(2)}) collective-permute-start(bf16[1024,256]{1,0:T(8,128)(2,1)S(1)} %add_convert_fusion.4), channel_id=1, source_target_pairs={{0,16},{8,24},{16,0},{24,8},{1,17},{9,25},{17,1},{25,9},{2,18},{10... | collective-permute-start | bytes 1572872 | tf_op jit(solution)/shard_map/attention_back/ppermute | solution.py:55
  415.2 134.8 %reduce-scatter.11.cloned.1.call-start = ((), (), s32[]{:S(2)}) async-start(), calls=%async_computation.9 | async-start | bytes 1310720 | tf_op jit(solution)/shard_map/out_grad/reduce_scatter | solution.py:1069
  415.3 19.5 %collective-permute-start.71 = (bf16[1024,256]{1,0:T(8,128)(2,1)}, bf16[1024,256]{1,0:T(8,128)(2,1)S(1)}, u32[]{:S(2)}, u32[]{:S(2)}) collective-permute-start(bf16[1024,256]{1,0:T(8,128)(2,1)} %add_convert_fusion.5), channel_id=1, source_target_pairs={{0,8},{8,0},{16,24},{24,16},{1,9},{9,1},{17,25},{25,17},{2,10},{10... | collective-permute-start | bytes 1572872 | tf_op jit(solution)/shard_map/attention_back/ppermute | solution.py:55
  416.8 20.5 %collective-permute-start.72 = (bf16[1024,256]{1,0:T(8,128)(2,1)}, bf16[1024,256]{1,0:T(8,128)(2,1)S(1)}, u32[]{:S(2)}, u32[]{:S(2)}) collective-permute-start(bf16[1024,256]{1,0:T(8,128)(2,1)} %get-tuple-element.624), channel_id=1, source_target_pairs={{0,16},{8,24},{16,0},{24,8},{1,17},{9,25},{17,1},{25,9},{2,18},{10... | collective-permute-start | bytes 1572872 | tf_op jit(solution)/shard_map/attention_back/ppermute | solution.py:55
  418.3 20.5 %collective-permute-start.73 = (bf16[2,64,1024]{2,1,0:T(8,128)(2,1)S(1)}, bf16[2,64,1024]{2,1,0:T(8,128)(2,1)S(1)}, u32[]{:S(2)}, u32[]{:S(2)}) collective-permute-start(bf16[2,64,1024]{2,1,0:T(8,128)(2,1)S(1)} %get-tuple-element.626), channel_id=1, source_target_pairs={{0,2},{1,3},{2,0},{3,1},{4,6},{5,7},{6,4},{7,5},{8,10},{9,11},{10,... | collective-permute-start | bytes 786440 | tf_op jit(solution)/shard_map/up_grad/ppermute | solution.py:55
  420.5 19.2 %collective-permute-start.74 = (bf16[2,64,1024]{2,1,0:T(8,128)(2,1)S(1)}, bf16[2,64,1024]{2,1,0:T(8,128)(2,1)S(1)}, u32[]{:S(2)}, u32[]{:S(2)}) collective-permute-start(bf16[2,64,1024]{2,1,0:T(8,128)(2,1)S(1)} %get-tuple-element.627), channel_id=1, source_target_pairs={{0,4},{1,5},{2,6},{3,7},{4,0},{5,1},{6,2},{7,3},{8,12},{9,13},{10,... | collective-permute-start | bytes 786440 | tf_op jit(solution)/shard_map/up_grad/ppermute | solution.py:55
  421.7 22.2 %collective-permute-start.75 = (bf16[2,64,1024]{2,1,0:T(8,128)(2,1)S(1)}, bf16[2,64,1024]{2,1,0:T(8,128)(2,1)S(1)}, u32[]{:S(2)}, u32[]{:S(2)}) collective-permute-start(bf16[2,64,1024]{2,1,0:T(8,128)(2,1)S(1)} %get-tuple-element.628), channel_id=1, source_target_pairs={{0,6},{1,7},{2,4},{3,5},{4,2},{5,3},{6,0},{7,1},{8,14},{9,15},{10,... | collective-permute-start | bytes 786440 | tf_op jit(solution)/shard_map/up_grad/ppermute | solution.py:55
  457.5 15.1 %collective-permute-start.77 = (bf16[128,2048]{1,0:T(8,128)(2,1)S(1)}, bf16[128,2048]{1,0:T(8,128)(2,1)S(1)}, u32[]{:S(2)}, u32[]{:S(2)}) collective-permute-start(bf16[128,2048]{1,0:T(8,128)(2,1)S(1)} %fusion.53), channel_id=1, source_target_pairs={{0,4},{1,5},{4,6},{5,7},{6,2},{7,3},{2,0},{3,1},{8,12},{9,13},{12,... | collective-permute-start | bytes 1572872 | tf_op jit(solution)/shard_map/d_normed/ppermute | solution.py:66
  474.1 15.2 %collective-permute-start.78 = (bf16[128,2048]{1,0:T(8,128)(2,1)S(1)}, bf16[128,2048]{1,0:T(8,128)(2,1)S(1)}, u32[]{:S(2)}, u32[]{:S(2)}) collective-permute-start(bf16[128,2048]{1,0:T(8,128)(2,1)S(1)} %fusion.35), channel_id=1, source_target_pairs={{0,4},{1,5},{4,6},{5,7},{6,2},{7,3},{2,0},{3,1},{8,12},{9,13},{12,... | collective-permute-start | bytes 1572872 | tf_op jit(solution)/shard_map/d_normed/ppermute | solution.py:66
  491.3 14.7 %collective-permute-start.84 = (bf16[128,2048]{1,0:T(8,128)(2,1)}, bf16[128,2048]{1,0:T(8,128)(2,1)}, u32[]{:S(2)}, u32[]{:S(2)}) collective-permute-start(bf16[128,2048]{1,0:T(8,128)(2,1)} %fusion.34), channel_id=1, source_target_pairs={{0,4},{1,5},{4,6},{5,7},{6,2},{7,3},{2,0},{3,1},{8,12},{9,13},{12,... | collective-permute-start | bytes 1572872 | tf_op jit(solution)/shard_map/d_normed/ppermute | solution.py:66
  491.6 23.1 %collective-permute-start.82 = (bf16[512,768]{1,0:T(8,128)(2,1)S(1)}, bf16[512,768]{1,0:T(8,128)(2,1)}, u32[]{:S(2)}, u32[]{:S(2)}) collective-permute-start(bf16[512,768]{1,0:T(8,128)(2,1)S(1)} %pad_maximum_fusion.1), channel_id=1, source_target_pairs={{0,8},{8,0},{16,24},{24,16},{1,9},{9,1},{17,25},{25,17},{2,10},{10... | collective-permute-start | bytes 2359304 | tf_op jit(solution)/shard_map/qkv_grad/ppermute | solution.py:55
  493.4 21.3 %collective-permute-start.83 = (bf16[512,768]{1,0:T(8,128)(2,1)}, bf16[512,768]{1,0:T(8,128)(2,1)}, u32[]{:S(2)}, u32[]{:S(2)}) collective-permute-start(bf16[512,768]{1,0:T(8,128)(2,1)} %pad_maximum_fusion.2), channel_id=1, source_target_pairs={{0,16},{8,24},{16,0},{24,8},{1,17},{9,25},{17,1},{25,9},{2,18},{10... | collective-permute-start | bytes 2359304 | tf_op jit(solution)/shard_map/qkv_grad/ppermute | solution.py:55
  521.5 13.5 %collective-permute-start.90 = (bf16[2,80,768]{2,1,0:T(8,128)(2,1)S(1)}, bf16[2,80,768]{2,1,0:T(8,128)(2,1)S(1)}, u32[]{:S(2)}, u32[]{:S(2)}) collective-permute-start(bf16[2,80,768]{2,1,0:T(8,128)(2,1)S(1)} %get-tuple-element.700), channel_id=1, source_target_pairs={{0,2},{1,3},{2,0},{3,1},{4,6},{5,7},{6,4},{7,5},{8,10},{9,11},{10,... | collective-permute-start | bytes 737288 | tf_op jit(solution)/shard_map/qkv_grad/ppermute | solution.py:55
  524.1 17.2 %collective-permute-start.91 = (bf16[2,80,768]{2,1,0:T(8,128)(2,1)S(1)}, bf16[2,80,768]{2,1,0:T(8,128)(2,1)S(1)}, u32[]{:S(2)}, u32[]{:S(2)}) collective-permute-start(bf16[2,80,768]{2,1,0:T(8,128)(2,1)S(1)} %get-tuple-element.701), channel_id=1, source_target_pairs={{0,4},{1,5},{2,6},{3,7},{4,0},{5,1},{6,2},{7,3},{8,12},{9,13},{10,... | collective-permute-start | bytes 737288 | tf_op jit(solution)/shard_map/qkv_grad/ppermute | solution.py:55
  524.4 23.1 %collective-permute-start.92 = (bf16[2,80,768]{2,1,0:T(8,128)(2,1)S(1)}, bf16[2,80,768]{2,1,0:T(8,128)(2,1)S(1)}, u32[]{:S(2)}, u32[]{:S(2)}) collective-permute-start(bf16[2,80,768]{2,1,0:T(8,128)(2,1)S(1)} %get-tuple-element.702), channel_id=1, source_target_pairs={{0,6},{1,7},{2,4},{3,5},{4,2},{5,3},{6,0},{7,1},{8,14},{9,15},{10,... | collective-permute-start | bytes 737288 | tf_op jit(solution)/shard_map/qkv_grad/ppermute | solution.py:55
  (96 other events, 1115.2 us)
Sparse Core Ops, SparseCore 0:
  10.5 36.4 all-gather.8
  129.5 44.0 all-gather.4
  175.5 56.4 all-gather.6
  307.7 51.7 reduce-scatter.4
  361.7 46.1 reduce-scatter.6
  415.4 58.0 reduce-scatter.8
  518.9 27.3 reduce-scatter.10
